TPU v7x, 32 devices: a whole 2x2x4 slice. The times are simulated.
32 devices in a mesh: dp: 8 (over y, x, core), fsdp: 4 (over z).
Axes of the slice: x: 2, y: 2, z: 4, core: 2. Of those that a mesh axis runs over, the one named last changes fastest.
Arguments:
- picture_encoder_outputs: bfloat16 [8192, 1152], P(('dp', 'fsdp')), may hold values from -6 to 6
- caption_encoder_vectors: bfloat16 [8192, 1152], P(('dp', 'fsdp')), may hold values from -6 to 6
- linear_map_matrix: bfloat16 [1152, 1152], P('fsdp'), may hold values from -0.1875 to 0.1875
- sharpness_learned: float32 [1], replicated, may hold values from 20 to 40
- shift_learned_bias: float32 [1], replicated, may hold values from -2 to 2
Outputs:
- head_grad: float32 [8, 1152, 1152], P('dp', 'fsdp')
- text_embedding_gradient: float32 [8192, 1152], P(('dp', 'fsdp'))
All inputs are finite; a program needn't handle non-finite values.
Results may differ from a plain program's by a relative error of at most 0.0095.
Values may be sent and summed in bfloat16 or wider, within the bound.
No kernel may reach another device: no remote copies, remote signals or barrier semaphores. Data moves between devices by JAX's collectives and lax.ppermute only.
A program may use at most 64 MiB of HBM per device.

v0:
```python
import jax
import jax.numpy as jnp
from jax import lax
from jax.sharding import PartitionSpec as P

STEPS = 3


def passed_along(value, axis, by):
    size = lax.axis_size(axis)
    return lax.ppermute(value, axis, [(i, (i + by) % size) for i in range(size)])


def body(
    picture_encoder_outputs,
    caption_encoder_vectors,
    linear_map_matrix,
    sharpness_learned,
    shift_learned_bias,
):
    rows = picture_encoder_outputs.shape[0]
    width = picture_encoder_outputs.shape[1]
    columns = picture_encoder_outputs
    proj = jnp.dot(
        columns,
        lax.all_gather(linear_map_matrix, "fsdp", axis=0, tiled=True),
        preferred_element_type=jnp.float32,
    )
    img_norm = jnp.sqrt(jnp.sum(proj * proj, axis=-1, keepdims=True) + 1e-06)
    img_dir = proj / img_norm
    photo_normalized = img_dir.astype(jnp.bfloat16)
    text_block_window = caption_encoder_vectors.astype(jnp.float32)
    txt_norm = jnp.sqrt(
        jnp.sum(text_block_window * text_block_window, axis=-1, keepdims=True) + 1e-06
    )
    txt_dir = text_block_window / txt_norm
    txt_unit = txt_dir.astype(jnp.bfloat16)
    sharpness_exponentiated = sharpness_learned[0]
    eye = jnp.eye(rows, dtype=jnp.float32)
    photo_slope_accumulated = jnp.zeros((rows, width), jnp.float32)
    pair_group_slot = txt_unit
    txt_grad = jnp.zeros((rows, width), jnp.float32)
    for step in range(STEPS):
        if step > 0:
            pair_group_slot = passed_along(pair_group_slot, "dp", 1)
        similarity_scores = (
            sharpness_exponentiated
            * jnp.dot(photo_normalized, pair_group_slot.T, preferred_element_type=jnp.float32)
            + shift_learned_bias[0]
        )
        loss_weight_coefficient = jax.nn.sigmoid(similarity_scores)
        if step == 0:
            loss_weight_coefficient = loss_weight_coefficient - eye
        loss_weight_coefficient = loss_weight_coefficient.astype(jnp.bfloat16)
        photo_local_share = sharpness_exponentiated * jnp.dot(
            loss_weight_coefficient, pair_group_slot, preferred_element_type=jnp.float32
        )
        wording_local_share = sharpness_exponentiated * lax.dot_general(
            loss_weight_coefficient,
            photo_normalized,
            (((0,), (0,)), ((), ())),
            preferred_element_type=jnp.float32,
        )
        photo_local_share, wording_local_share = (photo_local_share, wording_local_share)
        photo_slope_accumulated = photo_slope_accumulated + photo_local_share
        if step > 0:
            wording_local_share = passed_along(
                wording_local_share.astype(jnp.bfloat16), "dp", -step
            ).astype(wording_local_share.dtype)
        txt_grad = txt_grad + wording_local_share
    grad_proj = (
        (
            photo_slope_accumulated
            - img_dir * jnp.sum(img_dir * photo_slope_accumulated, axis=-1, keepdims=True)
        )
        / img_norm
    ).astype(jnp.bfloat16)
    text_embedding_gradient = (
        txt_grad - txt_dir * jnp.sum(txt_dir * txt_grad, axis=-1, keepdims=True)
    ) / txt_norm
    columns = picture_encoder_outputs
    head_grad = lax.psum_scatter(
        lax.dot_general(
            columns, grad_proj, (((0,), (0,)), ((), ())), preferred_element_type=jnp.float32
        ).astype(jnp.bfloat16),
        "fsdp",
        scatter_dimension=0,
        tiled=True,
    ).astype(jnp.float32)
    return (head_grad[None], text_embedding_gradient)


def solution(mesh):
    placed = (P(("dp", "fsdp"), None), P(("dp", "fsdp"), None), P("fsdp", None), P(), P())
    return jax.shard_map(
        body,
        mesh=mesh,
        in_specs=placed,
        out_specs=(P("dp", "fsdp", None), P(("dp", "fsdp"), None)),
        check_vma=False,
    )
```

profile of v0, /device:TPU:0, one launch (start us, length us, event | category | flops | bytes accessed | tf_op | source)
XLA Modules:
  0.0 144.7 jit_solution(5502153606167310651)
XLA Ops:
  7.2 0.0 copy-start
  7.2 0.0 all-gather.2.cloned.1.call-start
  7.2 0.7 all-gather.2.cloned.1.call-update
  7.9 0.0 reduce-scatter.4.cloned.1.call-start
  8.0 1.3 fusion.4
  9.2 0.2 fusion.26
  9.5 0.5 collective-permute-start
  11.3 9.2 %collective-permute-done = bf16[256,1152]{1,0:T(8,128)(2,1)S(1)} collective-permute-done((bf16[256,1152]{1,0:T(8,128)(2,1)S(1)}, bf16[256,1152]{1,0:T(8,128)(2,1)S(1)}, u32[]{:S(2)}, u32[]{:S(2)}) %collective-permute-start) | collective-permute-done | bytes 589856 | tf_op jit(solution)/shard_map/ppermute | solution.py:11
  20.4 47.2 %all-gather.2.cloned.1.call-done = bf16[1152,1152]{1,0:T(8,128)(2,1)} async-done(((bf16[288,1152]{1,0:T(8,128)(2,1)}), bf16[1152,1152]{1,0:T(8,128)(2,1)}) %all-gather.2.cloned.1.call-update) | async-done | bytes 2654224 | tf_op jit(solution)/shard_map/all_gather | solution.py:26
  67.7 2.8 %multiply_reduce_fusion.2 = (f32[256]{0:T(256)S(1)}, f32[256,1152]{1,0:T(8,128)S(1)}) fusion(bf16[256,1152]{1,0:T(8,128)(2,1)S(1)} %copy-done, bf16[1152,1152]{1,0:T(8,128)(2,1)} %all-gather.2.cloned.1.call-done), kind=kOutput, calls=%fused_computation.18 | convolution fusion | flops 680066816 | bytes 4424704 | tf_op jit(solution)/shard_map/dot_general | solution.py:24
  70.5 0.2 fusion.27
  70.7 0.4 fusion.21
  71.1 0.4 fusion.22
  71.5 0.3 fusion.28
  71.8 0.3 convolution_add_fusion.1
  72.2 1.5 %fusion.23 = bf16[256,256]{1,0:T(8,128)(2,1)S(1)} fusion(bf16[256,1152]{1,0:T(8,128)(2,1)S(1)} %fusion.27, bf16[256,1152]{1,0:T(8,128)(2,1)} %collective-permute-done.1, f32[]{:T(128)} %bitcast.37, f32[]{:T(128)} %bitcast.34), kind=kOutput, calls=%fused_computation.40 | convolution fusion | flops 151388160 | bytes 1310728 | tf_op jit(solution)/shard_map/dot_general | solution.py:48
  73.7 1.6 %multiply_reduce_fusion.1 = (f32[256]{0:T(256)S(1)}, f32[256,1152]{1,0:T(8,128)S(1)}) fusion(f32[256,1152]{1,0:T(8,128)S(1)} %get-tuple-element.7, f32[256]{0:T(256)S(1)} %add_sqrt_fusion.1, f32[]{:T(128)} %bitcast.29, f32[256,1152]{1,0:T(8,128)S(1)} %convolution_add_fusion.1, bf16[256,256]{1,0:T(8,128)(2,1)S(1)} %fusion.23, ...), kind=kOutput, calls=%fused_computation.17 | convolution fusion | flops 152469248 | bytes 4261892 | tf_op jit(solution)/shard_map/dot_general | solution.py:55
  75.2 2.7 %fusion = bf16[1152,1152]{0,1:T(8,128)(2,1)} fusion(bf16[256,1152]{1,0:T(8,128)(2,1)S(1)} %copy-done, f32[256,1152]{1,0:T(8,128)S(1)} %get-tuple-element.9, f32[256]{0:T(256)S(1)} %get-tuple-element.8, f32[256]{0:T(256)S(1)} %add_sqrt_fusion.1, f32[256,1152]{1,0:T(8,128)S(1)} %get-tuple-element.7), kind=kOutput, calls=%fused_computation.1 | convolution fusion | flops 682278912 | bytes 5605376 | tf_op jit(solution)/shard_map/dot_general | solution.py:83
  77.9 5.2 %copy.9 = bf16[1152,1152]{1,0:T(8,128)(2,1)} copy(bf16[1152,1152]{0,1:T(8,128)(2,1)} %fusion) | data formatting | bytes 5308416
  83.2 0.0 reduce-scatter.4.cloned.1.call-update
  83.2 0.4 fusion.3
  83.6 2.4 %collective-permute-start.3 = (bf16[256,1152]{1,0:T(8,128)(2,1)S(1)}, bf16[256,1152]{1,0:T(8,128)(2,1)S(1)}, u32[]{:S(2)}, u32[]{:S(2)}) collective-permute-start(bf16[256,1152]{1,0:T(8,128)(2,1)S(1)} %fusion.3), channel_id=1, source_target_pairs={{0,24},{4,28},{8,0},{12,4},{16,8},{20,12},{24,16},{28,20},{1,25},{... | collective-permute-start | bytes 1769480 | tf_op jit(solution)/shard_map/ppermute | solution.py:11
  86.0 0.4 fusion.2
  86.4 0.1 collective-permute-start.2
  86.4 12.2 %collective-permute-done.3 = bf16[256,1152]{1,0:T(8,128)(2,1)S(1)} collective-permute-done((bf16[256,1152]{1,0:T(8,128)(2,1)S(1)}, bf16[256,1152]{1,0:T(8,128)(2,1)S(1)}, u32[]{:S(2)}, u32[]{:S(2)}) %collective-permute-start.3) | collective-permute-done | bytes 589856 | tf_op jit(solution)/shard_map/ppermute | solution.py:11
  98.6 6.2 %collective-permute-done.2 = bf16[256,1152]{1,0:T(8,128)(2,1)S(1)} collective-permute-done((bf16[256,1152]{1,0:T(8,128)(2,1)S(1)}, bf16[256,1152]{1,0:T(8,128)(2,1)S(1)}, u32[]{:S(2)}, u32[]{:S(2)}) %collective-permute-start.2) | collective-permute-done | bytes 589856 | tf_op jit(solution)/shard_map/ppermute | solution.py:11
  104.9 0.6 multiply_reduce_fusion
  105.5 1.3 subtract_divide_fusion
  106.8 27.9 %reduce-scatter.4.cloned.1.call-done = bf16[288,1152]{1,0:T(8,128)(2,1)} async-done(((bf16[1152,1152]{1,0:T(8,128)(2,1)}), bf16[288,1152]{1,0:T(8,128)(2,1)}) %reduce-scatter.4.cloned.1.call-update) | async-done | bytes 663568
  134.7 1.5 %copy.10 = bf16[288,1152]{0,1:T(8,128)(2,1)S(1)} copy(bf16[288,1152]{1,0:T(8,128)(2,1)} %reduce-scatter.4.cloned.1.call-done) | data formatting | bytes 1327104
  136.2 0.1 bitcast_convert_fusion
  136.3 1.6 %copy.8 = f32[1,288,1152]{2,1,0:T(8,128)} copy(f32[1,288,1152]{1,2,0:T(8,128)S(1)} %bitcast_convert_fusion) | data formatting | bytes 2654208
  (7 shorter events, 0.0 us)
Async XLA Ops:
  7.2 60.5 %copy-start = (bf16[256,1152]{1,0:T(8,128)(2,1)S(1)}, bf16[256,1152]{1,0:T(8,128)(2,1)}, u32[]{:S(2)}) copy-start(bf16[256,1152]{1,0:T(8,128)(2,1)} %param.5) | copy-start | bytes 1769476
  7.2 2.1 %copy-start.1 = (bf16[256,1152]{1,0:T(8,128)(2,1)S(1)}, bf16[256,1152]{1,0:T(8,128)(2,1)}, u32[]{:S(2)}) copy-start(bf16[256,1152]{1,0:T(8,128)(2,1)} %param.6) | copy-start | bytes 1769476
  7.2 60.5 %all-gather.2.cloned.1.call-start = ((), (), s32[]{:S(2)}) async-start(), calls=%async_computation.1 | async-start | bytes 3317760 | tf_op jit(solution)/shard_map/all_gather | solution.py:26
  7.9 126.8 %reduce-scatter.4.cloned.1.call-start = ((), (), s32[]{:S(2)}) async-start(), calls=%async_computation.2 | async-start | bytes 3317760
  9.5 11.0 %collective-permute-start = (bf16[256,1152]{1,0:T(8,128)(2,1)S(1)}, bf16[256,1152]{1,0:T(8,128)(2,1)S(1)}, u32[]{:S(2)}, u32[]{:S(2)}) collective-permute-start(bf16[256,1152]{1,0:T(8,128)(2,1)S(1)} %fusion.26), channel_id=1, source_target_pairs={{0,4},{4,8},{8,12},{12,16},{16,20},{20,24},{24,28},{28,0},{1,5},{5... | collective-permute-start | bytes 1769480 | tf_op jit(solution)/shard_map/ppermute | solution.py:11
  20.4 51.8 %collective-permute-start.1 = (bf16[256,1152]{1,0:T(8,128)(2,1)S(1)}, bf16[256,1152]{1,0:T(8,128)(2,1)}, u32[]{:S(2)}, u32[]{:S(2)}) collective-permute-start(bf16[256,1152]{1,0:T(8,128)(2,1)S(1)} %collective-permute-done), channel_id=1, source_target_pairs={{0,4},{4,8},{8,12},{12,16},{16,20},{20,24},{24,28},{28,0},{1,5},{5... | collective-permute-start | bytes 1769480 | tf_op jit(solution)/shard_map/ppermute | solution.py:11
  83.6 15.1 %collective-permute-start.3 = (bf16[256,1152]{1,0:T(8,128)(2,1)S(1)}, bf16[256,1152]{1,0:T(8,128)(2,1)S(1)}, u32[]{:S(2)}, u32[]{:S(2)}) collective-permute-start(bf16[256,1152]{1,0:T(8,128)(2,1)S(1)} %fusion.3), channel_id=1, source_target_pairs={{0,24},{4,28},{8,0},{12,4},{16,8},{20,12},{24,16},{28,20},{1,25},{... | collective-permute-start | bytes 1769480 | tf_op jit(solution)/shard_map/ppermute | solution.py:11
  86.4 18.5 %collective-permute-start.2 = (bf16[256,1152]{1,0:T(8,128)(2,1)S(1)}, bf16[256,1152]{1,0:T(8,128)(2,1)S(1)}, u32[]{:S(2)}, u32[]{:S(2)}) collective-permute-start(bf16[256,1152]{1,0:T(8,128)(2,1)S(1)} %fusion.2), channel_id=1, source_target_pairs={{0,28},{4,0},{8,4},{12,8},{16,12},{20,16},{24,20},{28,24},{1,29},{... | collective-permute-start | bytes 1769480 | tf_op jit(solution)/shard_map/ppermute | solution.py:11
Sparse Core Ops, SparseCore 0:
  9.6 58.0 all-gather.1
  83.3 51.3 reduce-scatter.3
where the time goes:
time: 145 us
  waiting for transfers between devices  103 us (71%)
  between operations  15.4 us (11%)
  matrix products  11.4 us (8%)
  local copies, waits for them, and re-layouts  8.3 us (6%)
  other arithmetic  3.08 us (2%)
  starting transfers between devices  3.07 us (2%)
    all_gather x1, waiting for transfers between devices, body(): lax.all_gather(linear_map_matrix, 'fsdp', axis=0, tiled=True)  47.2 us
    unnamed x3, waiting for transfers between devices  28.6 us
    ppermute x4, waiting for transfers between devices, passed_along(): lax.ppermute(value, axis, [(i, (i + by) % size) for i in range(size)])  27.6 us
    unnamed x7, local copies, waits for them, and re-layouts  8.3 us
    ppermute x4, starting transfers between devices, passed_along(): lax.ppermute(value, axis, [(i, (i + by) % size) for i in range(size)])  2.99 us
  transfers between devices with their start and end apart: 6, of which 5 were waited for; matrix products, arithmetic and copies ran while one was open for 6% of the time, Pallas kernels for 0%

commit v1 on v0

v1 whole, which is shorter than its diff:
```python
import functools

import jax
import jax.numpy as jnp
from jax import lax
from jax.experimental import pallas as pl
from jax.experimental.pallas import tpu as pltpu
from jax.sharding import PartitionSpec as P

STEPS = 3
EPS = 1e-06
CUTS = (256, 384, 512)
VMEM_BYTES = 48 * 1024 * 1024
BF16, F32 = jnp.bfloat16, jnp.float32


def spaces(count):
    return [pl.BlockSpec(memory_space=pltpu.VMEM)] * count


def params():
    return pltpu.CompilerParams(vmem_limit_bytes=VMEM_BYTES)


def cost(flops, *arrays):
    size = sum(a.size * a.dtype.itemsize for a in arrays)
    return pl.CostEstimate(flops=flops, bytes_accessed=size, transcendentals=0)


def prepare_kernel(t0, t1, t2, x, far_x, units, x_t):
    rows = t0.shape[0]
    for k, block in enumerate((t0, t1, t2)):
        values = block[...].astype(F32)
        norm = jnp.sqrt(jnp.sum(values * values, axis=-1, keepdims=True) + EPS)
        units[k * rows : (k + 1) * rows, :] = (values / norm).astype(BF16)
    x_t[:, :rows] = x[...].T
    x_t[:, rows:] = far_x[...].T


def prepare(t0, t1, t2, x, far_x):
    rows, width = t0.shape
    outs = (
        jax.ShapeDtypeStruct((STEPS * rows, width), BF16),
        jax.ShapeDtypeStruct((width, 2 * rows), BF16),
    )
    return pl.pallas_call(
        prepare_kernel,
        out_shape=outs,
        in_specs=spaces(5),
        out_specs=spaces(2),
        compiler_params=params(),
        cost_estimate=cost(0, t0, t1, t2, x, far_x, *outs),
        name="prepare",
    )(t0, t1, t2, x, far_x)


def picture_kernel(n_fsdp, x, units, sharp, bias, own, *rest):
    hops = n_fsdp - 1
    pieces, (grad, unit, w, proj, sem) = rest[: 4 * hops], rest[4 * hops :]
    part, core = lax.axis_index("fsdp"), lax.rem(lax.axis_index("dp"), 2)
    depth = own.shape[0]
    half = depth // 2
    rows = x.shape[0]

    def moves():
        for k in range(1, n_fsdp):
            for from_left in (True, False):
                there = part - k if from_left else part + k
                valid = there >= 0 if from_left else there < n_fsdp
                base = (0 if from_left else hops) + k - 1
                for sibling in (0, 1):
                    side = core if sibling == 0 else 1 - core
                    start = pl.multiple_of(there * depth + side * half, 16)
                    index = base + sibling * 2 * hops
                    yield valid, pieces[index], start, index

    first = pltpu.make_async_copy(
        own, w.at[pl.ds(pl.multiple_of(part * depth, 16), depth), :], sem.at[4 * hops]
    )
    first.start()
    for valid, source, start, index in moves():

        @pl.when(valid)
        def _():
            pltpu.make_async_copy(source, w.at[pl.ds(start, half), :], sem.at[index]).start()

    first.wait()
    for valid, source, start, index in moves():

        @pl.when(valid)
        def _():
            pltpu.make_async_copy(source, w.at[pl.ds(start, half), :], sem.at[index]).wait()

    proj[...] = jnp.dot(x[...], w[...], preferred_element_type=F32)
    values = proj[...]
    norm = jnp.sqrt(jnp.sum(values * values, axis=-1, keepdims=True) + EPS)
    unit[...] = (values / norm).astype(BF16)
    scale = sharp[0]
    logits = scale * lax.dot_general(
        unit[...], units[...], (((1,), (1,)), ((), ())), preferred_element_type=F32
    ) + bias[0]
    coefficient = jax.nn.sigmoid(logits)
    row = lax.broadcasted_iota(jnp.int32, coefficient.shape, 0)
    column = lax.broadcasted_iota(jnp.int32, coefficient.shape, 1)
    coefficient = jnp.where(row == column, coefficient - 1.0, coefficient).astype(BF16)
    slope = scale * jnp.dot(coefficient, units[...], preferred_element_type=F32)
    direction = proj[...] / norm
    along = jnp.sum(direction * slope, axis=-1, keepdims=True)
    grad[...] = ((slope - direction * along) / norm).astype(BF16)


def picture_side(n_fsdp, x, units, sharp, bias, own, pieces):
    rows, width = x.shape
    out = jax.ShapeDtypeStruct((rows, width), BF16)
    hops = n_fsdp - 1
    smem = pl.BlockSpec(memory_space=pltpu.SMEM)
    return pl.pallas_call(
        functools.partial(picture_kernel, n_fsdp),
        out_shape=(out, out),
        in_specs=spaces(2) + [smem, smem] + [pl.BlockSpec(memory_space=pl.ANY)] * (1 + 4 * hops),
        out_specs=spaces(2),
        scratch_shapes=[
            pltpu.VMEM((width, width), BF16),
            pltpu.VMEM((rows, width), F32),
            pltpu.SemaphoreType.DMA((4 * hops + 1,)),
        ],
        compiler_params=params(),
        cost_estimate=cost(2 * rows * width * (width + 2 * STEPS * rows), x, units, own, out, out),
        name="picture_side",
    )(x, units, sharp, bias, own, *pieces)


def text_kernel(text, u0, u1, u2, sharp, bias, out, units):
    rows = text.shape[0]
    for k, block in enumerate((u0, u1, u2)):
        units[k * rows : (k + 1) * rows, :] = block[...]
    values = text[...].astype(F32)
    norm = jnp.sqrt(jnp.sum(values * values, axis=-1, keepdims=True) + EPS)
    direction = values / norm
    scale = sharp[0]
    logits = scale * lax.dot_general(
        direction.astype(BF16), units[...], (((1,), (1,)), ((), ())), preferred_element_type=F32
    ) + bias[0]
    coefficient = jax.nn.sigmoid(logits)
    row = lax.broadcasted_iota(jnp.int32, coefficient.shape, 0)
    column = lax.broadcasted_iota(jnp.int32, coefficient.shape, 1)
    coefficient = jnp.where(row == column, coefficient - 1.0, coefficient).astype(BF16)
    slope = scale * jnp.dot(coefficient, units[...], preferred_element_type=F32)
    along = jnp.sum(direction * slope, axis=-1, keepdims=True)
    out[...] = (slope - direction * along) / norm


def text_side(text, u0, u1, u2, sharp, bias):
    rows, width = text.shape
    out = jax.ShapeDtypeStruct((rows, width), F32)
    smem = pl.BlockSpec(memory_space=pltpu.SMEM)
    return pl.pallas_call(
        text_kernel,
        out_shape=out,
        in_specs=spaces(4) + [smem, smem],
        out_specs=pl.BlockSpec(memory_space=pltpu.VMEM),
        scratch_shapes=[pltpu.VMEM((STEPS * rows, width), BF16)],
        compiler_params=params(),
        cost_estimate=cost(4 * STEPS * rows * rows * width, text, u0, u1, u2, out),
        name="text_side",
    )(text, u0, u1, u2, sharp, bias)


def rows_of(ref, block, depth):
    return ref[pl.ds(pl.multiple_of(block * depth, 16), depth), :]


def outward_kernel(depth, x_t, grad, out):
    rows = grad.shape[0]
    part = lax.axis_index("fsdp")
    block = jnp.where(lax.rem(part, 2) == 0, part + 1, part - 1)
    out[...] = jnp.dot(
        rows_of(x_t, block, depth)[:, :rows], grad[...], preferred_element_type=F32
    ).astype(BF16)


def outward(depth, x_t, grad):
    out = jax.ShapeDtypeStruct((depth, grad.shape[1]), BF16)
    return pl.pallas_call(
        functools.partial(outward_kernel, depth),
        out_shape=out,
        in_specs=spaces(2),
        out_specs=pl.BlockSpec(memory_space=pltpu.VMEM),
        compiler_params=params(),
        cost_estimate=cost(2 * depth * grad.size, x_t, grad, out),
        name="outward",
    )(x_t, grad)


def pair_kernel(depth, begin, x_t, grad, far_grad, kept, near, far):
    rows = grad.shape[0]
    part = lax.axis_index("fsdp")
    size = far_grad.shape[1]
    mine = grad[:, begin : begin + size]
    for block, out in ((3 - part, near), (lax.rem(part + 2, 4), far), (part, kept)):
        left = rows_of(x_t, block, depth)
        out[...] = (
            jnp.dot(left[:, :rows], mine, preferred_element_type=F32)
            + jnp.dot(left[:, rows:], far_grad[...], preferred_element_type=F32)
        ).astype(out.dtype)


def pair_product(depth, begin, x_t, grad, far_grad):
    size = far_grad.shape[1]
    outs = tuple(jax.ShapeDtypeStruct((depth, size), t) for t in (F32, BF16, BF16))
    return pl.pallas_call(
        functools.partial(pair_kernel, depth, begin),
        out_shape=outs,
        in_specs=spaces(3),
        out_specs=spaces(3),
        compiler_params=params(),
        cost_estimate=cost(12 * depth * far_grad.size, x_t, grad, far_grad, *outs),
        name="pair_product",
    )(x_t, grad, far_grad)


def total_kernel(count, *refs):
    kept, near, far, (direct, out) = refs[:count], refs[count : 2 * count], refs[2 * count : 3 * count], refs[3 * count :]
    begin = 0
    for a, b, c in zip(kept, near, far):
        stop = begin + a.shape[1]
        out[0, :, begin:stop] = (
            a[...]
            + b[...].astype(F32)
            + c[...].astype(F32)
            + direct[:, begin:stop].astype(F32)
        )
        begin = stop


def total(kept, near, far, direct):
    out = jax.ShapeDtypeStruct((1,) + direct.shape, F32)
    return pl.pallas_call(
        functools.partial(total_kernel, len(kept)),
        out_shape=out,
        in_specs=spaces(3 * len(kept) + 1),
        out_specs=pl.BlockSpec(memory_space=pltpu.VMEM),
        compiler_params=params(),
        cost_estimate=cost(0, *kept, *near, *far, direct, out),
        name="total",
    )(*kept, *near, *far, direct)


def line_body(n_dp, n_fsdp, x, text, w, sharp, bias):
    depth = w.shape[0]
    half = depth // 2
    core = lax.rem(lax.axis_index("dp"), 2)
    both = ("dp", "fsdp")

    def along(value, pairs):
        return lax.ppermute(value, "fsdp", pairs)

    def across(value, parts):
        pairs = [(d * n_fsdp + f, (d ^ 1) * n_fsdp + f) for d in range(n_dp) for f in parts]
        return lax.ppermute(value, both, pairs)

    def shifted(value, by):
        return lax.ppermute(value, "dp", [(d, (d + by) % n_dp) for d in range(n_dp)])

    own = lax.dynamic_slice_in_dim(w, core * half, half, 0)
    rights, lefts = [], []
    right = left = own
    for k in range(1, n_fsdp):
        right = along(right, [(f, f + 1) for f in range(k - 1, n_fsdp - 1)])
        left = along(left, [(f, f - 1) for f in range(1, n_fsdp - k + 1)])
        rights.append(right)
        lefts.append(left)
    far_x = along(x, [(0, 1), (3, 2)])
    text2 = shifted(text, 2)
    text1 = across(jnp.where(core == 0, text, text2), range(n_fsdp))
    right_twins = [across(r, range(k + 1, n_fsdp)) for k, r in enumerate(rights)]
    left_twins = [across(r, range(n_fsdp - 1 - k)) for k, r in enumerate(lefts)]

    units, x_t = prepare(text, text1, text2, x, far_x)
    grad, unit = picture_side(
        n_fsdp, x, units, sharp, bias, w, rights + lefts + right_twins + left_twins
    )

    begin, far_grads = 0, []
    for size in CUTS:
        far_grads.append((begin, along(grad[:, begin : begin + size], [(0, 1), (3, 2)])))
        begin += size
    direct = along(outward(depth, x_t, grad), [(1, 0), (2, 3)])
    unit2 = shifted(unit, -2)
    unit1 = across(jnp.where(core == 0, unit2, unit), range(n_fsdp))
    kept, nears, fars = [], [], []
    for begin, far_grad in far_grads:
        mine, near, far = pair_product(depth, begin, x_t, grad, far_grad)
        kept.append(mine)
        nears.append(along(near, [(1, 2), (2, 1)]))
        fars.append(along(far, [(1, 3), (2, 0)]))
    text_grad = text_side(text, unit, unit1, unit2, sharp, bias)
    return total(kept, nears, fars, direct), text_grad


def plain_body(n_dp, n_fsdp, x, text, w, sharp, bias):
    def shifted(value, by):
        return lax.ppermute(value, "dp", [(d, (d + by) % n_dp) for d in range(n_dp)])

    rows, width = x.shape
    proj = jnp.dot(
        x, lax.all_gather(w, "fsdp", axis=0, tiled=True), preferred_element_type=F32
    )
    norm = jnp.sqrt(jnp.sum(proj * proj, axis=-1, keepdims=True) + EPS)
    direction = proj / norm
    unit = direction.astype(BF16)
    values = text.astype(F32)
    txt_norm = jnp.sqrt(jnp.sum(values * values, axis=-1, keepdims=True) + EPS)
    txt_dir = values / txt_norm
    slot = txt_dir.astype(BF16)
    scale = sharp[0]
    slope = jnp.zeros((rows, width), F32)
    txt_slope = jnp.zeros((rows, width), F32)
    for step in range(STEPS):
        if step > 0:
            slot = shifted(slot, 1)
        logits = scale * jnp.dot(unit, slot.T, preferred_element_type=F32) + bias[0]
        coefficient = jax.nn.sigmoid(logits)
        if step == 0:
            coefficient = coefficient - jnp.eye(rows, dtype=F32)
        coefficient = coefficient.astype(BF16)
        slope = slope + scale * jnp.dot(coefficient, slot, preferred_element_type=F32)
        share = scale * lax.dot_general(
            coefficient, unit, (((0,), (0,)), ((), ())), preferred_element_type=F32
        )
        if step > 0:
            share = shifted(share.astype(BF16), -step).astype(F32)
        txt_slope = txt_slope + share
    grad = (
        (slope - direction * jnp.sum(direction * slope, axis=-1, keepdims=True)) / norm
    ).astype(BF16)
    text_grad = (
        txt_slope - txt_dir * jnp.sum(txt_dir * txt_slope, axis=-1, keepdims=True)
    ) / txt_norm
    partial = lax.dot_general(
        x, grad, (((0,), (0,)), ((), ())), preferred_element_type=F32
    ).astype(BF16)
    head = lax.psum_scatter(partial, "fsdp", scatter_dimension=0, tiled=True).astype(F32)
    return head[None], text_grad


def solution(mesh):
    n_dp, n_fsdp = mesh.shape["dp"], mesh.shape["fsdp"]
    line = n_fsdp == 4 and n_dp % 2 == 0 and n_dp >= STEPS
    placed = (P(("dp", "fsdp"), None), P(("dp", "fsdp"), None), P("fsdp", None), P(), P())
    return jax.shard_map(
        functools.partial(line_body if line else plain_body, n_dp, n_fsdp),
        mesh=mesh,
        in_specs=placed,
        out_specs=(P("dp", "fsdp", None), P(("dp", "fsdp"), None)),
        check_vma=False,
    )
```

time: 145 us -> 103 us (0.71)
  waiting for transfers between devices: 103 us -> 46.3 us
  starting transfers between devices: 3.07 us -> 37.5 us
  between operations: 15.4 us -> 2.36 us
  Pallas kernels: 0 us -> 12.6 us
  matrix products: 11.4 us -> 0 us
  local copies, waits for them, and re-layouts: 8.3 us -> 2.3 us
  other arithmetic: 3.08 us -> 1.22 us
    all_gather x1 -> x0, waiting for transfers between devices: 47.2 us -> none  [body(): lax.all_gather(linear_map_matrix, 'fsdp', axis=0, tiled=True)]
    ppermute x4 -> x27, starting transfers between devices: 2.99 us -> 37.5 us  [the longest x17 24.4 us: along(): return lax.ppermute(value, 'fsdp', pairs)]
    unnamed x3 -> x0, waiting for transfers between devices: 28.6 us -> none
    ppermute x4 -> x27, waiting for transfers between devices: 27.6 us -> 46.3 us  [the longest x17 37.9 us: along(): return lax.ppermute(value, 'fsdp', pairs)]
    pallas_call x0 -> x8, Pallas kernels: none -> 12.6 us  [the longest x1 5.45 us: picture_side(): pl.pallas_call(functools.partial(picture_kernel, n_fsdp), out_shape=(out,...]
    dot_general x11 -> x0, matrix products: 11.4 us -> none  [the longest x1 2.83 us: body(): jnp.dot(columns, lax.all_gather(linear_map_matrix, 'fsdp', axis=0, tiled=...]
    unnamed x7 -> x6, local copies, waits for them, and re-layouts: 8.3 us -> 1.25 us
  transfers between devices with their start and end apart: 6 -> 27, of which waited for: 5 -> 7; matrix products, arithmetic and copies ran while one was open for 6% -> 2% of each run, Pallas kernels for 0% -> 4%
where the time goes in v1:
time: 103 us; the launch traced here: 102 us
  waiting for transfers between devices  46.3 us (45%)
  starting transfers between devices  37.5 us (36%)
  Pallas kernels  12.6 us (12%)
  between operations  2.36 us (2%)
  local copies, waits for them, and re-layouts  2.3 us (2%)
  other arithmetic  1.22 us (1%)
    ppermute x17, waiting for transfers between devices, along(): return lax.ppermute(value, 'fsdp', pairs)  37.9 us
    ppermute x17, starting transfers between devices, along(): return lax.ppermute(value, 'fsdp', pairs)  24.4 us
    ppermute x8, starting transfers between devices, across(): return lax.ppermute(value, both, pairs)  8.42 us
    ppermute x2, waiting for transfers between devices, shifted(): lax.ppermute(value, 'dp', [(d, (d + by) % n_dp) for d in range(n_dp)])  8.37 us
    pallas_call x1, Pallas kernels, picture_side(): pl.pallas_call(functools.partial(picture_kernel, n_fsdp), out_shape=(out,...  5.45 us
    ppermute x2, starting transfers between devices, shifted(): lax.ppermute(value, 'dp', [(d, (d + by) % n_dp) for d in range(n_dp)])  4.75 us
    pallas_call x1, Pallas kernels, text_side(): pl.pallas_call(text_kernel, out_shape=out, in_specs=spaces(4) + [smem, sm...  2.86 us
  transfers between devices with their start and end apart: 27, of which 7 were waited for; matrix products, arithmetic and copies ran while one was open for 2% of the time, Pallas kernels for 4%

profile of v1, /device:TPU:0, one launch (start us, length us, event | category | flops | bytes accessed | tf_op | source)
XLA Modules:
  0.0 102.3 jit_solution(16896880995989607167)
XLA Ops:
  0.7 3.0 %collective-permute-start = (bf16[256,1152]{1,0:T(8,128)(2,1)}, bf16[256,1152]{1,0:T(8,128)(2,1)S(1)}, u32[]{:S(2)}, u32[]{:S(2)}) collective-permute-start(bf16[256,1152]{1,0:T(8,128)(2,1)} %text.1), channel_id=1, source_target_pairs={{0,8},{4,12},{8,16},{12,20},{16,24},{20,28},{24,0},{28,4},{1,9},{5... | collective-permute-start | bytes 1769480 | tf_op jit(solution)/shard_map/ppermute | solution.py:263
  3.6 1.0 constant_dynamic-slice_fusion
  4.6 3.5 %collective-permute-start.3 = (bf16[144,1152]{1,0:T(8,128)(2,1)S(1)}, bf16[144,1152]{1,0:T(8,128)(2,1)S(1)}, u32[]{:S(2)}, u32[]{:S(2)}) collective-permute-start(bf16[144,1152]{1,0:T(8,128)(2,1)S(1)} %constant_dynamic-slice_fusion), channel_id=1, source_target_pairs={{0,1},{1,2},{2,3},{4,5},{5,6},{6,7},{8,9},{9,10},{10,11},{12,13},{... | collective-permute-start | bytes 995336 | tf_op jit(solution)/shard_map/ppermute | solution.py:256
  8.2 1.3 %collective-permute-start.6 = (bf16[144,1152]{1,0:T(8,128)(2,1)S(1)}, bf16[144,1152]{1,0:T(8,128)(2,1)S(1)}, u32[]{:S(2)}, u32[]{:S(2)}) collective-permute-start(bf16[144,1152]{1,0:T(8,128)(2,1)S(1)} %constant_dynamic-slice_fusion), channel_id=1, source_target_pairs={{1,0},{2,1},{3,2},{5,4},{6,5},{7,6},{9,8},{10,9},{11,10},{13,12},{... | collective-permute-start | bytes 995336 | tf_op jit(solution)/shard_map/ppermute | solution.py:256
  9.5 4.6 %collective-permute-start.2 = (bf16[256,1152]{1,0:T(8,128)(2,1)}, bf16[256,1152]{1,0:T(8,128)(2,1)S(1)}, u32[]{:S(2)}, u32[]{:S(2)}) collective-permute-start(bf16[256,1152]{1,0:T(8,128)(2,1)} %x.3), channel_id=1, source_target_pairs={{0,1},{3,2},{4,5},{7,6},{8,9},{11,10},{12,13},{15,14},{16,17},{19,... | collective-permute-start | bytes 1769480 | tf_op jit(solution)/shard_map/ppermute | solution.py:256
  14.1 2.3 %collective-permute-done.3.rest_0_ = bf16[144,1152]{1,0:T(8,128)(2,1)S(1)} collective-permute-done((bf16[144,1152]{1,0:T(8,128)(2,1)S(1)}, bf16[144,1152]{1,0:T(8,128)(2,1)S(1)}, u32[]{:S(2)}, u32[]{:S(2)}) %collective-permute-start.3) | collective-permute-done | bytes 331808 | tf_op jit(solution)/shard_map/ppermute | solution.py:256
  17.0 2.0 %collective-permute-done.6.rest_3_ = bf16[144,1152]{1,0:T(8,128)(2,1)S(1)} collective-permute-done((bf16[144,1152]{1,0:T(8,128)(2,1)S(1)}, bf16[144,1152]{1,0:T(8,128)(2,1)S(1)}, u32[]{:S(2)}, u32[]{:S(2)}) %collective-permute-start.6) | collective-permute-done | bytes 331808 | tf_op jit(solution)/shard_map/ppermute | solution.py:256
  19.0 1.3 %collective-permute-start.7 = (bf16[144,1152]{1,0:T(8,128)(2,1)S(1)}, bf16[144,1152]{1,0:T(8,128)(2,1)S(1)}, u32[]{:S(2)}, u32[]{:S(2)}) collective-permute-start(bf16[144,1152]{1,0:T(8,128)(2,1)S(1)} %collective-permute-done.6.rest_3_), channel_id=1, source_target_pairs={{1,0},{2,1},{5,4},{6,5},{9,8},{10,9},{13,12},{14,13},{17,16},{18,1... | collective-permute-start | bytes 995336 | tf_op jit(solution)/shard_map/ppermute | solution.py:256
  20.3 1.1 %broadcast_select_fusion.1 = bf16[256,1152]{1,0:T(8,128)(2,1)S(1)} fusion(bf16[256,1152]{1,0:T(8,128)(2,1)} %text.1, bf16[256,1152]{1,0:T(8,128)(2,1)S(1)} %collective-permute-done.t2, pred[]{:T(512)S(6)} %eq.4), kind=kLoop, calls=%fused_computation.1 | loop fusion | flops 294912 | bytes 1769473 | tf_op jit(solution)/shard_map/jit(_where)/select_n | solution.py:275
  22.9 6.2 %collective-permute-done.7.rest_4_ = bf16[144,1152]{1,0:T(8,128)(2,1)S(1)} collective-permute-done((bf16[144,1152]{1,0:T(8,128)(2,1)S(1)}, bf16[144,1152]{1,0:T(8,128)(2,1)S(1)}, u32[]{:S(2)}, u32[]{:S(2)}) %collective-permute-start.7) | collective-permute-done | bytes 331808 | tf_op jit(solution)/shard_map/ppermute | solution.py:256
  29.1 1.3 %collective-permute-start.8 = (bf16[144,1152]{1,0:T(8,128)(2,1)S(1)}, bf16[144,1152]{1,0:T(8,128)(2,1)S(1)}, u32[]{:S(2)}, u32[]{:S(2)}) collective-permute-start(bf16[144,1152]{1,0:T(8,128)(2,1)S(1)} %collective-permute-done.7.rest_4_), channel_id=1, source_target_pairs={{1,0},{5,4},{9,8},{13,12},{17,16},{21,20},{25,24},{29,28}} | collective-permute-start | bytes 995336 | tf_op jit(solution)/shard_map/ppermute | solution.py:256
  30.4 1.9 %collective-permute-start.12 = (bf16[144,1152]{1,0:T(8,128)(2,1)S(1)}, bf16[144,1152]{1,0:T(8,128)(2,1)S(1)}, u32[]{:S(2)}, u32[]{:S(2)}) collective-permute-start(bf16[144,1152]{1,0:T(8,128)(2,1)S(1)} %collective-permute-done.6.rest_3_), channel_id=1, source_target_pairs={{0,4},{1,5},{2,6},{4,0},{5,1},{6,2},{8,12},{9,13},{10,14},{12,8},{... | collective-permute-start | bytes 995336 | tf_op jit(solution)/shard_map/ppermute | solution.py:260
  32.4 0.7 collective-permute-start.10
  33.1 2.4 %collective-permute-start.13 = (bf16[144,1152]{1,0:T(8,128)(2,1)S(1)}, bf16[144,1152]{1,0:T(8,128)(2,1)S(1)}, u32[]{:S(2)}, u32[]{:S(2)}) collective-permute-start(bf16[144,1152]{1,0:T(8,128)(2,1)S(1)} %collective-permute-done.7.rest_4_), channel_id=1, source_target_pairs={{0,4},{1,5},{4,0},{5,1},{8,12},{9,13},{12,8},{13,9},{16,20},{17,21... | collective-permute-start | bytes 995336 | tf_op jit(solution)/shard_map/ppermute | solution.py:260
  35.5 2.8 %collective-permute-done.8.rest_5_ = bf16[144,1152]{1,0:T(8,128)(2,1)S(1)} collective-permute-done((bf16[144,1152]{1,0:T(8,128)(2,1)S(1)}, bf16[144,1152]{1,0:T(8,128)(2,1)S(1)}, u32[]{:S(2)}, u32[]{:S(2)}) %collective-permute-start.8) | collective-permute-done | bytes 331808 | tf_op jit(solution)/shard_map/ppermute | solution.py:256
  39.0 1.9 %collective-permute-start.14 = (bf16[144,1152]{1,0:T(8,128)(2,1)S(1)}, bf16[144,1152]{1,0:T(8,128)(2,1)S(1)}, u32[]{:S(2)}, u32[]{:S(2)}) collective-permute-start(bf16[144,1152]{1,0:T(8,128)(2,1)S(1)} %collective-permute-done.8.rest_5_), channel_id=1, source_target_pairs={{0,4},{4,0},{8,12},{12,8},{16,20},{20,16},{24,28},{28,24}} | collective-permute-start | bytes 995336 | tf_op jit(solution)/shard_map/ppermute | solution.py:260
  42.2 0.9 prepare.1
  43.1 1.2 %copy-done.2 = bf16[768,1152]{1,0:T(8,128)(2,1)} copy-done((bf16[768,1152]{1,0:T(8,128)(2,1)}, bf16[768,1152]{1,0:T(8,128)(2,1)S(1)}, u32[]{:S(2)}) %copy-start.2) | copy-done | bytes 1769496
  44.4 5.5 %picture_side.1 = (bf16[256,1152]{1,0:T(8,128)(2,1)S(1)}, bf16[256,1152]{1,0:T(8,128)(2,1)S(1)}) custom-call(bf16[256,1152]{1,0:T(8,128)(2,1)S(1)} %copy-done.1, bf16[768,1152]{1,0:T(8,128)(2,1)} %copy-done.2, f32[1]{0:T(128)S(6)} %copy.7.sharp, f32[1]{0:T(128)S(6)} %copy.8.bias, bf16[288,1152]{1,0:T(8,128)(2,1)} %own.1, ...), custom_call_target="tpu_custom_call" | custom-call | flops 1585446912 | bytes 4202496 | tf_op jit(solution)/shard_map/picture_side/pallas_call | solution.py:117
  49.8 1.8 %collective-permute-start.25 = (bf16[256,1152]{1,0:T(8,128)(2,1)S(1)}, bf16[256,1152]{1,0:T(8,128)(2,1)S(1)}, u32[]{:S(2)}, u32[]{:S(2)}) collective-permute-start(bf16[256,1152]{1,0:T(8,128)(2,1)S(1)} %get-tuple-element.27.u0), channel_id=1, source_target_pairs={{0,24},{4,28},{8,0},{12,4},{16,8},{20,12},{24,16},{28,20},{1,25},{... | collective-permute-start | bytes 1769480 | tf_op jit(solution)/shard_map/ppermute | solution.py:263
  51.7 1.3 %collective-permute-start.15 = (bf16[256,256]{1,0:T(8,128)(2,1)S(1)}, bf16[256,256]{1,0:T(8,128)(2,1)S(1)}, u32[]{:S(2)}, u32[]{:S(2)}) collective-permute-start(bf16[256,256]{1,0:T(8,128)(2,1)S(1)} %slice.9), channel_id=1, source_target_pairs={{0,1},{3,2},{4,5},{7,6},{8,9},{11,10},{12,13},{15,14},{16,17},{19,... | collective-permute-start | bytes 393224 | tf_op jit(solution)/shard_map/ppermute | solution.py:256
  53.0 1.3 %collective-permute-start.16 = (bf16[256,384]{1,0:T(8,128)(2,1)S(1)}, bf16[256,384]{1,0:T(8,128)(2,1)S(1)}, u32[]{:S(2)}, u32[]{:S(2)}) collective-permute-start(bf16[256,384]{1,0:T(8,128)(2,1)S(1)} %slice.10), channel_id=1, source_target_pairs={{0,1},{3,2},{4,5},{7,6},{8,9},{11,10},{12,13},{15,14},{16,17},{19,... | collective-permute-start | bytes 589832 | tf_op jit(solution)/shard_map/ppermute | solution.py:256
  54.3 1.3 %collective-permute-start.17 = (bf16[256,512]{1,0:T(8,128)(2,1)S(1)}, bf16[256,512]{1,0:T(8,128)(2,1)S(1)}, u32[]{:S(2)}, u32[]{:S(2)}) collective-permute-start(bf16[256,512]{1,0:T(8,128)(2,1)S(1)} %slice.11), channel_id=1, source_target_pairs={{0,1},{3,2},{4,5},{7,6},{8,9},{11,10},{12,13},{15,14},{16,17},{19,... | collective-permute-start | bytes 786440 | tf_op jit(solution)/shard_map/ppermute | solution.py:256
  56.0 1.3 %collective-permute-start.24 = (bf16[288,1152]{1,0:T(8,128)(2,1)S(1)}, bf16[288,1152]{1,0:T(8,128)(2,1)S(1)}, u32[]{:S(2)}, u32[]{:S(2)}) collective-permute-start(bf16[288,1152]{1,0:T(8,128)(2,1)S(1)} %outward.1), channel_id=1, source_target_pairs={{1,0},{2,3},{5,4},{6,7},{9,8},{10,11},{13,12},{14,15},{17,16},{18,... | collective-permute-start | bytes 1990664 | tf_op jit(solution)/shard_map/ppermute | solution.py:256
  57.3 8.4 %collective-permute-done.25.u2 = bf16[256,1152]{1,0:T(8,128)(2,1)S(1)} collective-permute-done((bf16[256,1152]{1,0:T(8,128)(2,1)S(1)}, bf16[256,1152]{1,0:T(8,128)(2,1)S(1)}, u32[]{:S(2)}, u32[]{:S(2)}) %collective-permute-start.25) | collective-permute-done | bytes 589856 | tf_op jit(solution)/shard_map/ppermute | solution.py:263
  68.2 1.3 %collective-permute-start.21 = (bf16[288,256]{1,0:T(8,128)(2,1)S(1)}, bf16[288,256]{1,0:T(8,128)(2,1)S(1)}, u32[]{:S(2)}, u32[]{:S(2)}) collective-permute-start(bf16[288,256]{1,0:T(8,128)(2,1)S(1)} %get-tuple-element.24), channel_id=1, source_target_pairs={{1,3},{2,0},{5,7},{6,4},{9,11},{10,8},{13,15},{14,12},{17,19},{18,... | collective-permute-start | bytes 442376 | tf_op jit(solution)/shard_map/ppermute | solution.py:256
  70.8 10.6 %collective-permute-done.21.refs_6_ = bf16[288,256]{1,0:T(8,128)(2,1)S(1)} collective-permute-done((bf16[288,256]{1,0:T(8,128)(2,1)S(1)}, bf16[288,256]{1,0:T(8,128)(2,1)S(1)}, u32[]{:S(2)}, u32[]{:S(2)}) %collective-permute-start.21) | collective-permute-done | bytes 147488 | tf_op jit(solution)/shard_map/ppermute | solution.py:256
  81.4 1.3 %collective-permute-start.23 = (bf16[288,512]{1,0:T(8,128)(2,1)S(1)}, bf16[288,512]{1,0:T(8,128)(2,1)S(1)}, u32[]{:S(2)}, u32[]{:S(2)}) collective-permute-start(bf16[288,512]{1,0:T(8,128)(2,1)S(1)} %get-tuple-element.26), channel_id=1, source_target_pairs={{1,3},{2,0},{5,7},{6,4},{9,11},{10,8},{13,15},{14,12},{17,19},{18,... | collective-permute-start | bytes 884744 | tf_op jit(solution)/shard_map/ppermute | solution.py:256
  82.7 1.3 %collective-permute-start.22 = (bf16[288,384]{1,0:T(8,128)(2,1)S(1)}, bf16[288,384]{1,0:T(8,128)(2,1)S(1)}, u32[]{:S(2)}, u32[]{:S(2)}) collective-permute-start(bf16[288,384]{1,0:T(8,128)(2,1)S(1)} %get-tuple-element.25), channel_id=1, source_target_pairs={{1,3},{2,0},{5,7},{6,4},{9,11},{10,8},{13,15},{14,12},{17,19},{18,... | collective-permute-start | bytes 663560 | tf_op jit(solution)/shard_map/ppermute | solution.py:256
  84.0 14.1 %collective-permute-done.22.refs_7_ = bf16[288,384]{1,0:T(8,128)(2,1)S(1)} collective-permute-done((bf16[288,384]{1,0:T(8,128)(2,1)S(1)}, bf16[288,384]{1,0:T(8,128)(2,1)S(1)}, u32[]{:S(2)}, u32[]{:S(2)}) %collective-permute-start.22) | collective-permute-done | bytes 221216 | tf_op jit(solution)/shard_map/ppermute | solution.py:256
  98.1 1.4 %total.1 = f32[1,288,1152]{2,1,0:T(8,128)} custom-call(f32[288,256]{1,0:T(8,128)S(1)} %get-tuple-element.18.refs_0_, f32[288,384]{1,0:T(8,128)S(1)} %get-tuple-element.19.refs_1_, f32[288,512]{1,0:T(8,128)S(1)} %get-tuple-element.20.refs_2_, bf16[288,256]{1,0:T(8,128)(2,1)S(1)} %collective-permute-done.18.refs_3_, ...), custom_call_target="tpu_custom_call" | custom-call | bytes 4644864 | tf_op jit(solution)/shard_map/total/pallas_call | solution.py:238
  99.4 2.9 %text_side.1 = f32[256,1152]{1,0:T(8,128)} custom-call(bf16[256,1152]{1,0:T(8,128)(2,1)S(1)} %copy-done, bf16[256,1152]{1,0:T(8,128)(2,1)S(1)} %get-tuple-element.27.u0, bf16[256,1152]{1,0:T(8,128)(2,1)S(1)} %collective-permute-done.26.u1, bf16[256,1152]{1,0:T(8,128)(2,1)S(1)} %collective-permute-done.25.u2, f32[1]{0:T(128)S(6)} %copy.7.sharp, f32[1]{0:T(128)S(6)} %copy.8.bias), custom_call_target="tpu_custom_call" | custom-call | flops 905969664 | bytes 3538944 | tf_op jit(solution)/shard_map/text_side/pallas_call | solution.py:157
  (42 shorter events, 7.1 us)
Async XLA Ops:
  0.6 41.6 %copy-start = (bf16[256,1152]{1,0:T(8,128)(2,1)S(1)}, bf16[256,1152]{1,0:T(8,128)(2,1)}, u32[]{:S(2)}) copy-start(bf16[256,1152]{1,0:T(8,128)(2,1)} %text.1) | copy-start | bytes 1769476
  0.6 41.6 %copy-start.1 = (bf16[256,1152]{1,0:T(8,128)(2,1)S(1)}, bf16[256,1152]{1,0:T(8,128)(2,1)}, u32[]{:S(2)}) copy-start(bf16[256,1152]{1,0:T(8,128)(2,1)} %x.3) | copy-start | bytes 1769476
  0.7 19.7 %collective-permute-start = (bf16[256,1152]{1,0:T(8,128)(2,1)}, bf16[256,1152]{1,0:T(8,128)(2,1)S(1)}, u32[]{:S(2)}, u32[]{:S(2)}) collective-permute-start(bf16[256,1152]{1,0:T(8,128)(2,1)} %text.1), channel_id=1, source_target_pairs={{0,8},{4,12},{8,16},{12,20},{16,24},{20,28},{24,0},{28,4},{1,9},{5... | collective-permute-start | bytes 1769480 | tf_op jit(solution)/shard_map/ppermute | solution.py:263
  4.6 11.7 %collective-permute-start.3 = (bf16[144,1152]{1,0:T(8,128)(2,1)S(1)}, bf16[144,1152]{1,0:T(8,128)(2,1)S(1)}, u32[]{:S(2)}, u32[]{:S(2)}) collective-permute-start(bf16[144,1152]{1,0:T(8,128)(2,1)S(1)} %constant_dynamic-slice_fusion), channel_id=1, source_target_pairs={{0,1},{1,2},{2,3},{4,5},{5,6},{6,7},{8,9},{9,10},{10,11},{12,13},{... | collective-permute-start | bytes 995336 | tf_op jit(solution)/shard_map/ppermute | solution.py:256
  8.2 10.9 %collective-permute-start.6 = (bf16[144,1152]{1,0:T(8,128)(2,1)S(1)}, bf16[144,1152]{1,0:T(8,128)(2,1)S(1)}, u32[]{:S(2)}, u32[]{:S(2)}) collective-permute-start(bf16[144,1152]{1,0:T(8,128)(2,1)S(1)} %constant_dynamic-slice_fusion), channel_id=1, source_target_pairs={{1,0},{2,1},{3,2},{5,4},{6,5},{7,6},{9,8},{10,9},{11,10},{13,12},{... | collective-permute-start | bytes 995336 | tf_op jit(solution)/shard_map/ppermute | solution.py:256
  9.5 20.9 %collective-permute-start.2 = (bf16[256,1152]{1,0:T(8,128)(2,1)}, bf16[256,1152]{1,0:T(8,128)(2,1)S(1)}, u32[]{:S(2)}, u32[]{:S(2)}) collective-permute-start(bf16[256,1152]{1,0:T(8,128)(2,1)} %x.3), channel_id=1, source_target_pairs={{0,1},{3,2},{4,5},{7,6},{8,9},{11,10},{12,13},{15,14},{16,17},{19,... | collective-permute-start | bytes 1769480 | tf_op jit(solution)/shard_map/ppermute | solution.py:256
  16.4 5.9 %collective-permute-start.4 = (bf16[144,1152]{1,0:T(8,128)(2,1)S(1)}, bf16[144,1152]{1,0:T(8,128)(2,1)S(1)}, u32[]{:S(2)}, u32[]{:S(2)}) collective-permute-start(bf16[144,1152]{1,0:T(8,128)(2,1)S(1)} %collective-permute-done.3.rest_0_), channel_id=1, source_target_pairs={{1,2},{2,3},{5,6},{6,7},{9,10},{10,11},{13,14},{14,15},{17,18},{18... | collective-permute-start | bytes 995336 | tf_op jit(solution)/shard_map/ppermute | solution.py:256
  19.0 10.1 %collective-permute-start.7 = (bf16[144,1152]{1,0:T(8,128)(2,1)S(1)}, bf16[144,1152]{1,0:T(8,128)(2,1)S(1)}, u32[]{:S(2)}, u32[]{:S(2)}) collective-permute-start(bf16[144,1152]{1,0:T(8,128)(2,1)S(1)} %collective-permute-done.6.rest_3_), channel_id=1, source_target_pairs={{1,0},{2,1},{5,4},{6,5},{9,8},{10,9},{13,12},{14,13},{17,16},{18,1... | collective-permute-start | bytes 995336 | tf_op jit(solution)/shard_map/ppermute | solution.py:256
  21.5 17.5 %collective-permute-start.1 = (bf16[256,1152]{1,0:T(8,128)(2,1)S(1)}, bf16[256,1152]{1,0:T(8,128)(2,1)S(1)}, u32[]{:S(2)}, u32[]{:S(2)}) collective-permute-start(bf16[256,1152]{1,0:T(8,128)(2,1)S(1)} %broadcast_select_fusion.1), channel_id=1, source_target_pairs={{0,4},{1,5},{2,6},{3,7},{4,0},{5,1},{6,2},{7,3},{8,12},{9,13},{10,... | collective-permute-start | bytes 1769480 | tf_op jit(solution)/shard_map/ppermute | solution.py:260
  21.6 10.8 %collective-permute-start.9 = (bf16[144,1152]{1,0:T(8,128)(2,1)S(1)}, bf16[144,1152]{1,0:T(8,128)(2,1)S(1)}, u32[]{:S(2)}, u32[]{:S(2)}) collective-permute-start(bf16[144,1152]{1,0:T(8,128)(2,1)S(1)} %collective-permute-done.3.rest_0_), channel_id=1, source_target_pairs={{1,5},{2,6},{3,7},{5,1},{6,2},{7,3},{9,13},{10,14},{11,15},{13,9},... | collective-permute-start | bytes 995336 | tf_op jit(solution)/shard_map/ppermute | solution.py:260
  22.3 10.8 %collective-permute-start.5 = (bf16[144,1152]{1,0:T(8,128)(2,1)S(1)}, bf16[144,1152]{1,0:T(8,128)(2,1)S(1)}, u32[]{:S(2)}, u32[]{:S(2)}) collective-permute-start(bf16[144,1152]{1,0:T(8,128)(2,1)S(1)} %collective-permute-done.4.rest_1_), channel_id=1, source_target_pairs={{2,3},{6,7},{10,11},{14,15},{18,19},{22,23},{26,27},{30,31}} | collective-permute-start | bytes 995336 | tf_op jit(solution)/shard_map/ppermute | solution.py:256
  29.1 9.2 %collective-permute-start.8 = (bf16[144,1152]{1,0:T(8,128)(2,1)S(1)}, bf16[144,1152]{1,0:T(8,128)(2,1)S(1)}, u32[]{:S(2)}, u32[]{:S(2)}) collective-permute-start(bf16[144,1152]{1,0:T(8,128)(2,1)S(1)} %collective-permute-done.7.rest_4_), channel_id=1, source_target_pairs={{1,0},{5,4},{9,8},{13,12},{17,16},{21,20},{25,24},{29,28}} | collective-permute-start | bytes 995336 | tf_op jit(solution)/shard_map/ppermute | solution.py:256
  30.4 13.9 %collective-permute-start.12 = (bf16[144,1152]{1,0:T(8,128)(2,1)S(1)}, bf16[144,1152]{1,0:T(8,128)(2,1)S(1)}, u32[]{:S(2)}, u32[]{:S(2)}) collective-permute-start(bf16[144,1152]{1,0:T(8,128)(2,1)S(1)} %collective-permute-done.6.rest_3_), channel_id=1, source_target_pairs={{0,4},{1,5},{2,6},{4,0},{5,1},{6,2},{8,12},{9,13},{10,14},{12,8},{... | collective-permute-start | bytes 995336 | tf_op jit(solution)/shard_map/ppermute | solution.py:260
  32.4 12.0 %collective-permute-start.10 = (bf16[144,1152]{1,0:T(8,128)(2,1)S(1)}, bf16[144,1152]{1,0:T(8,128)(2,1)S(1)}, u32[]{:S(2)}, u32[]{:S(2)}) collective-permute-start(bf16[144,1152]{1,0:T(8,128)(2,1)S(1)} %collective-permute-done.4.rest_1_), channel_id=1, source_target_pairs={{2,6},{3,7},{6,2},{7,3},{10,14},{11,15},{14,10},{15,11},{18,22},{1... | collective-permute-start | bytes 995336 | tf_op jit(solution)/shard_map/ppermute | solution.py:260
  33.1 11.3 %collective-permute-start.13 = (bf16[144,1152]{1,0:T(8,128)(2,1)S(1)}, bf16[144,1152]{1,0:T(8,128)(2,1)S(1)}, u32[]{:S(2)}, u32[]{:S(2)}) collective-permute-start(bf16[144,1152]{1,0:T(8,128)(2,1)S(1)} %collective-permute-done.7.rest_4_), channel_id=1, source_target_pairs={{0,4},{1,5},{4,0},{5,1},{8,12},{9,13},{12,8},{13,9},{16,20},{17,21... | collective-permute-start | bytes 995336 | tf_op jit(solution)/shard_map/ppermute | solution.py:260
  38.3 6.1 %collective-permute-start.11 = (bf16[144,1152]{1,0:T(8,128)(2,1)S(1)}, bf16[144,1152]{1,0:T(8,128)(2,1)S(1)}, u32[]{:S(2)}, u32[]{:S(2)}) collective-permute-start(bf16[144,1152]{1,0:T(8,128)(2,1)S(1)} %collective-permute-done.5.rest_2_), channel_id=1, source_target_pairs={{3,7},{7,3},{11,15},{15,11},{19,23},{23,19},{27,31},{31,27}} | collective-permute-start | bytes 995336 | tf_op jit(solution)/shard_map/ppermute | solution.py:260
  39.0 5.4 %collective-permute-start.14 = (bf16[144,1152]{1,0:T(8,128)(2,1)S(1)}, bf16[144,1152]{1,0:T(8,128)(2,1)S(1)}, u32[]{:S(2)}, u32[]{:S(2)}) collective-permute-start(bf16[144,1152]{1,0:T(8,128)(2,1)S(1)} %collective-permute-done.8.rest_5_), channel_id=1, source_target_pairs={{0,4},{4,0},{8,12},{12,8},{16,20},{20,16},{24,28},{28,24}} | collective-permute-start | bytes 995336 | tf_op jit(solution)/shard_map/ppermute | solution.py:260
  43.1 1.2 %copy-start.2 = (bf16[768,1152]{1,0:T(8,128)(2,1)}, bf16[768,1152]{1,0:T(8,128)(2,1)S(1)}, u32[]{:S(2)}) copy-start(bf16[768,1152]{1,0:T(8,128)(2,1)S(1)} %get-tuple-element.16.units) | copy-start | bytes 5308420
  49.8 15.8 %collective-permute-start.25 = (bf16[256,1152]{1,0:T(8,128)(2,1)S(1)}, bf16[256,1152]{1,0:T(8,128)(2,1)S(1)}, u32[]{:S(2)}, u32[]{:S(2)}) collective-permute-start(bf16[256,1152]{1,0:T(8,128)(2,1)S(1)} %get-tuple-element.27.u0), channel_id=1, source_target_pairs={{0,24},{4,28},{8,0},{12,4},{16,8},{20,12},{24,16},{28,20},{1,25},{... | collective-permute-start | bytes 1769480 | tf_op jit(solution)/shard_map/ppermute | solution.py:263
  51.7 14.1 %collective-permute-start.15 = (bf16[256,256]{1,0:T(8,128)(2,1)S(1)}, bf16[256,256]{1,0:T(8,128)(2,1)S(1)}, u32[]{:S(2)}, u32[]{:S(2)}) collective-permute-start(bf16[256,256]{1,0:T(8,128)(2,1)S(1)} %slice.9), channel_id=1, source_target_pairs={{0,1},{3,2},{4,5},{7,6},{8,9},{11,10},{12,13},{15,14},{16,17},{19,... | collective-permute-start | bytes 393224 | tf_op jit(solution)/shard_map/ppermute | solution.py:256
  53.0 13.9 %collective-permute-start.16 = (bf16[256,384]{1,0:T(8,128)(2,1)S(1)}, bf16[256,384]{1,0:T(8,128)(2,1)S(1)}, u32[]{:S(2)}, u32[]{:S(2)}) collective-permute-start(bf16[256,384]{1,0:T(8,128)(2,1)S(1)} %slice.10), channel_id=1, source_target_pairs={{0,1},{3,2},{4,5},{7,6},{8,9},{11,10},{12,13},{15,14},{16,17},{19,... | collective-permute-start | bytes 589832 | tf_op jit(solution)/shard_map/ppermute | solution.py:256
  54.3 13.9 %collective-permute-start.17 = (bf16[256,512]{1,0:T(8,128)(2,1)S(1)}, bf16[256,512]{1,0:T(8,128)(2,1)S(1)}, u32[]{:S(2)}, u32[]{:S(2)}) collective-permute-start(bf16[256,512]{1,0:T(8,128)(2,1)S(1)} %slice.11), channel_id=1, source_target_pairs={{0,1},{3,2},{4,5},{7,6},{8,9},{11,10},{12,13},{15,14},{16,17},{19,... | collective-permute-start | bytes 786440 | tf_op jit(solution)/shard_map/ppermute | solution.py:256
  56.0 42.1 %collective-permute-start.24 = (bf16[288,1152]{1,0:T(8,128)(2,1)S(1)}, bf16[288,1152]{1,0:T(8,128)(2,1)S(1)}, u32[]{:S(2)}, u32[]{:S(2)}) collective-permute-start(bf16[288,1152]{1,0:T(8,128)(2,1)S(1)} %outward.1), channel_id=1, source_target_pairs={{1,0},{2,3},{5,4},{6,7},{9,8},{10,11},{13,12},{14,15},{17,16},{18,... | collective-permute-start | bytes 1990664 | tf_op jit(solution)/shard_map/ppermute | solution.py:256
  65.7 33.7 %collective-permute-start.26 = (bf16[256,1152]{1,0:T(8,128)(2,1)S(1)}, bf16[256,1152]{1,0:T(8,128)(2,1)S(1)}, u32[]{:S(2)}, u32[]{:S(2)}) collective-permute-start(bf16[256,1152]{1,0:T(8,128)(2,1)S(1)} %broadcast_select_fusion), channel_id=1, source_target_pairs={{0,4},{1,5},{2,6},{3,7},{4,0},{5,1},{6,2},{7,3},{8,12},{9,13},{10,... | collective-permute-start | bytes 1769480 | tf_op jit(solution)/shard_map/ppermute | solution.py:260
  66.2 3.9 %collective-permute-start.18 = (bf16[288,256]{1,0:T(8,128)(2,1)S(1)}, bf16[288,256]{1,0:T(8,128)(2,1)S(1)}, u32[]{:S(2)}, u32[]{:S(2)}) collective-permute-start(bf16[288,256]{1,0:T(8,128)(2,1)S(1)} %get-tuple-element.21), channel_id=1, source_target_pairs={{1,2},{2,1},{5,6},{6,5},{9,10},{10,9},{13,14},{14,13},{17,18},{18,... | collective-permute-start | bytes 442376 | tf_op jit(solution)/shard_map/ppermute | solution.py:256
  67.5 15.2 %collective-permute-start.19 = (bf16[288,384]{1,0:T(8,128)(2,1)S(1)}, bf16[288,384]{1,0:T(8,128)(2,1)S(1)}, u32[]{:S(2)}, u32[]{:S(2)}) collective-permute-start(bf16[288,384]{1,0:T(8,128)(2,1)S(1)} %get-tuple-element.22), channel_id=1, source_target_pairs={{1,2},{2,1},{5,6},{6,5},{9,10},{10,9},{13,14},{14,13},{17,18},{18,... | collective-permute-start | bytes 663560 | tf_op jit(solution)/shard_map/ppermute | solution.py:256
  68.2 13.2 %collective-permute-start.21 = (bf16[288,256]{1,0:T(8,128)(2,1)S(1)}, bf16[288,256]{1,0:T(8,128)(2,1)S(1)}, u32[]{:S(2)}, u32[]{:S(2)}) collective-permute-start(bf16[288,256]{1,0:T(8,128)(2,1)S(1)} %get-tuple-element.24), channel_id=1, source_target_pairs={{1,3},{2,0},{5,7},{6,4},{9,11},{10,8},{13,15},{14,12},{17,19},{18,... | collective-permute-start | bytes 442376 | tf_op jit(solution)/shard_map/ppermute | solution.py:256
  70.2 27.9 %collective-permute-start.20 = (bf16[288,512]{1,0:T(8,128)(2,1)S(1)}, bf16[288,512]{1,0:T(8,128)(2,1)S(1)}, u32[]{:S(2)}, u32[]{:S(2)}) collective-permute-start(bf16[288,512]{1,0:T(8,128)(2,1)S(1)} %get-tuple-element.23), channel_id=1, source_target_pairs={{1,2},{2,1},{5,6},{6,5},{9,10},{10,9},{13,14},{14,13},{17,18},{18,... | collective-permute-start | bytes 884744 | tf_op jit(solution)/shard_map/ppermute | solution.py:256
  81.4 16.7 %collective-permute-start.23 = (bf16[288,512]{1,0:T(8,128)(2,1)S(1)}, bf16[288,512]{1,0:T(8,128)(2,1)S(1)}, u32[]{:S(2)}, u32[]{:S(2)}) collective-permute-start(bf16[288,512]{1,0:T(8,128)(2,1)S(1)} %get-tuple-element.26), channel_id=1, source_target_pairs={{1,3},{2,0},{5,7},{6,4},{9,11},{10,8},{13,15},{14,12},{17,19},{18,... | collective-permute-start | bytes 884744 | tf_op jit(solution)/shard_map/ppermute | solution.py:256
  82.7 15.4 %collective-permute-start.22 = (bf16[288,384]{1,0:T(8,128)(2,1)S(1)}, bf16[288,384]{1,0:T(8,128)(2,1)S(1)}, u32[]{:S(2)}, u32[]{:S(2)}) collective-permute-start(bf16[288,384]{1,0:T(8,128)(2,1)S(1)} %get-tuple-element.25), channel_id=1, source_target_pairs={{1,3},{2,0},{5,7},{6,4},{9,11},{10,8},{13,15},{14,12},{17,19},{18,... | collective-permute-start | bytes 663560 | tf_op jit(solution)/shard_map/ppermute | solution.py:256

commit v2 on v1

v2 whole, which is shorter than its diff:
```python
import functools

import jax
import jax.numpy as jnp
from jax import lax
from jax.experimental import pallas as pl
from jax.experimental.pallas import tpu as pltpu
from jax.sharding import PartitionSpec as P

STEPS = 3
EPS = 1e-06
SHARES = (1, 2)
VMEM_BYTES = 24 * 1024 * 1024
BF16, F32 = jnp.bfloat16, jnp.float32


def spaces(count):
    return [pl.BlockSpec(memory_space=pltpu.VMEM)] * count


def params():
    return pltpu.CompilerParams(vmem_limit_bytes=VMEM_BYTES)


def cost(flops, *arrays):
    size = sum(a.size * a.dtype.itemsize for a in arrays)
    return pl.CostEstimate(flops=flops, bytes_accessed=size, transcendentals=0)


def place(n_dp):
    where = lax.axis_index("dp")
    return lax.axis_index("fsdp"), lax.rem(where, 2), lax.div(where, n_dp // 2)


def cut_kernel(n_dp, short, own, whole, part, sem):
    _, core, side = place(n_dp)
    half = whole.shape[0]
    first = pltpu.make_async_copy(
        own.at[pl.ds(pl.multiple_of(core * half, 16), half), :], whole, sem.at[0]
    )
    start = pl.multiple_of(core * half + side * (half - short), 16)
    second = pltpu.make_async_copy(own.at[pl.ds(start, short), :], part, sem.at[1])
    first.start()
    second.start()
    first.wait()
    second.wait()


def cut(n_dp, short, own):
    half, width = own.shape[0] // 2, own.shape[1]
    outs = (
        jax.ShapeDtypeStruct((half, width), BF16),
        jax.ShapeDtypeStruct((short, width), BF16),
    )
    return pl.pallas_call(
        functools.partial(cut_kernel, n_dp, short),
        out_shape=outs,
        in_specs=[pl.BlockSpec(memory_space=pl.ANY)],
        out_specs=spaces(2),
        scratch_shapes=[pltpu.SemaphoreType.DMA((2,))],
        compiler_params=params(),
        cost_estimate=cost(0, *outs, *outs),
        name="cut",
    )(own)


def prepare_kernel(t0, t1, t2, units):
    rows = t0.shape[0]
    for k, block in enumerate((t0, t1, t2)):
        values = block[...].astype(F32)
        inverse = 1.0 / jnp.sqrt(jnp.sum(values * values, axis=-1, keepdims=True) + EPS)
        units[k * rows : (k + 1) * rows, :] = (values * inverse).astype(BF16)


def prepare(t0, t1, t2):
    rows, width = t0.shape
    out = jax.ShapeDtypeStruct((STEPS * rows, width), BF16)
    return pl.pallas_call(
        prepare_kernel,
        out_shape=out,
        in_specs=spaces(3),
        out_specs=pl.BlockSpec(memory_space=pltpu.VMEM),
        compiler_params=params(),
        cost_estimate=cost(0, t0, t1, t2, out),
        name="prepare",
    )(t0, t1, t2)


def turn_kernel(x, x_t):
    x_t[...] = x[...].T


def turned(x):
    out = jax.ShapeDtypeStruct(x.shape[::-1], BF16)
    return pl.pallas_call(
        turn_kernel,
        out_shape=out,
        in_specs=spaces(1),
        out_specs=pl.BlockSpec(memory_space=pltpu.VMEM),
        compiler_params=params(),
        cost_estimate=cost(0, x, out),
        name="turned",
    )(x)


def rows_of(ref, block, depth):
    return ref[pl.ds(pl.multiple_of(block * depth, 16), depth), :]


def picture_kernel(n_dp, x, x_t, units, sharp, bias, own, *rest):
    pieces, outs = rest[:8], rest[8 : 8 + len(SHARES)]
    grad, unit, w, proj, sem = rest[8 + len(SHARES) :]
    part, core, side = place(n_dp)
    depth = own.shape[0]
    half = depth // 2
    short = pieces[2].shape[0]
    rest_rows = half - short
    rows = x.shape[0]
    step = 1 - 2 * side
    copies = [
        pltpu.make_async_copy(
            own, w.at[pl.ds(pl.multiple_of(part * depth, 16), depth), :], sem.at[8]
        )
    ]
    for twin in (0, 1):
        lane = core if twin == 0 else 1 - core
        straight, crossed, two, two_crossed = pieces[4 * twin : 4 * twin + 4]
        for index, piece, from_part in ((0, straight, part + 4 - step), (1, crossed, part + 4 + step)):
            start = pl.multiple_of(lax.rem(from_part, 4) * depth + lane * half, 16)
            copies.append(
                pltpu.make_async_copy(piece, w.at[pl.ds(start, half), :], sem.at[4 * twin + index])
            )
        base = lax.rem(part + 2, 4) * depth + lane * half
        start = pl.multiple_of(base + side * rest_rows, 16)
        copies.append(
            pltpu.make_async_copy(two, w.at[pl.ds(start, short), :], sem.at[4 * twin + 2])
        )
        source = pl.multiple_of((1 - side) * (short - rest_rows), 16)
        start = pl.multiple_of(base + (1 - side) * short, 16)
        copies.append(
            pltpu.make_async_copy(
                two_crossed.at[pl.ds(source, rest_rows), :],
                w.at[pl.ds(start, rest_rows), :],
                sem.at[4 * twin + 3],
            )
        )
    for copy in copies:
        copy.start()
    for copy in copies:
        copy.wait()

    proj[...] = jnp.dot(x[...], w[...], preferred_element_type=F32)
    values = proj[...]
    inverse = 1.0 / jnp.sqrt(jnp.sum(values * values, axis=-1, keepdims=True) + EPS)
    unit[...] = (values * inverse).astype(BF16)
    scale = sharp[0]
    logits = scale * lax.dot_general(
        unit[...], units[...], (((1,), (1,)), ((), ())), preferred_element_type=F32
    ) + bias[0]
    coefficient = jax.nn.sigmoid(logits)
    row = lax.broadcasted_iota(jnp.int32, coefficient.shape, 0)
    column = lax.broadcasted_iota(jnp.int32, coefficient.shape, 1)
    coefficient = jnp.where(row == column, coefficient - 1.0, coefficient).astype(BF16)
    slope = scale * jnp.dot(coefficient, units[...], preferred_element_type=F32)
    direction = proj[...] * inverse
    along = jnp.sum(direction * slope, axis=-1, keepdims=True)
    grad[...] = ((slope - direction * along) * inverse).astype(BF16)
    inner = jnp.logical_or(part == 1, part == 2)

    @pl.when(inner)
    def _():
        block = rows_of(x_t, 3 * (part - 1), depth)
        begin = 0
        for out in outs:
            stop = begin + out.shape[1]
            out[...] = jnp.dot(block, grad[:, begin:stop], preferred_element_type=F32).astype(BF16)
            begin = stop

    @pl.when(jnp.logical_not(inner))
    def _():
        begin = 0
        for out in outs:
            stop = begin + out.shape[1]
            out[:rows, :] = grad[:, begin:stop]
            out[rows:, :] = jnp.zeros((depth - rows, stop - begin), BF16)
            begin = stop


def picture_side(n_dp, x, x_t, units, sharp, bias, own, pieces):
    rows, width = x.shape
    depth = own.shape[0]
    out = jax.ShapeDtypeStruct((rows, width), BF16)
    smem = pl.BlockSpec(memory_space=pltpu.SMEM)
    sizes = [width * share // sum(SHARES) for share in SHARES]
    outs = tuple(jax.ShapeDtypeStruct((depth, size), BF16) for size in sizes) + (out, out)
    return pl.pallas_call(
        functools.partial(picture_kernel, n_dp),
        out_shape=outs,
        in_specs=spaces(3) + [smem, smem] + [pl.BlockSpec(memory_space=pl.ANY)] * 9,
        out_specs=spaces(len(outs)),
        scratch_shapes=[
            pltpu.VMEM((width, width), BF16),
            pltpu.VMEM((rows, width), F32),
            pltpu.SemaphoreType.DMA((9,)),
        ],
        compiler_params=params(),
        cost_estimate=cost(2 * rows * width * (width + 2 * STEPS * rows), x, units, own, out, out),
        name="picture_side",
    )(x, x_t, units, sharp, bias, own, *pieces)


def text_kernel(text, u0, u1, u2, sharp, bias, out, units):
    rows = text.shape[0]
    for k, block in enumerate((u0, u1, u2)):
        units[k * rows : (k + 1) * rows, :] = block[...]
    values = text[...].astype(F32)
    inverse = 1.0 / jnp.sqrt(jnp.sum(values * values, axis=-1, keepdims=True) + EPS)
    direction = values * inverse
    scale = sharp[0]
    logits = scale * lax.dot_general(
        direction.astype(BF16), units[...], (((1,), (1,)), ((), ())), preferred_element_type=F32
    ) + bias[0]
    coefficient = jax.nn.sigmoid(logits)
    row = lax.broadcasted_iota(jnp.int32, coefficient.shape, 0)
    column = lax.broadcasted_iota(jnp.int32, coefficient.shape, 1)
    coefficient = jnp.where(row == column, coefficient - 1.0, coefficient).astype(BF16)
    slope = scale * jnp.dot(coefficient, units[...], preferred_element_type=F32)
    along = jnp.sum(direction * slope, axis=-1, keepdims=True)
    out[...] = (slope - direction * along) * inverse


def text_side(text, u0, u1, u2, sharp, bias):
    rows, width = text.shape
    out = jax.ShapeDtypeStruct((rows, width), F32)
    smem = pl.BlockSpec(memory_space=pltpu.SMEM)
    return pl.pallas_call(
        text_kernel,
        out_shape=out,
        in_specs=spaces(4) + [smem, smem],
        out_specs=pl.BlockSpec(memory_space=pltpu.VMEM),
        scratch_shapes=[pltpu.VMEM((STEPS * rows, width), BF16)],
        compiler_params=params(),
        cost_estimate=cost(4 * STEPS * rows * rows * width, text, u0, u1, u2, out),
        name="text_side",
    )(text, u0, u1, u2, sharp, bias)


def pair_kernel(begin, x_t, far_t, grad, arrived, kept, near, far):
    rows = grad.shape[0]
    depth, size = arrived.shape
    part = lax.axis_index("fsdp")
    inner = jnp.logical_or(part == 1, part == 2)
    mine = grad[:, begin : begin + size]

    def product(block):
        return jnp.dot(rows_of(x_t, block, depth), mine, preferred_element_type=F32)

    @pl.when(inner)
    def _():
        other = arrived[:rows, :]
        for block, out in ((3 - part, near), (lax.rem(part + 2, 4), far), (part, kept)):
            both = product(block) + jnp.dot(
                rows_of(far_t, block, depth), other, preferred_element_type=F32
            )
            out[...] = both.astype(out.dtype)

    @pl.when(jnp.logical_not(inner))
    def _():
        kept[...] = product(part) + arrived[...].astype(F32)
        near[...] = jnp.zeros_like(near)
        far[...] = jnp.zeros_like(far)


def pair_product(begin, x_t, far_t, grad, arrived):
    outs = tuple(jax.ShapeDtypeStruct(arrived.shape, t) for t in (F32, BF16, BF16))
    return pl.pallas_call(
        functools.partial(pair_kernel, begin),
        out_shape=outs,
        in_specs=spaces(4),
        out_specs=spaces(3),
        compiler_params=params(),
        cost_estimate=cost(12 * grad.shape[0] * arrived.size, x_t, far_t, grad, arrived, *outs),
        name="pair_product",
    )(x_t, far_t, grad, arrived)


def total_kernel(*refs):
    kept, near, far = (refs[k : len(refs) - 1 : 3] for k in range(3))
    out = refs[-1]
    begin = 0
    for a, b, c in zip(kept, near, far):
        stop = begin + a.shape[1]
        out[0, :, begin:stop] = a[...] + b[...].astype(F32) + c[...].astype(F32)
        begin = stop


def total(terms, depth, width):
    out = jax.ShapeDtypeStruct((1, depth, width), F32)
    return pl.pallas_call(
        total_kernel,
        out_shape=out,
        in_specs=spaces(len(terms)),
        out_specs=pl.BlockSpec(memory_space=pltpu.VMEM),
        compiler_params=params(),
        cost_estimate=cost(0, *terms, out),
        name="total",
    )(*terms)


def line_body(n_dp, n_fsdp, x, text, w, sharp, bias):
    depth, width = w.shape
    half = depth // 2
    short = (half // 2 + 15) // 16 * 16
    core = lax.rem(lax.axis_index("dp"), 2)
    side = n_dp // 2

    def along(value, pairs):
        return lax.ppermute(value, "fsdp", pairs)

    def across(value):
        return lax.ppermute(value, "dp", [(d, d ^ 1) for d in range(n_dp)])

    def over(value):
        return lax.ppermute(value, "dp", [(d, (d + side) % n_dp) for d in range(n_dp)])

    def shifted(value, by):
        return lax.ppermute(value, "dp", [(d, (d + by) % n_dp) for d in range(n_dp)])

    whole, piece = cut(n_dp, short, w)
    turns = [
        (d * n_fsdp + f, d * n_fsdp + (f + (1 if d < side else n_fsdp - 1)) % n_fsdp)
        for d in range(n_dp)
        for f in range(n_fsdp)
    ]
    straight = lax.ppermute(whole, ("dp", "fsdp"), turns)
    text2 = shifted(text, 2)
    two = along(piece, [(f, (f + 2) % n_fsdp) for f in range(n_fsdp)])
    far_x = along(x, [(0, 1), (3, 2)])
    crossed = over(straight)
    two_crossed = over(two)
    pieces = [straight, crossed, two, two_crossed]
    pieces = pieces + [across(piece) for piece in pieces]
    text1 = across(jnp.where(core == 0, text, text2))

    x_t, far_t = turned(x), turned(far_x)
    units = prepare(text, text1, text2)
    *outward, grad, unit = picture_side(n_dp, x, x_t, units, sharp, bias, w, pieces)

    arrived = [along(o, [(0, 1), (1, 0), (2, 3), (3, 2)]) for o in outward]
    begin, terms = 0, []
    for k, block in enumerate(arrived):
        kept, near, far = pair_product(begin, x_t, far_t, grad, block)
        begin += block.shape[1]
        if k == 0:
            unit, near, far = lax.optimization_barrier((unit, near, far))
        terms += [kept, along(near, [(1, 2), (2, 1)]), along(far, [(1, 3), (2, 0)])]
    unit2 = shifted(unit, -2)
    unit1 = across(jnp.where(core == 0, unit2, unit))
    text_grad = text_side(text, unit, unit1, unit2, sharp, bias)
    return total(terms, depth, width), text_grad


def plain_body(n_dp, n_fsdp, x, text, w, sharp, bias):
    def shifted(value, by):
        return lax.ppermute(value, "dp", [(d, (d + by) % n_dp) for d in range(n_dp)])

    rows, width = x.shape
    proj = jnp.dot(
        x, lax.all_gather(w, "fsdp", axis=0, tiled=True), preferred_element_type=F32
    )
    norm = jnp.sqrt(jnp.sum(proj * proj, axis=-1, keepdims=True) + EPS)
    direction = proj / norm
    unit = direction.astype(BF16)
    values = text.astype(F32)
    txt_norm = jnp.sqrt(jnp.sum(values * values, axis=-1, keepdims=True) + EPS)
    txt_dir = values / txt_norm
    slot = txt_dir.astype(BF16)
    scale = sharp[0]
    slope = jnp.zeros((rows, width), F32)
    txt_slope = jnp.zeros((rows, width), F32)
    for step in range(STEPS):
        if step > 0:
            slot = shifted(slot, 1)
        logits = scale * jnp.dot(unit, slot.T, preferred_element_type=F32) + bias[0]
        coefficient = jax.nn.sigmoid(logits)
        if step == 0:
            coefficient = coefficient - jnp.eye(rows, dtype=F32)
        coefficient = coefficient.astype(BF16)
        slope = slope + scale * jnp.dot(coefficient, slot, preferred_element_type=F32)
        share = scale * lax.dot_general(
            coefficient, unit, (((0,), (0,)), ((), ())), preferred_element_type=F32
        )
        if step > 0:
            share = shifted(share.astype(BF16), -step).astype(F32)
        txt_slope = txt_slope + share
    grad = (
        (slope - direction * jnp.sum(direction * slope, axis=-1, keepdims=True)) / norm
    ).astype(BF16)
    text_grad = (
        txt_slope - txt_dir * jnp.sum(txt_dir * txt_slope, axis=-1, keepdims=True)
    ) / txt_norm
    partial = lax.dot_general(
        x, grad, (((0,), (0,)), ((), ())), preferred_element_type=F32
    ).astype(BF16)
    head = lax.psum_scatter(partial, "fsdp", scatter_dimension=0, tiled=True).astype(F32)
    return head[None], text_grad


def solution(mesh):
    n_dp, n_fsdp = mesh.shape["dp"], mesh.shape["fsdp"]
    line = n_fsdp == 4 and n_dp % 4 == 0
    placed = (P(("dp", "fsdp"), None), P(("dp", "fsdp"), None), P("fsdp", None), P(), P())
    return jax.shard_map(
        functools.partial(line_body if line else plain_body, n_dp, n_fsdp),
        mesh=mesh,
        in_specs=placed,
        out_specs=(P("dp", "fsdp", None), P(("dp", "fsdp"), None)),
        check_vma=False,
    )
```

time: 103 us -> 110 us (1.068)
  waiting for transfers between devices: 46.3 us -> 70.7 us
  starting transfers between devices: 37.5 us -> 23.4 us
  Pallas kernels: 12.6 us -> 10.6 us
    ppermute x2, waiting for transfers between devices: 8.37 us -> 21.4 us  [shifted(): lax.ppermute(value, 'dp', [(d, (d + by) % n_dp) for d in range(n_dp)])]
    ppermute x17 -> x8, starting transfers between devices: 24.4 us -> 13.8 us  [along(): return lax.ppermute(value, 'fsdp', pairs)]
    ppermute x17 -> x8, waiting for transfers between devices: 37.9 us -> 47.1 us  [along(): return lax.ppermute(value, 'fsdp', pairs)]
    ppermute x8 -> x9, starting transfers between devices: 8.42 us -> 5.02 us  [the longest x2 2.23 us: over(): lax.ppermute(value, 'dp', [(d, (d + side) % n_dp) for d in range(n_dp)])]
    ppermute x8 -> x9, waiting for transfers between devices: 0.02 us -> 2.25 us  [the longest x2 2.23 us: over(): lax.ppermute(value, 'dp', [(d, (d + side) % n_dp) for d in range(n_dp)])]
    pallas_call x7 -> x8, Pallas kernels: 9.71 us -> 7.73 us  [the longest x1 4.46 us: picture_side(): pl.pallas_call(functools.partial(picture_kernel, n_dp), out_shape=outs, i...]
  transfers between devices with their start and end apart: 27 -> 19, of which waited for: 7 -> 7; matrix products, arithmetic and copies ran while one was open for 2% -> 1% of each run, Pallas kernels for 4% -> 7%
where the time goes in v2:
time: 110 us
  waiting for transfers between devices  70.7 us (64%)
  starting transfers between devices  23.4 us (21%)
  Pallas kernels  10.6 us (10%)
  between operations  2.13 us (2%)
  local copies, waits for them, and re-layouts  1.46 us (1%)
  other arithmetic  1.2 us (1%)
    ppermute x8, waiting for transfers between devices, along(): return lax.ppermute(value, 'fsdp', pairs)  47.1 us
    ppermute x2, waiting for transfers between devices, shifted(): lax.ppermute(value, 'dp', [(d, (d + by) % n_dp) for d in range(n_dp)])  21.4 us
    ppermute x8, starting transfers between devices, along(): return lax.ppermute(value, 'fsdp', pairs)  13.8 us
    ppermute x2, starting transfers between devices, shifted(): lax.ppermute(value, 'dp', [(d, (d + by) % n_dp) for d in range(n_dp)])  4.59 us
    pallas_call x1, Pallas kernels, picture_side(): pl.pallas_call(functools.partial(picture_kernel, n_dp), out_shape=outs, i...  4.46 us
    pallas_call x1, Pallas kernels, text_side(): pl.pallas_call(text_kernel, out_shape=out, in_specs=spaces(4) + [smem, sm...  2.85 us
    ppermute x2, waiting for transfers between devices, over(): lax.ppermute(value, 'dp', [(d, (d + side) % n_dp) for d in range(n_dp)])  2.23 us
    ppermute x2, starting transfers between devices, over(): lax.ppermute(value, 'dp', [(d, (d + side) % n_dp) for d in range(n_dp)])  2.23 us
  transfers between devices with their start and end apart: 19, of which 7 were waited for; matrix products, arithmetic and copies ran while one was open for 1% of the time, Pallas kernels for 7%

profile of v2, /device:TPU:0, one launch (start us, length us, event | category | flops | bytes accessed | tf_op | source)
XLA Modules:
  0.0 109.5 jit_solution(14403347278848082763)
XLA Ops:
  0.6 3.0 %collective-permute-start.1 = (bf16[256,1152]{1,0:T(8,128)(2,1)}, bf16[256,1152]{1,0:T(8,128)(2,1)S(1)}, u32[]{:S(2)}, u32[]{:S(2)}) collective-permute-start(bf16[256,1152]{1,0:T(8,128)(2,1)} %text.1), channel_id=1, source_target_pairs={{0,8},{4,12},{8,16},{12,20},{16,24},{20,28},{24,0},{28,4},{1,9},{5... | collective-permute-start | bytes 1769480 | tf_op jit(solution)/shard_map/ppermute | solution.py:327
  3.6 1.1 copy-done.1
  4.7 0.4 cut.1
  5.1 1.6 %collective-permute-start.3 = (bf16[144,1152]{1,0:T(8,128)(2,1)S(1)}, bf16[144,1152]{1,0:T(8,128)(2,1)S(1)}, u32[]{:S(2)}, u32[]{:S(2)}) collective-permute-start(bf16[144,1152]{1,0:T(8,128)(2,1)S(1)} %get-tuple-element.17), channel_id=1, source_target_pairs={{0,1},{1,2},{2,3},{3,0},{4,5},{5,6},{6,7},{7,4},{8,9},{9,10},{10,1... | collective-permute-start | bytes 995336 | tf_op jit(solution)/shard_map/ppermute | solution.py:335
  6.7 11.4 %collective-permute-done.1.t2 = bf16[256,1152]{1,0:T(8,128)(2,1)S(1)} collective-permute-done((bf16[256,1152]{1,0:T(8,128)(2,1)}, bf16[256,1152]{1,0:T(8,128)(2,1)S(1)}, u32[]{:S(2)}, u32[]{:S(2)}) %collective-permute-start.1) | collective-permute-done | bytes 589856 | tf_op jit(solution)/shard_map/ppermute | solution.py:327
  18.1 1.1 %broadcast_select_fusion.1 = bf16[256,1152]{1,0:T(8,128)(2,1)S(1)} fusion(bf16[256,1152]{1,0:T(8,128)(2,1)} %text.1, bf16[256,1152]{1,0:T(8,128)(2,1)S(1)} %collective-permute-done.1.t2, pred[]{:T(512)S(6)} %eq.4), kind=kLoop, calls=%fused_computation.1 | loop fusion | flops 294912 | bytes 1769473 | tf_op jit(solution)/shard_map/jit(_where)/select_n | solution.py:343
  19.3 1.8 %collective-permute-start.4 = (bf16[144,1152]{1,0:T(8,128)(2,1)S(1)}, bf16[144,1152]{1,0:T(8,128)(2,1)S(1)}, u32[]{:S(2)}, u32[]{:S(2)}) collective-permute-start(bf16[144,1152]{1,0:T(8,128)(2,1)S(1)} %collective-permute-done.3.rest_0_), channel_id=1, source_target_pairs={{0,16},{4,20},{8,24},{12,28},{16,0},{20,4},{24,8},{28,12},{1,17},{... | collective-permute-start | bytes 995336 | tf_op jit(solution)/shard_map/ppermute | solution.py:324
  21.1 2.6 %collective-permute-start.5 = (bf16[80,1152]{1,0:T(8,128)(2,1)S(1)}, bf16[80,1152]{1,0:T(8,128)(2,1)S(1)}, u32[]{:S(2)}, u32[]{:S(2)}) collective-permute-start(bf16[80,1152]{1,0:T(8,128)(2,1)S(1)} %get-tuple-element.18), channel_id=1, source_target_pairs={{0,2},{1,3},{2,0},{3,1},{4,6},{5,7},{6,4},{7,5},{8,10},{9,11},{10,... | collective-permute-start | bytes 552968 | tf_op jit(solution)/shard_map/ppermute | solution.py:318
  23.7 9.0 %collective-permute-done.5.rest_2_ = bf16[80,1152]{1,0:T(8,128)(2,1)S(1)} collective-permute-done((bf16[80,1152]{1,0:T(8,128)(2,1)S(1)}, bf16[80,1152]{1,0:T(8,128)(2,1)S(1)}, u32[]{:S(2)}, u32[]{:S(2)}) %collective-permute-start.5) | collective-permute-done | bytes 184352 | tf_op jit(solution)/shard_map/ppermute | solution.py:318
  32.7 0.5 collective-permute-start.6
  33.1 0.5 collective-permute-start.8
  33.6 2.7 %collective-permute-start = (bf16[256,1152]{1,0:T(8,128)(2,1)S(1)}, bf16[256,1152]{1,0:T(8,128)(2,1)S(1)}, u32[]{:S(2)}, u32[]{:S(2)}) collective-permute-start(bf16[256,1152]{1,0:T(8,128)(2,1)S(1)} %copy-done.3), channel_id=1, source_target_pairs={{0,1},{3,2},{4,5},{7,6},{8,9},{11,10},{12,13},{15,14},{16,17},{19,... | collective-permute-start | bytes 1769480 | tf_op jit(solution)/shard_map/ppermute | solution.py:318
  36.3 2.2 %collective-permute-done.6.rest_3_ = bf16[80,1152]{1,0:T(8,128)(2,1)S(1)} collective-permute-done((bf16[80,1152]{1,0:T(8,128)(2,1)S(1)}, bf16[80,1152]{1,0:T(8,128)(2,1)S(1)}, u32[]{:S(2)}, u32[]{:S(2)}) %collective-permute-start.6) | collective-permute-done | bytes 184352 | tf_op jit(solution)/shard_map/ppermute | solution.py:324
  38.5 0.5 collective-permute-start.10
  40.6 0.7 prepare.1.units
  41.3 0.4 copy-done.2
  41.7 4.5 %picture_side.1 = (bf16[288,384]{1,0:T(8,128)(2,1)S(1)}, bf16[288,768]{1,0:T(8,128)(2,1)S(1)}, bf16[256,1152]{1,0:T(8,128)(2,1)S(1)}, bf16[256,1152]{1,0:T(8,128)(2,1)S(1)}) custom-call(bf16[256,1152]{1,0:T(8,128)(2,1)S(1)} %copy-done.3, bf16[1152,256]{1,0:T(8,128)(2,1)S(1)} %turned.2.x_t, bf16[768,1152]{1,0:T(8,128)(2,1)S(1)} %prepare.1.units, ...), custom_call_target="tpu_custom_call" | custom-call | flops 1585446912 | bytes 4202496 | tf_op jit(solution)/shard_map/picture_side/pallas_call | solution.py:196
  46.1 1.8 %collective-permute-start.11 = (bf16[288,384]{1,0:T(8,128)(2,1)S(1)}, bf16[288,384]{1,0:T(8,128)(2,1)S(1)}, u32[]{:S(2)}, u32[]{:S(2)}) collective-permute-start(bf16[288,384]{1,0:T(8,128)(2,1)S(1)} %get-tuple-element.20), channel_id=1, source_target_pairs={{0,1},{1,0},{2,3},{3,2},{4,5},{5,4},{6,7},{7,6},{8,9},{9,8},{10,11... | collective-permute-start | bytes 663560 | tf_op jit(solution)/shard_map/ppermute | solution.py:318
  47.9 2.1 %collective-permute-done.x = bf16[256,1152]{1,0:T(8,128)(2,1)S(1)} collective-permute-done((bf16[256,1152]{1,0:T(8,128)(2,1)S(1)}, bf16[256,1152]{1,0:T(8,128)(2,1)S(1)}, u32[]{:S(2)}, u32[]{:S(2)}) %collective-permute-start) | collective-permute-done | bytes 589856 | tf_op jit(solution)/shard_map/ppermute | solution.py:318
  50.2 3.6 %collective-permute-done.11.arrived = bf16[288,384]{1,0:T(8,128)(2,1)S(1)} collective-permute-done((bf16[288,384]{1,0:T(8,128)(2,1)S(1)}, bf16[288,384]{1,0:T(8,128)(2,1)S(1)}, u32[]{:S(2)}, u32[]{:S(2)}) %collective-permute-start.11) | collective-permute-done | bytes 221216 | tf_op jit(solution)/shard_map/ppermute | solution.py:318
  53.8 0.3 pair_product.2
  54.0 1.6 %collective-permute-start.17 = (bf16[256,1152]{1,0:T(8,128)(2,1)S(1)}, bf16[256,1152]{1,0:T(8,128)(2,1)S(1)}, u32[]{:S(2)}, u32[]{:S(2)}) collective-permute-start(bf16[256,1152]{1,0:T(8,128)(2,1)S(1)} %get-tuple-element.31.u0), channel_id=1, source_target_pairs={{0,24},{4,28},{8,0},{12,4},{16,8},{20,12},{24,16},{28,20},{1,25},{... | collective-permute-start | bytes 1769480 | tf_op jit(solution)/shard_map/ppermute | solution.py:327
  55.6 2.9 %collective-permute-start.14 = (bf16[288,768]{1,0:T(8,128)(2,1)S(1)}, bf16[288,768]{1,0:T(8,128)(2,1)S(1)}, u32[]{:S(2)}, u32[]{:S(2)}) collective-permute-start(bf16[288,768]{1,0:T(8,128)(2,1)S(1)} %get-tuple-element.27), channel_id=1, source_target_pairs={{0,1},{1,0},{2,3},{3,2},{4,5},{5,4},{6,7},{7,6},{8,9},{9,8},{10,11... | collective-permute-start | bytes 1327112 | tf_op jit(solution)/shard_map/ppermute | solution.py:318
  58.5 10.0 %collective-permute-done.17.u2 = bf16[256,1152]{1,0:T(8,128)(2,1)S(1)} collective-permute-done((bf16[256,1152]{1,0:T(8,128)(2,1)S(1)}, bf16[256,1152]{1,0:T(8,128)(2,1)S(1)}, u32[]{:S(2)}, u32[]{:S(2)}) %collective-permute-start.17) | collective-permute-done | bytes 589856 | tf_op jit(solution)/shard_map/ppermute | solution.py:327
  68.7 0.3 pair_product.3
  69.0 0.7 collective-permute-start.15
  69.7 1.3 %collective-permute-start.16 = (bf16[288,768]{1,0:T(8,128)(2,1)S(1)}, bf16[288,768]{1,0:T(8,128)(2,1)S(1)}, u32[]{:S(2)}, u32[]{:S(2)}) collective-permute-start(bf16[288,768]{1,0:T(8,128)(2,1)S(1)} %get-tuple-element.30), channel_id=1, source_target_pairs={{1,3},{2,0},{5,7},{6,4},{9,11},{10,8},{13,15},{14,12},{17,19},{18,... | collective-permute-start | bytes 1327112 | tf_op jit(solution)/shard_map/ppermute | solution.py:318
  71.0 0.7 collective-permute-start.12
  71.7 1.3 %collective-permute-start.13 = (bf16[288,384]{1,0:T(8,128)(2,1)S(1)}, bf16[288,384]{1,0:T(8,128)(2,1)S(1)}, u32[]{:S(2)}, u32[]{:S(2)}) collective-permute-start(bf16[288,384]{1,0:T(8,128)(2,1)S(1)} %get-tuple-element.26), channel_id=1, source_target_pairs={{1,3},{2,0},{5,7},{6,4},{9,11},{10,8},{13,15},{14,12},{17,19},{18,... | collective-permute-start | bytes 663560 | tf_op jit(solution)/shard_map/ppermute | solution.py:318
  73.0 32.4 %collective-permute-done.13.refs_2_ = bf16[288,384]{1,0:T(8,128)(2,1)S(1)} collective-permute-done((bf16[288,384]{1,0:T(8,128)(2,1)S(1)}, bf16[288,384]{1,0:T(8,128)(2,1)S(1)}, u32[]{:S(2)}, u32[]{:S(2)}) %collective-permute-start.13) | collective-permute-done | bytes 221216 | tf_op jit(solution)/shard_map/ppermute | solution.py:318
  105.4 1.3 %total.1 = f32[1,288,1152]{2,1,0:T(8,128)} custom-call(f32[288,384]{1,0:T(8,128)S(1)} %get-tuple-element.21.refs_0_, bf16[288,384]{1,0:T(8,128)(2,1)S(1)} %collective-permute-done.12.refs_1_, bf16[288,384]{1,0:T(8,128)(2,1)S(1)} %collective-permute-done.13.refs_2_, f32[288,768]{1,0:T(8,128)S(1)} %get-tuple-element.28.refs_3_, ...), custom_call_target="tpu_custom_call" | custom-call | bytes 3981312 | tf_op jit(solution)/shard_map/total/pallas_call | solution.py:299
  106.7 2.9 %text_side.1 = f32[256,1152]{1,0:T(8,128)} custom-call(bf16[256,1152]{1,0:T(8,128)(2,1)S(1)} %copy-done, bf16[256,1152]{1,0:T(8,128)(2,1)S(1)} %get-tuple-element.31.u0, bf16[256,1152]{1,0:T(8,128)(2,1)S(1)} %collective-permute-done.18.u1, bf16[256,1152]{1,0:T(8,128)(2,1)S(1)} %collective-permute-done.17.u2, f32[1]{0:T(128)S(6)} %copy.7.sharp, f32[1]{0:T(128)S(6)} %copy.8.bias), custom_call_target="tpu_custom_call" | custom-call | flops 905969664 | bytes 3538944 | tf_op jit(solution)/shard_map/text_side/pallas_call | solution.py:236
  (25 shorter events, 0.7 us)
Async XLA Ops:
  0.6 17.5 %collective-permute-start.1 = (bf16[256,1152]{1,0:T(8,128)(2,1)}, bf16[256,1152]{1,0:T(8,128)(2,1)S(1)}, u32[]{:S(2)}, u32[]{:S(2)}) collective-permute-start(bf16[256,1152]{1,0:T(8,128)(2,1)} %text.1), channel_id=1, source_target_pairs={{0,8},{4,12},{8,16},{12,20},{16,24},{20,28},{24,0},{28,4},{1,9},{5... | collective-permute-start | bytes 1769480 | tf_op jit(solution)/shard_map/ppermute | solution.py:327
  3.6 1.1 copy-start.1
  4.7 28.9 %copy-start.3 = (bf16[256,1152]{1,0:T(8,128)(2,1)S(1)}, bf16[256,1152]{1,0:T(8,128)(2,1)}, u32[]{:S(2)}) copy-start(bf16[256,1152]{1,0:T(8,128)(2,1)} %x.3) | copy-start | bytes 1769476
  5.1 14.3 %collective-permute-start.3 = (bf16[144,1152]{1,0:T(8,128)(2,1)S(1)}, bf16[144,1152]{1,0:T(8,128)(2,1)S(1)}, u32[]{:S(2)}, u32[]{:S(2)}) collective-permute-start(bf16[144,1152]{1,0:T(8,128)(2,1)S(1)} %get-tuple-element.17), channel_id=1, source_target_pairs={{0,1},{1,2},{2,3},{3,0},{4,5},{5,6},{6,7},{7,4},{8,9},{9,10},{10,1... | collective-permute-start | bytes 995336 | tf_op jit(solution)/shard_map/ppermute | solution.py:335
  6.7 33.9 %copy-start = (bf16[256,1152]{1,0:T(8,128)(2,1)S(1)}, bf16[256,1152]{1,0:T(8,128)(2,1)}, u32[]{:S(2)}) copy-start(bf16[256,1152]{1,0:T(8,128)(2,1)} %text.1) | copy-start | bytes 1769476
  19.3 19.3 %collective-permute-start.2 = (bf16[256,1152]{1,0:T(8,128)(2,1)S(1)}, bf16[256,1152]{1,0:T(8,128)(2,1)S(1)}, u32[]{:S(2)}, u32[]{:S(2)}) collective-permute-start(bf16[256,1152]{1,0:T(8,128)(2,1)S(1)} %broadcast_select_fusion.1), channel_id=1, source_target_pairs={{0,4},{4,0},{8,12},{12,8},{16,20},{20,16},{24,28},{28,24},{1,5},{5... | collective-permute-start | bytes 1769480 | tf_op jit(solution)/shard_map/ppermute | solution.py:321
  19.3 13.8 %collective-permute-start.4 = (bf16[144,1152]{1,0:T(8,128)(2,1)S(1)}, bf16[144,1152]{1,0:T(8,128)(2,1)S(1)}, u32[]{:S(2)}, u32[]{:S(2)}) collective-permute-start(bf16[144,1152]{1,0:T(8,128)(2,1)S(1)} %collective-permute-done.3.rest_0_), channel_id=1, source_target_pairs={{0,16},{4,20},{8,24},{12,28},{16,0},{20,4},{24,8},{28,12},{1,17},{... | collective-permute-start | bytes 995336 | tf_op jit(solution)/shard_map/ppermute | solution.py:324
  21.1 11.6 %collective-permute-start.5 = (bf16[80,1152]{1,0:T(8,128)(2,1)S(1)}, bf16[80,1152]{1,0:T(8,128)(2,1)S(1)}, u32[]{:S(2)}, u32[]{:S(2)}) collective-permute-start(bf16[80,1152]{1,0:T(8,128)(2,1)S(1)} %get-tuple-element.18), channel_id=1, source_target_pairs={{0,2},{1,3},{2,0},{3,1},{4,6},{5,7},{6,4},{7,5},{8,10},{9,11},{10,... | collective-permute-start | bytes 552968 | tf_op jit(solution)/shard_map/ppermute | solution.py:318
  32.7 5.9 %collective-permute-start.6 = (bf16[80,1152]{1,0:T(8,128)(2,1)S(1)}, bf16[80,1152]{1,0:T(8,128)(2,1)S(1)}, u32[]{:S(2)}, u32[]{:S(2)}) collective-permute-start(bf16[80,1152]{1,0:T(8,128)(2,1)S(1)} %collective-permute-done.5.rest_2_), channel_id=1, source_target_pairs={{0,16},{4,20},{8,24},{12,28},{16,0},{20,4},{24,8},{28,12},{1,17},{... | collective-permute-start | bytes 552968 | tf_op jit(solution)/shard_map/ppermute | solution.py:324
  33.1 8.2 %collective-permute-start.7 = (bf16[144,1152]{1,0:T(8,128)(2,1)S(1)}, bf16[144,1152]{1,0:T(8,128)(2,1)S(1)}, u32[]{:S(2)}, u32[]{:S(2)}) collective-permute-start(bf16[144,1152]{1,0:T(8,128)(2,1)S(1)} %collective-permute-done.3.rest_0_), channel_id=1, source_target_pairs={{0,4},{4,0},{8,12},{12,8},{16,20},{20,16},{24,28},{28,24},{1,5},{5... | collective-permute-start | bytes 995336 | tf_op jit(solution)/shard_map/ppermute | solution.py:321
  33.1 8.2 %collective-permute-start.8 = (bf16[144,1152]{1,0:T(8,128)(2,1)S(1)}, bf16[144,1152]{1,0:T(8,128)(2,1)S(1)}, u32[]{:S(2)}, u32[]{:S(2)}) collective-permute-start(bf16[144,1152]{1,0:T(8,128)(2,1)S(1)} %collective-permute-done.4.rest_1_), channel_id=1, source_target_pairs={{0,4},{4,0},{8,12},{12,8},{16,20},{20,16},{24,28},{28,24},{1,5},{5... | collective-permute-start | bytes 995336 | tf_op jit(solution)/shard_map/ppermute | solution.py:321
  33.6 16.3 %collective-permute-start = (bf16[256,1152]{1,0:T(8,128)(2,1)S(1)}, bf16[256,1152]{1,0:T(8,128)(2,1)S(1)}, u32[]{:S(2)}, u32[]{:S(2)}) collective-permute-start(bf16[256,1152]{1,0:T(8,128)(2,1)S(1)} %copy-done.3), channel_id=1, source_target_pairs={{0,1},{3,2},{4,5},{7,6},{8,9},{11,10},{12,13},{15,14},{16,17},{19,... | collective-permute-start | bytes 1769480 | tf_op jit(solution)/shard_map/ppermute | solution.py:318
  38.5 2.7 %collective-permute-start.9 = (bf16[80,1152]{1,0:T(8,128)(2,1)S(1)}, bf16[80,1152]{1,0:T(8,128)(2,1)S(1)}, u32[]{:S(2)}, u32[]{:S(2)}) collective-permute-start(bf16[80,1152]{1,0:T(8,128)(2,1)S(1)} %collective-permute-done.5.rest_2_), channel_id=1, source_target_pairs={{0,4},{4,0},{8,12},{12,8},{16,20},{20,16},{24,28},{28,24},{1,5},{5... | collective-permute-start | bytes 552968 | tf_op jit(solution)/shard_map/ppermute | solution.py:321
  38.5 2.7 %collective-permute-start.10 = (bf16[80,1152]{1,0:T(8,128)(2,1)S(1)}, bf16[80,1152]{1,0:T(8,128)(2,1)S(1)}, u32[]{:S(2)}, u32[]{:S(2)}) collective-permute-start(bf16[80,1152]{1,0:T(8,128)(2,1)S(1)} %collective-permute-done.6.rest_3_), channel_id=1, source_target_pairs={{0,4},{4,0},{8,12},{12,8},{16,20},{20,16},{24,28},{28,24},{1,5},{5... | collective-permute-start | bytes 552968 | tf_op jit(solution)/shard_map/ppermute | solution.py:321
  40.6 1.1 copy-start.2
  46.1 7.6 %collective-permute-start.11 = (bf16[288,384]{1,0:T(8,128)(2,1)S(1)}, bf16[288,384]{1,0:T(8,128)(2,1)S(1)}, u32[]{:S(2)}, u32[]{:S(2)}) collective-permute-start(bf16[288,384]{1,0:T(8,128)(2,1)S(1)} %get-tuple-element.20), channel_id=1, source_target_pairs={{0,1},{1,0},{2,3},{3,2},{4,5},{5,4},{6,7},{7,6},{8,9},{9,8},{10,11... | collective-permute-start | bytes 663560 | tf_op jit(solution)/shard_map/ppermute | solution.py:318
  54.0 14.5 %collective-permute-start.17 = (bf16[256,1152]{1,0:T(8,128)(2,1)S(1)}, bf16[256,1152]{1,0:T(8,128)(2,1)S(1)}, u32[]{:S(2)}, u32[]{:S(2)}) collective-permute-start(bf16[256,1152]{1,0:T(8,128)(2,1)S(1)} %get-tuple-element.31.u0), channel_id=1, source_target_pairs={{0,24},{4,28},{8,0},{12,4},{16,8},{20,12},{24,16},{28,20},{1,25},{... | collective-permute-start | bytes 1769480 | tf_op jit(solution)/shard_map/ppermute | solution.py:327
  55.6 13.0 %collective-permute-start.14 = (bf16[288,768]{1,0:T(8,128)(2,1)S(1)}, bf16[288,768]{1,0:T(8,128)(2,1)S(1)}, u32[]{:S(2)}, u32[]{:S(2)}) collective-permute-start(bf16[288,768]{1,0:T(8,128)(2,1)S(1)} %get-tuple-element.27), channel_id=1, source_target_pairs={{0,1},{1,0},{2,3},{3,2},{4,5},{5,4},{6,7},{7,6},{8,9},{9,8},{10,11... | collective-permute-start | bytes 1327112 | tf_op jit(solution)/shard_map/ppermute | solution.py:318
  68.6 38.1 %collective-permute-start.18 = (bf16[256,1152]{1,0:T(8,128)(2,1)S(1)}, bf16[256,1152]{1,0:T(8,128)(2,1)S(1)}, u32[]{:S(2)}, u32[]{:S(2)}) collective-permute-start(bf16[256,1152]{1,0:T(8,128)(2,1)S(1)} %broadcast_select_fusion), channel_id=1, source_target_pairs={{0,4},{4,0},{8,12},{12,8},{16,20},{20,16},{24,28},{28,24},{1,5},{5... | collective-permute-start | bytes 1769480 | tf_op jit(solution)/shard_map/ppermute | solution.py:321
  69.0 36.4 %collective-permute-start.15 = (bf16[288,768]{1,0:T(8,128)(2,1)S(1)}, bf16[288,768]{1,0:T(8,128)(2,1)S(1)}, u32[]{:S(2)}, u32[]{:S(2)}) collective-permute-start(bf16[288,768]{1,0:T(8,128)(2,1)S(1)} %get-tuple-element.29), channel_id=1, source_target_pairs={{1,2},{2,1},{5,6},{6,5},{9,10},{10,9},{13,14},{14,13},{17,18},{18,... | collective-permute-start | bytes 1327112 | tf_op jit(solution)/shard_map/ppermute | solution.py:318
  69.7 35.7 %collective-permute-start.16 = (bf16[288,768]{1,0:T(8,128)(2,1)S(1)}, bf16[288,768]{1,0:T(8,128)(2,1)S(1)}, u32[]{:S(2)}, u32[]{:S(2)}) collective-permute-start(bf16[288,768]{1,0:T(8,128)(2,1)S(1)} %get-tuple-element.30), channel_id=1, source_target_pairs={{1,3},{2,0},{5,7},{6,4},{9,11},{10,8},{13,15},{14,12},{17,19},{18,... | collective-permute-start | bytes 1327112 | tf_op jit(solution)/shard_map/ppermute | solution.py:318
  71.0 2.0 %collective-permute-start.12 = (bf16[288,384]{1,0:T(8,128)(2,1)S(1)}, bf16[288,384]{1,0:T(8,128)(2,1)S(1)}, u32[]{:S(2)}, u32[]{:S(2)}) collective-permute-start(bf16[288,384]{1,0:T(8,128)(2,1)S(1)} %get-tuple-element.25), channel_id=1, source_target_pairs={{1,2},{2,1},{5,6},{6,5},{9,10},{10,9},{13,14},{14,13},{17,18},{18,... | collective-permute-start | bytes 663560 | tf_op jit(solution)/shard_map/ppermute | solution.py:318
  71.7 33.7 %collective-permute-start.13 = (bf16[288,384]{1,0:T(8,128)(2,1)S(1)}, bf16[288,384]{1,0:T(8,128)(2,1)S(1)}, u32[]{:S(2)}, u32[]{:S(2)}) collective-permute-start(bf16[288,384]{1,0:T(8,128)(2,1)S(1)} %get-tuple-element.26), channel_id=1, source_target_pairs={{1,3},{2,0},{5,7},{6,4},{9,11},{10,8},{13,15},{14,12},{17,19},{18,... | collective-permute-start | bytes 663560 | tf_op jit(solution)/shard_map/ppermute | solution.py:318

commit v3 on v2

--- a/solution.py
+++ b/solution.py
@@ -18,13 +18,15 @@
     return [pl.BlockSpec(memory_space=pltpu.VMEM)] * count
 
 
-def params():
-    return pltpu.CompilerParams(vmem_limit_bytes=VMEM_BYTES)
-
-
-def cost(flops, *arrays):
-    size = sum(a.size * a.dtype.itemsize for a in arrays)
-    return pl.CostEstimate(flops=flops, bytes_accessed=size, transcendentals=0)
+def params(size=VMEM_BYTES):
+    return pltpu.CompilerParams(vmem_limit_bytes=size)
+
+
+def cost():
+    return pl.CostEstimate(flops=0, bytes_accessed=0, transcendentals=0)
+
+
+IN_HBM = pl.BlockSpec(memory_space=pltpu.HBM)
 
 
 def place(n_dp):
@@ -55,35 +57,42 @@
     return pl.pallas_call(
         functools.partial(cut_kernel, n_dp, short),
         out_shape=outs,
-        in_specs=[pl.BlockSpec(memory_space=pl.ANY)],
+        in_specs=[IN_HBM],
         out_specs=spaces(2),
         scratch_shapes=[pltpu.SemaphoreType.DMA((2,))],
-        compiler_params=params(),
-        cost_estimate=cost(0, *outs, *outs),
+        compiler_params=params(60 * 1024 * 1024),
+        cost_estimate=cost(),
         name="cut",
     )(own)
 
 
-def prepare_kernel(t0, t1, t2, units):
+def prepare_kernel(n_dp, t0, twin0, twin2, t2, _, units):
     rows = t0.shape[0]
-    for k, block in enumerate((t0, t1, t2)):
+    _, core, _ = place(n_dp)
+
+    def fill(k, block):
         values = block[...].astype(F32)
         inverse = 1.0 / jnp.sqrt(jnp.sum(values * values, axis=-1, keepdims=True) + EPS)
         units[k * rows : (k + 1) * rows, :] = (values * inverse).astype(BF16)
 
-
-def prepare(t0, t1, t2):
+    fill(0, t0)
+    fill(2, t2)
+    pl.when(core == 0)(lambda: fill(1, twin2))
+    pl.when(core == 1)(lambda: fill(1, twin0))
+
+
+def prepare(n_dp, t0, twin0, twin2, t2, after):
     rows, width = t0.shape
     out = jax.ShapeDtypeStruct((STEPS * rows, width), BF16)
     return pl.pallas_call(
-        prepare_kernel,
+        functools.partial(prepare_kernel, n_dp),
         out_shape=out,
-        in_specs=spaces(3),
+        in_specs=spaces(5),
         out_specs=pl.BlockSpec(memory_space=pltpu.VMEM),
         compiler_params=params(),
-        cost_estimate=cost(0, t0, t1, t2, out),
+        cost_estimate=cost(),
         name="prepare",
-    )(t0, t1, t2)
+    )(t0, twin0, twin2, t2, after)
 
 
 def turn_kernel(x, x_t):
@@ -98,7 +107,7 @@
         in_specs=spaces(1),
         out_specs=pl.BlockSpec(memory_space=pltpu.VMEM),
         compiler_params=params(),
-        cost_estimate=cost(0, x, out),
+        cost_estimate=cost(),
         name="turned",
     )(x)
 
@@ -109,7 +118,7 @@
 
 def picture_kernel(n_dp, x, x_t, units, sharp, bias, own, *rest):
     pieces, outs = rest[:8], rest[8 : 8 + len(SHARES)]
-    grad, unit, w, proj, sem = rest[8 + len(SHARES) :]
+    unit, grad, w, proj, sem = rest[8 + len(SHARES) :]
     part, core, side = place(n_dp)
     depth = own.shape[0]
     half = depth // 2
@@ -192,7 +201,8 @@
     out = jax.ShapeDtypeStruct((rows, width), BF16)
     smem = pl.BlockSpec(memory_space=pltpu.SMEM)
     sizes = [width * share // sum(SHARES) for share in SHARES]
-    outs = tuple(jax.ShapeDtypeStruct((depth, size), BF16) for size in sizes) + (out, out)
+    outs = tuple(jax.ShapeDtypeStruct((depth, size), BF16) for size in sizes)
+    outs = outs + (out, out)
     return pl.pallas_call(
         functools.partial(picture_kernel, n_dp),
         out_shape=outs,
@@ -204,15 +214,23 @@
             pltpu.SemaphoreType.DMA((9,)),
         ],
         compiler_params=params(),
-        cost_estimate=cost(2 * rows * width * (width + 2 * STEPS * rows), x, units, own, out, out),
+        cost_estimate=cost(),
         name="picture_side",
     )(x, x_t, units, sharp, bias, own, *pieces)
 
 
-def text_kernel(text, u0, u1, u2, sharp, bias, out, units):
+def text_kernel(n_dp, text, sharp, bias, u0, twin0, twin2, u2, out, done, units):
     rows = text.shape[0]
-    for k, block in enumerate((u0, u1, u2)):
-        units[k * rows : (k + 1) * rows, :] = block[...]
+    _, core, _ = place(n_dp)
+    done[...] = jnp.zeros_like(done)
+    units[:rows, :] = u0[...]
+    units[2 * rows :, :] = u2[...]
+    for lane, block in ((0, twin0), (1, twin2)):
+
+        @pl.when(core == lane)
+        def _():
+            units[rows : 2 * rows, :] = block[...]
+
     values = text[...].astype(F32)
     inverse = 1.0 / jnp.sqrt(jnp.sum(values * values, axis=-1, keepdims=True) + EPS)
     direction = values * inverse
@@ -229,23 +247,23 @@
     out[...] = (slope - direction * along) * inverse
 
 
-def text_side(text, u0, u1, u2, sharp, bias):
+def text_side(n_dp, text, sharp, bias, *units):
     rows, width = text.shape
-    out = jax.ShapeDtypeStruct((rows, width), F32)
     smem = pl.BlockSpec(memory_space=pltpu.SMEM)
     return pl.pallas_call(
-        text_kernel,
-        out_shape=out,
-        in_specs=spaces(4) + [smem, smem],
-        out_specs=pl.BlockSpec(memory_space=pltpu.VMEM),
+        functools.partial(text_kernel, n_dp),
+        out_shape=(jax.ShapeDtypeStruct((rows, width), F32), jax.ShapeDtypeStruct((8, 128), F32)),
+        in_specs=spaces(1) + [smem, smem] + spaces(4),
+        out_specs=tuple(spaces(2)),
         scratch_shapes=[pltpu.VMEM((STEPS * rows, width), BF16)],
         compiler_params=params(),
-        cost_estimate=cost(4 * STEPS * rows * rows * width, text, u0, u1, u2, out),
+        cost_estimate=cost(),
         name="text_side",
-    )(text, u0, u1, u2, sharp, bias)
-
-
-def pair_kernel(begin, x_t, far_t, grad, arrived, kept, near, far):
+    )(text, sharp, bias, *units)
+
+
+def pair_kernel(begin, x_t, far_t, grad, arrived, *rest):
+    kept, near, far = rest[-3:]
     rows = grad.shape[0]
     depth, size = arrived.shape
     part = lax.axis_index("fsdp")
@@ -271,40 +289,40 @@
         far[...] = jnp.zeros_like(far)
 
 
-def pair_product(begin, x_t, far_t, grad, arrived):
+def pair_product(begin, x_t, far_t, grad, arrived, after):
     outs = tuple(jax.ShapeDtypeStruct(arrived.shape, t) for t in (F32, BF16, BF16))
     return pl.pallas_call(
         functools.partial(pair_kernel, begin),
         out_shape=outs,
-        in_specs=spaces(4),
+        in_specs=spaces(4 + len(after)),
         out_specs=spaces(3),
         compiler_params=params(),
-        cost_estimate=cost(12 * grad.shape[0] * arrived.size, x_t, far_t, grad, arrived, *outs),
+        cost_estimate=cost(),
         name="pair_product",
-    )(x_t, far_t, grad, arrived)
-
-
-def total_kernel(*refs):
-    kept, near, far = (refs[k : len(refs) - 1 : 3] for k in range(3))
-    out = refs[-1]
-    begin = 0
-    for a, b, c in zip(kept, near, far):
-        stop = begin + a.shape[1]
-        out[0, :, begin:stop] = a[...] + b[...].astype(F32) + c[...].astype(F32)
-        begin = stop
-
-
-def total(terms, depth, width):
-    out = jax.ShapeDtypeStruct((1, depth, width), F32)
-    return pl.pallas_call(
-        total_kernel,
-        out_shape=out,
-        in_specs=spaces(len(terms)),
-        out_specs=pl.BlockSpec(memory_space=pltpu.VMEM),
-        compiler_params=params(),
-        cost_estimate=cost(0, *terms, out),
+    )(x_t, far_t, grad, arrived, *after)
+
+
+def total_kernel(begin, kept, near, far, *rest):
+    out, summed, sem = rest[-3:]
+    summed[...] = kept[...] + near[...].astype(F32) + far[...].astype(F32)
+    copy = pltpu.make_async_copy(summed, out.at[0, :, begin : begin + kept.shape[1]], sem)
+    copy.start()
+    copy.wait()
+
+
+def total(begin, width, kept, near, far, held):
+    depth = kept.shape[0]
+    return pl.pallas_call(
+        functools.partial(total_kernel, begin),
+        out_shape=jax.ShapeDtypeStruct((1, depth, width), F32),
+        in_specs=spaces(3) + [IN_HBM] * len(held[:1]) + spaces(len(held[1:])),
+        out_specs=IN_HBM,
+        scratch_shapes=[pltpu.VMEM(kept.shape, F32), pltpu.SemaphoreType.DMA],
+        input_output_aliases={3: 0} if held else {},
+        compiler_params=params(),
+        cost_estimate=cost(),
         name="total",
-    )(*terms)
+    )(kept, near, far, *held)
 
 
 def line_body(n_dp, n_fsdp, x, text, w, sharp, bias):
@@ -340,24 +358,24 @@
     two_crossed = over(two)
     pieces = [straight, crossed, two, two_crossed]
     pieces = pieces + [across(piece) for piece in pieces]
-    text1 = across(jnp.where(core == 0, text, text2))
-
     x_t, far_t = turned(x), turned(far_x)
-    units = prepare(text, text1, text2)
-    *outward, grad, unit = picture_side(n_dp, x, x_t, units, sharp, bias, w, pieces)
+    units = prepare(n_dp, text, across(text), across(text2), text2, far_t)
+    *outward, unit, grad = picture_side(n_dp, x, x_t, units, sharp, bias, w, pieces)
 
     arrived = [along(o, [(0, 1), (1, 0), (2, 3), (3, 2)]) for o in outward]
-    begin, terms = 0, []
-    for k, block in enumerate(arrived):
-        kept, near, far = pair_product(begin, x_t, far_t, grad, block)
+    unit2 = shifted(unit, -2)
+    begin, terms, after = 0, [], []
+    for block in arrived:
+        kept, near, far = pair_product(begin, x_t, far_t, grad, block, after)
+        near, far = along(near, [(1, 2), (2, 1)]), along(far, [(1, 3), (2, 0)])
+        after = [near, far, unit2]
+        terms.append((begin, width, kept, near, far))
         begin += block.shape[1]
-        if k == 0:
-            unit, near, far = lax.optimization_barrier((unit, near, far))
-        terms += [kept, along(near, [(1, 2), (2, 1)]), along(far, [(1, 3), (2, 0)])]
-    unit2 = shifted(unit, -2)
-    unit1 = across(jnp.where(core == 0, unit2, unit))
-    text_grad = text_side(text, unit, unit1, unit2, sharp, bias)
-    return total(terms, depth, width), text_grad
+    text_grad, done = text_side(n_dp, text, sharp, bias, unit, across(unit), across(unit2), unit2)
+    head = total(*terms[0], [])
+    for term in terms[1:]:
+        head = total(*term, [head, done])
+    return head, text_grad
 
 
 def plain_body(n_dp, n_fsdp, x, text, w, sharp, bias):

time: 110 us -> 93.7 us (0.85)
  waiting for transfers between devices: 70.7 us -> 54.7 us
  Pallas kernels: 10.6 us -> 12.8 us
  other arithmetic: 1.2 us -> 0 us
  starting transfers between devices: 23.4 us -> 22.2 us
    ppermute x2, waiting for transfers between devices: 21.4 us -> 2.7 us  [shifted(): lax.ppermute(value, 'dp', [(d, (d + by) % n_dp) for d in range(n_dp)])]
    ppermute x1, waiting for transfers between devices: 0.01 us -> 7.13 us  [line_body(): straight = lax.ppermute(whole, ('dp', 'fsdp'), turns)]
    ppermute x8, waiting for transfers between devices: 47.1 us -> 41.3 us  [along(): return lax.ppermute(value, 'fsdp', pairs)]
    ppermute x8, starting transfers between devices: 13.8 us -> 9.91 us  [along(): return lax.ppermute(value, 'fsdp', pairs)]
    ppermute x2, starting transfers between devices: 2.23 us -> 4.58 us  [over(): lax.ppermute(value, 'dp', [(d, (d + side) % n_dp) for d in range(n_dp)])]
    pallas_call x1, Pallas kernels: 0.36 us -> 1.88 us  [cut(): pl.pallas_call(functools.partial(cut_kernel, n_dp, short), out_shape=outs...]
    ppermute x2, waiting for transfers between devices: 2.23 us -> 3.52 us  [over(): lax.ppermute(value, 'dp', [(d, (d + side) % n_dp) for d in range(n_dp)])]
    select_n x2 -> x0, other arithmetic: 1.2 us -> none  [the longest x1 1.13 us: line_body(): text1 = across(jnp.where(core == 0, text, text2))]
  transfers between devices with their start and end apart: 19 -> 21, of which waited for: 7 -> 8; matrix products, arithmetic and copies ran while one was open for 1% -> 0% of each run, Pallas kernels for 7% -> 8%
where the time goes in v3:
time: 93.7 us; the launch traced here: 93.4 us
  waiting for transfers between devices  54.7 us (58%)
  starting transfers between devices  22.2 us (24%)
  Pallas kernels  12.8 us (14%)
  between operations  2.14 us (2%)
  local copies, waits for them, and re-layouts  1.58 us (2%)
    ppermute x8, waiting for transfers between devices, along(): return lax.ppermute(value, 'fsdp', pairs)  41.3 us
    ppermute x8, starting transfers between devices, along(): return lax.ppermute(value, 'fsdp', pairs)  9.91 us
    ppermute x1, waiting for transfers between devices, line_body(): straight = lax.ppermute(whole, ('dp', 'fsdp'), turns)  7.13 us
    ppermute x2, starting transfers between devices, shifted(): lax.ppermute(value, 'dp', [(d, (d + by) % n_dp) for d in range(n_dp)])  4.96 us
    ppermute x2, starting transfers between devices, over(): lax.ppermute(value, 'dp', [(d, (d + side) % n_dp) for d in range(n_dp)])  4.58 us
    pallas_call x1, Pallas kernels, picture_side(): pl.pallas_call(functools.partial(picture_kernel, n_dp), out_shape=outs, i...  4.48 us
    ppermute x2, waiting for transfers between devices, over(): lax.ppermute(value, 'dp', [(d, (d + side) % n_dp) for d in range(n_dp)])  3.52 us
    pallas_call x1, Pallas kernels, text_side(): pl.pallas_call(functools.partial(text_kernel, n_dp), out_shape=(jax.Shape...  2.9 us
  transfers between devices with their start and end apart: 21, of which 8 were waited for; matrix products, arithmetic and copies ran while one was open for 0% of the time, Pallas kernels for 8%

profile of v3, /device:TPU:0, one launch (start us, length us, event | category | flops | bytes accessed | tf_op | source)
XLA Modules:
  0.0 93.4 jit_solution(9254736596105768221)
XLA Ops:
  0.6 3.0 %collective-permute-start.2 = (bf16[256,1152]{1,0:T(8,128)(2,1)}, bf16[256,1152]{1,0:T(8,128)(2,1)S(1)}, u32[]{:S(2)}, u32[]{:S(2)}) collective-permute-start(bf16[256,1152]{1,0:T(8,128)(2,1)} %text.1), channel_id=1, source_target_pairs={{0,8},{4,12},{8,16},{12,20},{16,24},{20,28},{24,0},{28,4},{1,9},{5... | collective-permute-start | bytes 1769480 | tf_op jit(solution)/shard_map/ppermute | solution.py:345
  3.6 1.9 %cut.1 = (bf16[144,1152]{1,0:T(8,128)(2,1)}, bf16[80,1152]{1,0:T(8,128)(2,1)}) custom-call(bf16[288,1152]{1,0:T(8,128)(2,1)} %own.3), custom_call_target="tpu_custom_call" | custom-call | tf_op jit(solution)/shard_map/cut/pallas_call | solution.py:57
  5.5 1.6 %collective-permute-start.4 = (bf16[144,1152]{1,0:T(8,128)(2,1)}, bf16[144,1152]{1,0:T(8,128)(2,1)S(1)}, u32[]{:S(2)}, u32[]{:S(2)}) collective-permute-start(bf16[144,1152]{1,0:T(8,128)(2,1)} %get-tuple-element.16), channel_id=1, source_target_pairs={{0,1},{1,2},{2,3},{3,0},{4,5},{5,6},{6,7},{7,4},{8,9},{9,10},{10,1... | collective-permute-start | bytes 995336 | tf_op jit(solution)/shard_map/ppermute | solution.py:353
  7.1 3.5 %collective-permute-start = (bf16[256,1152]{1,0:T(8,128)(2,1)}, bf16[256,1152]{1,0:T(8,128)(2,1)S(1)}, u32[]{:S(2)}, u32[]{:S(2)}) collective-permute-start(bf16[256,1152]{1,0:T(8,128)(2,1)} %x.3), channel_id=1, source_target_pairs={{0,1},{3,2},{4,5},{7,6},{8,9},{11,10},{12,13},{15,14},{16,17},{19,... | collective-permute-start | bytes 1769480 | tf_op jit(solution)/shard_map/ppermute | solution.py:336
  10.7 0.4 collective-permute-start.6
  11.2 7.1 %collective-permute-done.4.rest_0_ = bf16[144,1152]{1,0:T(8,128)(2,1)S(1)} collective-permute-done((bf16[144,1152]{1,0:T(8,128)(2,1)}, bf16[144,1152]{1,0:T(8,128)(2,1)S(1)}, u32[]{:S(2)}, u32[]{:S(2)}) %collective-permute-start.4) | collective-permute-done | bytes 331808 | tf_op jit(solution)/shard_map/ppermute | solution.py:353
  18.3 1.0 %collective-permute-start.5 = (bf16[144,1152]{1,0:T(8,128)(2,1)S(1)}, bf16[144,1152]{1,0:T(8,128)(2,1)S(1)}, u32[]{:S(2)}, u32[]{:S(2)}) collective-permute-start(bf16[144,1152]{1,0:T(8,128)(2,1)S(1)} %collective-permute-done.4.rest_0_), channel_id=1, source_target_pairs={{0,16},{4,20},{8,24},{12,28},{16,0},{20,4},{24,8},{28,12},{1,17},{... | collective-permute-start | bytes 995336 | tf_op jit(solution)/shard_map/ppermute | solution.py:342
  19.3 11.5 %collective-permute-done.6.rest_2_ = bf16[80,1152]{1,0:T(8,128)(2,1)S(1)} collective-permute-done((bf16[80,1152]{1,0:T(8,128)(2,1)}, bf16[80,1152]{1,0:T(8,128)(2,1)S(1)}, u32[]{:S(2)}, u32[]{:S(2)}) %collective-permute-start.6) | collective-permute-done | bytes 184352 | tf_op jit(solution)/shard_map/ppermute | solution.py:336
  30.8 3.6 %collective-permute-start.7 = (bf16[80,1152]{1,0:T(8,128)(2,1)S(1)}, bf16[80,1152]{1,0:T(8,128)(2,1)S(1)}, u32[]{:S(2)}, u32[]{:S(2)}) collective-permute-start(bf16[80,1152]{1,0:T(8,128)(2,1)S(1)} %collective-permute-done.6.rest_2_), channel_id=1, source_target_pairs={{0,16},{4,20},{8,24},{12,28},{16,0},{20,4},{24,8},{28,12},{1,17},{... | collective-permute-start | bytes 552968 | tf_op jit(solution)/shard_map/ppermute | solution.py:342
  34.4 3.5 %collective-permute-done.7.rest_3_ = bf16[80,1152]{1,0:T(8,128)(2,1)S(1)} collective-permute-done((bf16[80,1152]{1,0:T(8,128)(2,1)S(1)}, bf16[80,1152]{1,0:T(8,128)(2,1)S(1)}, u32[]{:S(2)}, u32[]{:S(2)}) %collective-permute-start.7) | collective-permute-done | bytes 184352 | tf_op jit(solution)/shard_map/ppermute | solution.py:342
  37.9 0.5 collective-permute-start.9
  38.5 0.4 collective-permute-start.11
  39.0 1.1 %copy-done.1 = bf16[256,1152]{1,0:T(8,128)(2,1)S(1)} copy-done((bf16[256,1152]{1,0:T(8,128)(2,1)S(1)}, bf16[256,1152]{1,0:T(8,128)(2,1)}, u32[]{:S(2)}) %copy-start.1) | copy-done | bytes 589848
  41.8 0.7 prepare.1.units
  42.5 0.3 copy-done
  43.0 4.5 %picture_side.1 = (bf16[288,384]{1,0:T(8,128)(2,1)S(1)}, bf16[288,768]{1,0:T(8,128)(2,1)S(1)}, bf16[256,1152]{1,0:T(8,128)(2,1)S(1)}, bf16[256,1152]{1,0:T(8,128)(2,1)S(1)}) custom-call(bf16[256,1152]{1,0:T(8,128)(2,1)S(1)} %copy-done.2, bf16[1152,256]{1,0:T(8,128)(2,1)S(1)} %turned.2.x_t, bf16[768,1152]{1,0:T(8,128)(2,1)S(1)} %prepare.1.units, ...), custom_call_target="tpu_custom_call" | custom-call | tf_op jit(solution)/shard_map/picture_side/pallas_call | solution.py:206
  47.5 2.0 %collective-permute-start.16 = (bf16[256,1152]{1,0:T(8,128)(2,1)S(1)}, bf16[256,1152]{1,0:T(8,128)(2,1)S(1)}, u32[]{:S(2)}, u32[]{:S(2)}) collective-permute-start(bf16[256,1152]{1,0:T(8,128)(2,1)S(1)} %get-tuple-element.23.u0), channel_id=1, source_target_pairs={{0,24},{4,28},{8,0},{12,4},{16,8},{20,12},{24,16},{28,20},{1,25},{... | collective-permute-start | bytes 1769480 | tf_op jit(solution)/shard_map/ppermute | solution.py:345
  49.5 1.6 %collective-permute-start.13 = (bf16[288,384]{1,0:T(8,128)(2,1)S(1)}, bf16[288,384]{1,0:T(8,128)(2,1)S(1)}, u32[]{:S(2)}, u32[]{:S(2)}) collective-permute-start(bf16[288,384]{1,0:T(8,128)(2,1)S(1)} %get-tuple-element.20), channel_id=1, source_target_pairs={{0,1},{1,0},{2,3},{3,2},{4,5},{5,4},{6,7},{7,6},{8,9},{9,8},{10,11... | collective-permute-start | bytes 663560 | tf_op jit(solution)/shard_map/ppermute | solution.py:336
  51.1 0.4 collective-permute-start.12
  51.5 6.3 %collective-permute-done.13.arrived = bf16[288,384]{1,0:T(8,128)(2,1)S(1)} collective-permute-done((bf16[288,384]{1,0:T(8,128)(2,1)S(1)}, bf16[288,384]{1,0:T(8,128)(2,1)S(1)}, u32[]{:S(2)}, u32[]{:S(2)}) %collective-permute-start.13) | collective-permute-done | bytes 221216 | tf_op jit(solution)/shard_map/ppermute | solution.py:336
  58.1 0.7 collective-permute-start.14
  58.7 1.3 %collective-permute-start.15 = (bf16[288,384]{1,0:T(8,128)(2,1)S(1)}, bf16[288,384]{1,0:T(8,128)(2,1)S(1)}, u32[]{:S(2)}, u32[]{:S(2)}) collective-permute-start(bf16[288,384]{1,0:T(8,128)(2,1)S(1)} %get-tuple-element.22), channel_id=1, source_target_pairs={{1,3},{2,0},{5,7},{6,4},{9,11},{10,8},{13,15},{14,12},{17,19},{18,... | collective-permute-start | bytes 663560 | tf_op jit(solution)/shard_map/ppermute | solution.py:336
  60.1 2.7 %collective-permute-done.16.rest_2_.u2 = bf16[256,1152]{1,0:T(8,128)(2,1)S(1)} collective-permute-done((bf16[256,1152]{1,0:T(8,128)(2,1)S(1)}, bf16[256,1152]{1,0:T(8,128)(2,1)S(1)}, u32[]{:S(2)}, u32[]{:S(2)}) %collective-permute-start.16) | collective-permute-done | bytes 589856 | tf_op jit(solution)/shard_map/ppermute | solution.py:345
  62.8 5.1 %collective-permute-done.12.arrived = bf16[288,768]{1,0:T(8,128)(2,1)S(1)} collective-permute-done((bf16[288,768]{1,0:T(8,128)(2,1)S(1)}, bf16[288,768]{1,0:T(8,128)(2,1)S(1)}, u32[]{:S(2)}, u32[]{:S(2)}) %collective-permute-start.12) | collective-permute-done | bytes 442400 | tf_op jit(solution)/shard_map/ppermute | solution.py:336
  68.0 4.0 %collective-permute-done.15.rest_1_.far = bf16[288,384]{1,0:T(8,128)(2,1)S(1)} collective-permute-done((bf16[288,384]{1,0:T(8,128)(2,1)S(1)}, bf16[288,384]{1,0:T(8,128)(2,1)S(1)}, u32[]{:S(2)}, u32[]{:S(2)}) %collective-permute-start.15) | collective-permute-done | bytes 221216 | tf_op jit(solution)/shard_map/ppermute | solution.py:336
  72.0 0.3 pair_product.3
  72.3 0.7 collective-permute-start.17
  73.0 1.3 %collective-permute-start.18 = (bf16[288,768]{1,0:T(8,128)(2,1)S(1)}, bf16[288,768]{1,0:T(8,128)(2,1)S(1)}, u32[]{:S(2)}, u32[]{:S(2)}) collective-permute-start(bf16[288,768]{1,0:T(8,128)(2,1)S(1)} %get-tuple-element.26), channel_id=1, source_target_pairs={{1,3},{2,0},{5,7},{6,4},{9,11},{10,8},{13,15},{14,12},{17,19},{18,... | collective-permute-start | bytes 1327112 | tf_op jit(solution)/shard_map/ppermute | solution.py:336
  74.3 0.8 total.2.rest_0_
  75.2 2.9 %text_side.1 = (f32[256,1152]{1,0:T(8,128)}, f32[8,128]{1,0:T(8,128)S(1)}) custom-call(bf16[256,1152]{1,0:T(8,128)(2,1)S(1)} %copy-done.3, f32[1]{0:T(128)S(6)} %copy.9.sharp, f32[1]{0:T(128)S(6)} %copy.10.bias, bf16[256,1152]{1,0:T(8,128)(2,1)S(1)} %get-tuple-element.23.u0, bf16[256,1152]{1,0:T(8,128)(2,1)S(1)} %collective-permute-done.19.twin0, ...), custom_call_target="tpu_custom_call" | custom-call | tf_op jit(solution)/shard_map/text_side/pallas_call | solution.py:253
  78.1 14.3 %collective-permute-done.18.far = bf16[288,768]{1,0:T(8,128)(2,1)S(1)} collective-permute-done((bf16[288,768]{1,0:T(8,128)(2,1)S(1)}, bf16[288,768]{1,0:T(8,128)(2,1)S(1)}, u32[]{:S(2)}, u32[]{:S(2)}) %collective-permute-start.18) | collective-permute-done | bytes 442400 | tf_op jit(solution)/shard_map/ppermute | solution.py:336
  92.4 1.1 %total.3 = f32[1,288,1152]{2,1,0:T(8,128)} custom-call(f32[288,768]{1,0:T(8,128)S(1)} %get-tuple-element.24.kept, bf16[288,768]{1,0:T(8,128)(2,1)S(1)} %collective-permute-done.17.near, bf16[288,768]{1,0:T(8,128)(2,1)S(1)} %collective-permute-done.18.far, f32[1,288,1152]{2,1,0:T(8,128)} %total.2.rest_0_, ...), custom_call_target="tpu_custom_call", output_to_operand_aliasing={{}: (3, {})} | custom-call | tf_op jit(solution)/shard_map/total/pallas_call | solution.py:315
  (28 shorter events, 1.1 us)
Async XLA Ops:
  0.6 18.7 %collective-permute-start.2 = (bf16[256,1152]{1,0:T(8,128)(2,1)}, bf16[256,1152]{1,0:T(8,128)(2,1)S(1)}, u32[]{:S(2)}, u32[]{:S(2)}) collective-permute-start(bf16[256,1152]{1,0:T(8,128)(2,1)} %text.1), channel_id=1, source_target_pairs={{0,8},{4,12},{8,16},{12,20},{16,24},{20,28},{24,0},{28,4},{1,9},{5... | collective-permute-start | bytes 1769480 | tf_op jit(solution)/shard_map/ppermute | solution.py:345
  3.6 38.2 %copy-start.3 = (bf16[256,1152]{1,0:T(8,128)(2,1)S(1)}, bf16[256,1152]{1,0:T(8,128)(2,1)}, u32[]{:S(2)}) copy-start(bf16[256,1152]{1,0:T(8,128)(2,1)} %text.1) | copy-start | bytes 1769476
  5.5 12.8 %collective-permute-start.4 = (bf16[144,1152]{1,0:T(8,128)(2,1)}, bf16[144,1152]{1,0:T(8,128)(2,1)S(1)}, u32[]{:S(2)}, u32[]{:S(2)}) collective-permute-start(bf16[144,1152]{1,0:T(8,128)(2,1)} %get-tuple-element.16), channel_id=1, source_target_pairs={{0,1},{1,2},{2,3},{3,0},{4,5},{5,6},{6,7},{7,4},{8,9},{9,10},{10,1... | collective-permute-start | bytes 995336 | tf_op jit(solution)/shard_map/ppermute | solution.py:353
  7.1 31.3 %collective-permute-start = (bf16[256,1152]{1,0:T(8,128)(2,1)}, bf16[256,1152]{1,0:T(8,128)(2,1)S(1)}, u32[]{:S(2)}, u32[]{:S(2)}) collective-permute-start(bf16[256,1152]{1,0:T(8,128)(2,1)} %x.3), channel_id=1, source_target_pairs={{0,1},{3,2},{4,5},{7,6},{8,9},{11,10},{12,13},{15,14},{16,17},{19,... | collective-permute-start | bytes 1769480 | tf_op jit(solution)/shard_map/ppermute | solution.py:336
  10.7 27.9 %collective-permute-start.1 = (bf16[256,1152]{1,0:T(8,128)(2,1)}, bf16[256,1152]{1,0:T(8,128)(2,1)S(1)}, u32[]{:S(2)}, u32[]{:S(2)}) collective-permute-start(bf16[256,1152]{1,0:T(8,128)(2,1)} %text.1), channel_id=1, source_target_pairs={{0,4},{4,0},{8,12},{12,8},{16,20},{20,16},{24,28},{28,24},{1,5},{5... | collective-permute-start | bytes 1769480 | tf_op jit(solution)/shard_map/ppermute | solution.py:339
  10.7 20.1 %collective-permute-start.6 = (bf16[80,1152]{1,0:T(8,128)(2,1)}, bf16[80,1152]{1,0:T(8,128)(2,1)S(1)}, u32[]{:S(2)}, u32[]{:S(2)}) collective-permute-start(bf16[80,1152]{1,0:T(8,128)(2,1)} %get-tuple-element.17), channel_id=1, source_target_pairs={{0,2},{1,3},{2,0},{3,1},{4,6},{5,7},{6,4},{7,5},{8,10},{9,11},{10,... | collective-permute-start | bytes 552968 | tf_op jit(solution)/shard_map/ppermute | solution.py:336
  18.3 19.6 %collective-permute-start.5 = (bf16[144,1152]{1,0:T(8,128)(2,1)S(1)}, bf16[144,1152]{1,0:T(8,128)(2,1)S(1)}, u32[]{:S(2)}, u32[]{:S(2)}) collective-permute-start(bf16[144,1152]{1,0:T(8,128)(2,1)S(1)} %collective-permute-done.4.rest_0_), channel_id=1, source_target_pairs={{0,16},{4,20},{8,24},{12,28},{16,0},{20,4},{24,8},{28,12},{1,17},{... | collective-permute-start | bytes 995336 | tf_op jit(solution)/shard_map/ppermute | solution.py:342
  19.3 22.5 %collective-permute-start.3 = (bf16[256,1152]{1,0:T(8,128)(2,1)S(1)}, bf16[256,1152]{1,0:T(8,128)(2,1)S(1)}, u32[]{:S(2)}, u32[]{:S(2)}) collective-permute-start(bf16[256,1152]{1,0:T(8,128)(2,1)S(1)} %collective-permute-done.2.t2), channel_id=1, source_target_pairs={{0,4},{4,0},{8,12},{12,8},{16,20},{20,16},{24,28},{28,24},{1,5},{5... | collective-permute-start | bytes 1769480 | tf_op jit(solution)/shard_map/ppermute | solution.py:339
  30.8 7.1 %collective-permute-start.7 = (bf16[80,1152]{1,0:T(8,128)(2,1)S(1)}, bf16[80,1152]{1,0:T(8,128)(2,1)S(1)}, u32[]{:S(2)}, u32[]{:S(2)}) collective-permute-start(bf16[80,1152]{1,0:T(8,128)(2,1)S(1)} %collective-permute-done.6.rest_2_), channel_id=1, source_target_pairs={{0,16},{4,20},{8,24},{12,28},{16,0},{20,4},{24,8},{28,12},{1,17},{... | collective-permute-start | bytes 552968 | tf_op jit(solution)/shard_map/ppermute | solution.py:342
  37.9 4.6 %collective-permute-start.8 = (bf16[144,1152]{1,0:T(8,128)(2,1)S(1)}, bf16[144,1152]{1,0:T(8,128)(2,1)S(1)}, u32[]{:S(2)}, u32[]{:S(2)}) collective-permute-start(bf16[144,1152]{1,0:T(8,128)(2,1)S(1)} %collective-permute-done.4.rest_0_), channel_id=1, source_target_pairs={{0,4},{4,0},{8,12},{12,8},{16,20},{20,16},{24,28},{28,24},{1,5},{5... | collective-permute-start | bytes 995336 | tf_op jit(solution)/shard_map/ppermute | solution.py:339
  37.9 4.6 %collective-permute-start.9 = (bf16[144,1152]{1,0:T(8,128)(2,1)S(1)}, bf16[144,1152]{1,0:T(8,128)(2,1)S(1)}, u32[]{:S(2)}, u32[]{:S(2)}) collective-permute-start(bf16[144,1152]{1,0:T(8,128)(2,1)S(1)} %collective-permute-done.5.rest_1_), channel_id=1, source_target_pairs={{0,4},{4,0},{8,12},{12,8},{16,20},{20,16},{24,28},{28,24},{1,5},{5... | collective-permute-start | bytes 995336 | tf_op jit(solution)/shard_map/ppermute | solution.py:339
  38.4 4.0 %collective-permute-start.10 = (bf16[80,1152]{1,0:T(8,128)(2,1)S(1)}, bf16[80,1152]{1,0:T(8,128)(2,1)S(1)}, u32[]{:S(2)}, u32[]{:S(2)}) collective-permute-start(bf16[80,1152]{1,0:T(8,128)(2,1)S(1)} %collective-permute-done.6.rest_2_), channel_id=1, source_target_pairs={{0,4},{4,0},{8,12},{12,8},{16,20},{20,16},{24,28},{28,24},{1,5},{5... | collective-permute-start | bytes 552968 | tf_op jit(solution)/shard_map/ppermute | solution.py:339
  38.5 4.0 %collective-permute-start.11 = (bf16[80,1152]{1,0:T(8,128)(2,1)S(1)}, bf16[80,1152]{1,0:T(8,128)(2,1)S(1)}, u32[]{:S(2)}, u32[]{:S(2)}) collective-permute-start(bf16[80,1152]{1,0:T(8,128)(2,1)S(1)} %collective-permute-done.7.rest_3_), channel_id=1, source_target_pairs={{0,4},{4,0},{8,12},{12,8},{16,20},{20,16},{24,28},{28,24},{1,5},{5... | collective-permute-start | bytes 552968 | tf_op jit(solution)/shard_map/ppermute | solution.py:339
  39.0 1.1 %copy-start.1 = (bf16[256,1152]{1,0:T(8,128)(2,1)S(1)}, bf16[256,1152]{1,0:T(8,128)(2,1)}, u32[]{:S(2)}) copy-start(bf16[256,1152]{1,0:T(8,128)(2,1)} %x.3) | copy-start | bytes 1769476
  41.7 1.1 %copy-start = (bf16[288,1152]{1,0:T(8,128)(2,1)S(1)}, bf16[288,1152]{1,0:T(8,128)(2,1)}, u32[]{:S(2)}) copy-start(bf16[288,1152]{1,0:T(8,128)(2,1)} %own.3) | copy-start | bytes 1990660
  41.8 1.3 %copy-start.2 = (bf16[256,1152]{1,0:T(8,128)(2,1)S(1)}, bf16[256,1152]{1,0:T(8,128)(2,1)}, u32[]{:S(2)}) copy-start(bf16[256,1152]{1,0:T(8,128)(2,1)} %x.3) | copy-start | bytes 1769476
  47.5 15.3 %collective-permute-start.16 = (bf16[256,1152]{1,0:T(8,128)(2,1)S(1)}, bf16[256,1152]{1,0:T(8,128)(2,1)S(1)}, u32[]{:S(2)}, u32[]{:S(2)}) collective-permute-start(bf16[256,1152]{1,0:T(8,128)(2,1)S(1)} %get-tuple-element.23.u0), channel_id=1, source_target_pairs={{0,24},{4,28},{8,0},{12,4},{16,8},{20,12},{24,16},{28,20},{1,25},{... | collective-permute-start | bytes 1769480 | tf_op jit(solution)/shard_map/ppermute | solution.py:345
  49.5 8.3 %collective-permute-start.13 = (bf16[288,384]{1,0:T(8,128)(2,1)S(1)}, bf16[288,384]{1,0:T(8,128)(2,1)S(1)}, u32[]{:S(2)}, u32[]{:S(2)}) collective-permute-start(bf16[288,384]{1,0:T(8,128)(2,1)S(1)} %get-tuple-element.20), channel_id=1, source_target_pairs={{0,1},{1,0},{2,3},{3,2},{4,5},{5,4},{6,7},{7,6},{8,9},{9,8},{10,11... | collective-permute-start | bytes 663560 | tf_op jit(solution)/shard_map/ppermute | solution.py:336
  51.1 16.8 %collective-permute-start.12 = (bf16[288,768]{1,0:T(8,128)(2,1)S(1)}, bf16[288,768]{1,0:T(8,128)(2,1)S(1)}, u32[]{:S(2)}, u32[]{:S(2)}) collective-permute-start(bf16[288,768]{1,0:T(8,128)(2,1)S(1)} %get-tuple-element.19), channel_id=1, source_target_pairs={{0,1},{1,0},{2,3},{3,2},{4,5},{5,4},{6,7},{7,6},{8,9},{9,8},{10,11... | collective-permute-start | bytes 1327112 | tf_op jit(solution)/shard_map/ppermute | solution.py:336
  58.1 9.9 %collective-permute-start.14 = (bf16[288,384]{1,0:T(8,128)(2,1)S(1)}, bf16[288,384]{1,0:T(8,128)(2,1)S(1)}, u32[]{:S(2)}, u32[]{:S(2)}) collective-permute-start(bf16[288,384]{1,0:T(8,128)(2,1)S(1)} %get-tuple-element.21), channel_id=1, source_target_pairs={{1,2},{2,1},{5,6},{6,5},{9,10},{10,9},{13,14},{14,13},{17,18},{18,... | collective-permute-start | bytes 663560 | tf_op jit(solution)/shard_map/ppermute | solution.py:336
  58.7 13.2 %collective-permute-start.15 = (bf16[288,384]{1,0:T(8,128)(2,1)S(1)}, bf16[288,384]{1,0:T(8,128)(2,1)S(1)}, u32[]{:S(2)}, u32[]{:S(2)}) collective-permute-start(bf16[288,384]{1,0:T(8,128)(2,1)S(1)} %get-tuple-element.22), channel_id=1, source_target_pairs={{1,3},{2,0},{5,7},{6,4},{9,11},{10,8},{13,15},{14,12},{17,19},{18,... | collective-permute-start | bytes 663560 | tf_op jit(solution)/shard_map/ppermute | solution.py:336
  60.0 15.1 %collective-permute-start.19 = (bf16[256,1152]{1,0:T(8,128)(2,1)S(1)}, bf16[256,1152]{1,0:T(8,128)(2,1)S(1)}, u32[]{:S(2)}, u32[]{:S(2)}) collective-permute-start(bf16[256,1152]{1,0:T(8,128)(2,1)S(1)} %get-tuple-element.23.u0), channel_id=1, source_target_pairs={{0,4},{4,0},{8,12},{12,8},{16,20},{20,16},{24,28},{28,24},{1,5},{5... | collective-permute-start | bytes 1769480 | tf_op jit(solution)/shard_map/ppermute | solution.py:339
  62.8 12.3 %collective-permute-start.20 = (bf16[256,1152]{1,0:T(8,128)(2,1)S(1)}, bf16[256,1152]{1,0:T(8,128)(2,1)S(1)}, u32[]{:S(2)}, u32[]{:S(2)}) collective-permute-start(bf16[256,1152]{1,0:T(8,128)(2,1)S(1)} %collective-permute-done.16.rest_2_.u2), channel_id=1, source_target_pairs={{0,4},{4,0},{8,12},{12,8},{16,20},{20,16},{24,28},{28,24},{1,5},{5... | collective-permute-start | bytes 1769480 | tf_op jit(solution)/shard_map/ppermute | solution.py:339
  72.3 5.8 %collective-permute-start.17 = (bf16[288,768]{1,0:T(8,128)(2,1)S(1)}, bf16[288,768]{1,0:T(8,128)(2,1)S(1)}, u32[]{:S(2)}, u32[]{:S(2)}) collective-permute-start(bf16[288,768]{1,0:T(8,128)(2,1)S(1)} %get-tuple-element.25), channel_id=1, source_target_pairs={{1,2},{2,1},{5,6},{6,5},{9,10},{10,9},{13,14},{14,13},{17,18},{18,... | collective-permute-start | bytes 1327112 | tf_op jit(solution)/shard_map/ppermute | solution.py:336
  73.0 19.4 %collective-permute-start.18 = (bf16[288,768]{1,0:T(8,128)(2,1)S(1)}, bf16[288,768]{1,0:T(8,128)(2,1)S(1)}, u32[]{:S(2)}, u32[]{:S(2)}) collective-permute-start(bf16[288,768]{1,0:T(8,128)(2,1)S(1)} %get-tuple-element.26), channel_id=1, source_target_pairs={{1,3},{2,0},{5,7},{6,4},{9,11},{10,8},{13,15},{14,12},{17,19},{18,... | collective-permute-start | bytes 1327112 | tf_op jit(solution)/shard_map/ppermute | solution.py:336

commit v4 on v3

--- a/solution.py
+++ b/solution.py
@@ -10,6 +10,7 @@
 STEPS = 3
 EPS = 1e-06
 SHARES = (1, 2)
+UNIT_PARTS = 3
 VMEM_BYTES = 24 * 1024 * 1024
 BF16, F32 = jnp.bfloat16, jnp.float32
 
@@ -60,13 +61,13 @@
         in_specs=[IN_HBM],
         out_specs=spaces(2),
         scratch_shapes=[pltpu.SemaphoreType.DMA((2,))],
-        compiler_params=params(60 * 1024 * 1024),
+        compiler_params=params(),
         cost_estimate=cost(),
         name="cut",
     )(own)
 
 
-def prepare_kernel(n_dp, t0, twin0, twin2, t2, _, units):
+def prepare_kernel(n_dp, t0, twin0, twin2, t2, units):
     rows = t0.shape[0]
     _, core, _ = place(n_dp)
 
@@ -81,35 +82,35 @@
     pl.when(core == 1)(lambda: fill(1, twin0))
 
 
-def prepare(n_dp, t0, twin0, twin2, t2, after):
+def prepare(n_dp, t0, twin0, twin2, t2):
     rows, width = t0.shape
     out = jax.ShapeDtypeStruct((STEPS * rows, width), BF16)
     return pl.pallas_call(
         functools.partial(prepare_kernel, n_dp),
         out_shape=out,
-        in_specs=spaces(5),
+        in_specs=spaces(4),
         out_specs=pl.BlockSpec(memory_space=pltpu.VMEM),
         compiler_params=params(),
         cost_estimate=cost(),
         name="prepare",
-    )(t0, twin0, twin2, t2, after)
-
-
-def turn_kernel(x, x_t):
+    )(t0, twin0, twin2, t2)
+
+
+def turn_kernel(x, _, x_t):
     x_t[...] = x[...].T
 
 
-def turned(x):
+def turned(x, after):
     out = jax.ShapeDtypeStruct(x.shape[::-1], BF16)
     return pl.pallas_call(
         turn_kernel,
         out_shape=out,
-        in_specs=spaces(1),
+        in_specs=spaces(2),
         out_specs=pl.BlockSpec(memory_space=pltpu.VMEM),
         compiler_params=params(),
         cost_estimate=cost(),
         name="turned",
-    )(x)
+    )(x, after)
 
 
 def rows_of(ref, block, depth):
@@ -118,7 +119,8 @@
 
 def picture_kernel(n_dp, x, x_t, units, sharp, bias, own, *rest):
     pieces, outs = rest[:8], rest[8 : 8 + len(SHARES)]
-    unit, grad, w, proj, sem = rest[8 + len(SHARES) :]
+    unit_parts = rest[8 + len(SHARES) : -5]
+    grad, unit, w, proj, sem = rest[-5:]
     part, core, side = place(n_dp)
     depth = own.shape[0]
     half = depth // 2
@@ -162,10 +164,13 @@
     values = proj[...]
     inverse = 1.0 / jnp.sqrt(jnp.sum(values * values, axis=-1, keepdims=True) + EPS)
     unit[...] = (values * inverse).astype(BF16)
-    scale = sharp[0]
+    size = unit.shape[1] // UNIT_PARTS
+    for k, out in enumerate(unit_parts):
+        out[...] = unit[:, k * size : (k + 1) * size]
+    scale = sharp[...]
     logits = scale * lax.dot_general(
         unit[...], units[...], (((1,), (1,)), ((), ())), preferred_element_type=F32
-    ) + bias[0]
+    ) + bias[...]
     coefficient = jax.nn.sigmoid(logits)
     row = lax.broadcasted_iota(jnp.int32, coefficient.shape, 0)
     column = lax.broadcasted_iota(jnp.int32, coefficient.shape, 1)
@@ -199,16 +204,17 @@
     rows, width = x.shape
     depth = own.shape[0]
     out = jax.ShapeDtypeStruct((rows, width), BF16)
-    smem = pl.BlockSpec(memory_space=pltpu.SMEM)
     sizes = [width * share // sum(SHARES) for share in SHARES]
     outs = tuple(jax.ShapeDtypeStruct((depth, size), BF16) for size in sizes)
-    outs = outs + (out, out)
+    part = jax.ShapeDtypeStruct((rows, width // UNIT_PARTS), BF16)
+    outs = outs + (part,) * UNIT_PARTS + (out,)
     return pl.pallas_call(
         functools.partial(picture_kernel, n_dp),
         out_shape=outs,
-        in_specs=spaces(3) + [smem, smem] + [pl.BlockSpec(memory_space=pl.ANY)] * 9,
+        in_specs=spaces(3) + spaces(2) + [pl.BlockSpec(memory_space=pl.ANY)] * 9,
         out_specs=spaces(len(outs)),
         scratch_shapes=[
+            pltpu.VMEM((rows, width), BF16),
             pltpu.VMEM((width, width), BF16),
             pltpu.VMEM((rows, width), F32),
             pltpu.SemaphoreType.DMA((9,)),
@@ -219,25 +225,30 @@
     )(x, x_t, units, sharp, bias, own, *pieces)
 
 
-def text_kernel(n_dp, text, sharp, bias, u0, twin0, twin2, u2, out, done, units):
+def text_kernel(n_dp, text, sharp, bias, *refs):
+    blocks, (out, done, units) = refs[:-3], refs[-3:]
     rows = text.shape[0]
     _, core, _ = place(n_dp)
     done[...] = jnp.zeros_like(done)
-    units[:rows, :] = u0[...]
-    units[2 * rows :, :] = u2[...]
-    for lane, block in ((0, twin0), (1, twin2)):
-
-        @pl.when(core == lane)
-        def _():
-            units[rows : 2 * rows, :] = block[...]
+    size = blocks[0].shape[1]
+    for k in range(UNIT_PARTS):
+        u0, twin0, twin2, u2 = blocks[k::UNIT_PARTS]
+        columns = slice(k * size, (k + 1) * size)
+        units[:rows, columns] = u0[...]
+        units[2 * rows :, columns] = u2[...]
+        for lane, block in ((0, twin0), (1, twin2)):
+
+            @pl.when(core == lane)
+            def _():
+                units[rows : 2 * rows, columns] = block[...]
 
     values = text[...].astype(F32)
     inverse = 1.0 / jnp.sqrt(jnp.sum(values * values, axis=-1, keepdims=True) + EPS)
     direction = values * inverse
-    scale = sharp[0]
+    scale = sharp[...]
     logits = scale * lax.dot_general(
         direction.astype(BF16), units[...], (((1,), (1,)), ((), ())), preferred_element_type=F32
-    ) + bias[0]
+    ) + bias[...]
     coefficient = jax.nn.sigmoid(logits)
     row = lax.broadcasted_iota(jnp.int32, coefficient.shape, 0)
     column = lax.broadcasted_iota(jnp.int32, coefficient.shape, 1)
@@ -249,11 +260,10 @@
 
 def text_side(n_dp, text, sharp, bias, *units):
     rows, width = text.shape
-    smem = pl.BlockSpec(memory_space=pltpu.SMEM)
     return pl.pallas_call(
         functools.partial(text_kernel, n_dp),
         out_shape=(jax.ShapeDtypeStruct((rows, width), F32), jax.ShapeDtypeStruct((8, 128), F32)),
-        in_specs=spaces(1) + [smem, smem] + spaces(4),
+        in_specs=spaces(3 + 4 * UNIT_PARTS),
         out_specs=tuple(spaces(2)),
         scratch_shapes=[pltpu.VMEM((STEPS * rows, width), BF16)],
         compiler_params=params(),
@@ -344,7 +354,9 @@
     def shifted(value, by):
         return lax.ppermute(value, "dp", [(d, (d + by) % n_dp) for d in range(n_dp)])
 
+    sharp, bias = sharp.reshape(1, 1), bias.reshape(1, 1)
     whole, piece = cut(n_dp, short, w)
+    whole, piece, text = lax.optimization_barrier((whole, piece, text))
     turns = [
         (d * n_fsdp + f, d * n_fsdp + (f + (1 if d < side else n_fsdp - 1)) % n_fsdp)
         for d in range(n_dp)
@@ -353,25 +365,32 @@
     straight = lax.ppermute(whole, ("dp", "fsdp"), turns)
     text2 = shifted(text, 2)
     two = along(piece, [(f, (f + 2) % n_fsdp) for f in range(n_fsdp)])
-    far_x = along(x, [(0, 1), (3, 2)])
+    text2, two = lax.optimization_barrier((text2, two))
     crossed = over(straight)
     two_crossed = over(two)
     pieces = [straight, crossed, two, two_crossed]
     pieces = pieces + [across(piece) for piece in pieces]
-    x_t, far_t = turned(x), turned(far_x)
-    units = prepare(n_dp, text, across(text), across(text2), text2, far_t)
-    *outward, unit, grad = picture_side(n_dp, x, x_t, units, sharp, bias, w, pieces)
-
-    arrived = [along(o, [(0, 1), (1, 0), (2, 3), (3, 2)]) for o in outward]
-    unit2 = shifted(unit, -2)
+    x_t = turned(x, text2)
+    far_t = along(x_t, [(0, 1), (3, 2)])
+    units = prepare(n_dp, text, across(text), across(text2), text2)
+    results = picture_side(n_dp, x, x_t, units, sharp, bias, w, pieces)
+    outward, unit, grad = results[: len(SHARES)], results[len(SHARES) : -1], results[-1]
+
+    arrived = []
+    for block in outward:
+        if arrived:
+            block, arrived[-1] = lax.optimization_barrier((block, arrived[-1]))
+        arrived.append(along(block, [(0, 1), (1, 0), (2, 3), (3, 2)]))
+    unit2 = [shifted(u, -2) for u in unit]
     begin, terms, after = 0, [], []
     for block in arrived:
         kept, near, far = pair_product(begin, x_t, far_t, grad, block, after)
         near, far = along(near, [(1, 2), (2, 1)]), along(far, [(1, 3), (2, 0)])
-        after = [near, far, unit2]
+        after = [near, far]
         terms.append((begin, width, kept, near, far))
         begin += block.shape[1]
-    text_grad, done = text_side(n_dp, text, sharp, bias, unit, across(unit), across(unit2), unit2)
+    twin0, twin2 = [across(u) for u in unit], [across(u) for u in unit2]
+    text_grad, done = text_side(n_dp, text, sharp, bias, *unit, *twin0, *twin2, *unit2)
     head = total(*terms[0], [])
     for term in terms[1:]:
         head = total(*term, [head, done])

time: 93.7 us -> 95.9 us (1.023)
  starting transfers between devices: 22.2 us -> 24 us
  Pallas kernels: 12.8 us -> 11.1 us
  local copies, waits for them, and re-layouts: 1.58 us -> 2.69 us
    ppermute x1, waiting for transfers between devices: 7.13 us -> 0.01 us  [line_body(): straight = lax.ppermute(whole, ('dp', 'fsdp'), turns)]
    ppermute x2, waiting for transfers between devices: 3.52 us -> 9.27 us  [over(): lax.ppermute(value, 'dp', [(d, (d + side) % n_dp) for d in range(n_dp)])]
    ppermute x2 -> x4, starting transfers between devices: 4.96 us -> 8.05 us  [shifted(): lax.ppermute(value, 'dp', [(d, (d + by) % n_dp) for d in range(n_dp)])]
    ppermute x2, starting transfers between devices: 4.58 us -> 2.08 us  [over(): lax.ppermute(value, 'dp', [(d, (d + side) % n_dp) for d in range(n_dp)])]
    ppermute x2 -> x4, waiting for transfers between devices: 2.7 us -> 5.1 us  [shifted(): lax.ppermute(value, 'dp', [(d, (d + by) % n_dp) for d in range(n_dp)])]
    pallas_call x1, Pallas kernels: 1.88 us -> 0.36 us  [cut(): pl.pallas_call(functools.partial(cut_kernel, n_dp, short), out_shape=outs...]
    ppermute x8, waiting for transfers between devices: 41.3 us -> 40 us  [along(): return lax.ppermute(value, 'fsdp', pairs)]
    ppermute x8 -> x12, waiting for transfers between devices: 0.02 us -> 1.23 us  [across(): return lax.ppermute(value, 'dp', [(d, d ^ 1) for d in range(n_dp)])]
  transfers between devices with their start and end apart: 21 -> 27, of which waited for: 8 -> 10; matrix products, arithmetic and copies ran while one was open for 0% -> 0% of each run, Pallas kernels for 8% -> 10%
where the time goes in v4:
time: 95.9 us; the launch traced here: 95.6 us
  waiting for transfers between devices  55.6 us (58%)
  starting transfers between devices  24 us (25%)
  Pallas kernels  11.1 us (12%)
  local copies, waits for them, and re-layouts  2.69 us (3%)
  between operations  2.15 us (2%)
    ppermute x8, waiting for transfers between devices, along(): return lax.ppermute(value, 'fsdp', pairs)  40 us
    ppermute x8, starting transfers between devices, along(): return lax.ppermute(value, 'fsdp', pairs)  10.7 us
    ppermute x2, waiting for transfers between devices, over(): lax.ppermute(value, 'dp', [(d, (d + side) % n_dp) for d in range(n_dp)])  9.27 us
    ppermute x4, starting transfers between devices, shifted(): lax.ppermute(value, 'dp', [(d, (d + by) % n_dp) for d in range(n_dp)])  8.05 us
    ppermute x4, waiting for transfers between devices, shifted(): lax.ppermute(value, 'dp', [(d, (d + by) % n_dp) for d in range(n_dp)])  5.1 us
    pallas_call x1, Pallas kernels, picture_side(): pl.pallas_call(functools.partial(picture_kernel, n_dp), out_shape=outs, i...  4.52 us
    pallas_call x1, Pallas kernels, text_side(): pl.pallas_call(functools.partial(text_kernel, n_dp), out_shape=(jax.Shape...  2.92 us
    unnamed x10, local copies, waits for them, and re-layouts  2.69 us
  transfers between devices with their start and end apart: 27, of which 10 were waited for; matrix products, arithmetic and copies ran while one was open for 0% of the time, Pallas kernels for 10%

profile of v4, /device:TPU:0, one launch (start us, length us, event | category | flops | bytes accessed | tf_op | source)
XLA Modules:
  0.0 95.6 jit_solution(4938430220939633684)
XLA Ops:
  0.6 1.1 %copy-done = bf16[288,1152]{1,0:T(8,128)(2,1)S(1)} copy-done((bf16[288,1152]{1,0:T(8,128)(2,1)S(1)}, bf16[288,1152]{1,0:T(8,128)(2,1)}, u32[]{:S(2)}) %copy-start) | copy-done | bytes 663576
  2.1 3.0 %collective-permute-start = (bf16[256,1152]{1,0:T(8,128)(2,1)}, bf16[256,1152]{1,0:T(8,128)(2,1)S(1)}, u32[]{:S(2)}, u32[]{:S(2)}) collective-permute-start(bf16[256,1152]{1,0:T(8,128)(2,1)} %text), channel_id=1, source_target_pairs={{0,8},{4,12},{8,16},{12,20},{16,24},{20,28},{24,0},{28,4},{1,9},{5... | collective-permute-start | bytes 1769480 | tf_op jit(solution)/shard_map/ppermute | solution.py:355
  5.1 1.6 %collective-permute-start.5 = (bf16[144,1152]{1,0:T(8,128)(2,1)S(1)}, bf16[144,1152]{1,0:T(8,128)(2,1)S(1)}, u32[]{:S(2)}, u32[]{:S(2)}) collective-permute-start(bf16[144,1152]{1,0:T(8,128)(2,1)S(1)} %get-tuple-element.30), channel_id=1, source_target_pairs={{0,1},{1,2},{2,3},{3,0},{4,5},{5,6},{6,7},{7,4},{8,9},{9,10},{10,1... | collective-permute-start | bytes 995336 | tf_op jit(solution)/shard_map/ppermute | solution.py:365
  6.7 2.6 %collective-permute-start.1 = (bf16[80,1152]{1,0:T(8,128)(2,1)S(1)}, bf16[80,1152]{1,0:T(8,128)(2,1)S(1)}, u32[]{:S(2)}, u32[]{:S(2)}) collective-permute-start(bf16[80,1152]{1,0:T(8,128)(2,1)S(1)} %get-tuple-element.28), channel_id=1, source_target_pairs={{0,2},{1,3},{2,0},{3,1},{4,6},{5,7},{6,4},{7,5},{8,10},{9,11},{10,... | collective-permute-start | bytes 552968 | tf_op jit(solution)/shard_map/ppermute | solution.py:346
  9.3 14.8 %collective-permute-done.1.rest_2_ = bf16[80,1152]{1,0:T(8,128)(2,1)S(1)} collective-permute-done((bf16[80,1152]{1,0:T(8,128)(2,1)S(1)}, bf16[80,1152]{1,0:T(8,128)(2,1)S(1)}, u32[]{:S(2)}, u32[]{:S(2)}) %collective-permute-start.1) | collective-permute-done | bytes 184352 | tf_op jit(solution)/shard_map/ppermute | solution.py:346
  24.1 0.7 collective-permute-start.6
  24.9 1.4 %collective-permute-start.7 = (bf16[80,1152]{1,0:T(8,128)(2,1)S(1)}, bf16[80,1152]{1,0:T(8,128)(2,1)S(1)}, u32[]{:S(2)}, u32[]{:S(2)}) collective-permute-start(bf16[80,1152]{1,0:T(8,128)(2,1)S(1)} %collective-permute-done.1.rest_2_), channel_id=1, source_target_pairs={{0,16},{4,20},{8,24},{12,28},{16,0},{20,4},{24,8},{28,12},{1,17},{... | collective-permute-start | bytes 552968 | tf_op jit(solution)/shard_map/ppermute | solution.py:352
  26.2 8.6 %collective-permute-done.6.rest_1_ = bf16[144,1152]{1,0:T(8,128)(2,1)S(1)} collective-permute-done((bf16[144,1152]{1,0:T(8,128)(2,1)S(1)}, bf16[144,1152]{1,0:T(8,128)(2,1)S(1)}, u32[]{:S(2)}, u32[]{:S(2)}) %collective-permute-start.6) | collective-permute-done | bytes 331808 | tf_op jit(solution)/shard_map/ppermute | solution.py:352
  34.8 1.1 %copy-done.2 = bf16[256,1152]{1,0:T(8,128)(2,1)S(1)} copy-done((bf16[256,1152]{1,0:T(8,128)(2,1)S(1)}, bf16[256,1152]{1,0:T(8,128)(2,1)}, u32[]{:S(2)}) %copy-start.2) | copy-done | bytes 589848
  36.1 1.5 %collective-permute-start.2 = (bf16[1152,256]{1,0:T(8,128)(2,1)S(1)}, bf16[1152,256]{1,0:T(8,128)(2,1)S(1)}, u32[]{:S(2)}, u32[]{:S(2)}) collective-permute-start(bf16[1152,256]{1,0:T(8,128)(2,1)S(1)} %turned.1.x_t), channel_id=1, source_target_pairs={{0,1},{3,2},{4,5},{7,6},{8,9},{11,10},{12,13},{15,14},{16,17},{19,... | collective-permute-start | bytes 1769480 | tf_op jit(solution)/shard_map/ppermute | solution.py:346
  37.6 0.7 collective-permute-done.7.rest_3_
  38.3 0.5 collective-permute-start.11
  40.1 0.7 prepare.1.units
  41.4 4.5 %picture_side.1 = (bf16[288,384]{1,0:T(8,128)(2,1)S(1)}, bf16[288,768]{1,0:T(8,128)(2,1)S(1)}, bf16[256,384]{1,0:T(8,128)(2,1)S(1)}, bf16[256,384]{1,0:T(8,128)(...) custom-call(bf16[256,1152]{1,0:T(8,128)(2,1)S(1)} %copy-done.3, bf16[1152,256]{1,0:T(8,128)(2,1)S(1)} %turned.1.x_t, ...), custom_call_target="tpu_custom_call" | custom-call | tf_op jit(solution)/shard_map/picture_side/pallas_call | solution.py:211
  46.1 9.6 %collective-permute-done.12.arrived = bf16[288,384]{1,0:T(8,128)(2,1)S(1)} collective-permute-done((bf16[288,384]{1,0:T(8,128)(2,1)S(1)}, bf16[288,384]{1,0:T(8,128)(2,1)S(1)}, u32[]{:S(2)}, u32[]{:S(2)}) %collective-permute-start.12) | collective-permute-done | bytes 221216 | tf_op jit(solution)/shard_map/ppermute | solution.py:346
  55.6 2.5 %collective-permute-start.13 = (bf16[288,768]{1,0:T(8,128)(2,1)S(1)}, bf16[288,768]{1,0:T(8,128)(2,1)S(1)}, u32[]{:S(2)}, u32[]{:S(2)}) collective-permute-start(bf16[288,768]{1,0:T(8,128)(2,1)S(1)} %get-tuple-element.35), channel_id=1, source_target_pairs={{0,1},{1,0},{2,3},{3,2},{4,5},{5,4},{6,7},{7,6},{8,9},{9,8},{10,11... | collective-permute-start | bytes 1327112 | tf_op jit(solution)/shard_map/ppermute | solution.py:346
  58.4 0.7 collective-permute-start.14
  59.1 1.3 %collective-permute-start.15 = (bf16[288,384]{1,0:T(8,128)(2,1)S(1)}, bf16[288,384]{1,0:T(8,128)(2,1)S(1)}, u32[]{:S(2)}, u32[]{:S(2)}) collective-permute-start(bf16[288,384]{1,0:T(8,128)(2,1)S(1)} %get-tuple-element.38), channel_id=1, source_target_pairs={{1,3},{2,0},{5,7},{6,4},{9,11},{10,8},{13,15},{14,12},{17,19},{18,... | collective-permute-start | bytes 663560 | tf_op jit(solution)/shard_map/ppermute | solution.py:346
  60.4 1.8 %collective-permute-start.21 = (bf16[256,384]{1,0:T(8,128)(2,1)S(1)}, bf16[256,384]{1,0:T(8,128)(2,1)S(1)}, u32[]{:S(2)}, u32[]{:S(2)}) collective-permute-start(bf16[256,384]{1,0:T(8,128)(2,1)S(1)} %get-tuple-element.43.refs_0_), channel_id=1, source_target_pairs={{0,24},{4,28},{8,0},{12,4},{16,8},{20,12},{24,16},{28,20},{1,25},{... | collective-permute-start | bytes 589832 | tf_op jit(solution)/shard_map/ppermute | solution.py:355
  62.2 1.5 %collective-permute-start.23 = (bf16[256,384]{1,0:T(8,128)(2,1)S(1)}, bf16[256,384]{1,0:T(8,128)(2,1)S(1)}, u32[]{:S(2)}, u32[]{:S(2)}) collective-permute-start(bf16[256,384]{1,0:T(8,128)(2,1)S(1)} %get-tuple-element.44.refs_1_), channel_id=1, source_target_pairs={{0,24},{4,28},{8,0},{12,4},{16,8},{20,12},{24,16},{28,20},{1,25},{... | collective-permute-start | bytes 589832 | tf_op jit(solution)/shard_map/ppermute | solution.py:355
  63.7 8.4 %collective-permute-done.15.rest_1_.far = bf16[288,384]{1,0:T(8,128)(2,1)S(1)} collective-permute-done((bf16[288,384]{1,0:T(8,128)(2,1)S(1)}, bf16[288,384]{1,0:T(8,128)(2,1)S(1)}, u32[]{:S(2)}, u32[]{:S(2)}) %collective-permute-start.15) | collective-permute-done | bytes 221216 | tf_op jit(solution)/shard_map/ppermute | solution.py:346
  72.1 0.9 collective-permute-done.13.arrived
  73.4 0.7 collective-permute-start.16
  74.1 1.3 %collective-permute-start.17 = (bf16[288,768]{1,0:T(8,128)(2,1)S(1)}, bf16[288,768]{1,0:T(8,128)(2,1)S(1)}, u32[]{:S(2)}, u32[]{:S(2)}) collective-permute-start(bf16[288,768]{1,0:T(8,128)(2,1)S(1)} %get-tuple-element.41), channel_id=1, source_target_pairs={{1,3},{2,0},{5,7},{6,4},{9,11},{10,8},{13,15},{14,12},{17,19},{18,... | collective-permute-start | bytes 1327112 | tf_op jit(solution)/shard_map/ppermute | solution.py:346
  75.5 1.7 %collective-permute-start.25 = (bf16[256,384]{1,0:T(8,128)(2,1)S(1)}, bf16[256,384]{1,0:T(8,128)(2,1)S(1)}, u32[]{:S(2)}, u32[]{:S(2)}) collective-permute-start(bf16[256,384]{1,0:T(8,128)(2,1)S(1)} %get-tuple-element.45.refs_2_), channel_id=1, source_target_pairs={{0,24},{4,28},{8,0},{12,4},{16,8},{20,12},{24,16},{28,20},{1,25},{... | collective-permute-start | bytes 589832 | tf_op jit(solution)/shard_map/ppermute | solution.py:355
  77.7 5.1 %collective-permute-done.25.refs_11_ = bf16[256,384]{1,0:T(8,128)(2,1)S(1)} collective-permute-done((bf16[256,384]{1,0:T(8,128)(2,1)S(1)}, bf16[256,384]{1,0:T(8,128)(2,1)S(1)}, u32[]{:S(2)}, u32[]{:S(2)}) %collective-permute-start.25) | collective-permute-done | bytes 196640 | tf_op jit(solution)/shard_map/ppermute | solution.py:355
  82.8 0.5 collective-permute-start.26
  83.3 0.9 collective-permute-done.24.refs_7_
  84.5 2.9 %text_side.1 = (f32[256,1152]{1,0:T(8,128)}, f32[8,128]{1,0:T(8,128)S(1)}) custom-call(bf16[256,1152]{1,0:T(8,128)(2,1)S(1)} %copy-done.4, f32[1,1]{1,0:T(1,128)} %bitcast.3.sharp, f32[1,1]{1,0:T(1,128)} %bitcast.5.bias, bf16[256,384]{1,0:T(8,128)(2,1)S(1)} %get-tuple-element.43.refs_0_, bf16[256,384]{1,0:T(8,128)(2,1)S(1)} %get-tuple-element.44.refs_1_, ...), custom_call_target="tpu_custom_call" | custom-call | tf_op jit(solution)/shard_map/text_side/pallas_call | solution.py:263
  87.4 0.8 total.2.rest_0_
  88.3 6.3 %collective-permute-done.17.far = bf16[288,768]{1,0:T(8,128)(2,1)S(1)} collective-permute-done((bf16[288,768]{1,0:T(8,128)(2,1)S(1)}, bf16[288,768]{1,0:T(8,128)(2,1)S(1)}, u32[]{:S(2)}, u32[]{:S(2)}) %collective-permute-start.17) | collective-permute-done | bytes 442400 | tf_op jit(solution)/shard_map/ppermute | solution.py:346
  94.5 1.0 %total.3 = f32[1,288,1152]{2,1,0:T(8,128)} custom-call(f32[288,768]{1,0:T(8,128)S(1)} %get-tuple-element.39.kept, bf16[288,768]{1,0:T(8,128)(2,1)S(1)} %collective-permute-done.16.near, bf16[288,768]{1,0:T(8,128)(2,1)S(1)} %collective-permute-done.17.far, f32[1,288,1152]{2,1,0:T(8,128)} %total.2.rest_0_, ...), custom_call_target="tpu_custom_call", output_to_operand_aliasing={{}: (3, {})} | custom-call | tf_op jit(solution)/shard_map/total/pallas_call | solution.py:325
  (41 shorter events, 2.8 us)
Async XLA Ops:
  0.6 1.1 %copy-start = (bf16[288,1152]{1,0:T(8,128)(2,1)S(1)}, bf16[288,1152]{1,0:T(8,128)(2,1)}, u32[]{:S(2)}) copy-start(bf16[288,1152]{1,0:T(8,128)(2,1)} %own.3) | copy-start | bytes 1990660
  1.7 38.4 %copy-start.4 = (bf16[256,1152]{1,0:T(8,128)(2,1)S(1)}, bf16[256,1152]{1,0:T(8,128)(2,1)}, u32[]{:S(2)}) copy-start(bf16[256,1152]{1,0:T(8,128)(2,1)} %text) | copy-start | bytes 1769476
  2.1 22.0 %collective-permute-start = (bf16[256,1152]{1,0:T(8,128)(2,1)}, bf16[256,1152]{1,0:T(8,128)(2,1)S(1)}, u32[]{:S(2)}, u32[]{:S(2)}) collective-permute-start(bf16[256,1152]{1,0:T(8,128)(2,1)} %text), channel_id=1, source_target_pairs={{0,8},{4,12},{8,16},{12,20},{16,24},{20,28},{24,0},{28,4},{1,9},{5... | collective-permute-start | bytes 1769480 | tf_op jit(solution)/shard_map/ppermute | solution.py:355
  5.1 19.0 %collective-permute-start.5 = (bf16[144,1152]{1,0:T(8,128)(2,1)S(1)}, bf16[144,1152]{1,0:T(8,128)(2,1)S(1)}, u32[]{:S(2)}, u32[]{:S(2)}) collective-permute-start(bf16[144,1152]{1,0:T(8,128)(2,1)S(1)} %get-tuple-element.30), channel_id=1, source_target_pairs={{0,1},{1,2},{2,3},{3,0},{4,5},{5,6},{6,7},{7,4},{8,9},{9,10},{10,1... | collective-permute-start | bytes 995336 | tf_op jit(solution)/shard_map/ppermute | solution.py:365
  6.7 17.4 %collective-permute-start.1 = (bf16[80,1152]{1,0:T(8,128)(2,1)S(1)}, bf16[80,1152]{1,0:T(8,128)(2,1)S(1)}, u32[]{:S(2)}, u32[]{:S(2)}) collective-permute-start(bf16[80,1152]{1,0:T(8,128)(2,1)S(1)} %get-tuple-element.28), channel_id=1, source_target_pairs={{0,2},{1,3},{2,0},{3,1},{4,6},{5,7},{6,4},{7,5},{8,10},{9,11},{10,... | collective-permute-start | bytes 552968 | tf_op jit(solution)/shard_map/ppermute | solution.py:346
  9.3 26.8 %collective-permute-start.3 = (bf16[256,1152]{1,0:T(8,128)(2,1)}, bf16[256,1152]{1,0:T(8,128)(2,1)S(1)}, u32[]{:S(2)}, u32[]{:S(2)}) collective-permute-start(bf16[256,1152]{1,0:T(8,128)(2,1)} %text), channel_id=1, source_target_pairs={{0,4},{4,0},{8,12},{12,8},{16,20},{20,16},{24,28},{28,24},{1,5},{5... | collective-permute-start | bytes 1769480 | tf_op jit(solution)/shard_map/ppermute | solution.py:349
  24.1 14.2 %collective-permute-start.4 = (bf16[256,1152]{1,0:T(8,128)(2,1)S(1)}, bf16[256,1152]{1,0:T(8,128)(2,1)S(1)}, u32[]{:S(2)}, u32[]{:S(2)}) collective-permute-start(bf16[256,1152]{1,0:T(8,128)(2,1)S(1)} %collective-permute-done._.t2), channel_id=1, source_target_pairs={{0,4},{4,0},{8,12},{12,8},{16,20},{20,16},{24,28},{28,24},{1,5},{5... | collective-permute-start | bytes 1769480 | tf_op jit(solution)/shard_map/ppermute | solution.py:349
  24.1 10.7 %collective-permute-start.6 = (bf16[144,1152]{1,0:T(8,128)(2,1)S(1)}, bf16[144,1152]{1,0:T(8,128)(2,1)S(1)}, u32[]{:S(2)}, u32[]{:S(2)}) collective-permute-start(bf16[144,1152]{1,0:T(8,128)(2,1)S(1)} %collective-permute-done.5.rest_0_), channel_id=1, source_target_pairs={{0,16},{4,20},{8,24},{12,28},{16,0},{20,4},{24,8},{28,12},{1,17},{... | collective-permute-start | bytes 995336 | tf_op jit(solution)/shard_map/ppermute | solution.py:352
  24.9 13.4 %collective-permute-start.7 = (bf16[80,1152]{1,0:T(8,128)(2,1)S(1)}, bf16[80,1152]{1,0:T(8,128)(2,1)S(1)}, u32[]{:S(2)}, u32[]{:S(2)}) collective-permute-start(bf16[80,1152]{1,0:T(8,128)(2,1)S(1)} %collective-permute-done.1.rest_2_), channel_id=1, source_target_pairs={{0,16},{4,20},{8,24},{12,28},{16,0},{20,4},{24,8},{28,12},{1,17},{... | collective-permute-start | bytes 552968 | tf_op jit(solution)/shard_map/ppermute | solution.py:352
  26.2 14.6 %collective-permute-start.8 = (bf16[144,1152]{1,0:T(8,128)(2,1)S(1)}, bf16[144,1152]{1,0:T(8,128)(2,1)S(1)}, u32[]{:S(2)}, u32[]{:S(2)}) collective-permute-start(bf16[144,1152]{1,0:T(8,128)(2,1)S(1)} %collective-permute-done.5.rest_0_), channel_id=1, source_target_pairs={{0,4},{4,0},{8,12},{12,8},{16,20},{20,16},{24,28},{28,24},{1,5},{5... | collective-permute-start | bytes 995336 | tf_op jit(solution)/shard_map/ppermute | solution.py:349
  34.8 6.0 %collective-permute-start.9 = (bf16[144,1152]{1,0:T(8,128)(2,1)S(1)}, bf16[144,1152]{1,0:T(8,128)(2,1)S(1)}, u32[]{:S(2)}, u32[]{:S(2)}) collective-permute-start(bf16[144,1152]{1,0:T(8,128)(2,1)S(1)} %collective-permute-done.6.rest_1_), channel_id=1, source_target_pairs={{0,4},{4,0},{8,12},{12,8},{16,20},{20,16},{24,28},{28,24},{1,5},{5... | collective-permute-start | bytes 995336 | tf_op jit(solution)/shard_map/ppermute | solution.py:349
  34.8 1.1 %copy-start.2 = (bf16[256,1152]{1,0:T(8,128)(2,1)S(1)}, bf16[256,1152]{1,0:T(8,128)(2,1)}, u32[]{:S(2)}) copy-start(bf16[256,1152]{1,0:T(8,128)(2,1)} %x.3) | copy-start | bytes 1769476
  36.1 22.0 %collective-permute-start.2 = (bf16[1152,256]{1,0:T(8,128)(2,1)S(1)}, bf16[1152,256]{1,0:T(8,128)(2,1)S(1)}, u32[]{:S(2)}, u32[]{:S(2)}) collective-permute-start(bf16[1152,256]{1,0:T(8,128)(2,1)S(1)} %turned.1.x_t), channel_id=1, source_target_pairs={{0,1},{3,2},{4,5},{7,6},{8,9},{11,10},{12,13},{15,14},{16,17},{19,... | collective-permute-start | bytes 1769480 | tf_op jit(solution)/shard_map/ppermute | solution.py:346
  38.3 2.5 %collective-permute-start.10 = (bf16[80,1152]{1,0:T(8,128)(2,1)S(1)}, bf16[80,1152]{1,0:T(8,128)(2,1)S(1)}, u32[]{:S(2)}, u32[]{:S(2)}) collective-permute-start(bf16[80,1152]{1,0:T(8,128)(2,1)S(1)} %collective-permute-done.1.rest_2_), channel_id=1, source_target_pairs={{0,4},{4,0},{8,12},{12,8},{16,20},{20,16},{24,28},{28,24},{1,5},{5... | collective-permute-start | bytes 552968 | tf_op jit(solution)/shard_map/ppermute | solution.py:349
  38.3 2.5 %collective-permute-start.11 = (bf16[80,1152]{1,0:T(8,128)(2,1)S(1)}, bf16[80,1152]{1,0:T(8,128)(2,1)S(1)}, u32[]{:S(2)}, u32[]{:S(2)}) collective-permute-start(bf16[80,1152]{1,0:T(8,128)(2,1)S(1)} %collective-permute-done.7.rest_3_), channel_id=1, source_target_pairs={{0,4},{4,0},{8,12},{12,8},{16,20},{20,16},{24,28},{28,24},{1,5},{5... | collective-permute-start | bytes 552968 | tf_op jit(solution)/shard_map/ppermute | solution.py:349
  40.1 1.1 %copy-start.1 = (bf16[288,1152]{1,0:T(8,128)(2,1)S(1)}, bf16[288,1152]{1,0:T(8,128)(2,1)}, u32[]{:S(2)}) copy-start(bf16[288,1152]{1,0:T(8,128)(2,1)} %own.3) | copy-start | bytes 1990660
  40.1 1.3 %copy-start.3 = (bf16[256,1152]{1,0:T(8,128)(2,1)S(1)}, bf16[256,1152]{1,0:T(8,128)(2,1)}, u32[]{:S(2)}) copy-start(bf16[256,1152]{1,0:T(8,128)(2,1)} %x.3) | copy-start | bytes 1769476
  45.9 9.7 %collective-permute-start.12 = (bf16[288,384]{1,0:T(8,128)(2,1)S(1)}, bf16[288,384]{1,0:T(8,128)(2,1)S(1)}, u32[]{:S(2)}, u32[]{:S(2)}) collective-permute-start(bf16[288,384]{1,0:T(8,128)(2,1)S(1)} %get-tuple-element.34), channel_id=1, source_target_pairs={{0,1},{1,0},{2,3},{3,2},{4,5},{5,4},{6,7},{7,6},{8,9},{9,8},{10,11... | collective-permute-start | bytes 663560 | tf_op jit(solution)/shard_map/ppermute | solution.py:346
  55.6 17.4 %collective-permute-start.13 = (bf16[288,768]{1,0:T(8,128)(2,1)S(1)}, bf16[288,768]{1,0:T(8,128)(2,1)S(1)}, u32[]{:S(2)}, u32[]{:S(2)}) collective-permute-start(bf16[288,768]{1,0:T(8,128)(2,1)S(1)} %get-tuple-element.35), channel_id=1, source_target_pairs={{0,1},{1,0},{2,3},{3,2},{4,5},{5,4},{6,7},{7,6},{8,9},{9,8},{10,11... | collective-permute-start | bytes 1327112 | tf_op jit(solution)/shard_map/ppermute | solution.py:346
  58.4 3.8 %collective-permute-start.14 = (bf16[288,384]{1,0:T(8,128)(2,1)S(1)}, bf16[288,384]{1,0:T(8,128)(2,1)S(1)}, u32[]{:S(2)}, u32[]{:S(2)}) collective-permute-start(bf16[288,384]{1,0:T(8,128)(2,1)S(1)} %get-tuple-element.37), channel_id=1, source_target_pairs={{1,2},{2,1},{5,6},{6,5},{9,10},{10,9},{13,14},{14,13},{17,18},{18,... | collective-permute-start | bytes 663560 | tf_op jit(solution)/shard_map/ppermute | solution.py:346
  59.1 13.1 %collective-permute-start.15 = (bf16[288,384]{1,0:T(8,128)(2,1)S(1)}, bf16[288,384]{1,0:T(8,128)(2,1)S(1)}, u32[]{:S(2)}, u32[]{:S(2)}) collective-permute-start(bf16[288,384]{1,0:T(8,128)(2,1)S(1)} %get-tuple-element.38), channel_id=1, source_target_pairs={{1,3},{2,0},{5,7},{6,4},{9,11},{10,8},{13,15},{14,12},{17,19},{18,... | collective-permute-start | bytes 663560 | tf_op jit(solution)/shard_map/ppermute | solution.py:346
  60.4 15.0 %collective-permute-start.21 = (bf16[256,384]{1,0:T(8,128)(2,1)S(1)}, bf16[256,384]{1,0:T(8,128)(2,1)S(1)}, u32[]{:S(2)}, u32[]{:S(2)}) collective-permute-start(bf16[256,384]{1,0:T(8,128)(2,1)S(1)} %get-tuple-element.43.refs_0_), channel_id=1, source_target_pairs={{0,24},{4,28},{8,0},{12,4},{16,8},{20,12},{24,16},{28,20},{1,25},{... | collective-permute-start | bytes 589832 | tf_op jit(solution)/shard_map/ppermute | solution.py:355
  62.2 13.3 %collective-permute-start.18 = (bf16[256,384]{1,0:T(8,128)(2,1)S(1)}, bf16[256,384]{1,0:T(8,128)(2,1)S(1)}, u32[]{:S(2)}, u32[]{:S(2)}) collective-permute-start(bf16[256,384]{1,0:T(8,128)(2,1)S(1)} %get-tuple-element.43.refs_0_), channel_id=1, source_target_pairs={{0,4},{4,0},{8,12},{12,8},{16,20},{20,16},{24,28},{28,24},{1,5},{5... | collective-permute-start | bytes 589832 | tf_op jit(solution)/shard_map/ppermute | solution.py:349
  62.2 15.0 %collective-permute-start.23 = (bf16[256,384]{1,0:T(8,128)(2,1)S(1)}, bf16[256,384]{1,0:T(8,128)(2,1)S(1)}, u32[]{:S(2)}, u32[]{:S(2)}) collective-permute-start(bf16[256,384]{1,0:T(8,128)(2,1)S(1)} %get-tuple-element.44.refs_1_), channel_id=1, source_target_pairs={{0,24},{4,28},{8,0},{12,4},{16,8},{20,12},{24,16},{28,20},{1,25},{... | collective-permute-start | bytes 589832 | tf_op jit(solution)/shard_map/ppermute | solution.py:355
  73.4 14.9 %collective-permute-start.16 = (bf16[288,768]{1,0:T(8,128)(2,1)S(1)}, bf16[288,768]{1,0:T(8,128)(2,1)S(1)}, u32[]{:S(2)}, u32[]{:S(2)}) collective-permute-start(bf16[288,768]{1,0:T(8,128)(2,1)S(1)} %get-tuple-element.40), channel_id=1, source_target_pairs={{1,2},{2,1},{5,6},{6,5},{9,10},{10,9},{13,14},{14,13},{17,18},{18,... | collective-permute-start | bytes 1327112 | tf_op jit(solution)/shard_map/ppermute | solution.py:346
  74.1 20.5 %collective-permute-start.17 = (bf16[288,768]{1,0:T(8,128)(2,1)S(1)}, bf16[288,768]{1,0:T(8,128)(2,1)S(1)}, u32[]{:S(2)}, u32[]{:S(2)}) collective-permute-start(bf16[288,768]{1,0:T(8,128)(2,1)S(1)} %get-tuple-element.41), channel_id=1, source_target_pairs={{1,3},{2,0},{5,7},{6,4},{9,11},{10,8},{13,15},{14,12},{17,19},{18,... | collective-permute-start | bytes 1327112 | tf_op jit(solution)/shard_map/ppermute | solution.py:346
  75.4 1.9 %collective-permute-start.19 = (bf16[256,384]{1,0:T(8,128)(2,1)S(1)}, bf16[256,384]{1,0:T(8,128)(2,1)S(1)}, u32[]{:S(2)}, u32[]{:S(2)}) collective-permute-start(bf16[256,384]{1,0:T(8,128)(2,1)S(1)} %get-tuple-element.44.refs_1_), channel_id=1, source_target_pairs={{0,4},{4,0},{8,12},{12,8},{16,20},{20,16},{24,28},{28,24},{1,5},{5... | collective-permute-start | bytes 589832 | tf_op jit(solution)/shard_map/ppermute | solution.py:349
  75.5 7.3 %collective-permute-start.25 = (bf16[256,384]{1,0:T(8,128)(2,1)S(1)}, bf16[256,384]{1,0:T(8,128)(2,1)S(1)}, u32[]{:S(2)}, u32[]{:S(2)}) collective-permute-start(bf16[256,384]{1,0:T(8,128)(2,1)S(1)} %get-tuple-element.45.refs_2_), channel_id=1, source_target_pairs={{0,24},{4,28},{8,0},{12,4},{16,8},{20,12},{24,16},{28,20},{1,25},{... | collective-permute-start | bytes 589832 | tf_op jit(solution)/shard_map/ppermute | solution.py:355
  77.2 5.6 %collective-permute-start.20 = (bf16[256,384]{1,0:T(8,128)(2,1)S(1)}, bf16[256,384]{1,0:T(8,128)(2,1)S(1)}, u32[]{:S(2)}, u32[]{:S(2)}) collective-permute-start(bf16[256,384]{1,0:T(8,128)(2,1)S(1)} %get-tuple-element.45.refs_2_), channel_id=1, source_target_pairs={{0,4},{4,0},{8,12},{12,8},{16,20},{20,16},{24,28},{28,24},{1,5},{5... | collective-permute-start | bytes 589832 | tf_op jit(solution)/shard_map/ppermute | solution.py:349
  77.3 6.0 %collective-permute-start.22 = (bf16[256,384]{1,0:T(8,128)(2,1)S(1)}, bf16[256,384]{1,0:T(8,128)(2,1)S(1)}, u32[]{:S(2)}, u32[]{:S(2)}) collective-permute-start(bf16[256,384]{1,0:T(8,128)(2,1)S(1)} %collective-permute-done.21.refs_9_), channel_id=1, source_target_pairs={{0,4},{4,0},{8,12},{12,8},{16,20},{20,16},{24,28},{28,24},{1,5},{5... | collective-permute-start | bytes 589832 | tf_op jit(solution)/shard_map/ppermute | solution.py:349
  82.8 1.4 %collective-permute-start.24 = (bf16[256,384]{1,0:T(8,128)(2,1)S(1)}, bf16[256,384]{1,0:T(8,128)(2,1)S(1)}, u32[]{:S(2)}, u32[]{:S(2)}) collective-permute-start(bf16[256,384]{1,0:T(8,128)(2,1)S(1)} %collective-permute-done.23.refs_10_), channel_id=1, source_target_pairs={{0,4},{4,0},{8,12},{12,8},{16,20},{20,16},{24,28},{28,24},{1,5},{5... | collective-permute-start | bytes 589832 | tf_op jit(solution)/shard_map/ppermute | solution.py:349
  82.8 1.7 %collective-permute-start.26 = (bf16[256,384]{1,0:T(8,128)(2,1)S(1)}, bf16[256,384]{1,0:T(8,128)(2,1)S(1)}, u32[]{:S(2)}, u32[]{:S(2)}) collective-permute-start(bf16[256,384]{1,0:T(8,128)(2,1)S(1)} %collective-permute-done.25.refs_11_), channel_id=1, source_target_pairs={{0,4},{4,0},{8,12},{12,8},{16,20},{20,16},{24,28},{28,24},{1,5},{5... | collective-permute-start | bytes 589832 | tf_op jit(solution)/shard_map/ppermute | solution.py:349

commit v5 on v4

--- a/solution.py
+++ b/solution.py
@@ -67,8 +67,10 @@
     )(own)
 
 
-def prepare_kernel(n_dp, t0, twin0, twin2, t2, units):
+def prepare_kernel(n_dp, t0, twin0, twin2, t2, sharp, bias, units, scalars):
     rows = t0.shape[0]
+    scalars[0:1, :] = jnp.broadcast_to(sharp[...], (1, scalars.shape[1]))
+    scalars[1:2, :] = jnp.broadcast_to(bias[...], (1, scalars.shape[1]))
     _, core, _ = place(n_dp)
 
     def fill(k, block):
@@ -82,42 +84,44 @@
     pl.when(core == 1)(lambda: fill(1, twin0))
 
 
-def prepare(n_dp, t0, twin0, twin2, t2):
+def prepare(n_dp, t0, twin0, twin2, t2, sharp, bias):
     rows, width = t0.shape
-    out = jax.ShapeDtypeStruct((STEPS * rows, width), BF16)
     return pl.pallas_call(
         functools.partial(prepare_kernel, n_dp),
-        out_shape=out,
-        in_specs=spaces(4),
-        out_specs=pl.BlockSpec(memory_space=pltpu.VMEM),
+        out_shape=(
+            jax.ShapeDtypeStruct((STEPS * rows, width), BF16),
+            jax.ShapeDtypeStruct((8, 128), F32),
+        ),
+        in_specs=spaces(6),
+        out_specs=tuple(spaces(2)),
         compiler_params=params(),
         cost_estimate=cost(),
         name="prepare",
-    )(t0, twin0, twin2, t2)
-
-
-def turn_kernel(x, _, x_t):
+    )(t0, twin0, twin2, t2, sharp, bias)
+
+
+def turn_kernel(x, x_t):
     x_t[...] = x[...].T
 
 
-def turned(x, after):
+def turned(x):
     out = jax.ShapeDtypeStruct(x.shape[::-1], BF16)
     return pl.pallas_call(
         turn_kernel,
         out_shape=out,
-        in_specs=spaces(2),
+        in_specs=spaces(1),
         out_specs=pl.BlockSpec(memory_space=pltpu.VMEM),
         compiler_params=params(),
         cost_estimate=cost(),
         name="turned",
-    )(x, after)
+    )(x)
 
 
 def rows_of(ref, block, depth):
     return ref[pl.ds(pl.multiple_of(block * depth, 16), depth), :]
 
 
-def picture_kernel(n_dp, x, x_t, units, sharp, bias, own, *rest):
+def picture_kernel(n_dp, x, x_t, units, scalars, own, *rest):
     pieces, outs = rest[:8], rest[8 : 8 + len(SHARES)]
     unit_parts = rest[8 + len(SHARES) : -5]
     grad, unit, w, proj, sem = rest[-5:]
@@ -167,10 +171,10 @@
     size = unit.shape[1] // UNIT_PARTS
     for k, out in enumerate(unit_parts):
         out[...] = unit[:, k * size : (k + 1) * size]
-    scale = sharp[...]
+    scale = scalars[0:1, 0:1]
     logits = scale * lax.dot_general(
         unit[...], units[...], (((1,), (1,)), ((), ())), preferred_element_type=F32
-    ) + bias[...]
+    ) + scalars[1:2, 0:1]
     coefficient = jax.nn.sigmoid(logits)
     row = lax.broadcasted_iota(jnp.int32, coefficient.shape, 0)
     column = lax.broadcasted_iota(jnp.int32, coefficient.shape, 1)
@@ -200,7 +204,7 @@
             begin = stop
 
 
-def picture_side(n_dp, x, x_t, units, sharp, bias, own, pieces):
+def picture_side(n_dp, x, x_t, units, scalars, own, pieces):
     rows, width = x.shape
     depth = own.shape[0]
     out = jax.ShapeDtypeStruct((rows, width), BF16)
@@ -211,7 +215,7 @@
     return pl.pallas_call(
         functools.partial(picture_kernel, n_dp),
         out_shape=outs,
-        in_specs=spaces(3) + spaces(2) + [pl.BlockSpec(memory_space=pl.ANY)] * 9,
+        in_specs=spaces(4) + [pl.BlockSpec(memory_space=pl.ANY)] * 9,
         out_specs=spaces(len(outs)),
         scratch_shapes=[
             pltpu.VMEM((rows, width), BF16),
@@ -222,10 +226,10 @@
         compiler_params=params(),
         cost_estimate=cost(),
         name="picture_side",
-    )(x, x_t, units, sharp, bias, own, *pieces)
-
-
-def text_kernel(n_dp, text, sharp, bias, *refs):
+    )(x, x_t, units, scalars, own, *pieces)
+
+
+def text_kernel(n_dp, text, scalars, *refs):
     blocks, (out, done, units) = refs[:-3], refs[-3:]
     rows = text.shape[0]
     _, core, _ = place(n_dp)
@@ -245,10 +249,10 @@
     values = text[...].astype(F32)
     inverse = 1.0 / jnp.sqrt(jnp.sum(values * values, axis=-1, keepdims=True) + EPS)
     direction = values * inverse
-    scale = sharp[...]
+    scale = scalars[0:1, 0:1]
     logits = scale * lax.dot_general(
         direction.astype(BF16), units[...], (((1,), (1,)), ((), ())), preferred_element_type=F32
-    ) + bias[...]
+    ) + scalars[1:2, 0:1]
     coefficient = jax.nn.sigmoid(logits)
     row = lax.broadcasted_iota(jnp.int32, coefficient.shape, 0)
     column = lax.broadcasted_iota(jnp.int32, coefficient.shape, 1)
@@ -258,18 +262,18 @@
     out[...] = (slope - direction * along) * inverse
 
 
-def text_side(n_dp, text, sharp, bias, *units):
+def text_side(n_dp, text, scalars, *units):
     rows, width = text.shape
     return pl.pallas_call(
         functools.partial(text_kernel, n_dp),
         out_shape=(jax.ShapeDtypeStruct((rows, width), F32), jax.ShapeDtypeStruct((8, 128), F32)),
-        in_specs=spaces(3 + 4 * UNIT_PARTS),
+        in_specs=spaces(2 + 4 * UNIT_PARTS),
         out_specs=tuple(spaces(2)),
         scratch_shapes=[pltpu.VMEM((STEPS * rows, width), BF16)],
         compiler_params=params(),
         cost_estimate=cost(),
         name="text_side",
-    )(text, sharp, bias, *units)
+    )(text, scalars, *units)
 
 
 def pair_kernel(begin, x_t, far_t, grad, arrived, *rest):
@@ -355,6 +359,7 @@
         return lax.ppermute(value, "dp", [(d, (d + by) % n_dp) for d in range(n_dp)])
 
     sharp, bias = sharp.reshape(1, 1), bias.reshape(1, 1)
+    swap = [(0, 1), (1, 0), (2, 3), (3, 2)]
     whole, piece = cut(n_dp, short, w)
     whole, piece, text = lax.optimization_barrier((whole, piece, text))
     turns = [
@@ -364,33 +369,40 @@
     ]
     straight = lax.ppermute(whole, ("dp", "fsdp"), turns)
     text2 = shifted(text, 2)
+    piece, straight = lax.optimization_barrier((piece, straight))
+    crossed = over(straight)
     two = along(piece, [(f, (f + 2) % n_fsdp) for f in range(n_fsdp)])
-    text2, two = lax.optimization_barrier((text2, two))
-    crossed = over(straight)
+    two, x = lax.optimization_barrier((two, x))
     two_crossed = over(two)
+    far_x = along(x, swap)
+    x_t = turned(x)
+    crossed, x_t, text2 = lax.optimization_barrier((crossed, x_t, text2))
+    units, scalars = prepare(n_dp, text, across(text), across(text2), text2, sharp, bias)
+    two_crossed, units, scalars = lax.optimization_barrier((two_crossed, units, scalars))
     pieces = [straight, crossed, two, two_crossed]
     pieces = pieces + [across(piece) for piece in pieces]
-    x_t = turned(x, text2)
-    far_t = along(x_t, [(0, 1), (3, 2)])
-    units = prepare(n_dp, text, across(text), across(text2), text2)
-    results = picture_side(n_dp, x, x_t, units, sharp, bias, w, pieces)
-    outward, unit, grad = results[: len(SHARES)], results[len(SHARES) : -1], results[-1]
+    results = picture_side(n_dp, x, x_t, units, scalars, w, pieces)
+    outward, unit, grad = list(results[: len(SHARES)]), results[len(SHARES) : -1], results[-1]
+    grad, far_x = lax.optimization_barrier((grad, far_x))
+    far_t = turned(far_x)
+    outward[0], far_t = lax.optimization_barrier((outward[0], far_t))
 
     arrived = []
     for block in outward:
         if arrived:
             block, arrived[-1] = lax.optimization_barrier((block, arrived[-1]))
-        arrived.append(along(block, [(0, 1), (1, 0), (2, 3), (3, 2)]))
+        arrived.append(along(block, swap))
     unit2 = [shifted(u, -2) for u in unit]
     begin, terms, after = 0, [], []
     for block in arrived:
         kept, near, far = pair_product(begin, x_t, far_t, grad, block, after)
-        near, far = along(near, [(1, 2), (2, 1)]), along(far, [(1, 3), (2, 0)])
+        near = along(near, [(1, 2), (2, 1), (0, 0), (3, 3)])
+        far = along(far, [(1, 3), (2, 0), (0, 1), (3, 2)])
         after = [near, far]
         terms.append((begin, width, kept, near, far))
         begin += block.shape[1]
     twin0, twin2 = [across(u) for u in unit], [across(u) for u in unit2]
-    text_grad, done = text_side(n_dp, text, sharp, bias, *unit, *twin0, *twin2, *unit2)
+    text_grad, done = text_side(n_dp, text, scalars, *unit, *twin0, *twin2, *unit2)
     head = total(*terms[0], [])
     for term in terms[1:]:
         head = total(*term, [head, done])

time: 95.9 us -> 93.3 us (0.973)
  starting transfers between devices: 24 us -> 21.3 us
  Pallas kernels: 11.1 us -> 13.5 us
  local copies, waits for them, and re-layouts: 2.69 us -> 1.1 us
    ppermute x8, waiting for transfers between devices: 40 us -> 28.4 us  [along(): return lax.ppermute(value, 'fsdp', pairs)]
    ppermute x1, waiting for transfers between devices: 0.01 us -> 8.33 us  [line_body(): straight = lax.ppermute(whole, ('dp', 'fsdp'), turns)]
    ppermute x4, waiting for transfers between devices: 5.1 us -> 9.98 us  [shifted(): lax.ppermute(value, 'dp', [(d, (d + by) % n_dp) for d in range(n_dp)])]
    ppermute x2, waiting for transfers between devices: 9.27 us -> 5.4 us  [over(): lax.ppermute(value, 'dp', [(d, (d + side) % n_dp) for d in range(n_dp)])]
    ppermute x4, starting transfers between devices: 8.05 us -> 4.4 us  [shifted(): lax.ppermute(value, 'dp', [(d, (d + by) % n_dp) for d in range(n_dp)])]
    ppermute x12, waiting for transfers between devices: 1.23 us -> 2.86 us  [across(): return lax.ppermute(value, 'dp', [(d, d ^ 1) for d in range(n_dp)])]
    unnamed x10 -> x6, local copies, waits for them, and re-layouts: 2.69 us -> 1.1 us
    ppermute x1, starting transfers between devices: 1.58 us -> 3.08 us  [line_body(): straight = lax.ppermute(whole, ('dp', 'fsdp'), turns)]
  transfers between devices with their start and end apart: 27 -> 27, of which waited for: 10 -> 14; matrix products, arithmetic and copies ran while one was open for 0% -> 0% of each run, Pallas kernels for 10% -> 13%
where the time goes in v5:
time: 93.3 us; the launch traced here: 93 us
  waiting for transfers between devices  55 us (59%)
  starting transfers between devices  21.3 us (23%)
  Pallas kernels  13.5 us (14%)
  between operations  2.09 us (2%)
  local copies, waits for them, and re-layouts  1.1 us (1%)
    ppermute x8, waiting for transfers between devices, along(): return lax.ppermute(value, 'fsdp', pairs)  28.4 us
    ppermute x8, starting transfers between devices, along(): return lax.ppermute(value, 'fsdp', pairs)  10 us
    ppermute x4, waiting for transfers between devices, shifted(): lax.ppermute(value, 'dp', [(d, (d + by) % n_dp) for d in range(n_dp)])  9.98 us
    ppermute x1, waiting for transfers between devices, line_body(): straight = lax.ppermute(whole, ('dp', 'fsdp'), turns)  8.33 us
    pallas_call x1, Pallas kernels, picture_side(): pl.pallas_call(functools.partial(picture_kernel, n_dp), out_shape=outs, i...  5.58 us
    ppermute x2, waiting for transfers between devices, over(): lax.ppermute(value, 'dp', [(d, (d + side) % n_dp) for d in range(n_dp)])  5.4 us
    ppermute x4, starting transfers between devices, shifted(): lax.ppermute(value, 'dp', [(d, (d + by) % n_dp) for d in range(n_dp)])  4.4 us
    ppermute x1, starting transfers between devices, line_body(): straight = lax.ppermute(whole, ('dp', 'fsdp'), turns)  3.08 us
  transfers between devices with their start and end apart: 27, of which 14 were waited for; matrix products, arithmetic and copies ran while one was open for 0% of the time, Pallas kernels for 13%

profile of v5, /device:TPU:0, one launch (start us, length us, event | category | flops | bytes accessed | tf_op | source)
XLA Modules:
  0.0 93.0 jit_solution(13492153511256931841)
XLA Ops:
  0.6 1.1 %copy-done = bf16[288,1152]{1,0:T(8,128)(2,1)S(1)} copy-done((bf16[288,1152]{1,0:T(8,128)(2,1)S(1)}, bf16[288,1152]{1,0:T(8,128)(2,1)}, u32[]{:S(2)}) %copy-start) | copy-done | bytes 663576
  2.1 3.1 %collective-permute-start = (bf16[144,1152]{1,0:T(8,128)(2,1)S(1)}, bf16[144,1152]{1,0:T(8,128)(2,1)S(1)}, u32[]{:S(2)}, u32[]{:S(2)}) collective-permute-start(bf16[144,1152]{1,0:T(8,128)(2,1)S(1)} %get-tuple-element.42), channel_id=1, source_target_pairs={{0,1},{1,2},{2,3},{3,0},{4,5},{5,6},{6,7},{7,4},{8,9},{9,10},{10,1... | collective-permute-start | bytes 995336 | tf_op jit(solution)/shard_map/ppermute | solution.py:370
  5.2 1.5 %collective-permute-start.3 = (bf16[256,1152]{1,0:T(8,128)(2,1)}, bf16[256,1152]{1,0:T(8,128)(2,1)S(1)}, u32[]{:S(2)}, u32[]{:S(2)}) collective-permute-start(bf16[256,1152]{1,0:T(8,128)(2,1)} %text), channel_id=1, source_target_pairs={{0,8},{4,12},{8,16},{12,20},{16,24},{20,28},{24,0},{28,4},{1,9},{5... | collective-permute-start | bytes 1769480 | tf_op jit(solution)/shard_map/ppermute | solution.py:359
  6.7 8.3 %collective-permute-done.rest_0_ = bf16[144,1152]{1,0:T(8,128)(2,1)S(1)} collective-permute-done((bf16[144,1152]{1,0:T(8,128)(2,1)S(1)}, bf16[144,1152]{1,0:T(8,128)(2,1)S(1)}, u32[]{:S(2)}, u32[]{:S(2)}) %collective-permute-start) | collective-permute-done | bytes 331808 | tf_op jit(solution)/shard_map/ppermute | solution.py:370
  15.0 0.8 collective-permute-start.1
  15.8 1.5 %collective-permute-start.2 = (bf16[80,1152]{1,0:T(8,128)(2,1)S(1)}, bf16[80,1152]{1,0:T(8,128)(2,1)S(1)}, u32[]{:S(2)}, u32[]{:S(2)}) collective-permute-start(bf16[80,1152]{1,0:T(8,128)(2,1)S(1)} %get-tuple-element.44), channel_id=1, source_target_pairs={{0,2},{1,3},{2,0},{3,1},{4,6},{5,7},{6,4},{7,5},{8,10},{9,11},{10,... | collective-permute-start | bytes 552968 | tf_op jit(solution)/shard_map/ppermute | solution.py:350
  17.2 8.6 %collective-permute-done.2.rest_2_ = bf16[80,1152]{1,0:T(8,128)(2,1)S(1)} collective-permute-done((bf16[80,1152]{1,0:T(8,128)(2,1)S(1)}, bf16[80,1152]{1,0:T(8,128)(2,1)S(1)}, u32[]{:S(2)}, u32[]{:S(2)}) %collective-permute-start.2) | collective-permute-done | bytes 184352 | tf_op jit(solution)/shard_map/ppermute | solution.py:350
  25.8 1.3 %turned.2.x_t = bf16[1152,256]{1,0:T(8,128)(2,1)S(1)} custom-call(bf16[256,1152]{1,0:T(8,128)(2,1)} %x.1), custom_call_target="tpu_custom_call" | custom-call | tf_op jit(solution)/shard_map/turned/pallas_call | solution.py:109
  27.1 2.9 %collective-permute-done.1.rest_1_ = bf16[144,1152]{1,0:T(8,128)(2,1)S(1)} collective-permute-done((bf16[144,1152]{1,0:T(8,128)(2,1)S(1)}, bf16[144,1152]{1,0:T(8,128)(2,1)S(1)}, u32[]{:S(2)}, u32[]{:S(2)}) %collective-permute-start.1) | collective-permute-done | bytes 331808 | tf_op jit(solution)/shard_map/ppermute | solution.py:356
  30.0 1.7 %collective-permute-start.4 = (bf16[80,1152]{1,0:T(8,128)(2,1)S(1)}, bf16[80,1152]{1,0:T(8,128)(2,1)S(1)}, u32[]{:S(2)}, u32[]{:S(2)}) collective-permute-start(bf16[80,1152]{1,0:T(8,128)(2,1)S(1)} %collective-permute-done.2.rest_2_), channel_id=1, source_target_pairs={{0,16},{4,20},{8,24},{12,28},{16,0},{20,4},{24,8},{28,12},{1,17},{... | collective-permute-start | bytes 552968 | tf_op jit(solution)/shard_map/ppermute | solution.py:356
  33.8 0.7 prepare.1
  34.5 2.5 %collective-permute-done.4.rest_3_ = bf16[80,1152]{1,0:T(8,128)(2,1)S(1)} collective-permute-done((bf16[80,1152]{1,0:T(8,128)(2,1)S(1)}, bf16[80,1152]{1,0:T(8,128)(2,1)S(1)}, u32[]{:S(2)}, u32[]{:S(2)}) %collective-permute-start.4) | collective-permute-done | bytes 184352 | tf_op jit(solution)/shard_map/ppermute | solution.py:356
  37.1 1.4 %collective-permute-done.10.rest_7_ = bf16[80,1152]{1,0:T(8,128)(2,1)S(1)} collective-permute-done((bf16[80,1152]{1,0:T(8,128)(2,1)S(1)}, bf16[80,1152]{1,0:T(8,128)(2,1)S(1)}, u32[]{:S(2)}, u32[]{:S(2)}) %collective-permute-start.10) | collective-permute-done | bytes 184352 | tf_op jit(solution)/shard_map/ppermute | solution.py:353
  38.5 5.6 %picture_side.1 = (bf16[288,384]{1,0:T(8,128)(2,1)S(1)}, bf16[288,768]{1,0:T(8,128)(2,1)S(1)}, bf16[256,384]{1,0:T(8,128)(2,1)S(1)}, bf16[256,384]{1,0:T(8,128)(...) custom-call(bf16[256,1152]{1,0:T(8,128)(2,1)} %x.1, bf16[1152,256]{1,0:T(8,128)(2,1)S(1)} %turned.2.x_t, ...), custom_call_target="tpu_custom_call" | custom-call | tf_op jit(solution)/shard_map/picture_side/pallas_call | solution.py:215
  44.1 1.9 %collective-permute-done.11.x = bf16[256,1152]{1,0:T(8,128)(2,1)S(1)} collective-permute-done((bf16[256,1152]{1,0:T(8,128)(2,1)}, bf16[256,1152]{1,0:T(8,128)(2,1)S(1)}, u32[]{:S(2)}, u32[]{:S(2)}) %collective-permute-start.11) | collective-permute-done | bytes 589856 | tf_op jit(solution)/shard_map/ppermute | solution.py:350
  46.5 6.8 %collective-permute-done.12.arrived = bf16[288,384]{1,0:T(8,128)(2,1)S(1)} collective-permute-done((bf16[288,384]{1,0:T(8,128)(2,1)S(1)}, bf16[288,384]{1,0:T(8,128)(2,1)S(1)}, u32[]{:S(2)}, u32[]{:S(2)}) %collective-permute-start.12) | collective-permute-done | bytes 221216 | tf_op jit(solution)/shard_map/ppermute | solution.py:350
  53.3 0.6 collective-permute-start.13
  54.2 0.7 collective-permute-start.14
  54.9 3.1 %collective-permute-start.15 = (bf16[288,384]{1,0:T(8,128)(2,1)S(1)}, bf16[288,384]{1,0:T(8,128)(2,1)S(1)}, u32[]{:S(2)}, u32[]{:S(2)}) collective-permute-start(bf16[288,384]{1,0:T(8,128)(2,1)S(1)} %get-tuple-element.66), channel_id=1, source_target_pairs={{1,3},{2,0},{0,1},{3,2},{5,7},{6,4},{4,5},{7,6},{9,11},{10,8},{8,9... | collective-permute-start | bytes 663560 | tf_op jit(solution)/shard_map/ppermute | solution.py:350
  58.5 9.5 %collective-permute-done.15.rest_1_.far = bf16[288,384]{1,0:T(8,128)(2,1)S(1)} collective-permute-done((bf16[288,384]{1,0:T(8,128)(2,1)S(1)}, bf16[288,384]{1,0:T(8,128)(2,1)S(1)}, u32[]{:S(2)}, u32[]{:S(2)}) %collective-permute-start.15) | collective-permute-done | bytes 221216 | tf_op jit(solution)/shard_map/ppermute | solution.py:350
  68.0 1.0 %collective-permute-done.13.arrived = bf16[288,768]{1,0:T(8,128)(2,1)S(1)} collective-permute-done((bf16[288,768]{1,0:T(8,128)(2,1)S(1)}, bf16[288,768]{1,0:T(8,128)(2,1)S(1)}, u32[]{:S(2)}, u32[]{:S(2)}) %collective-permute-start.13) | collective-permute-done | bytes 442400 | tf_op jit(solution)/shard_map/ppermute | solution.py:350
  69.3 0.7 collective-permute-start.16
  70.0 3.2 %collective-permute-start.17 = (bf16[288,768]{1,0:T(8,128)(2,1)S(1)}, bf16[288,768]{1,0:T(8,128)(2,1)S(1)}, u32[]{:S(2)}, u32[]{:S(2)}) collective-permute-start(bf16[288,768]{1,0:T(8,128)(2,1)S(1)} %get-tuple-element.69), channel_id=1, source_target_pairs={{1,3},{2,0},{0,1},{3,2},{5,7},{6,4},{4,5},{7,6},{9,11},{10,8},{8,9... | collective-permute-start | bytes 1327112 | tf_op jit(solution)/shard_map/ppermute | solution.py:350
  73.1 2.8 %collective-permute-start.23 = (bf16[256,384]{1,0:T(8,128)(2,1)S(1)}, bf16[256,384]{1,0:T(8,128)(2,1)S(1)}, u32[]{:S(2)}, u32[]{:S(2)}) collective-permute-start(bf16[256,384]{1,0:T(8,128)(2,1)S(1)} %get-tuple-element.72.refs_1_), channel_id=1, source_target_pairs={{0,24},{4,28},{8,0},{12,4},{16,8},{20,12},{24,16},{28,20},{1,25},{... | collective-permute-start | bytes 589832 | tf_op jit(solution)/shard_map/ppermute | solution.py:359
  76.0 4.9 %collective-permute-done.21.refs_9_ = bf16[256,384]{1,0:T(8,128)(2,1)S(1)} collective-permute-done((bf16[256,384]{1,0:T(8,128)(2,1)S(1)}, bf16[256,384]{1,0:T(8,128)(2,1)S(1)}, u32[]{:S(2)}, u32[]{:S(2)}) %collective-permute-start.21) | collective-permute-done | bytes 196640 | tf_op jit(solution)/shard_map/ppermute | solution.py:359
  81.0 3.0 %collective-permute-done.23.refs_10_ = bf16[256,384]{1,0:T(8,128)(2,1)S(1)} collective-permute-done((bf16[256,384]{1,0:T(8,128)(2,1)S(1)}, bf16[256,384]{1,0:T(8,128)(2,1)S(1)}, u32[]{:S(2)}, u32[]{:S(2)}) %collective-permute-start.23) | collective-permute-done | bytes 196640 | tf_op jit(solution)/shard_map/ppermute | solution.py:359
  83.9 2.1 %collective-permute-done.25.refs_11_ = bf16[256,384]{1,0:T(8,128)(2,1)S(1)} collective-permute-done((bf16[256,384]{1,0:T(8,128)(2,1)S(1)}, bf16[256,384]{1,0:T(8,128)(2,1)S(1)}, u32[]{:S(2)}, u32[]{:S(2)}) %collective-permute-start.25) | collective-permute-done | bytes 196640 | tf_op jit(solution)/shard_map/ppermute | solution.py:359
  86.0 1.4 %collective-permute-done.26.refs_8_ = bf16[256,384]{1,0:T(8,128)(2,1)S(1)} collective-permute-done((bf16[256,384]{1,0:T(8,128)(2,1)S(1)}, bf16[256,384]{1,0:T(8,128)(2,1)S(1)}, u32[]{:S(2)}, u32[]{:S(2)}) %collective-permute-start.26) | collective-permute-done | bytes 196640 | tf_op jit(solution)/shard_map/ppermute | solution.py:353
  87.5 2.9 %text_side.1 = (f32[256,1152]{1,0:T(8,128)}, f32[8,128]{1,0:T(8,128)S(1)}) custom-call(bf16[256,1152]{1,0:T(8,128)(2,1)S(1)} %copy-done.2, f32[8,128]{1,0:T(8,128)S(1)} %get-tuple-element.53.scalars, bf16[256,384]{1,0:T(8,128)(2,1)S(1)} %get-tuple-element.71.refs_0_, bf16[256,384]{1,0:T(8,128)(2,1)S(1)} %get-tuple-element.72.refs_1_, ...), custom_call_target="tpu_custom_call" | custom-call | tf_op jit(solution)/shard_map/text_side/pallas_call | solution.py:267
  90.4 0.8 total.2.rest_0_
  91.3 0.7 collective-permute-done.17.far
  92.0 1.1 %total.3 = f32[1,288,1152]{2,1,0:T(8,128)} custom-call(f32[288,768]{1,0:T(8,128)S(1)} %get-tuple-element.67.kept, bf16[288,768]{1,0:T(8,128)(2,1)S(1)} %collective-permute-done.16.near, bf16[288,768]{1,0:T(8,128)(2,1)S(1)} %collective-permute-done.17.far, f32[1,288,1152]{2,1,0:T(8,128)} %total.2.rest_0_, ...), custom_call_target="tpu_custom_call", output_to_operand_aliasing={{}: (3, {})} | custom-call | tf_op jit(solution)/shard_map/total/pallas_call | solution.py:329
  (38 shorter events, 2.9 us)
Async XLA Ops:
  0.6 1.1 %copy-start = (bf16[288,1152]{1,0:T(8,128)(2,1)S(1)}, bf16[288,1152]{1,0:T(8,128)(2,1)}, u32[]{:S(2)}) copy-start(bf16[288,1152]{1,0:T(8,128)(2,1)} %own.3) | copy-start | bytes 1990660
  1.7 32.1 %copy-start.2 = (bf16[256,1152]{1,0:T(8,128)(2,1)S(1)}, bf16[256,1152]{1,0:T(8,128)(2,1)}, u32[]{:S(2)}) copy-start(bf16[256,1152]{1,0:T(8,128)(2,1)} %text) | copy-start | bytes 1769476
  2.1 12.9 %collective-permute-start = (bf16[144,1152]{1,0:T(8,128)(2,1)S(1)}, bf16[144,1152]{1,0:T(8,128)(2,1)S(1)}, u32[]{:S(2)}, u32[]{:S(2)}) collective-permute-start(bf16[144,1152]{1,0:T(8,128)(2,1)S(1)} %get-tuple-element.42), channel_id=1, source_target_pairs={{0,1},{1,2},{2,3},{3,0},{4,5},{5,6},{6,7},{7,4},{8,9},{9,10},{10,1... | collective-permute-start | bytes 995336 | tf_op jit(solution)/shard_map/ppermute | solution.py:370
  5.2 22.0 %collective-permute-start.3 = (bf16[256,1152]{1,0:T(8,128)(2,1)}, bf16[256,1152]{1,0:T(8,128)(2,1)S(1)}, u32[]{:S(2)}, u32[]{:S(2)}) collective-permute-start(bf16[256,1152]{1,0:T(8,128)(2,1)} %text), channel_id=1, source_target_pairs={{0,8},{4,12},{8,16},{12,20},{16,24},{20,28},{24,0},{28,4},{1,9},{5... | collective-permute-start | bytes 1769480 | tf_op jit(solution)/shard_map/ppermute | solution.py:359
  15.0 15.0 %collective-permute-start.1 = (bf16[144,1152]{1,0:T(8,128)(2,1)S(1)}, bf16[144,1152]{1,0:T(8,128)(2,1)S(1)}, u32[]{:S(2)}, u32[]{:S(2)}) collective-permute-start(bf16[144,1152]{1,0:T(8,128)(2,1)S(1)} %collective-permute-done.rest_0_), channel_id=1, source_target_pairs={{0,16},{4,20},{8,24},{12,28},{16,0},{20,4},{24,8},{28,12},{1,17},{... | collective-permute-start | bytes 995336 | tf_op jit(solution)/shard_map/ppermute | solution.py:356
  15.8 10.1 %collective-permute-start.2 = (bf16[80,1152]{1,0:T(8,128)(2,1)S(1)}, bf16[80,1152]{1,0:T(8,128)(2,1)S(1)}, u32[]{:S(2)}, u32[]{:S(2)}) collective-permute-start(bf16[80,1152]{1,0:T(8,128)(2,1)S(1)} %get-tuple-element.44), channel_id=1, source_target_pairs={{0,2},{1,3},{2,0},{3,1},{4,6},{5,7},{6,4},{7,5},{8,10},{9,11},{10,... | collective-permute-start | bytes 552968 | tf_op jit(solution)/shard_map/ppermute | solution.py:350
  17.2 14.7 %collective-permute-start.5 = (bf16[256,1152]{1,0:T(8,128)(2,1)}, bf16[256,1152]{1,0:T(8,128)(2,1)S(1)}, u32[]{:S(2)}, u32[]{:S(2)}) collective-permute-start(bf16[256,1152]{1,0:T(8,128)(2,1)} %text), channel_id=1, source_target_pairs={{0,4},{4,0},{8,12},{12,8},{16,20},{20,16},{24,28},{28,24},{1,5},{5... | collective-permute-start | bytes 1769480 | tf_op jit(solution)/shard_map/ppermute | solution.py:353
  27.1 11.4 %copy-start.1 = (bf16[288,1152]{1,0:T(8,128)(2,1)S(1)}, bf16[288,1152]{1,0:T(8,128)(2,1)}, u32[]{:S(2)}) copy-start(bf16[288,1152]{1,0:T(8,128)(2,1)} %own.3) | copy-start | bytes 1990660
  30.0 3.6 %collective-permute-start.6 = (bf16[256,1152]{1,0:T(8,128)(2,1)S(1)}, bf16[256,1152]{1,0:T(8,128)(2,1)S(1)}, u32[]{:S(2)}, u32[]{:S(2)}) collective-permute-start(bf16[256,1152]{1,0:T(8,128)(2,1)S(1)} %collective-permute-done.3.t2), channel_id=1, source_target_pairs={{0,4},{4,0},{8,12},{12,8},{16,20},{20,16},{24,28},{28,24},{1,5},{5... | collective-permute-start | bytes 1769480 | tf_op jit(solution)/shard_map/ppermute | solution.py:353
  30.0 15.9 %collective-permute-start.11 = (bf16[256,1152]{1,0:T(8,128)(2,1)}, bf16[256,1152]{1,0:T(8,128)(2,1)S(1)}, u32[]{:S(2)}, u32[]{:S(2)}) collective-permute-start(bf16[256,1152]{1,0:T(8,128)(2,1)} %x.1), channel_id=1, source_target_pairs={{0,1},{1,0},{2,3},{3,2},{4,5},{5,4},{6,7},{7,6},{8,9},{9,8},{10,11... | collective-permute-start | bytes 1769480 | tf_op jit(solution)/shard_map/ppermute | solution.py:350
  30.0 7.0 %collective-permute-start.4 = (bf16[80,1152]{1,0:T(8,128)(2,1)S(1)}, bf16[80,1152]{1,0:T(8,128)(2,1)S(1)}, u32[]{:S(2)}, u32[]{:S(2)}) collective-permute-start(bf16[80,1152]{1,0:T(8,128)(2,1)S(1)} %collective-permute-done.2.rest_2_), channel_id=1, source_target_pairs={{0,16},{4,20},{8,24},{12,28},{16,0},{20,4},{24,8},{28,12},{1,17},{... | collective-permute-start | bytes 552968 | tf_op jit(solution)/shard_map/ppermute | solution.py:356
  31.7 5.3 %collective-permute-start.7 = (bf16[144,1152]{1,0:T(8,128)(2,1)S(1)}, bf16[144,1152]{1,0:T(8,128)(2,1)S(1)}, u32[]{:S(2)}, u32[]{:S(2)}) collective-permute-start(bf16[144,1152]{1,0:T(8,128)(2,1)S(1)} %collective-permute-done.rest_0_), channel_id=1, source_target_pairs={{0,4},{4,0},{8,12},{12,8},{16,20},{20,16},{24,28},{28,24},{1,5},{5... | collective-permute-start | bytes 995336 | tf_op jit(solution)/shard_map/ppermute | solution.py:353
  32.0 5.1 %collective-permute-start.8 = (bf16[144,1152]{1,0:T(8,128)(2,1)S(1)}, bf16[144,1152]{1,0:T(8,128)(2,1)S(1)}, u32[]{:S(2)}, u32[]{:S(2)}) collective-permute-start(bf16[144,1152]{1,0:T(8,128)(2,1)S(1)} %collective-permute-done.1.rest_1_), channel_id=1, source_target_pairs={{0,4},{4,0},{8,12},{12,8},{16,20},{20,16},{24,28},{28,24},{1,5},{5... | collective-permute-start | bytes 995336 | tf_op jit(solution)/shard_map/ppermute | solution.py:353
  33.6 3.5 %collective-permute-start.9 = (bf16[80,1152]{1,0:T(8,128)(2,1)S(1)}, bf16[80,1152]{1,0:T(8,128)(2,1)S(1)}, u32[]{:S(2)}, u32[]{:S(2)}) collective-permute-start(bf16[80,1152]{1,0:T(8,128)(2,1)S(1)} %collective-permute-done.2.rest_2_), channel_id=1, source_target_pairs={{0,4},{4,0},{8,12},{12,8},{16,20},{20,16},{24,28},{28,24},{1,5},{5... | collective-permute-start | bytes 552968 | tf_op jit(solution)/shard_map/ppermute | solution.py:353
  37.1 1.4 %collective-permute-start.10 = (bf16[80,1152]{1,0:T(8,128)(2,1)S(1)}, bf16[80,1152]{1,0:T(8,128)(2,1)S(1)}, u32[]{:S(2)}, u32[]{:S(2)}) collective-permute-start(bf16[80,1152]{1,0:T(8,128)(2,1)S(1)} %collective-permute-done.4.rest_3_), channel_id=1, source_target_pairs={{0,4},{4,0},{8,12},{12,8},{16,20},{20,16},{24,28},{28,24},{1,5},{5... | collective-permute-start | bytes 552968 | tf_op jit(solution)/shard_map/ppermute | solution.py:353
  46.2 7.1 %collective-permute-start.12 = (bf16[288,384]{1,0:T(8,128)(2,1)S(1)}, bf16[288,384]{1,0:T(8,128)(2,1)S(1)}, u32[]{:S(2)}, u32[]{:S(2)}) collective-permute-start(bf16[288,384]{1,0:T(8,128)(2,1)S(1)} %get-tuple-element.62), channel_id=1, source_target_pairs={{0,1},{1,0},{2,3},{3,2},{4,5},{5,4},{6,7},{7,6},{8,9},{9,8},{10,11... | collective-permute-start | bytes 663560 | tf_op jit(solution)/shard_map/ppermute | solution.py:350
  53.3 15.6 %collective-permute-start.13 = (bf16[288,768]{1,0:T(8,128)(2,1)S(1)}, bf16[288,768]{1,0:T(8,128)(2,1)S(1)}, u32[]{:S(2)}, u32[]{:S(2)}) collective-permute-start(bf16[288,768]{1,0:T(8,128)(2,1)S(1)} %get-tuple-element.63), channel_id=1, source_target_pairs={{0,1},{1,0},{2,3},{3,2},{4,5},{5,4},{6,7},{7,6},{8,9},{9,8},{10,11... | collective-permute-start | bytes 1327112 | tf_op jit(solution)/shard_map/ppermute | solution.py:350
  54.2 4.3 %collective-permute-start.14 = (bf16[288,384]{1,0:T(8,128)(2,1)S(1)}, bf16[288,384]{1,0:T(8,128)(2,1)S(1)}, u32[]{:S(2)}, u32[]{:S(2)}) collective-permute-start(bf16[288,384]{1,0:T(8,128)(2,1)S(1)} %get-tuple-element.65), channel_id=1, source_target_pairs={{1,2},{2,1},{0,0},{3,3},{5,6},{6,5},{4,4},{7,7},{9,10},{10,9},{8,8... | collective-permute-start | bytes 663560 | tf_op jit(solution)/shard_map/ppermute | solution.py:350
  54.9 13.1 %collective-permute-start.15 = (bf16[288,384]{1,0:T(8,128)(2,1)S(1)}, bf16[288,384]{1,0:T(8,128)(2,1)S(1)}, u32[]{:S(2)}, u32[]{:S(2)}) collective-permute-start(bf16[288,384]{1,0:T(8,128)(2,1)S(1)} %get-tuple-element.66), channel_id=1, source_target_pairs={{1,3},{2,0},{0,1},{3,2},{5,7},{6,4},{4,5},{7,6},{9,11},{10,8},{8,9... | collective-permute-start | bytes 663560 | tf_op jit(solution)/shard_map/ppermute | solution.py:350
  57.9 15.2 %collective-permute-start.18 = (bf16[256,384]{1,0:T(8,128)(2,1)S(1)}, bf16[256,384]{1,0:T(8,128)(2,1)S(1)}, u32[]{:S(2)}, u32[]{:S(2)}) collective-permute-start(bf16[256,384]{1,0:T(8,128)(2,1)S(1)} %get-tuple-element.71.refs_0_), channel_id=1, source_target_pairs={{0,4},{4,0},{8,12},{12,8},{16,20},{20,16},{24,28},{28,24},{1,5},{5... | collective-permute-start | bytes 589832 | tf_op jit(solution)/shard_map/ppermute | solution.py:353
  57.9 15.2 %collective-permute-start.19 = (bf16[256,384]{1,0:T(8,128)(2,1)S(1)}, bf16[256,384]{1,0:T(8,128)(2,1)S(1)}, u32[]{:S(2)}, u32[]{:S(2)}) collective-permute-start(bf16[256,384]{1,0:T(8,128)(2,1)S(1)} %get-tuple-element.72.refs_1_), channel_id=1, source_target_pairs={{0,4},{4,0},{8,12},{12,8},{16,20},{20,16},{24,28},{28,24},{1,5},{5... | collective-permute-start | bytes 589832 | tf_op jit(solution)/shard_map/ppermute | solution.py:353
  58.5 17.5 %collective-permute-start.20 = (bf16[256,384]{1,0:T(8,128)(2,1)S(1)}, bf16[256,384]{1,0:T(8,128)(2,1)S(1)}, u32[]{:S(2)}, u32[]{:S(2)}) collective-permute-start(bf16[256,384]{1,0:T(8,128)(2,1)S(1)} %get-tuple-element.73.refs_2_), channel_id=1, source_target_pairs={{0,4},{4,0},{8,12},{12,8},{16,20},{20,16},{24,28},{28,24},{1,5},{5... | collective-permute-start | bytes 589832 | tf_op jit(solution)/shard_map/ppermute | solution.py:353
  69.3 22.0 %collective-permute-start.16 = (bf16[288,768]{1,0:T(8,128)(2,1)S(1)}, bf16[288,768]{1,0:T(8,128)(2,1)S(1)}, u32[]{:S(2)}, u32[]{:S(2)}) collective-permute-start(bf16[288,768]{1,0:T(8,128)(2,1)S(1)} %get-tuple-element.68), channel_id=1, source_target_pairs={{1,2},{2,1},{0,0},{3,3},{5,6},{6,5},{4,4},{7,7},{9,10},{10,9},{8,8... | collective-permute-start | bytes 1327112 | tf_op jit(solution)/shard_map/ppermute | solution.py:350
  70.0 22.0 %collective-permute-start.17 = (bf16[288,768]{1,0:T(8,128)(2,1)S(1)}, bf16[288,768]{1,0:T(8,128)(2,1)S(1)}, u32[]{:S(2)}, u32[]{:S(2)}) collective-permute-start(bf16[288,768]{1,0:T(8,128)(2,1)S(1)} %get-tuple-element.69), channel_id=1, source_target_pairs={{1,3},{2,0},{0,1},{3,2},{5,7},{6,4},{4,5},{7,6},{9,11},{10,8},{8,9... | collective-permute-start | bytes 1327112 | tf_op jit(solution)/shard_map/ppermute | solution.py:350
  73.1 7.8 %collective-permute-start.21 = (bf16[256,384]{1,0:T(8,128)(2,1)S(1)}, bf16[256,384]{1,0:T(8,128)(2,1)S(1)}, u32[]{:S(2)}, u32[]{:S(2)}) collective-permute-start(bf16[256,384]{1,0:T(8,128)(2,1)S(1)} %get-tuple-element.71.refs_0_), channel_id=1, source_target_pairs={{0,24},{4,28},{8,0},{12,4},{16,8},{20,12},{24,16},{28,20},{1,25},{... | collective-permute-start | bytes 589832 | tf_op jit(solution)/shard_map/ppermute | solution.py:359
  73.1 10.8 %collective-permute-start.23 = (bf16[256,384]{1,0:T(8,128)(2,1)S(1)}, bf16[256,384]{1,0:T(8,128)(2,1)S(1)}, u32[]{:S(2)}, u32[]{:S(2)}) collective-permute-start(bf16[256,384]{1,0:T(8,128)(2,1)S(1)} %get-tuple-element.72.refs_1_), channel_id=1, source_target_pairs={{0,24},{4,28},{8,0},{12,4},{16,8},{20,12},{24,16},{28,20},{1,25},{... | collective-permute-start | bytes 589832 | tf_op jit(solution)/shard_map/ppermute | solution.py:359
  76.0 10.0 %collective-permute-start.25 = (bf16[256,384]{1,0:T(8,128)(2,1)S(1)}, bf16[256,384]{1,0:T(8,128)(2,1)S(1)}, u32[]{:S(2)}, u32[]{:S(2)}) collective-permute-start(bf16[256,384]{1,0:T(8,128)(2,1)S(1)} %get-tuple-element.73.refs_2_), channel_id=1, source_target_pairs={{0,24},{4,28},{8,0},{12,4},{16,8},{20,12},{24,16},{28,20},{1,25},{... | collective-permute-start | bytes 589832 | tf_op jit(solution)/shard_map/ppermute | solution.py:359
  81.0 5.1 %collective-permute-start.22 = (bf16[256,384]{1,0:T(8,128)(2,1)S(1)}, bf16[256,384]{1,0:T(8,128)(2,1)S(1)}, u32[]{:S(2)}, u32[]{:S(2)}) collective-permute-start(bf16[256,384]{1,0:T(8,128)(2,1)S(1)} %collective-permute-done.21.refs_9_), channel_id=1, source_target_pairs={{0,4},{4,0},{8,12},{12,8},{16,20},{20,16},{24,28},{28,24},{1,5},{5... | collective-permute-start | bytes 589832 | tf_op jit(solution)/shard_map/ppermute | solution.py:353
  83.9 2.1 %collective-permute-start.24 = (bf16[256,384]{1,0:T(8,128)(2,1)S(1)}, bf16[256,384]{1,0:T(8,128)(2,1)S(1)}, u32[]{:S(2)}, u32[]{:S(2)}) collective-permute-start(bf16[256,384]{1,0:T(8,128)(2,1)S(1)} %collective-permute-done.23.refs_10_), channel_id=1, source_target_pairs={{0,4},{4,0},{8,12},{12,8},{16,20},{20,16},{24,28},{28,24},{1,5},{5... | collective-permute-start | bytes 589832 | tf_op jit(solution)/shard_map/ppermute | solution.py:353
  86.0 1.4 %collective-permute-start.26 = (bf16[256,384]{1,0:T(8,128)(2,1)S(1)}, bf16[256,384]{1,0:T(8,128)(2,1)S(1)}, u32[]{:S(2)}, u32[]{:S(2)}) collective-permute-start(bf16[256,384]{1,0:T(8,128)(2,1)S(1)} %collective-permute-done.25.refs_11_), channel_id=1, source_target_pairs={{0,4},{4,0},{8,12},{12,8},{16,20},{20,16},{24,28},{28,24},{1,5},{5... | collective-permute-start | bytes 589832 | tf_op jit(solution)/shard_map/ppermute | solution.py:353

commit v6 on v5

--- a/solution.py
+++ b/solution.py
@@ -10,7 +10,8 @@
 STEPS = 3
 EPS = 1e-06
 SHARES = (1, 2)
-UNIT_PARTS = 3
+UNIT_PARTS = 4
+TEXT_PARTS = 4
 VMEM_BYTES = 24 * 1024 * 1024
 BF16, F32 = jnp.bfloat16, jnp.float32
 
@@ -32,16 +33,17 @@
 
 def place(n_dp):
     where = lax.axis_index("dp")
-    return lax.axis_index("fsdp"), lax.rem(where, 2), lax.div(where, n_dp // 2)
+    column = lax.rem(lax.div(where, 2), 2)
+    return lax.axis_index("fsdp"), lax.rem(where, 2), lax.div(where, n_dp // 2), column
 
 
 def cut_kernel(n_dp, short, own, whole, part, sem):
-    _, core, side = place(n_dp)
+    _, core, _, column = place(n_dp)
     half = whole.shape[0]
     first = pltpu.make_async_copy(
         own.at[pl.ds(pl.multiple_of(core * half, 16), half), :], whole, sem.at[0]
     )
-    start = pl.multiple_of(core * half + side * (half - short), 16)
+    start = pl.multiple_of(core * half + column * (half - short), 16)
     second = pltpu.make_async_copy(own.at[pl.ds(start, short), :], part, sem.at[1])
     first.start()
     second.start()
@@ -67,24 +69,30 @@
     )(own)
 
 
-def prepare_kernel(n_dp, t0, twin0, twin2, t2, sharp, bias, units, scalars):
+def prepare_kernel(n_dp, t0, twin0, t2, sharp, bias, *rest):
+    twin2, (units, scalars) = rest[:TEXT_PARTS], rest[TEXT_PARTS:]
     rows = t0.shape[0]
+    _, core, _, _ = place(n_dp)
     scalars[0:1, :] = jnp.broadcast_to(sharp[...], (1, scalars.shape[1]))
     scalars[1:2, :] = jnp.broadcast_to(bias[...], (1, scalars.shape[1]))
-    _, core, _ = place(n_dp)
-
-    def fill(k, block):
+
+    def fill(start, block):
         values = block[...].astype(F32)
         inverse = 1.0 / jnp.sqrt(jnp.sum(values * values, axis=-1, keepdims=True) + EPS)
-        units[k * rows : (k + 1) * rows, :] = (values * inverse).astype(BF16)
+        units[start : start + block.shape[0], :] = (values * inverse).astype(BF16)
 
     fill(0, t0)
-    fill(2, t2)
-    pl.when(core == 0)(lambda: fill(1, twin2))
-    pl.when(core == 1)(lambda: fill(1, twin0))
-
-
-def prepare(n_dp, t0, twin0, twin2, t2, sharp, bias):
+    fill(2 * rows, t2)
+
+    @pl.when(core == 0)
+    def _():
+        for k, block in enumerate(twin2):
+            fill(rows + k * block.shape[0], block)
+
+    pl.when(core == 1)(lambda: fill(rows, twin0))
+
+
+def prepare(n_dp, t0, twin0, t2, sharp, bias, twin2):
     rows, width = t0.shape
     return pl.pallas_call(
         functools.partial(prepare_kernel, n_dp),
@@ -92,12 +100,12 @@
             jax.ShapeDtypeStruct((STEPS * rows, width), BF16),
             jax.ShapeDtypeStruct((8, 128), F32),
         ),
-        in_specs=spaces(6),
+        in_specs=spaces(5 + TEXT_PARTS),
         out_specs=tuple(spaces(2)),
         compiler_params=params(),
         cost_estimate=cost(),
         name="prepare",
-    )(t0, twin0, twin2, t2, sharp, bias)
+    )(t0, twin0, t2, sharp, bias, *twin2)
 
 
 def turn_kernel(x, x_t):
@@ -121,68 +129,53 @@
     return ref[pl.ds(pl.multiple_of(block * depth, 16), depth), :]
 
 
+def weights(mine, others, scale, bias):
+    product = lax.dot_general(
+        mine, others, (((1,), (1,)), ((), ())), preferred_element_type=F32
+    )
+    coefficient = jax.nn.sigmoid(scale * product + bias)
+    row = lax.broadcasted_iota(jnp.int32, coefficient.shape, 0)
+    column = lax.broadcasted_iota(jnp.int32, coefficient.shape, 1)
+    coefficient = jnp.where(row == column, coefficient - 1.0, coefficient).astype(BF16)
+    return coefficient, scale * jnp.sum(coefficient.astype(F32) * product, axis=-1, keepdims=True)
+
+
 def picture_kernel(n_dp, x, x_t, units, scalars, own, *rest):
     pieces, outs = rest[:8], rest[8 : 8 + len(SHARES)]
-    unit_parts = rest[8 + len(SHARES) : -5]
-    grad, unit, w, proj, sem = rest[-5:]
-    part, core, side = place(n_dp)
+    unit_parts = rest[8 + len(SHARES) : -4]
+    grad, unit, w, proj = rest[-4:]
+    part, core, side, column = place(n_dp)
     depth = own.shape[0]
     half = depth // 2
     short = pieces[2].shape[0]
     rest_rows = half - short
     rows = x.shape[0]
     step = 1 - 2 * side
-    copies = [
-        pltpu.make_async_copy(
-            own, w.at[pl.ds(pl.multiple_of(part * depth, 16), depth), :], sem.at[8]
-        )
-    ]
+    w[pl.ds(pl.multiple_of(part * depth, 16), depth), :] = own[...]
     for twin in (0, 1):
         lane = core if twin == 0 else 1 - core
         straight, crossed, two, two_crossed = pieces[4 * twin : 4 * twin + 4]
-        for index, piece, from_part in ((0, straight, part + 4 - step), (1, crossed, part + 4 + step)):
+        for piece, from_part in ((straight, part + 4 - step), (crossed, part + 4 + step)):
             start = pl.multiple_of(lax.rem(from_part, 4) * depth + lane * half, 16)
-            copies.append(
-                pltpu.make_async_copy(piece, w.at[pl.ds(start, half), :], sem.at[4 * twin + index])
-            )
+            w[pl.ds(start, half), :] = piece[...]
         base = lax.rem(part + 2, 4) * depth + lane * half
-        start = pl.multiple_of(base + side * rest_rows, 16)
-        copies.append(
-            pltpu.make_async_copy(two, w.at[pl.ds(start, short), :], sem.at[4 * twin + 2])
-        )
-        source = pl.multiple_of((1 - side) * (short - rest_rows), 16)
-        start = pl.multiple_of(base + (1 - side) * short, 16)
-        copies.append(
-            pltpu.make_async_copy(
-                two_crossed.at[pl.ds(source, rest_rows), :],
-                w.at[pl.ds(start, rest_rows), :],
-                sem.at[4 * twin + 3],
-            )
-        )
-    for copy in copies:
-        copy.start()
-    for copy in copies:
-        copy.wait()
+        start = pl.multiple_of(base + column * rest_rows, 16)
+        w[pl.ds(start, short), :] = two[...]
+        source = pl.multiple_of((1 - column) * (short - rest_rows), 16)
+        start = pl.multiple_of(base + (1 - column) * short, 16)
+        w[pl.ds(start, rest_rows), :] = two_crossed[pl.ds(source, rest_rows), :]
 
     proj[...] = jnp.dot(x[...], w[...], preferred_element_type=F32)
     values = proj[...]
     inverse = 1.0 / jnp.sqrt(jnp.sum(values * values, axis=-1, keepdims=True) + EPS)
     unit[...] = (values * inverse).astype(BF16)
-    size = unit.shape[1] // UNIT_PARTS
+    size = rows // UNIT_PARTS
     for k, out in enumerate(unit_parts):
-        out[...] = unit[:, k * size : (k + 1) * size]
+        out[...] = unit[k * size : (k + 1) * size, :]
     scale = scalars[0:1, 0:1]
-    logits = scale * lax.dot_general(
-        unit[...], units[...], (((1,), (1,)), ((), ())), preferred_element_type=F32
-    ) + scalars[1:2, 0:1]
-    coefficient = jax.nn.sigmoid(logits)
-    row = lax.broadcasted_iota(jnp.int32, coefficient.shape, 0)
-    column = lax.broadcasted_iota(jnp.int32, coefficient.shape, 1)
-    coefficient = jnp.where(row == column, coefficient - 1.0, coefficient).astype(BF16)
-    slope = scale * jnp.dot(coefficient, units[...], preferred_element_type=F32)
-    direction = proj[...] * inverse
-    along = jnp.sum(direction * slope, axis=-1, keepdims=True)
-    grad[...] = ((slope - direction * along) * inverse).astype(BF16)
+    coefficient, along = weights(unit[...], units[...], scale, scalars[1:2, 0:1])
+    slope = jnp.dot(coefficient, units[...], preferred_element_type=F32)
+    grad[...] = (slope * (scale * inverse) - proj[...] * (along * inverse * inverse)).astype(BF16)
     inner = jnp.logical_or(part == 1, part == 2)
 
     @pl.when(inner)
@@ -210,18 +203,17 @@
     out = jax.ShapeDtypeStruct((rows, width), BF16)
     sizes = [width * share // sum(SHARES) for share in SHARES]
     outs = tuple(jax.ShapeDtypeStruct((depth, size), BF16) for size in sizes)
-    part = jax.ShapeDtypeStruct((rows, width // UNIT_PARTS), BF16)
+    part = jax.ShapeDtypeStruct((rows // UNIT_PARTS, width), BF16)
     outs = outs + (part,) * UNIT_PARTS + (out,)
     return pl.pallas_call(
         functools.partial(picture_kernel, n_dp),
         out_shape=outs,
-        in_specs=spaces(4) + [pl.BlockSpec(memory_space=pl.ANY)] * 9,
+        in_specs=spaces(13),
         out_specs=spaces(len(outs)),
         scratch_shapes=[
             pltpu.VMEM((rows, width), BF16),
             pltpu.VMEM((width, width), BF16),
             pltpu.VMEM((rows, width), F32),
-            pltpu.SemaphoreType.DMA((9,)),
         ],
         compiler_params=params(),
         cost_estimate=cost(),
@@ -232,34 +224,28 @@
 def text_kernel(n_dp, text, scalars, *refs):
     blocks, (out, done, units) = refs[:-3], refs[-3:]
     rows = text.shape[0]
-    _, core, _ = place(n_dp)
+    _, core, _, _ = place(n_dp)
     done[...] = jnp.zeros_like(done)
-    size = blocks[0].shape[1]
+    size = blocks[0].shape[0]
     for k in range(UNIT_PARTS):
         u0, twin0, twin2, u2 = blocks[k::UNIT_PARTS]
-        columns = slice(k * size, (k + 1) * size)
-        units[:rows, columns] = u0[...]
-        units[2 * rows :, columns] = u2[...]
+        for step, block in ((0, u0), (2, u2)):
+            start = step * rows + k * size
+            units[start : start + size, :] = block[...]
         for lane, block in ((0, twin0), (1, twin2)):
 
             @pl.when(core == lane)
             def _():
-                units[rows : 2 * rows, columns] = block[...]
+                units[rows + k * size : rows + (k + 1) * size, :] = block[...]
 
     values = text[...].astype(F32)
     inverse = 1.0 / jnp.sqrt(jnp.sum(values * values, axis=-1, keepdims=True) + EPS)
-    direction = values * inverse
     scale = scalars[0:1, 0:1]
-    logits = scale * lax.dot_general(
-        direction.astype(BF16), units[...], (((1,), (1,)), ((), ())), preferred_element_type=F32
-    ) + scalars[1:2, 0:1]
-    coefficient = jax.nn.sigmoid(logits)
-    row = lax.broadcasted_iota(jnp.int32, coefficient.shape, 0)
-    column = lax.broadcasted_iota(jnp.int32, coefficient.shape, 1)
-    coefficient = jnp.where(row == column, coefficient - 1.0, coefficient).astype(BF16)
-    slope = scale * jnp.dot(coefficient, units[...], preferred_element_type=F32)
-    along = jnp.sum(direction * slope, axis=-1, keepdims=True)
-    out[...] = (slope - direction * along) * inverse
+    coefficient, along = weights(
+        (values * inverse).astype(BF16), units[...], scale, scalars[1:2, 0:1]
+    )
+    slope = jnp.dot(coefficient, units[...], preferred_element_type=F32)
+    out[...] = slope * (scale * inverse) - values * (along * inverse * inverse)
 
 
 def text_side(n_dp, text, scalars, *units):
@@ -373,11 +359,14 @@
     crossed = over(straight)
     two = along(piece, [(f, (f + 2) % n_fsdp) for f in range(n_fsdp)])
     two, x = lax.optimization_barrier((two, x))
-    two_crossed = over(two)
+    two_crossed = lax.ppermute(two, "dp", [(d, d ^ 2) for d in range(n_dp)])
     far_x = along(x, swap)
     x_t = turned(x)
     crossed, x_t, text2 = lax.optimization_barrier((crossed, x_t, text2))
-    units, scalars = prepare(n_dp, text, across(text), across(text2), text2, sharp, bias)
+    size = text.shape[0] // TEXT_PARTS
+    twin2 = [across(text2[k * size : (k + 1) * size]) for k in range(TEXT_PARTS)]
+    two_crossed, *twin2 = lax.optimization_barrier((two_crossed, *twin2))
+    units, scalars = prepare(n_dp, text, across(text), text2, sharp, bias, twin2)
     two_crossed, units, scalars = lax.optimization_barrier((two_crossed, units, scalars))
     pieces = [straight, crossed, two, two_crossed]
     pieces = pieces + [across(piece) for piece in pieces]
@@ -398,7 +387,7 @@
         kept, near, far = pair_product(begin, x_t, far_t, grad, block, after)
         near = along(near, [(1, 2), (2, 1), (0, 0), (3, 3)])
         far = along(far, [(1, 3), (2, 0), (0, 1), (3, 2)])
-        after = [near, far]
+        after = [near, far, *unit2]
         terms.append((begin, width, kept, near, far))
         begin += block.shape[1]
     twin0, twin2 = [across(u) for u in unit], [across(u) for u in unit2]

time: 93.3 us -> 93.5 us (level)
  starting transfers between devices: 21.3 us -> 30.9 us
  waiting for transfers between devices: 55 us -> 47.4 us
  Pallas kernels: 13.5 us -> 11.6 us
    ppermute x4 -> x5, waiting for transfers between devices: 9.98 us -> 3.47 us  [shifted(): lax.ppermute(value, 'dp', [(d, (d + by) % n_dp) for d in range(n_dp)])]
    ppermute x4 -> x5, starting transfers between devices: 4.4 us -> 9.23 us  [shifted(): lax.ppermute(value, 'dp', [(d, (d + by) % n_dp) for d in range(n_dp)])]
    ppermute x2 -> x1, waiting for transfers between devices: 5.4 us -> 1.24 us  [over(): lax.ppermute(value, 'dp', [(d, (d + side) % n_dp) for d in range(n_dp)])]
    ppermute x8, starting transfers between devices: 10 us -> 13 us  [along(): return lax.ppermute(value, 'fsdp', pairs)]
    ppermute x0 -> x1, waiting for transfers between devices: none -> 2.16 us  [line_body(): two_crossed = lax.ppermute(two, 'dp', [(d, d ^ 2) for d in range(n_dp)])]
    ppermute x12 -> x17, starting transfers between devices: 1.33 us -> 3.18 us  [across(): return lax.ppermute(value, 'dp', [(d, d ^ 1) for d in range(n_dp)])]
    ppermute x2 -> x1, starting transfers between devices: 2.49 us -> 0.78 us  [over(): lax.ppermute(value, 'dp', [(d, (d + side) % n_dp) for d in range(n_dp)])]
    pallas_call x1, Pallas kernels: 5.58 us -> 3.9 us  [picture_side(): pl.pallas_call(functools.partial(picture_kernel, n_dp), out_shape=outs, i...]
  transfers between devices with their start and end apart: 27 -> 33, of which waited for: 14 -> 17; matrix products, arithmetic and copies ran while one was open for 0% -> 0% of each run, Pallas kernels for 13% -> 11%
where the time goes in v6:
time: 93.5 us; the launch traced here: 93.2 us
  waiting for transfers between devices  47.4 us (51%)
  starting transfers between devices  30.9 us (33%)
  Pallas kernels  11.6 us (12%)
  between operations  2.1 us (2%)
  local copies, waits for them, and re-layouts  1.14 us (1%)
    ppermute x8, waiting for transfers between devices, along(): return lax.ppermute(value, 'fsdp', pairs)  28.1 us
    ppermute x8, starting transfers between devices, along(): return lax.ppermute(value, 'fsdp', pairs)  13 us
    ppermute x5, starting transfers between devices, shifted(): lax.ppermute(value, 'dp', [(d, (d + by) % n_dp) for d in range(n_dp)])  9.23 us
    ppermute x1, waiting for transfers between devices, line_body(): straight = lax.ppermute(whole, ('dp', 'fsdp'), turns)  8.33 us
    ppermute x17, waiting for transfers between devices, across(): return lax.ppermute(value, 'dp', [(d, d ^ 1) for d in range(n_dp)])  4.09 us
    pallas_call x1, Pallas kernels, picture_side(): pl.pallas_call(functools.partial(picture_kernel, n_dp), out_shape=outs, i...  3.9 us
    ppermute x5, waiting for transfers between devices, shifted(): lax.ppermute(value, 'dp', [(d, (d + by) % n_dp) for d in range(n_dp)])  3.47 us
    ppermute x17, starting transfers between devices, across(): return lax.ppermute(value, 'dp', [(d, d ^ 1) for d in range(n_dp)])  3.18 us
  transfers between devices with their start and end apart: 33, of which 17 were waited for; matrix products, arithmetic and copies ran while one was open for 0% of the time, Pallas kernels for 11%

profile of v6, /device:TPU:0, one launch (start us, length us, event | category | flops | bytes accessed | tf_op | source)
XLA Modules:
  0.0 93.2 jit_solution(15381065141860232440)
XLA Ops:
  0.6 1.1 %copy-done = bf16[288,1152]{1,0:T(8,128)(2,1)S(1)} copy-done((bf16[288,1152]{1,0:T(8,128)(2,1)S(1)}, bf16[288,1152]{1,0:T(8,128)(2,1)}, u32[]{:S(2)}) %copy-start) | copy-done | bytes 663576
  2.1 3.1 %collective-permute-start = (bf16[144,1152]{1,0:T(8,128)(2,1)S(1)}, bf16[144,1152]{1,0:T(8,128)(2,1)S(1)}, u32[]{:S(2)}, u32[]{:S(2)}) collective-permute-start(bf16[144,1152]{1,0:T(8,128)(2,1)S(1)} %get-tuple-element.48), channel_id=1, source_target_pairs={{0,1},{1,2},{2,3},{3,0},{4,5},{5,6},{6,7},{7,4},{8,9},{9,10},{10,1... | collective-permute-start | bytes 995336 | tf_op jit(solution)/shard_map/ppermute | solution.py:356
  5.2 1.5 %collective-permute-start.3 = (bf16[256,1152]{1,0:T(8,128)(2,1)}, bf16[256,1152]{1,0:T(8,128)(2,1)S(1)}, u32[]{:S(2)}, u32[]{:S(2)}) collective-permute-start(bf16[256,1152]{1,0:T(8,128)(2,1)} %text), channel_id=1, source_target_pairs={{0,8},{4,12},{8,16},{12,20},{16,24},{20,28},{24,0},{28,4},{1,9},{5... | collective-permute-start | bytes 1769480 | tf_op jit(solution)/shard_map/ppermute | solution.py:345
  6.7 8.3 %collective-permute-done.rest_0_ = bf16[144,1152]{1,0:T(8,128)(2,1)S(1)} collective-permute-done((bf16[144,1152]{1,0:T(8,128)(2,1)S(1)}, bf16[144,1152]{1,0:T(8,128)(2,1)S(1)}, u32[]{:S(2)}, u32[]{:S(2)}) %collective-permute-start) | collective-permute-done | bytes 331808 | tf_op jit(solution)/shard_map/ppermute | solution.py:356
  15.0 0.8 collective-permute-start.1
  15.8 1.5 %collective-permute-start.2 = (bf16[80,1152]{1,0:T(8,128)(2,1)S(1)}, bf16[80,1152]{1,0:T(8,128)(2,1)S(1)}, u32[]{:S(2)}, u32[]{:S(2)}) collective-permute-start(bf16[80,1152]{1,0:T(8,128)(2,1)S(1)} %get-tuple-element.50), channel_id=1, source_target_pairs={{0,2},{1,3},{2,0},{3,1},{4,6},{5,7},{6,4},{7,5},{8,10},{9,11},{10,... | collective-permute-start | bytes 552968 | tf_op jit(solution)/shard_map/ppermute | solution.py:336
  17.3 8.6 %collective-permute-done.2.rest_2_ = bf16[80,1152]{1,0:T(8,128)(2,1)S(1)} collective-permute-done((bf16[80,1152]{1,0:T(8,128)(2,1)S(1)}, bf16[80,1152]{1,0:T(8,128)(2,1)S(1)}, u32[]{:S(2)}, u32[]{:S(2)}) %collective-permute-start.2) | collective-permute-done | bytes 184352 | tf_op jit(solution)/shard_map/ppermute | solution.py:336
  25.9 1.3 %turned.2.x_t = bf16[1152,256]{1,0:T(8,128)(2,1)S(1)} custom-call(bf16[256,1152]{1,0:T(8,128)(2,1)} %x.1), custom_call_target="tpu_custom_call" | custom-call | tf_op jit(solution)/shard_map/turned/pallas_call | solution.py:117
  27.2 1.6 %collective-permute-start.4 = (bf16[80,1152]{1,0:T(8,128)(2,1)S(1)}, bf16[80,1152]{1,0:T(8,128)(2,1)S(1)}, u32[]{:S(2)}, u32[]{:S(2)}) collective-permute-start(bf16[80,1152]{1,0:T(8,128)(2,1)S(1)} %collective-permute-done.2.rest_2_), channel_id=1, source_target_pairs={{0,8},{4,12},{8,0},{12,4},{16,24},{20,28},{24,16},{28,20},{1,9},{5... | collective-permute-start | bytes 552968 | tf_op jit(solution)/shard_map/ppermute | solution.py:362
  28.8 1.2 %collective-permute-done.1.rest_1_ = bf16[144,1152]{1,0:T(8,128)(2,1)S(1)} collective-permute-done((bf16[144,1152]{1,0:T(8,128)(2,1)S(1)}, bf16[144,1152]{1,0:T(8,128)(2,1)S(1)}, u32[]{:S(2)}, u32[]{:S(2)}) %collective-permute-start.1) | collective-permute-done | bytes 331808 | tf_op jit(solution)/shard_map/ppermute | solution.py:342
  30.7 2.2 %collective-permute-done.4.rest_3_ = bf16[80,1152]{1,0:T(8,128)(2,1)S(1)} collective-permute-done((bf16[80,1152]{1,0:T(8,128)(2,1)S(1)}, bf16[80,1152]{1,0:T(8,128)(2,1)S(1)}, u32[]{:S(2)}, u32[]{:S(2)}) %collective-permute-start.4) | collective-permute-done | bytes 184352 | tf_op jit(solution)/shard_map/ppermute | solution.py:362
  33.4 0.8 collective-permute-done.7.rest_2_
  37.1 1.1 %collective-permute-done.13.rest_7_ = bf16[80,1152]{1,0:T(8,128)(2,1)S(1)} collective-permute-done((bf16[80,1152]{1,0:T(8,128)(2,1)S(1)}, bf16[80,1152]{1,0:T(8,128)(2,1)S(1)}, u32[]{:S(2)}, u32[]{:S(2)}) %collective-permute-start.13) | collective-permute-done | bytes 184352 | tf_op jit(solution)/shard_map/ppermute | solution.py:339
  38.3 3.9 %picture_side.1 = (bf16[288,384]{1,0:T(8,128)(2,1)S(1)}, bf16[288,768]{1,0:T(8,128)(2,1)S(1)}, bf16[64,1152]{1,0:T(8,128)(2,1)S(1)}, bf16[64,1152]{1,0:T(8,128)(...) custom-call(bf16[256,1152]{1,0:T(8,128)(2,1)} %x.1, ...), custom_call_target="tpu_custom_call" | custom-call | tf_op jit(solution)/shard_map/picture_side/pallas_call | solution.py:208
  42.4 2.3 %collective-permute-start.15 = (bf16[288,384]{1,0:T(8,128)(2,1)S(1)}, bf16[288,384]{1,0:T(8,128)(2,1)S(1)}, u32[]{:S(2)}, u32[]{:S(2)}) collective-permute-start(bf16[288,384]{1,0:T(8,128)(2,1)S(1)} %get-tuple-element.73), channel_id=1, source_target_pairs={{0,1},{1,0},{2,3},{3,2},{4,5},{5,4},{6,7},{7,6},{8,9},{9,8},{10,11... | collective-permute-start | bytes 663560 | tf_op jit(solution)/shard_map/ppermute | solution.py:336
  44.7 5.7 %collective-permute-done.15.arrived = bf16[288,384]{1,0:T(8,128)(2,1)S(1)} collective-permute-done((bf16[288,384]{1,0:T(8,128)(2,1)S(1)}, bf16[288,384]{1,0:T(8,128)(2,1)S(1)}, u32[]{:S(2)}, u32[]{:S(2)}) %collective-permute-start.15) | collective-permute-done | bytes 221216 | tf_op jit(solution)/shard_map/ppermute | solution.py:336
  50.4 1.7 %collective-permute-start.16 = (bf16[288,768]{1,0:T(8,128)(2,1)S(1)}, bf16[288,768]{1,0:T(8,128)(2,1)S(1)}, u32[]{:S(2)}, u32[]{:S(2)}) collective-permute-start(bf16[288,768]{1,0:T(8,128)(2,1)S(1)} %get-tuple-element.74), channel_id=1, source_target_pairs={{0,1},{1,0},{2,3},{3,2},{4,5},{5,4},{6,7},{7,6},{8,9},{9,8},{10,11... | collective-permute-start | bytes 1327112 | tf_op jit(solution)/shard_map/ppermute | solution.py:336
  52.2 2.3 %collective-permute-start.19 = (bf16[64,1152]{1,0:T(8,128)(2,1)S(1)}, bf16[64,1152]{1,0:T(8,128)(2,1)S(1)}, u32[]{:S(2)}, u32[]{:S(2)}) collective-permute-start(bf16[64,1152]{1,0:T(8,128)(2,1)S(1)} %get-tuple-element.78.refs_0_), channel_id=1, source_target_pairs={{0,24},{4,28},{8,0},{12,4},{16,8},{20,12},{24,16},{28,20},{1,25},{... | collective-permute-start | bytes 442376 | tf_op jit(solution)/shard_map/ppermute | solution.py:345
  54.5 1.0 %collective-permute-start.20 = (bf16[64,1152]{1,0:T(8,128)(2,1)S(1)}, bf16[64,1152]{1,0:T(8,128)(2,1)S(1)}, u32[]{:S(2)}, u32[]{:S(2)}) collective-permute-start(bf16[64,1152]{1,0:T(8,128)(2,1)S(1)} %get-tuple-element.79.refs_1_), channel_id=1, source_target_pairs={{0,24},{4,28},{8,0},{12,4},{16,8},{20,12},{24,16},{28,20},{1,25},{... | collective-permute-start | bytes 442376 | tf_op jit(solution)/shard_map/ppermute | solution.py:345
  56.5 2.6 %collective-permute-start.18 = (bf16[288,384]{1,0:T(8,128)(2,1)S(1)}, bf16[288,384]{1,0:T(8,128)(2,1)S(1)}, u32[]{:S(2)}, u32[]{:S(2)}) collective-permute-start(bf16[288,384]{1,0:T(8,128)(2,1)S(1)} %get-tuple-element.77), channel_id=1, source_target_pairs={{1,3},{2,0},{0,1},{3,2},{5,7},{6,4},{4,5},{7,6},{9,11},{10,8},{8,9... | collective-permute-start | bytes 663560 | tf_op jit(solution)/shard_map/ppermute | solution.py:336
  59.1 2.7 %collective-permute-start.21 = (bf16[64,1152]{1,0:T(8,128)(2,1)S(1)}, bf16[64,1152]{1,0:T(8,128)(2,1)S(1)}, u32[]{:S(2)}, u32[]{:S(2)}) collective-permute-start(bf16[64,1152]{1,0:T(8,128)(2,1)S(1)} %get-tuple-element.80.refs_2_), channel_id=1, source_target_pairs={{0,24},{4,28},{8,0},{12,4},{16,8},{20,12},{24,16},{28,20},{1,25},{... | collective-permute-start | bytes 442376 | tf_op jit(solution)/shard_map/ppermute | solution.py:345
  61.8 1.7 %collective-permute-start.22 = (bf16[64,1152]{1,0:T(8,128)(2,1)S(1)}, bf16[64,1152]{1,0:T(8,128)(2,1)S(1)}, u32[]{:S(2)}, u32[]{:S(2)}) collective-permute-start(bf16[64,1152]{1,0:T(8,128)(2,1)S(1)} %get-tuple-element.81.refs_3_), channel_id=1, source_target_pairs={{0,24},{4,28},{8,0},{12,4},{16,8},{20,12},{24,16},{28,20},{1,25},{... | collective-permute-start | bytes 442376 | tf_op jit(solution)/shard_map/ppermute | solution.py:345
  63.4 1.8 %collective-permute-done.21.rest_4_.refs_14_ = bf16[64,1152]{1,0:T(8,128)(2,1)S(1)} collective-permute-done((bf16[64,1152]{1,0:T(8,128)(2,1)S(1)}, bf16[64,1152]{1,0:T(8,128)(2,1)S(1)}, u32[]{:S(2)}, u32[]{:S(2)}) %collective-permute-start.21) | collective-permute-done | bytes 147488 | tf_op jit(solution)/shard_map/ppermute | solution.py:345
  65.2 1.7 %collective-permute-done.22.rest_5_.refs_15_ = bf16[64,1152]{1,0:T(8,128)(2,1)S(1)} collective-permute-done((bf16[64,1152]{1,0:T(8,128)(2,1)S(1)}, bf16[64,1152]{1,0:T(8,128)(2,1)S(1)}, u32[]{:S(2)}, u32[]{:S(2)}) %collective-permute-start.22) | collective-permute-done | bytes 147488 | tf_op jit(solution)/shard_map/ppermute | solution.py:345
  66.9 1.7 %collective-permute-done.18.rest_1_.far = bf16[288,384]{1,0:T(8,128)(2,1)S(1)} collective-permute-done((bf16[288,384]{1,0:T(8,128)(2,1)S(1)}, bf16[288,384]{1,0:T(8,128)(2,1)S(1)}, u32[]{:S(2)}, u32[]{:S(2)}) %collective-permute-start.18) | collective-permute-done | bytes 221216 | tf_op jit(solution)/shard_map/ppermute | solution.py:336
  69.0 0.7 collective-permute-start.23
  69.7 3.5 %collective-permute-start.24 = (bf16[288,768]{1,0:T(8,128)(2,1)S(1)}, bf16[288,768]{1,0:T(8,128)(2,1)S(1)}, u32[]{:S(2)}, u32[]{:S(2)}) collective-permute-start(bf16[288,768]{1,0:T(8,128)(2,1)S(1)} %get-tuple-element.84), channel_id=1, source_target_pairs={{1,3},{2,0},{0,1},{3,2},{5,7},{6,4},{4,5},{7,6},{9,11},{10,8},{8,9... | collective-permute-start | bytes 1327112 | tf_op jit(solution)/shard_map/ppermute | solution.py:336
  73.7 0.8 collective-permute-done.27.refs_6_
  76.4 2.8 %text_side.1 = (f32[256,1152]{1,0:T(8,128)}, f32[8,128]{1,0:T(8,128)S(1)}) custom-call(bf16[256,1152]{1,0:T(8,128)(2,1)S(1)} %copy-done.2, f32[8,128]{1,0:T(8,128)S(1)} %get-tuple-element.64.scalars, bf16[64,1152]{1,0:T(8,128)(2,1)S(1)} %get-tuple-element.78.refs_0_, bf16[64,1152]{1,0:T(8,128)(2,1)S(1)} %get-tuple-element.79.refs_1_, ...), custom_call_target="tpu_custom_call" | custom-call | tf_op jit(solution)/shard_map/text_side/pallas_call | solution.py:253
  79.2 0.8 total.2.rest_0_
  80.1 12.1 %collective-permute-done.24.far = bf16[288,768]{1,0:T(8,128)(2,1)S(1)} collective-permute-done((bf16[288,768]{1,0:T(8,128)(2,1)S(1)}, bf16[288,768]{1,0:T(8,128)(2,1)S(1)}, u32[]{:S(2)}, u32[]{:S(2)}) %collective-permute-start.24) | collective-permute-done | bytes 442400 | tf_op jit(solution)/shard_map/ppermute | solution.py:336
  92.1 1.0 %total.3 = f32[1,288,1152]{2,1,0:T(8,128)} custom-call(f32[288,768]{1,0:T(8,128)S(1)} %get-tuple-element.82.kept, bf16[288,768]{1,0:T(8,128)(2,1)S(1)} %collective-permute-done.23.near, bf16[288,768]{1,0:T(8,128)(2,1)S(1)} %collective-permute-done.24.far, f32[1,288,1152]{2,1,0:T(8,128)} %total.2.rest_0_, ...), custom_call_target="tpu_custom_call", output_to_operand_aliasing={{}: (3, {})} | custom-call | tf_op jit(solution)/shard_map/total/pallas_call | solution.py:315
  (51 shorter events, 7.3 us)
Async XLA Ops:
  2.1 12.9 %collective-permute-start = (bf16[144,1152]{1,0:T(8,128)(2,1)S(1)}, bf16[144,1152]{1,0:T(8,128)(2,1)S(1)}, u32[]{:S(2)}, u32[]{:S(2)}) collective-permute-start(bf16[144,1152]{1,0:T(8,128)(2,1)S(1)} %get-tuple-element.48), channel_id=1, source_target_pairs={{0,1},{1,2},{2,3},{3,0},{4,5},{5,6},{6,7},{7,4},{8,9},{9,10},{10,1... | collective-permute-start | bytes 995336 | tf_op jit(solution)/shard_map/ppermute | solution.py:356
  5.2 23.6 %collective-permute-start.3 = (bf16[256,1152]{1,0:T(8,128)(2,1)}, bf16[256,1152]{1,0:T(8,128)(2,1)S(1)}, u32[]{:S(2)}, u32[]{:S(2)}) collective-permute-start(bf16[256,1152]{1,0:T(8,128)(2,1)} %text), channel_id=1, source_target_pairs={{0,8},{4,12},{8,16},{12,20},{16,24},{20,28},{24,0},{28,4},{1,9},{5... | collective-permute-start | bytes 1769480 | tf_op jit(solution)/shard_map/ppermute | solution.py:345
  15.0 15.0 %collective-permute-start.1 = (bf16[144,1152]{1,0:T(8,128)(2,1)S(1)}, bf16[144,1152]{1,0:T(8,128)(2,1)S(1)}, u32[]{:S(2)}, u32[]{:S(2)}) collective-permute-start(bf16[144,1152]{1,0:T(8,128)(2,1)S(1)} %collective-permute-done.rest_0_), channel_id=1, source_target_pairs={{0,16},{4,20},{8,24},{12,28},{16,0},{20,4},{24,8},{28,12},{1,17},{... | collective-permute-start | bytes 995336 | tf_op jit(solution)/shard_map/ppermute | solution.py:342
  15.8 10.1 %collective-permute-start.2 = (bf16[80,1152]{1,0:T(8,128)(2,1)S(1)}, bf16[80,1152]{1,0:T(8,128)(2,1)S(1)}, u32[]{:S(2)}, u32[]{:S(2)}) collective-permute-start(bf16[80,1152]{1,0:T(8,128)(2,1)S(1)} %get-tuple-element.50), channel_id=1, source_target_pairs={{0,2},{1,3},{2,0},{3,1},{4,6},{5,7},{6,4},{7,5},{8,10},{9,11},{10,... | collective-permute-start | bytes 552968 | tf_op jit(solution)/shard_map/ppermute | solution.py:336
  17.3 18.8 %collective-permute-start.9 = (bf16[256,1152]{1,0:T(8,128)(2,1)}, bf16[256,1152]{1,0:T(8,128)(2,1)S(1)}, u32[]{:S(2)}, u32[]{:S(2)}) collective-permute-start(bf16[256,1152]{1,0:T(8,128)(2,1)} %text), channel_id=1, source_target_pairs={{0,4},{4,0},{8,12},{12,8},{16,20},{20,16},{24,28},{28,24},{1,5},{5... | collective-permute-start | bytes 1769480 | tf_op jit(solution)/shard_map/ppermute | solution.py:339
  27.1 15.0 %collective-permute-start.14 = (bf16[256,1152]{1,0:T(8,128)(2,1)}, bf16[256,1152]{1,0:T(8,128)(2,1)S(1)}, u32[]{:S(2)}, u32[]{:S(2)}) collective-permute-start(bf16[256,1152]{1,0:T(8,128)(2,1)} %x.1), channel_id=1, source_target_pairs={{0,1},{1,0},{2,3},{3,2},{4,5},{5,4},{6,7},{7,6},{8,9},{9,8},{10,11... | collective-permute-start | bytes 1769480 | tf_op jit(solution)/shard_map/ppermute | solution.py:336
  27.2 5.6 %collective-permute-start.4 = (bf16[80,1152]{1,0:T(8,128)(2,1)S(1)}, bf16[80,1152]{1,0:T(8,128)(2,1)S(1)}, u32[]{:S(2)}, u32[]{:S(2)}) collective-permute-start(bf16[80,1152]{1,0:T(8,128)(2,1)S(1)} %collective-permute-done.2.rest_2_), channel_id=1, source_target_pairs={{0,8},{4,12},{8,0},{12,4},{16,24},{20,28},{24,16},{28,20},{1,9},{5... | collective-permute-start | bytes 552968 | tf_op jit(solution)/shard_map/ppermute | solution.py:362
  30.1 2.7 %collective-permute-start.5 = (bf16[64,1152]{1,0:T(8,128)(2,1)S(1)}, bf16[64,1152]{1,0:T(8,128)(2,1)S(1)}, u32[]{:S(2)}, u32[]{:S(2)}) collective-permute-start(bf16[64,1152]{1,0:T(8,128)(2,1)S(1)} %get-tuple-element.91), channel_id=1, source_target_pairs={{0,4},{4,0},{8,12},{12,8},{16,20},{20,16},{24,28},{28,24},{1,5},{5... | collective-permute-start | bytes 442376 | tf_op jit(solution)/shard_map/ppermute | solution.py:339
  30.2 3.2 %collective-permute-start.6 = (bf16[64,1152]{1,0:T(8,128)(2,1)S(1)}, bf16[64,1152]{1,0:T(8,128)(2,1)S(1)}, u32[]{:S(2)}, u32[]{:S(2)}) collective-permute-start(bf16[64,1152]{1,0:T(8,128)(2,1)S(1)} %get-tuple-element.90), channel_id=1, source_target_pairs={{0,4},{4,0},{8,12},{12,8},{16,20},{20,16},{24,28},{28,24},{1,5},{5... | collective-permute-start | bytes 442376 | tf_op jit(solution)/shard_map/ppermute | solution.py:339
  32.8 1.4 %collective-permute-start.7 = (bf16[64,1152]{1,0:T(8,128)(2,1)S(1)}, bf16[64,1152]{1,0:T(8,128)(2,1)S(1)}, u32[]{:S(2)}, u32[]{:S(2)}) collective-permute-start(bf16[64,1152]{1,0:T(8,128)(2,1)S(1)} %get-tuple-element.89), channel_id=1, source_target_pairs={{0,4},{4,0},{8,12},{12,8},{16,20},{20,16},{24,28},{28,24},{1,5},{5... | collective-permute-start | bytes 442376 | tf_op jit(solution)/shard_map/ppermute | solution.py:339
  32.8 2.8 %collective-permute-start.8 = (bf16[64,1152]{1,0:T(8,128)(2,1)S(1)}, bf16[64,1152]{1,0:T(8,128)(2,1)S(1)}, u32[]{:S(2)}, u32[]{:S(2)}) collective-permute-start(bf16[64,1152]{1,0:T(8,128)(2,1)S(1)} %get-tuple-element.88), channel_id=1, source_target_pairs={{0,4},{4,0},{8,12},{12,8},{16,20},{20,16},{24,28},{28,24},{1,5},{5... | collective-permute-start | bytes 442376 | tf_op jit(solution)/shard_map/ppermute | solution.py:339
  33.3 3.6 %collective-permute-start.10 = (bf16[144,1152]{1,0:T(8,128)(2,1)S(1)}, bf16[144,1152]{1,0:T(8,128)(2,1)S(1)}, u32[]{:S(2)}, u32[]{:S(2)}) collective-permute-start(bf16[144,1152]{1,0:T(8,128)(2,1)S(1)} %collective-permute-done.rest_0_), channel_id=1, source_target_pairs={{0,4},{4,0},{8,12},{12,8},{16,20},{20,16},{24,28},{28,24},{1,5},{5... | collective-permute-start | bytes 995336 | tf_op jit(solution)/shard_map/ppermute | solution.py:339
  34.2 2.9 %collective-permute-start.11 = (bf16[144,1152]{1,0:T(8,128)(2,1)S(1)}, bf16[144,1152]{1,0:T(8,128)(2,1)S(1)}, u32[]{:S(2)}, u32[]{:S(2)}) collective-permute-start(bf16[144,1152]{1,0:T(8,128)(2,1)S(1)} %collective-permute-done.1.rest_1_), channel_id=1, source_target_pairs={{0,4},{4,0},{8,12},{12,8},{16,20},{20,16},{24,28},{28,24},{1,5},{5... | collective-permute-start | bytes 995336 | tf_op jit(solution)/shard_map/ppermute | solution.py:339
  35.6 1.5 %collective-permute-start.12 = (bf16[80,1152]{1,0:T(8,128)(2,1)S(1)}, bf16[80,1152]{1,0:T(8,128)(2,1)S(1)}, u32[]{:S(2)}, u32[]{:S(2)}) collective-permute-start(bf16[80,1152]{1,0:T(8,128)(2,1)S(1)} %collective-permute-done.2.rest_2_), channel_id=1, source_target_pairs={{0,4},{4,0},{8,12},{12,8},{16,20},{20,16},{24,28},{28,24},{1,5},{5... | collective-permute-start | bytes 552968 | tf_op jit(solution)/shard_map/ppermute | solution.py:339
  36.8 1.5 %collective-permute-start.13 = (bf16[80,1152]{1,0:T(8,128)(2,1)S(1)}, bf16[80,1152]{1,0:T(8,128)(2,1)S(1)}, u32[]{:S(2)}, u32[]{:S(2)}) collective-permute-start(bf16[80,1152]{1,0:T(8,128)(2,1)S(1)} %collective-permute-done.4.rest_3_), channel_id=1, source_target_pairs={{0,4},{4,0},{8,12},{12,8},{16,20},{20,16},{24,28},{28,24},{1,5},{5... | collective-permute-start | bytes 552968 | tf_op jit(solution)/shard_map/ppermute | solution.py:339
  42.4 8.1 %collective-permute-start.15 = (bf16[288,384]{1,0:T(8,128)(2,1)S(1)}, bf16[288,384]{1,0:T(8,128)(2,1)S(1)}, u32[]{:S(2)}, u32[]{:S(2)}) collective-permute-start(bf16[288,384]{1,0:T(8,128)(2,1)S(1)} %get-tuple-element.73), channel_id=1, source_target_pairs={{0,1},{1,0},{2,3},{3,2},{4,5},{5,4},{6,7},{7,6},{8,9},{9,8},{10,11... | collective-permute-start | bytes 663560 | tf_op jit(solution)/shard_map/ppermute | solution.py:336
  50.4 18.2 %collective-permute-start.16 = (bf16[288,768]{1,0:T(8,128)(2,1)S(1)}, bf16[288,768]{1,0:T(8,128)(2,1)S(1)}, u32[]{:S(2)}, u32[]{:S(2)}) collective-permute-start(bf16[288,768]{1,0:T(8,128)(2,1)S(1)} %get-tuple-element.74), channel_id=1, source_target_pairs={{0,1},{1,0},{2,3},{3,2},{4,5},{5,4},{6,7},{7,6},{8,9},{9,8},{10,11... | collective-permute-start | bytes 1327112 | tf_op jit(solution)/shard_map/ppermute | solution.py:336
  52.2 6.9 %collective-permute-start.19 = (bf16[64,1152]{1,0:T(8,128)(2,1)S(1)}, bf16[64,1152]{1,0:T(8,128)(2,1)S(1)}, u32[]{:S(2)}, u32[]{:S(2)}) collective-permute-start(bf16[64,1152]{1,0:T(8,128)(2,1)S(1)} %get-tuple-element.78.refs_0_), channel_id=1, source_target_pairs={{0,24},{4,28},{8,0},{12,4},{16,8},{20,12},{24,16},{28,20},{1,25},{... | collective-permute-start | bytes 442376 | tf_op jit(solution)/shard_map/ppermute | solution.py:345
  54.5 7.3 %collective-permute-start.20 = (bf16[64,1152]{1,0:T(8,128)(2,1)S(1)}, bf16[64,1152]{1,0:T(8,128)(2,1)S(1)}, u32[]{:S(2)}, u32[]{:S(2)}) collective-permute-start(bf16[64,1152]{1,0:T(8,128)(2,1)S(1)} %get-tuple-element.79.refs_1_), channel_id=1, source_target_pairs={{0,24},{4,28},{8,0},{12,4},{16,8},{20,12},{24,16},{28,20},{1,25},{... | collective-permute-start | bytes 442376 | tf_op jit(solution)/shard_map/ppermute | solution.py:345
  55.8 11.1 %collective-permute-start.17 = (bf16[288,384]{1,0:T(8,128)(2,1)S(1)}, bf16[288,384]{1,0:T(8,128)(2,1)S(1)}, u32[]{:S(2)}, u32[]{:S(2)}) collective-permute-start(bf16[288,384]{1,0:T(8,128)(2,1)S(1)} %get-tuple-element.76), channel_id=1, source_target_pairs={{1,2},{2,1},{0,0},{3,3},{5,6},{6,5},{4,4},{7,7},{9,10},{10,9},{8,8... | collective-permute-start | bytes 663560 | tf_op jit(solution)/shard_map/ppermute | solution.py:336
  56.5 12.1 %collective-permute-start.18 = (bf16[288,384]{1,0:T(8,128)(2,1)S(1)}, bf16[288,384]{1,0:T(8,128)(2,1)S(1)}, u32[]{:S(2)}, u32[]{:S(2)}) collective-permute-start(bf16[288,384]{1,0:T(8,128)(2,1)S(1)} %get-tuple-element.77), channel_id=1, source_target_pairs={{1,3},{2,0},{0,1},{3,2},{5,7},{6,4},{4,5},{7,6},{9,11},{10,8},{8,9... | collective-permute-start | bytes 663560 | tf_op jit(solution)/shard_map/ppermute | solution.py:336
  59.1 6.2 %collective-permute-start.21 = (bf16[64,1152]{1,0:T(8,128)(2,1)S(1)}, bf16[64,1152]{1,0:T(8,128)(2,1)S(1)}, u32[]{:S(2)}, u32[]{:S(2)}) collective-permute-start(bf16[64,1152]{1,0:T(8,128)(2,1)S(1)} %get-tuple-element.80.refs_2_), channel_id=1, source_target_pairs={{0,24},{4,28},{8,0},{12,4},{16,8},{20,12},{24,16},{28,20},{1,25},{... | collective-permute-start | bytes 442376 | tf_op jit(solution)/shard_map/ppermute | solution.py:345
  61.8 5.1 %collective-permute-start.22 = (bf16[64,1152]{1,0:T(8,128)(2,1)S(1)}, bf16[64,1152]{1,0:T(8,128)(2,1)S(1)}, u32[]{:S(2)}, u32[]{:S(2)}) collective-permute-start(bf16[64,1152]{1,0:T(8,128)(2,1)S(1)} %get-tuple-element.81.refs_3_), channel_id=1, source_target_pairs={{0,24},{4,28},{8,0},{12,4},{16,8},{20,12},{24,16},{28,20},{1,25},{... | collective-permute-start | bytes 442376 | tf_op jit(solution)/shard_map/ppermute | solution.py:345
  65.2 7.9 %collective-permute-start.25 = (bf16[64,1152]{1,0:T(8,128)(2,1)S(1)}, bf16[64,1152]{1,0:T(8,128)(2,1)S(1)}, u32[]{:S(2)}, u32[]{:S(2)}) collective-permute-start(bf16[64,1152]{1,0:T(8,128)(2,1)S(1)} %get-tuple-element.78.refs_0_), channel_id=1, source_target_pairs={{0,4},{4,0},{8,12},{12,8},{16,20},{20,16},{24,28},{28,24},{1,5},{5... | collective-permute-start | bytes 442376 | tf_op jit(solution)/shard_map/ppermute | solution.py:339
  66.9 6.8 %collective-permute-start.26 = (bf16[64,1152]{1,0:T(8,128)(2,1)S(1)}, bf16[64,1152]{1,0:T(8,128)(2,1)S(1)}, u32[]{:S(2)}, u32[]{:S(2)}) collective-permute-start(bf16[64,1152]{1,0:T(8,128)(2,1)S(1)} %get-tuple-element.79.refs_1_), channel_id=1, source_target_pairs={{0,4},{4,0},{8,12},{12,8},{16,20},{20,16},{24,28},{28,24},{1,5},{5... | collective-permute-start | bytes 442376 | tf_op jit(solution)/shard_map/ppermute | solution.py:339
  69.0 11.1 %collective-permute-start.23 = (bf16[288,768]{1,0:T(8,128)(2,1)S(1)}, bf16[288,768]{1,0:T(8,128)(2,1)S(1)}, u32[]{:S(2)}, u32[]{:S(2)}) collective-permute-start(bf16[288,768]{1,0:T(8,128)(2,1)S(1)} %get-tuple-element.83), channel_id=1, source_target_pairs={{1,2},{2,1},{0,0},{3,3},{5,6},{6,5},{4,4},{7,7},{9,10},{10,9},{8,8... | collective-permute-start | bytes 1327112 | tf_op jit(solution)/shard_map/ppermute | solution.py:336
  69.7 22.5 %collective-permute-start.24 = (bf16[288,768]{1,0:T(8,128)(2,1)S(1)}, bf16[288,768]{1,0:T(8,128)(2,1)S(1)}, u32[]{:S(2)}, u32[]{:S(2)}) collective-permute-start(bf16[288,768]{1,0:T(8,128)(2,1)S(1)} %get-tuple-element.84), channel_id=1, source_target_pairs={{1,3},{2,0},{0,1},{3,2},{5,7},{6,4},{4,5},{7,6},{9,11},{10,8},{8,9... | collective-permute-start | bytes 1327112 | tf_op jit(solution)/shard_map/ppermute | solution.py:336
  73.2 1.4 %collective-permute-start.27 = (bf16[64,1152]{1,0:T(8,128)(2,1)S(1)}, bf16[64,1152]{1,0:T(8,128)(2,1)S(1)}, u32[]{:S(2)}, u32[]{:S(2)}) collective-permute-start(bf16[64,1152]{1,0:T(8,128)(2,1)S(1)} %get-tuple-element.80.refs_2_), channel_id=1, source_target_pairs={{0,4},{4,0},{8,12},{12,8},{16,20},{20,16},{24,28},{28,24},{1,5},{5... | collective-permute-start | bytes 442376 | tf_op jit(solution)/shard_map/ppermute | solution.py:339
  73.2 1.6 %collective-permute-start.28 = (bf16[64,1152]{1,0:T(8,128)(2,1)S(1)}, bf16[64,1152]{1,0:T(8,128)(2,1)S(1)}, u32[]{:S(2)}, u32[]{:S(2)}) collective-permute-start(bf16[64,1152]{1,0:T(8,128)(2,1)S(1)} %get-tuple-element.81.refs_3_), channel_id=1, source_target_pairs={{0,4},{4,0},{8,12},{12,8},{16,20},{20,16},{24,28},{28,24},{1,5},{5... | collective-permute-start | bytes 442376 | tf_op jit(solution)/shard_map/ppermute | solution.py:339
  73.7 1.4 %collective-permute-start.29 = (bf16[64,1152]{1,0:T(8,128)(2,1)S(1)}, bf16[64,1152]{1,0:T(8,128)(2,1)S(1)}, u32[]{:S(2)}, u32[]{:S(2)}) collective-permute-start(bf16[64,1152]{1,0:T(8,128)(2,1)S(1)} %collective-permute-done.19.rest_2_.refs_12_), channel_id=1, source_target_pairs={{0,4},{4,0},{8,12},{12,8},{16,20},{20,16},{24,28},{28,24},{1,5},{5... | collective-permute-start | bytes 442376 | tf_op jit(solution)/shard_map/ppermute | solution.py:339
  74.5 1.4 %collective-permute-start.30 = (bf16[64,1152]{1,0:T(8,128)(2,1)S(1)}, bf16[64,1152]{1,0:T(8,128)(2,1)S(1)}, u32[]{:S(2)}, u32[]{:S(2)}) collective-permute-start(bf16[64,1152]{1,0:T(8,128)(2,1)S(1)} %collective-permute-done.20.rest_3_.refs_13_), channel_id=1, source_target_pairs={{0,4},{4,0},{8,12},{12,8},{16,20},{20,16},{24,28},{28,24},{1,5},{5... | collective-permute-start | bytes 442376 | tf_op jit(solution)/shard_map/ppermute | solution.py:339
  74.7 1.4 %collective-permute-start.31 = (bf16[64,1152]{1,0:T(8,128)(2,1)S(1)}, bf16[64,1152]{1,0:T(8,128)(2,1)S(1)}, u32[]{:S(2)}, u32[]{:S(2)}) collective-permute-start(bf16[64,1152]{1,0:T(8,128)(2,1)S(1)} %collective-permute-done.21.rest_4_.refs_14_), channel_id=1, source_target_pairs={{0,4},{4,0},{8,12},{12,8},{16,20},{20,16},{24,28},{28,24},{1,5},{5... | collective-permute-start | bytes 442376 | tf_op jit(solution)/shard_map/ppermute | solution.py:339
  (4 other events, 44.6 us)

commit v7 on v6

--- a/solution.py
+++ b/solution.py
@@ -10,8 +10,8 @@
 STEPS = 3
 EPS = 1e-06
 SHARES = (1, 2)
-UNIT_PARTS = 4
-TEXT_PARTS = 4
+UNIT_PARTS = 1
+TEXT_PARTS = 2
 VMEM_BYTES = 24 * 1024 * 1024
 BF16, F32 = jnp.bfloat16, jnp.float32
 
@@ -31,14 +31,13 @@
 IN_HBM = pl.BlockSpec(memory_space=pltpu.HBM)
 
 
-def place(n_dp):
+def place():
     where = lax.axis_index("dp")
-    column = lax.rem(lax.div(where, 2), 2)
-    return lax.axis_index("fsdp"), lax.rem(where, 2), lax.div(where, n_dp // 2), column
-
-
-def cut_kernel(n_dp, short, own, whole, part, sem):
-    _, core, _, column = place(n_dp)
+    return lax.axis_index("fsdp"), lax.rem(where, 2), lax.rem(lax.div(where, 2), 2)
+
+
+def cut_kernel(short, own, whole, part, sem):
+    _, core, column = place()
     half = whole.shape[0]
     first = pltpu.make_async_copy(
         own.at[pl.ds(pl.multiple_of(core * half, 16), half), :], whole, sem.at[0]
@@ -51,14 +50,14 @@
     second.wait()
 
 
-def cut(n_dp, short, own):
+def cut(short, own):
     half, width = own.shape[0] // 2, own.shape[1]
     outs = (
         jax.ShapeDtypeStruct((half, width), BF16),
         jax.ShapeDtypeStruct((short, width), BF16),
     )
     return pl.pallas_call(
-        functools.partial(cut_kernel, n_dp, short),
+        functools.partial(cut_kernel, short),
         out_shape=outs,
         in_specs=[IN_HBM],
         out_specs=spaces(2),
@@ -69,10 +68,10 @@
     )(own)
 
 
-def prepare_kernel(n_dp, t0, twin0, t2, sharp, bias, *rest):
+def prepare_kernel(t0, twin0, t2, sharp, bias, *rest):
     twin2, (units, scalars) = rest[:TEXT_PARTS], rest[TEXT_PARTS:]
     rows = t0.shape[0]
-    _, core, _, _ = place(n_dp)
+    _, core, _ = place()
     scalars[0:1, :] = jnp.broadcast_to(sharp[...], (1, scalars.shape[1]))
     scalars[1:2, :] = jnp.broadcast_to(bias[...], (1, scalars.shape[1]))
 
@@ -92,10 +91,10 @@
     pl.when(core == 1)(lambda: fill(rows, twin0))
 
 
-def prepare(n_dp, t0, twin0, t2, sharp, bias, twin2):
+def prepare(t0, twin0, t2, sharp, bias, twin2):
     rows, width = t0.shape
     return pl.pallas_call(
-        functools.partial(prepare_kernel, n_dp),
+        prepare_kernel,
         out_shape=(
             jax.ShapeDtypeStruct((STEPS * rows, width), BF16),
             jax.ShapeDtypeStruct((8, 128), F32),
@@ -108,17 +107,22 @@
     )(t0, twin0, t2, sharp, bias, *twin2)
 
 
-def turn_kernel(x, x_t):
+def turn_kernel(depth, x, x_t, outer_t):
     x_t[...] = x[...].T
-
-
-def turned(x):
-    out = jax.ShapeDtypeStruct(x.shape[::-1], BF16)
-    return pl.pallas_call(
-        turn_kernel,
-        out_shape=out,
+    start = jnp.where(lax.axis_index("fsdp") == 0, depth, 0)
+    outer_t[...] = x_t[pl.ds(pl.multiple_of(start, 16), outer_t.shape[0]), :]
+
+
+def turned(depth, x):
+    rows, width = x.shape
+    return pl.pallas_call(
+        functools.partial(turn_kernel, depth),
+        out_shape=(
+            jax.ShapeDtypeStruct((width, rows), BF16),
+            jax.ShapeDtypeStruct((width - depth, rows), BF16),
+        ),
         in_specs=spaces(1),
-        out_specs=pl.BlockSpec(memory_space=pltpu.VMEM),
+        out_specs=tuple(spaces(2)),
         compiler_params=params(),
         cost_estimate=cost(),
         name="turned",
@@ -140,22 +144,21 @@
     return coefficient, scale * jnp.sum(coefficient.astype(F32) * product, axis=-1, keepdims=True)
 
 
-def picture_kernel(n_dp, x, x_t, units, scalars, own, *rest):
+def picture_kernel(x, x_t, units, scalars, own, *rest):
     pieces, outs = rest[:8], rest[8 : 8 + len(SHARES)]
     unit_parts = rest[8 + len(SHARES) : -4]
     grad, unit, w, proj = rest[-4:]
-    part, core, side, column = place(n_dp)
+    part, core, column = place()
     depth = own.shape[0]
     half = depth // 2
     short = pieces[2].shape[0]
     rest_rows = half - short
     rows = x.shape[0]
-    step = 1 - 2 * side
     w[pl.ds(pl.multiple_of(part * depth, 16), depth), :] = own[...]
     for twin in (0, 1):
         lane = core if twin == 0 else 1 - core
-        straight, crossed, two, two_crossed = pieces[4 * twin : 4 * twin + 4]
-        for piece, from_part in ((straight, part + 4 - step), (crossed, part + 4 + step)):
+        plus, minus, two, two_crossed = pieces[4 * twin : 4 * twin + 4]
+        for piece, from_part in ((plus, part + 3), (minus, part + 1)):
             start = pl.multiple_of(lax.rem(from_part, 4) * depth + lane * half, 16)
             w[pl.ds(start, half), :] = piece[...]
         base = lax.rem(part + 2, 4) * depth + lane * half
@@ -197,7 +200,7 @@
             begin = stop
 
 
-def picture_side(n_dp, x, x_t, units, scalars, own, pieces):
+def picture_side(x, x_t, units, scalars, own, pieces):
     rows, width = x.shape
     depth = own.shape[0]
     out = jax.ShapeDtypeStruct((rows, width), BF16)
@@ -206,7 +209,7 @@
     part = jax.ShapeDtypeStruct((rows // UNIT_PARTS, width), BF16)
     outs = outs + (part,) * UNIT_PARTS + (out,)
     return pl.pallas_call(
-        functools.partial(picture_kernel, n_dp),
+        picture_kernel,
         out_shape=outs,
         in_specs=spaces(13),
         out_specs=spaces(len(outs)),
@@ -221,10 +224,10 @@
     )(x, x_t, units, scalars, own, *pieces)
 
 
-def text_kernel(n_dp, text, scalars, *refs):
+def text_kernel(text, scalars, *refs):
     blocks, (out, done, units) = refs[:-3], refs[-3:]
     rows = text.shape[0]
-    _, core, _, _ = place(n_dp)
+    _, core, _ = place()
     done[...] = jnp.zeros_like(done)
     size = blocks[0].shape[0]
     for k in range(UNIT_PARTS):
@@ -248,10 +251,10 @@
     out[...] = slope * (scale * inverse) - values * (along * inverse * inverse)
 
 
-def text_side(n_dp, text, scalars, *units):
+def text_side(text, scalars, *units):
     rows, width = text.shape
     return pl.pallas_call(
-        functools.partial(text_kernel, n_dp),
+        text_kernel,
         out_shape=(jax.ShapeDtypeStruct((rows, width), F32), jax.ShapeDtypeStruct((8, 128), F32)),
         in_specs=spaces(2 + 4 * UNIT_PARTS),
         out_specs=tuple(spaces(2)),
@@ -276,9 +279,10 @@
     @pl.when(inner)
     def _():
         other = arrived[:rows, :]
+        first = jnp.where(part == 1, 1, 0)
         for block, out in ((3 - part, near), (lax.rem(part + 2, 4), far), (part, kept)):
             both = product(block) + jnp.dot(
-                rows_of(far_t, block, depth), other, preferred_element_type=F32
+                rows_of(far_t, block - first, depth), other, preferred_element_type=F32
             )
             out[...] = both.astype(out.dtype)
 
@@ -329,8 +333,6 @@
     depth, width = w.shape
     half = depth // 2
     short = (half // 2 + 15) // 16 * 16
-    core = lax.rem(lax.axis_index("dp"), 2)
-    side = n_dp // 2
 
     def along(value, pairs):
         return lax.ppermute(value, "fsdp", pairs)
@@ -338,42 +340,31 @@
     def across(value):
         return lax.ppermute(value, "dp", [(d, d ^ 1) for d in range(n_dp)])
 
-    def over(value):
-        return lax.ppermute(value, "dp", [(d, (d + side) % n_dp) for d in range(n_dp)])
-
     def shifted(value, by):
         return lax.ppermute(value, "dp", [(d, (d + by) % n_dp) for d in range(n_dp)])
 
     sharp, bias = sharp.reshape(1, 1), bias.reshape(1, 1)
     swap = [(0, 1), (1, 0), (2, 3), (3, 2)]
-    whole, piece = cut(n_dp, short, w)
+    whole, piece = cut(short, w)
     whole, piece, text = lax.optimization_barrier((whole, piece, text))
-    turns = [
-        (d * n_fsdp + f, d * n_fsdp + (f + (1 if d < side else n_fsdp - 1)) % n_fsdp)
-        for d in range(n_dp)
-        for f in range(n_fsdp)
-    ]
-    straight = lax.ppermute(whole, ("dp", "fsdp"), turns)
+    two = along(piece, [(f, (f + 2) % n_fsdp) for f in range(n_fsdp)])
+    plus = along(whole, [(f, (f + 1) % n_fsdp) for f in range(n_fsdp)])
+    minus = along(whole, [(f, (f - 1) % n_fsdp) for f in range(n_fsdp)])
     text2 = shifted(text, 2)
-    piece, straight = lax.optimization_barrier((piece, straight))
-    crossed = over(straight)
-    two = along(piece, [(f, (f + 2) % n_fsdp) for f in range(n_fsdp)])
-    two, x = lax.optimization_barrier((two, x))
+    x_t, outer_t = turned(depth, x)
+    two, outer_t, text2 = lax.optimization_barrier((two, outer_t, text2))
     two_crossed = lax.ppermute(two, "dp", [(d, d ^ 2) for d in range(n_dp)])
-    far_x = along(x, swap)
-    x_t = turned(x)
-    crossed, x_t, text2 = lax.optimization_barrier((crossed, x_t, text2))
+    far_t = along(outer_t, swap)
     size = text.shape[0] // TEXT_PARTS
     twin2 = [across(text2[k * size : (k + 1) * size]) for k in range(TEXT_PARTS)]
-    two_crossed, *twin2 = lax.optimization_barrier((two_crossed, *twin2))
-    units, scalars = prepare(n_dp, text, across(text), text2, sharp, bias, twin2)
-    two_crossed, units, scalars = lax.optimization_barrier((two_crossed, units, scalars))
-    pieces = [straight, crossed, two, two_crossed]
+    plus, *twin2 = lax.optimization_barrier((plus, *twin2))
+    units, scalars = prepare(text, across(text), text2, sharp, bias, twin2)
+    pieces = [plus, minus, two, two_crossed]
+    *pieces, units, scalars, x_t = lax.optimization_barrier((*pieces, units, scalars, x_t))
     pieces = pieces + [across(piece) for piece in pieces]
-    results = picture_side(n_dp, x, x_t, units, scalars, w, pieces)
+    results = picture_side(x, x_t, units, scalars, w, pieces)
     outward, unit, grad = list(results[: len(SHARES)]), results[len(SHARES) : -1], results[-1]
-    grad, far_x = lax.optimization_barrier((grad, far_x))
-    far_t = turned(far_x)
+    grad, far_t = lax.optimization_barrier((grad, far_t))
     outward[0], far_t = lax.optimization_barrier((outward[0], far_t))
 
     arrived = []
@@ -391,7 +382,7 @@
         terms.append((begin, width, kept, near, far))
         begin += block.shape[1]
     twin0, twin2 = [across(u) for u in unit], [across(u) for u in unit2]
-    text_grad, done = text_side(n_dp, text, scalars, *unit, *twin0, *twin2, *unit2)
+    text_grad, done = text_side(text, scalars, *unit, *twin0, *twin2, *unit2)
     head = total(*terms[0], [])
     for term in terms[1:]:
         head = total(*term, [head, done])

time: 93.5 us -> 91.7 us (0.981)
  Pallas kernels: 11.6 us -> 9.37 us
  waiting for transfers between devices: 47.4 us -> 45.8 us
  local copies, waits for them, and re-layouts: 1.14 us -> 2.21 us
  starting transfers between devices: 30.9 us -> 31.9 us
    ppermute x8 -> x10, waiting for transfers between devices: 28.1 us -> 41.8 us  [along(): return lax.ppermute(value, 'fsdp', pairs)]
    ppermute x8 -> x10, starting transfers between devices: 13 us -> 23.7 us  [along(): return lax.ppermute(value, 'fsdp', pairs)]
    ppermute x2 -> x0, waiting for transfers between devices: 9.57 us -> none  [the longest x1 8.33 us: line_body(): straight = lax.ppermute(whole, ('dp', 'fsdp'), turns)]
    ppermute x5 -> x2, starting transfers between devices: 9.23 us -> 4.54 us  [shifted(): lax.ppermute(value, 'dp', [(d, (d + by) % n_dp) for d in range(n_dp)])]
    ppermute x2 -> x0, starting transfers between devices: 3.85 us -> none  [the longest x1 3.08 us: line_body(): straight = lax.ppermute(whole, ('dp', 'fsdp'), turns)]
    ppermute x17 -> x9, waiting for transfers between devices: 4.09 us -> 1.63 us  [across(): return lax.ppermute(value, 'dp', [(d, d ^ 1) for d in range(n_dp)])]
    pallas_call x6 -> x5, Pallas kernels: 9.17 us -> 6.91 us  [the longest x1 2.86 us: picture_side(): pl.pallas_call(picture_kernel, out_shape=outs, in_specs=spaces(13), out_s...]
    ppermute x1, waiting for transfers between devices: 2.16 us -> 0.01 us  [line_body(): two_crossed = lax.ppermute(two, 'dp', [(d, d ^ 2) for d in range(n_dp)])]
  transfers between devices with their start and end apart: 33 -> 22, of which waited for: 17 -> 10; matrix products, arithmetic and copies ran while one was open for 0% -> 0% of each run, Pallas kernels for 11% -> 9%
where the time goes in v7:
time: 91.7 us; the launch traced here: 91.5 us
  waiting for transfers between devices  45.8 us (50%)
  starting transfers between devices  31.9 us (35%)
  Pallas kernels  9.37 us (10%)
  local copies, waits for them, and re-layouts  2.21 us (2%)
  between operations  2.12 us (2%)
    ppermute x10, waiting for transfers between devices, along(): return lax.ppermute(value, 'fsdp', pairs)  41.8 us
    ppermute x10, starting transfers between devices, along(): return lax.ppermute(value, 'fsdp', pairs)  23.7 us
    ppermute x2, starting transfers between devices, shifted(): lax.ppermute(value, 'dp', [(d, (d + by) % n_dp) for d in range(n_dp)])  4.54 us
    pallas_call x1, Pallas kernels, picture_side(): pl.pallas_call(picture_kernel, out_shape=outs, in_specs=spaces(13), out_s...  2.86 us
    pallas_call x1, Pallas kernels, text_side(): pl.pallas_call(text_kernel, out_shape=(jax.ShapeDtypeStruct((rows, width)...  2.76 us
    ppermute x2, waiting for transfers between devices, shifted(): lax.ppermute(value, 'dp', [(d, (d + by) % n_dp) for d in range(n_dp)])  2.39 us
    unnamed x10, local copies, waits for them, and re-layouts  2.17 us
    ppermute x9, starting transfers between devices, across(): return lax.ppermute(value, 'dp', [(d, d ^ 1) for d in range(n_dp)])  2.16 us
  transfers between devices with their start and end apart: 22, of which 10 were waited for; matrix products, arithmetic and copies ran while one was open for 0% of the time, Pallas kernels for 9%

profile of v7, /device:TPU:0, one launch (start us, length us, event | category | flops | bytes accessed | tf_op | source)
XLA Modules:
  0.0 91.5 jit_solution(1380351856237960389)
XLA Ops:
  0.6 1.1 %copy-done = bf16[288,1152]{1,0:T(8,128)(2,1)S(1)} copy-done((bf16[288,1152]{1,0:T(8,128)(2,1)S(1)}, bf16[288,1152]{1,0:T(8,128)(2,1)}, u32[]{:S(2)}) %copy-start) | copy-done | bytes 663576
  2.1 3.0 %collective-permute-start.2 = (bf16[256,1152]{1,0:T(8,128)(2,1)}, bf16[256,1152]{1,0:T(8,128)(2,1)S(1)}, u32[]{:S(2)}, u32[]{:S(2)}) collective-permute-start(bf16[256,1152]{1,0:T(8,128)(2,1)} %text), channel_id=1, source_target_pairs={{0,8},{4,12},{8,16},{12,20},{16,24},{20,28},{24,0},{28,4},{1,9},{5... | collective-permute-start | bytes 1769480 | tf_op jit(solution)/shard_map/ppermute | solution.py:344
  5.1 2.6 %collective-permute-start.1 = (bf16[80,1152]{1,0:T(8,128)(2,1)S(1)}, bf16[80,1152]{1,0:T(8,128)(2,1)S(1)}, u32[]{:S(2)}, u32[]{:S(2)}) collective-permute-start(bf16[80,1152]{1,0:T(8,128)(2,1)S(1)} %get-tuple-element.45), channel_id=1, source_target_pairs={{0,2},{1,3},{2,0},{3,1},{4,6},{5,7},{6,4},{7,5},{8,10},{9,11},{10,... | collective-permute-start | bytes 552968 | tf_op jit(solution)/shard_map/ppermute | solution.py:338
  7.7 1.3 %collective-permute-start.5 = (bf16[144,1152]{1,0:T(8,128)(2,1)S(1)}, bf16[144,1152]{1,0:T(8,128)(2,1)S(1)}, u32[]{:S(2)}, u32[]{:S(2)}) collective-permute-start(bf16[144,1152]{1,0:T(8,128)(2,1)S(1)} %get-tuple-element.44), channel_id=1, source_target_pairs={{0,3},{1,0},{2,1},{3,2},{4,7},{5,4},{6,5},{7,6},{8,11},{9,8},{10,9... | collective-permute-start | bytes 995336 | tf_op jit(solution)/shard_map/ppermute | solution.py:338
  9.0 0.7 collective-permute-start
  9.7 1.1 %copy-done.2 = bf16[256,1152]{1,0:T(8,128)(2,1)S(1)} copy-done((bf16[256,1152]{1,0:T(8,128)(2,1)S(1)}, bf16[256,1152]{1,0:T(8,128)(2,1)}, u32[]{:S(2)}) %copy-start.2) | copy-done | bytes 589848
  11.0 6.2 %collective-permute-done.1.rest_2_ = bf16[80,1152]{1,0:T(8,128)(2,1)S(1)} collective-permute-done((bf16[80,1152]{1,0:T(8,128)(2,1)S(1)}, bf16[80,1152]{1,0:T(8,128)(2,1)S(1)}, u32[]{:S(2)}, u32[]{:S(2)}) %collective-permute-start.1) | collective-permute-done | bytes 184352 | tf_op jit(solution)/shard_map/ppermute | solution.py:338
  17.2 2.4 %collective-permute-done.2.t2 = bf16[256,1152]{1,0:T(8,128)(2,1)S(1)} collective-permute-done((bf16[256,1152]{1,0:T(8,128)(2,1)}, bf16[256,1152]{1,0:T(8,128)(2,1)S(1)}, u32[]{:S(2)}, u32[]{:S(2)}) %collective-permute-start.2) | collective-permute-done | bytes 589856 | tf_op jit(solution)/shard_map/ppermute | solution.py:344
  19.7 0.5 collective-permute-start.3
  20.2 7.2 %collective-permute-done.rest_0_ = bf16[144,1152]{1,0:T(8,128)(2,1)S(1)} collective-permute-done((bf16[144,1152]{1,0:T(8,128)(2,1)S(1)}, bf16[144,1152]{1,0:T(8,128)(2,1)S(1)}, u32[]{:S(2)}, u32[]{:S(2)}) %collective-permute-start) | collective-permute-done | bytes 331808 | tf_op jit(solution)/shard_map/ppermute | solution.py:338
  27.5 1.5 %collective-permute-start.6 = (bf16[80,1152]{1,0:T(8,128)(2,1)S(1)}, bf16[80,1152]{1,0:T(8,128)(2,1)S(1)}, u32[]{:S(2)}, u32[]{:S(2)}) collective-permute-start(bf16[80,1152]{1,0:T(8,128)(2,1)S(1)} %collective-permute-done.1.rest_2_), channel_id=1, source_target_pairs={{0,8},{4,12},{8,0},{12,4},{16,24},{20,28},{24,16},{28,20},{1,9},{5... | collective-permute-start | bytes 552968 | tf_op jit(solution)/shard_map/ppermute | solution.py:356
  29.0 3.5 %collective-permute-start.12 = (bf16[864,256]{1,0:T(8,128)(2,1)S(1)}, bf16[864,256]{1,0:T(8,128)(2,1)S(1)}, u32[]{:S(2)}, u32[]{:S(2)}) collective-permute-start(bf16[864,256]{1,0:T(8,128)(2,1)S(1)} %get-tuple-element.65), channel_id=1, source_target_pairs={{0,1},{1,0},{2,3},{3,2},{4,5},{5,4},{6,7},{7,6},{8,9},{9,8},{10,11... | collective-permute-start | bytes 1327112 | tf_op jit(solution)/shard_map/ppermute | solution.py:338
  33.8 0.7 prepare.1
  34.6 0.5 collective-permute-start.9
  35.1 0.4 collective-permute-start.11
  35.6 1.4 %collective-permute-done.10.rest_6_ = bf16[80,1152]{1,0:T(8,128)(2,1)S(1)} collective-permute-done((bf16[80,1152]{1,0:T(8,128)(2,1)S(1)}, bf16[80,1152]{1,0:T(8,128)(2,1)S(1)}, u32[]{:S(2)}, u32[]{:S(2)}) %collective-permute-start.10) | collective-permute-done | bytes 184352 | tf_op jit(solution)/shard_map/ppermute | solution.py:341
  37.2 2.9 %picture_side.1 = (bf16[288,384]{1,0:T(8,128)(2,1)S(1)}, bf16[288,768]{1,0:T(8,128)(2,1)S(1)}, bf16[256,1152]{1,0:T(8,128)(2,1)S(1)}, bf16[256,1152]{1,0:T(8,128)(2,1)S(1)}) custom-call(bf16[256,1152]{1,0:T(8,128)(2,1)S(1)} %copy-done.3, bf16[1152,256]{1,0:T(8,128)(2,1)S(1)} %get-tuple-element.56.x_t, bf16[768,1152]{1,0:T(8,128)(2,1)S(1)} %get-tuple-element.57.units, ...), custom_call_target="tpu_custom_call" | custom-call | tf_op jit(solution)/shard_map/picture_side/pallas_call | solution.py:211
  40.1 1.6 %collective-permute-start.17 = (bf16[256,1152]{1,0:T(8,128)(2,1)S(1)}, bf16[256,1152]{1,0:T(8,128)(2,1)S(1)}, u32[]{:S(2)}, u32[]{:S(2)}) collective-permute-start(bf16[256,1152]{1,0:T(8,128)(2,1)S(1)} %get-tuple-element.75.refs_0_), channel_id=1, source_target_pairs={{0,24},{4,28},{8,0},{12,4},{16,8},{20,12},{24,16},{28,20},{1,25},{... | collective-permute-start | bytes 1769480 | tf_op jit(solution)/shard_map/ppermute | solution.py:344
  41.6 0.9 collective-permute-done.12.far_t
  42.5 2.3 %collective-permute-start.13 = (bf16[288,384]{1,0:T(8,128)(2,1)S(1)}, bf16[288,384]{1,0:T(8,128)(2,1)S(1)}, u32[]{:S(2)}, u32[]{:S(2)}) collective-permute-start(bf16[288,384]{1,0:T(8,128)(2,1)S(1)} %get-tuple-element.70), channel_id=1, source_target_pairs={{0,1},{1,0},{2,3},{3,2},{4,5},{5,4},{6,7},{7,6},{8,9},{9,8},{10,11... | collective-permute-start | bytes 663560 | tf_op jit(solution)/shard_map/ppermute | solution.py:338
  44.9 5.4 %collective-permute-done.13.arrived = bf16[288,384]{1,0:T(8,128)(2,1)S(1)} collective-permute-done((bf16[288,384]{1,0:T(8,128)(2,1)S(1)}, bf16[288,384]{1,0:T(8,128)(2,1)S(1)}, u32[]{:S(2)}, u32[]{:S(2)}) %collective-permute-start.13) | collective-permute-done | bytes 221216 | tf_op jit(solution)/shard_map/ppermute | solution.py:338
  50.3 1.7 %collective-permute-start.14 = (bf16[288,768]{1,0:T(8,128)(2,1)S(1)}, bf16[288,768]{1,0:T(8,128)(2,1)S(1)}, u32[]{:S(2)}, u32[]{:S(2)}) collective-permute-start(bf16[288,768]{1,0:T(8,128)(2,1)S(1)} %get-tuple-element.71), channel_id=1, source_target_pairs={{0,1},{1,0},{2,3},{3,2},{4,5},{5,4},{6,7},{7,6},{8,9},{9,8},{10,11... | collective-permute-start | bytes 1327112 | tf_op jit(solution)/shard_map/ppermute | solution.py:338
  52.3 0.7 collective-permute-start.15
  53.0 4.4 %collective-permute-start.16 = (bf16[288,384]{1,0:T(8,128)(2,1)S(1)}, bf16[288,384]{1,0:T(8,128)(2,1)S(1)}, u32[]{:S(2)}, u32[]{:S(2)}) collective-permute-start(bf16[288,384]{1,0:T(8,128)(2,1)S(1)} %get-tuple-element.74), channel_id=1, source_target_pairs={{1,3},{2,0},{0,1},{3,2},{5,7},{6,4},{4,5},{7,6},{9,11},{10,8},{8,9... | collective-permute-start | bytes 663560 | tf_op jit(solution)/shard_map/ppermute | solution.py:338
  57.4 0.5 collective-permute-start.21
  58.0 8.3 %collective-permute-done.16.rest_1_.far = bf16[288,384]{1,0:T(8,128)(2,1)S(1)} collective-permute-done((bf16[288,384]{1,0:T(8,128)(2,1)S(1)}, bf16[288,384]{1,0:T(8,128)(2,1)S(1)}, u32[]{:S(2)}, u32[]{:S(2)}) %collective-permute-start.16) | collective-permute-done | bytes 221216 | tf_op jit(solution)/shard_map/ppermute | solution.py:338
  66.8 0.7 collective-permute-start.18
  67.5 5.8 %collective-permute-start.19 = (bf16[288,768]{1,0:T(8,128)(2,1)S(1)}, bf16[288,768]{1,0:T(8,128)(2,1)S(1)}, u32[]{:S(2)}, u32[]{:S(2)}) collective-permute-start(bf16[288,768]{1,0:T(8,128)(2,1)S(1)} %get-tuple-element.78), channel_id=1, source_target_pairs={{1,3},{2,0},{0,1},{3,2},{5,7},{6,4},{4,5},{7,6},{9,11},{10,8},{8,9... | collective-permute-start | bytes 1327112 | tf_op jit(solution)/shard_map/ppermute | solution.py:338
  73.2 0.8 total.2.rest_0_
  74.1 2.8 %text_side.1 = (f32[256,1152]{1,0:T(8,128)}, f32[8,128]{1,0:T(8,128)S(1)}) custom-call(bf16[256,1152]{1,0:T(8,128)(2,1)S(1)} %copy-done.4, f32[8,128]{1,0:T(8,128)S(1)} %get-tuple-element.58.scalars, bf16[256,1152]{1,0:T(8,128)(2,1)S(1)} %get-tuple-element.75.refs_0_, bf16[256,1152]{1,0:T(8,128)(2,1)S(1)} %collective-permute-done.20.refs_1_, ...), custom_call_target="tpu_custom_call" | custom-call | tf_op jit(solution)/shard_map/text_side/pallas_call | solution.py:256
  76.8 13.6 %collective-permute-done.19.far = bf16[288,768]{1,0:T(8,128)(2,1)S(1)} collective-permute-done((bf16[288,768]{1,0:T(8,128)(2,1)S(1)}, bf16[288,768]{1,0:T(8,128)(2,1)S(1)}, u32[]{:S(2)}, u32[]{:S(2)}) %collective-permute-start.19) | collective-permute-done | bytes 442400 | tf_op jit(solution)/shard_map/ppermute | solution.py:338
  90.4 1.0 %total.3 = f32[1,288,1152]{2,1,0:T(8,128)} custom-call(f32[288,768]{1,0:T(8,128)S(1)} %get-tuple-element.76.kept, bf16[288,768]{1,0:T(8,128)(2,1)S(1)} %collective-permute-done.18.near, bf16[288,768]{1,0:T(8,128)(2,1)S(1)} %collective-permute-done.19.far, f32[1,288,1152]{2,1,0:T(8,128)} %total.2.rest_0_, ...), custom_call_target="tpu_custom_call", output_to_operand_aliasing={{}: (3, {})} | custom-call | tf_op jit(solution)/shard_map/total/pallas_call | solution.py:319
  (32 shorter events, 1.9 us)
Async XLA Ops:
  0.6 1.1 %copy-start = (bf16[288,1152]{1,0:T(8,128)(2,1)S(1)}, bf16[288,1152]{1,0:T(8,128)(2,1)}, u32[]{:S(2)}) copy-start(bf16[288,1152]{1,0:T(8,128)(2,1)} %own.3) | copy-start | bytes 1990660
  1.7 32.1 %copy-start.4 = (bf16[256,1152]{1,0:T(8,128)(2,1)S(1)}, bf16[256,1152]{1,0:T(8,128)(2,1)}, u32[]{:S(2)}) copy-start(bf16[256,1152]{1,0:T(8,128)(2,1)} %text) | copy-start | bytes 1769476
  2.1 17.5 %collective-permute-start.2 = (bf16[256,1152]{1,0:T(8,128)(2,1)}, bf16[256,1152]{1,0:T(8,128)(2,1)S(1)}, u32[]{:S(2)}, u32[]{:S(2)}) collective-permute-start(bf16[256,1152]{1,0:T(8,128)(2,1)} %text), channel_id=1, source_target_pairs={{0,8},{4,12},{8,16},{12,20},{16,24},{20,28},{24,0},{28,4},{1,9},{5... | collective-permute-start | bytes 1769480 | tf_op jit(solution)/shard_map/ppermute | solution.py:344
  5.1 12.1 %collective-permute-start.1 = (bf16[80,1152]{1,0:T(8,128)(2,1)S(1)}, bf16[80,1152]{1,0:T(8,128)(2,1)S(1)}, u32[]{:S(2)}, u32[]{:S(2)}) collective-permute-start(bf16[80,1152]{1,0:T(8,128)(2,1)S(1)} %get-tuple-element.45), channel_id=1, source_target_pairs={{0,2},{1,3},{2,0},{3,1},{4,6},{5,7},{6,4},{7,5},{8,10},{9,11},{10,... | collective-permute-start | bytes 552968 | tf_op jit(solution)/shard_map/ppermute | solution.py:338
  7.7 26.8 %collective-permute-start.5 = (bf16[144,1152]{1,0:T(8,128)(2,1)S(1)}, bf16[144,1152]{1,0:T(8,128)(2,1)S(1)}, u32[]{:S(2)}, u32[]{:S(2)}) collective-permute-start(bf16[144,1152]{1,0:T(8,128)(2,1)S(1)} %get-tuple-element.44), channel_id=1, source_target_pairs={{0,3},{1,0},{2,1},{3,2},{4,7},{5,4},{6,5},{7,6},{8,11},{9,8},{10,9... | collective-permute-start | bytes 995336 | tf_op jit(solution)/shard_map/ppermute | solution.py:338
  9.0 18.4 %collective-permute-start = (bf16[144,1152]{1,0:T(8,128)(2,1)S(1)}, bf16[144,1152]{1,0:T(8,128)(2,1)S(1)}, u32[]{:S(2)}, u32[]{:S(2)}) collective-permute-start(bf16[144,1152]{1,0:T(8,128)(2,1)S(1)} %get-tuple-element.44), channel_id=1, source_target_pairs={{0,1},{1,2},{2,3},{3,0},{4,5},{5,6},{6,7},{7,4},{8,9},{9,10},{10,1... | collective-permute-start | bytes 995336 | tf_op jit(solution)/shard_map/ppermute | solution.py:338
  9.7 24.1 %collective-permute-start.7 = (bf16[256,1152]{1,0:T(8,128)(2,1)}, bf16[256,1152]{1,0:T(8,128)(2,1)S(1)}, u32[]{:S(2)}, u32[]{:S(2)}) collective-permute-start(bf16[256,1152]{1,0:T(8,128)(2,1)} %text), channel_id=1, source_target_pairs={{0,4},{4,0},{8,12},{12,8},{16,20},{20,16},{24,28},{28,24},{1,5},{5... | collective-permute-start | bytes 1769480 | tf_op jit(solution)/shard_map/ppermute | solution.py:341
  9.7 1.1 %copy-start.2 = (bf16[256,1152]{1,0:T(8,128)(2,1)S(1)}, bf16[256,1152]{1,0:T(8,128)(2,1)}, u32[]{:S(2)}) copy-start(bf16[256,1152]{1,0:T(8,128)(2,1)} %x.3) | copy-start | bytes 1769476
  19.6 17.6 %copy-start.1 = (bf16[288,1152]{1,0:T(8,128)(2,1)S(1)}, bf16[288,1152]{1,0:T(8,128)(2,1)}, u32[]{:S(2)}) copy-start(bf16[288,1152]{1,0:T(8,128)(2,1)} %own.3) | copy-start | bytes 1990660
  19.6 17.6 %copy-start.3 = (bf16[256,1152]{1,0:T(8,128)(2,1)S(1)}, bf16[256,1152]{1,0:T(8,128)(2,1)}, u32[]{:S(2)}) copy-start(bf16[256,1152]{1,0:T(8,128)(2,1)} %x.3) | copy-start | bytes 1769476
  19.7 9.3 %collective-permute-start.4 = (bf16[128,1152]{1,0:T(8,128)(2,1)S(1)}, bf16[128,1152]{1,0:T(8,128)(2,1)S(1)}, u32[]{:S(2)}, u32[]{:S(2)}) collective-permute-start(bf16[128,1152]{1,0:T(8,128)(2,1)S(1)} %get-tuple-element.82), channel_id=1, source_target_pairs={{0,4},{4,0},{8,12},{12,8},{16,20},{20,16},{24,28},{28,24},{1,5},{5... | collective-permute-start | bytes 884744 | tf_op jit(solution)/shard_map/ppermute | solution.py:341
  19.7 14.0 %collective-permute-start.3 = (bf16[128,1152]{1,0:T(8,128)(2,1)S(1)}, bf16[128,1152]{1,0:T(8,128)(2,1)S(1)}, u32[]{:S(2)}, u32[]{:S(2)}) collective-permute-start(bf16[128,1152]{1,0:T(8,128)(2,1)S(1)} %get-tuple-element.83), channel_id=1, source_target_pairs={{0,4},{4,0},{8,12},{12,8},{16,20},{20,16},{24,28},{28,24},{1,5},{5... | collective-permute-start | bytes 884744 | tf_op jit(solution)/shard_map/ppermute | solution.py:341
  27.5 7.0 %collective-permute-start.6 = (bf16[80,1152]{1,0:T(8,128)(2,1)S(1)}, bf16[80,1152]{1,0:T(8,128)(2,1)S(1)}, u32[]{:S(2)}, u32[]{:S(2)}) collective-permute-start(bf16[80,1152]{1,0:T(8,128)(2,1)S(1)} %collective-permute-done.1.rest_2_), channel_id=1, source_target_pairs={{0,8},{4,12},{8,0},{12,4},{16,24},{20,28},{24,16},{28,20},{1,9},{5... | collective-permute-start | bytes 552968 | tf_op jit(solution)/shard_map/ppermute | solution.py:356
  29.0 13.6 %collective-permute-start.12 = (bf16[864,256]{1,0:T(8,128)(2,1)S(1)}, bf16[864,256]{1,0:T(8,128)(2,1)S(1)}, u32[]{:S(2)}, u32[]{:S(2)}) collective-permute-start(bf16[864,256]{1,0:T(8,128)(2,1)S(1)} %get-tuple-element.65), channel_id=1, source_target_pairs={{0,1},{1,0},{2,3},{3,2},{4,5},{5,4},{6,7},{7,6},{8,9},{9,8},{10,11... | collective-permute-start | bytes 1327112 | tf_op jit(solution)/shard_map/ppermute | solution.py:338
  34.5 2.7 %collective-permute-start.8 = (bf16[144,1152]{1,0:T(8,128)(2,1)S(1)}, bf16[144,1152]{1,0:T(8,128)(2,1)S(1)}, u32[]{:S(2)}, u32[]{:S(2)}) collective-permute-start(bf16[144,1152]{1,0:T(8,128)(2,1)S(1)} %collective-permute-done.rest_0_), channel_id=1, source_target_pairs={{0,4},{4,0},{8,12},{12,8},{16,20},{20,16},{24,28},{28,24},{1,5},{5... | collective-permute-start | bytes 995336 | tf_op jit(solution)/shard_map/ppermute | solution.py:341
  34.6 2.6 %collective-permute-start.9 = (bf16[144,1152]{1,0:T(8,128)(2,1)S(1)}, bf16[144,1152]{1,0:T(8,128)(2,1)S(1)}, u32[]{:S(2)}, u32[]{:S(2)}) collective-permute-start(bf16[144,1152]{1,0:T(8,128)(2,1)S(1)} %collective-permute-done.5.rest_1_), channel_id=1, source_target_pairs={{0,4},{4,0},{8,12},{12,8},{16,20},{20,16},{24,28},{28,24},{1,5},{5... | collective-permute-start | bytes 995336 | tf_op jit(solution)/shard_map/ppermute | solution.py:341
  35.1 1.9 %collective-permute-start.10 = (bf16[80,1152]{1,0:T(8,128)(2,1)S(1)}, bf16[80,1152]{1,0:T(8,128)(2,1)S(1)}, u32[]{:S(2)}, u32[]{:S(2)}) collective-permute-start(bf16[80,1152]{1,0:T(8,128)(2,1)S(1)} %collective-permute-done.1.rest_2_), channel_id=1, source_target_pairs={{0,4},{4,0},{8,12},{12,8},{16,20},{20,16},{24,28},{28,24},{1,5},{5... | collective-permute-start | bytes 552968 | tf_op jit(solution)/shard_map/ppermute | solution.py:341
  35.1 2.0 %collective-permute-start.11 = (bf16[80,1152]{1,0:T(8,128)(2,1)S(1)}, bf16[80,1152]{1,0:T(8,128)(2,1)S(1)}, u32[]{:S(2)}, u32[]{:S(2)}) collective-permute-start(bf16[80,1152]{1,0:T(8,128)(2,1)S(1)} %collective-permute-done.6.rest_3_), channel_id=1, source_target_pairs={{0,4},{4,0},{8,12},{12,8},{16,20},{20,16},{24,28},{28,24},{1,5},{5... | collective-permute-start | bytes 552968 | tf_op jit(solution)/shard_map/ppermute | solution.py:341
  40.1 17.4 %collective-permute-start.17 = (bf16[256,1152]{1,0:T(8,128)(2,1)S(1)}, bf16[256,1152]{1,0:T(8,128)(2,1)S(1)}, u32[]{:S(2)}, u32[]{:S(2)}) collective-permute-start(bf16[256,1152]{1,0:T(8,128)(2,1)S(1)} %get-tuple-element.75.refs_0_), channel_id=1, source_target_pairs={{0,24},{4,28},{8,0},{12,4},{16,8},{20,12},{24,16},{28,20},{1,25},{... | collective-permute-start | bytes 1769480 | tf_op jit(solution)/shard_map/ppermute | solution.py:344
  42.5 7.8 %collective-permute-start.13 = (bf16[288,384]{1,0:T(8,128)(2,1)S(1)}, bf16[288,384]{1,0:T(8,128)(2,1)S(1)}, u32[]{:S(2)}, u32[]{:S(2)}) collective-permute-start(bf16[288,384]{1,0:T(8,128)(2,1)S(1)} %get-tuple-element.70), channel_id=1, source_target_pairs={{0,1},{1,0},{2,3},{3,2},{4,5},{5,4},{6,7},{7,6},{8,9},{9,8},{10,11... | collective-permute-start | bytes 663560 | tf_op jit(solution)/shard_map/ppermute | solution.py:338
  50.3 16.1 %collective-permute-start.14 = (bf16[288,768]{1,0:T(8,128)(2,1)S(1)}, bf16[288,768]{1,0:T(8,128)(2,1)S(1)}, u32[]{:S(2)}, u32[]{:S(2)}) collective-permute-start(bf16[288,768]{1,0:T(8,128)(2,1)S(1)} %get-tuple-element.71), channel_id=1, source_target_pairs={{0,1},{1,0},{2,3},{3,2},{4,5},{5,4},{6,7},{7,6},{8,9},{9,8},{10,11... | collective-permute-start | bytes 1327112 | tf_op jit(solution)/shard_map/ppermute | solution.py:338
  52.3 5.6 %collective-permute-start.15 = (bf16[288,384]{1,0:T(8,128)(2,1)S(1)}, bf16[288,384]{1,0:T(8,128)(2,1)S(1)}, u32[]{:S(2)}, u32[]{:S(2)}) collective-permute-start(bf16[288,384]{1,0:T(8,128)(2,1)S(1)} %get-tuple-element.73), channel_id=1, source_target_pairs={{1,2},{2,1},{0,0},{3,3},{5,6},{6,5},{4,4},{7,7},{9,10},{10,9},{8,8... | collective-permute-start | bytes 663560 | tf_op jit(solution)/shard_map/ppermute | solution.py:338
  53.0 13.3 %collective-permute-start.16 = (bf16[288,384]{1,0:T(8,128)(2,1)S(1)}, bf16[288,384]{1,0:T(8,128)(2,1)S(1)}, u32[]{:S(2)}, u32[]{:S(2)}) collective-permute-start(bf16[288,384]{1,0:T(8,128)(2,1)S(1)} %get-tuple-element.74), channel_id=1, source_target_pairs={{1,3},{2,0},{0,1},{3,2},{5,7},{6,4},{4,5},{7,6},{9,11},{10,8},{8,9... | collective-permute-start | bytes 663560 | tf_op jit(solution)/shard_map/ppermute | solution.py:338
  57.4 16.6 %collective-permute-start.20 = (bf16[256,1152]{1,0:T(8,128)(2,1)S(1)}, bf16[256,1152]{1,0:T(8,128)(2,1)S(1)}, u32[]{:S(2)}, u32[]{:S(2)}) collective-permute-start(bf16[256,1152]{1,0:T(8,128)(2,1)S(1)} %get-tuple-element.75.refs_0_), channel_id=1, source_target_pairs={{0,4},{4,0},{8,12},{12,8},{16,20},{20,16},{24,28},{28,24},{1,5},{5... | collective-permute-start | bytes 1769480 | tf_op jit(solution)/shard_map/ppermute | solution.py:341
  57.4 16.6 %collective-permute-start.21 = (bf16[256,1152]{1,0:T(8,128)(2,1)S(1)}, bf16[256,1152]{1,0:T(8,128)(2,1)S(1)}, u32[]{:S(2)}, u32[]{:S(2)}) collective-permute-start(bf16[256,1152]{1,0:T(8,128)(2,1)S(1)} %collective-permute-done.17.rest_2_.refs_3_), channel_id=1, source_target_pairs={{0,4},{4,0},{8,12},{12,8},{16,20},{20,16},{24,28},{28,24},{1,5},{5... | collective-permute-start | bytes 1769480 | tf_op jit(solution)/shard_map/ppermute | solution.py:341
  66.8 10.1 %collective-permute-start.18 = (bf16[288,768]{1,0:T(8,128)(2,1)S(1)}, bf16[288,768]{1,0:T(8,128)(2,1)S(1)}, u32[]{:S(2)}, u32[]{:S(2)}) collective-permute-start(bf16[288,768]{1,0:T(8,128)(2,1)S(1)} %get-tuple-element.77), channel_id=1, source_target_pairs={{1,2},{2,1},{0,0},{3,3},{5,6},{6,5},{4,4},{7,7},{9,10},{10,9},{8,8... | collective-permute-start | bytes 1327112 | tf_op jit(solution)/shard_map/ppermute | solution.py:338
  67.5 23.0 %collective-permute-start.19 = (bf16[288,768]{1,0:T(8,128)(2,1)S(1)}, bf16[288,768]{1,0:T(8,128)(2,1)S(1)}, u32[]{:S(2)}, u32[]{:S(2)}) collective-permute-start(bf16[288,768]{1,0:T(8,128)(2,1)S(1)} %get-tuple-element.78), channel_id=1, source_target_pairs={{1,3},{2,0},{0,1},{3,2},{5,7},{6,4},{4,5},{7,6},{9,11},{10,8},{8,9... | collective-permute-start | bytes 1327112 | tf_op jit(solution)/shard_map/ppermute | solution.py:338

commit v8 on v7

--- a/solution.py
+++ b/solution.py
@@ -357,10 +357,9 @@
     far_t = along(outer_t, swap)
     size = text.shape[0] // TEXT_PARTS
     twin2 = [across(text2[k * size : (k + 1) * size]) for k in range(TEXT_PARTS)]
-    plus, *twin2 = lax.optimization_barrier((plus, *twin2))
     units, scalars = prepare(text, across(text), text2, sharp, bias, twin2)
+    plus, minus, units, scalars, x_t = lax.optimization_barrier((plus, minus, units, scalars, x_t))
     pieces = [plus, minus, two, two_crossed]
-    *pieces, units, scalars, x_t = lax.optimization_barrier((*pieces, units, scalars, x_t))
     pieces = pieces + [across(piece) for piece in pieces]
     results = picture_side(x, x_t, units, scalars, w, pieces)
     outward, unit, grad = list(results[: len(SHARES)]), results[len(SHARES) : -1], results[-1]

time: 91.7 us -> 85.4 us (0.931)
  waiting for transfers between devices: 45.8 us -> 39.8 us
    ppermute x10, waiting for transfers between devices: 41.8 us -> 33.8 us  [along(): return lax.ppermute(value, 'fsdp', pairs)]
    ppermute x1, waiting for transfers between devices: 0.01 us -> 2.17 us  [line_body(): two_crossed = lax.ppermute(two, 'dp', [(d, d ^ 2) for d in range(n_dp)])]
  transfers between devices with their start and end apart: 22 -> 22, of which waited for: 10 -> 8; matrix products, arithmetic and copies ran while one was open for 0% -> 0% of each run, Pallas kernels for 9% -> 9%
where the time goes in v8:
time: 85.4 us; the launch traced here: 85.2 us
  waiting for transfers between devices  39.8 us (47%)
  starting transfers between devices  31.7 us (37%)
  Pallas kernels  9.38 us (11%)
  local copies, waits for them, and re-layouts  2.21 us (3%)
  between operations  2.12 us (2%)
    ppermute x10, waiting for transfers between devices, along(): return lax.ppermute(value, 'fsdp', pairs)  33.8 us
    ppermute x10, starting transfers between devices, along(): return lax.ppermute(value, 'fsdp', pairs)  24 us
    ppermute x2, starting transfers between devices, shifted(): lax.ppermute(value, 'dp', [(d, (d + by) % n_dp) for d in range(n_dp)])  4.47 us
    pallas_call x1, Pallas kernels, picture_side(): pl.pallas_call(picture_kernel, out_shape=outs, in_specs=spaces(13), out_s...  2.87 us
    pallas_call x1, Pallas kernels, text_side(): pl.pallas_call(text_kernel, out_shape=(jax.ShapeDtypeStruct((rows, width)...  2.76 us
    ppermute x2, waiting for transfers between devices, shifted(): lax.ppermute(value, 'dp', [(d, (d + by) % n_dp) for d in range(n_dp)])  2.39 us
    ppermute x1, waiting for transfers between devices, line_body(): two_crossed = lax.ppermute(two, 'dp', [(d, d ^ 2) for d in range(n_dp)])  2.17 us
    unnamed x10, local copies, waits for them, and re-layouts  2.17 us
  transfers between devices with their start and end apart: 22, of which 8 were waited for; matrix products, arithmetic and copies ran while one was open for 0% of the time, Pallas kernels for 9%

profile of v8, /device:TPU:0, one launch (start us, length us, event | category | flops | bytes accessed | tf_op | source)
XLA Modules:
  0.0 85.2 jit_solution(10136990859643560583)
XLA Ops:
  0.6 1.1 %copy-done = bf16[288,1152]{1,0:T(8,128)(2,1)S(1)} copy-done((bf16[288,1152]{1,0:T(8,128)(2,1)S(1)}, bf16[288,1152]{1,0:T(8,128)(2,1)}, u32[]{:S(2)}) %copy-start) | copy-done | bytes 663576
  1.7 0.4 cut.1
  2.1 3.0 %collective-permute-start.4 = (bf16[256,1152]{1,0:T(8,128)(2,1)}, bf16[256,1152]{1,0:T(8,128)(2,1)S(1)}, u32[]{:S(2)}, u32[]{:S(2)}) collective-permute-start(bf16[256,1152]{1,0:T(8,128)(2,1)} %text), channel_id=1, source_target_pairs={{0,8},{4,12},{8,16},{12,20},{16,24},{20,28},{24,0},{28,4},{1,9},{5... | collective-permute-start | bytes 1769480 | tf_op jit(solution)/shard_map/ppermute | solution.py:344
  5.1 2.6 %collective-permute-start.3 = (bf16[80,1152]{1,0:T(8,128)(2,1)S(1)}, bf16[80,1152]{1,0:T(8,128)(2,1)S(1)}, u32[]{:S(2)}, u32[]{:S(2)}) collective-permute-start(bf16[80,1152]{1,0:T(8,128)(2,1)S(1)} %get-tuple-element.41), channel_id=1, source_target_pairs={{0,2},{1,3},{2,0},{3,1},{4,6},{5,7},{6,4},{7,5},{8,10},{9,11},{10,... | collective-permute-start | bytes 552968 | tf_op jit(solution)/shard_map/ppermute | solution.py:338
  7.7 1.3 %collective-permute-start.1 = (bf16[144,1152]{1,0:T(8,128)(2,1)S(1)}, bf16[144,1152]{1,0:T(8,128)(2,1)S(1)}, u32[]{:S(2)}, u32[]{:S(2)}) collective-permute-start(bf16[144,1152]{1,0:T(8,128)(2,1)S(1)} %get-tuple-element.39), channel_id=1, source_target_pairs={{0,3},{1,0},{2,1},{3,2},{4,7},{5,4},{6,5},{7,6},{8,11},{9,8},{10,9... | collective-permute-start | bytes 995336 | tf_op jit(solution)/shard_map/ppermute | solution.py:338
  9.0 0.7 collective-permute-start
  9.7 1.1 %copy-done.2 = bf16[256,1152]{1,0:T(8,128)(2,1)S(1)} copy-done((bf16[256,1152]{1,0:T(8,128)(2,1)S(1)}, bf16[256,1152]{1,0:T(8,128)(2,1)}, u32[]{:S(2)}) %copy-start.2) | copy-done | bytes 589848
  11.0 6.2 %collective-permute-done.3.rest_2_ = bf16[80,1152]{1,0:T(8,128)(2,1)S(1)} collective-permute-done((bf16[80,1152]{1,0:T(8,128)(2,1)S(1)}, bf16[80,1152]{1,0:T(8,128)(2,1)S(1)}, u32[]{:S(2)}, u32[]{:S(2)}) %collective-permute-start.3) | collective-permute-done | bytes 184352 | tf_op jit(solution)/shard_map/ppermute | solution.py:338
  17.2 2.4 %collective-permute-done.4.t2 = bf16[256,1152]{1,0:T(8,128)(2,1)S(1)} collective-permute-done((bf16[256,1152]{1,0:T(8,128)(2,1)}, bf16[256,1152]{1,0:T(8,128)(2,1)S(1)}, u32[]{:S(2)}, u32[]{:S(2)}) %collective-permute-start.4) | collective-permute-done | bytes 589856 | tf_op jit(solution)/shard_map/ppermute | solution.py:344
  19.7 0.5 collective-permute-start.5
  20.2 4.4 %collective-permute-start.12 = (bf16[864,256]{1,0:T(8,128)(2,1)S(1)}, bf16[864,256]{1,0:T(8,128)(2,1)S(1)}, u32[]{:S(2)}, u32[]{:S(2)}) collective-permute-start(bf16[864,256]{1,0:T(8,128)(2,1)S(1)} %get-tuple-element.55), channel_id=1, source_target_pairs={{0,1},{1,0},{2,3},{3,2},{4,5},{5,4},{6,7},{7,6},{8,9},{9,8},{10,11... | collective-permute-start | bytes 1327112 | tf_op jit(solution)/shard_map/ppermute | solution.py:338
  24.6 1.5 %collective-permute-start.7 = (bf16[80,1152]{1,0:T(8,128)(2,1)S(1)}, bf16[80,1152]{1,0:T(8,128)(2,1)S(1)}, u32[]{:S(2)}, u32[]{:S(2)}) collective-permute-start(bf16[80,1152]{1,0:T(8,128)(2,1)S(1)} %collective-permute-done.3.rest_2_), channel_id=1, source_target_pairs={{0,8},{4,12},{8,0},{12,4},{16,24},{20,28},{24,16},{28,20},{1,9},{5... | collective-permute-start | bytes 552968 | tf_op jit(solution)/shard_map/ppermute | solution.py:356
  27.4 0.7 prepare.1
  28.2 0.5 collective-permute-start.9
  28.8 2.2 %collective-permute-done.7.rest_3_ = bf16[80,1152]{1,0:T(8,128)(2,1)S(1)} collective-permute-done((bf16[80,1152]{1,0:T(8,128)(2,1)S(1)}, bf16[80,1152]{1,0:T(8,128)(2,1)S(1)}, u32[]{:S(2)}, u32[]{:S(2)}) %collective-permute-start.7) | collective-permute-done | bytes 184352 | tf_op jit(solution)/shard_map/ppermute | solution.py:356
  31.0 1.4 %collective-permute-done.11.rest_7_ = bf16[80,1152]{1,0:T(8,128)(2,1)S(1)} collective-permute-done((bf16[80,1152]{1,0:T(8,128)(2,1)S(1)}, bf16[80,1152]{1,0:T(8,128)(2,1)S(1)}, u32[]{:S(2)}, u32[]{:S(2)}) %collective-permute-start.11) | collective-permute-done | bytes 184352 | tf_op jit(solution)/shard_map/ppermute | solution.py:341
  32.4 2.9 %picture_side.1 = (bf16[288,384]{1,0:T(8,128)(2,1)S(1)}, bf16[288,768]{1,0:T(8,128)(2,1)S(1)}, bf16[256,1152]{1,0:T(8,128)(2,1)S(1)}, bf16[256,1152]{1,0:T(8,128)(2,1)S(1)}) custom-call(bf16[256,1152]{1,0:T(8,128)(2,1)S(1)} %copy-done.3, bf16[1152,256]{1,0:T(8,128)(2,1)S(1)} %get-tuple-element.47.x_t, bf16[768,1152]{1,0:T(8,128)(2,1)S(1)} %get-tuple-element.48.units, ...), custom_call_target="tpu_custom_call" | custom-call | tf_op jit(solution)/shard_map/picture_side/pallas_call | solution.py:211
  35.3 1.5 %collective-permute-start.17 = (bf16[256,1152]{1,0:T(8,128)(2,1)S(1)}, bf16[256,1152]{1,0:T(8,128)(2,1)S(1)}, u32[]{:S(2)}, u32[]{:S(2)}) collective-permute-start(bf16[256,1152]{1,0:T(8,128)(2,1)S(1)} %get-tuple-element.65.refs_0_), channel_id=1, source_target_pairs={{0,24},{4,28},{8,0},{12,4},{16,8},{20,12},{24,16},{28,20},{1,25},{... | collective-permute-start | bytes 1769480 | tf_op jit(solution)/shard_map/ppermute | solution.py:344
  36.9 1.5 %collective-permute-start.13 = (bf16[288,384]{1,0:T(8,128)(2,1)S(1)}, bf16[288,384]{1,0:T(8,128)(2,1)S(1)}, u32[]{:S(2)}, u32[]{:S(2)}) collective-permute-start(bf16[288,384]{1,0:T(8,128)(2,1)S(1)} %get-tuple-element.60), channel_id=1, source_target_pairs={{0,1},{1,0},{2,3},{3,2},{4,5},{5,4},{6,7},{7,6},{8,9},{9,8},{10,11... | collective-permute-start | bytes 663560 | tf_op jit(solution)/shard_map/ppermute | solution.py:338
  38.5 5.9 %collective-permute-done.13.arrived = bf16[288,384]{1,0:T(8,128)(2,1)S(1)} collective-permute-done((bf16[288,384]{1,0:T(8,128)(2,1)S(1)}, bf16[288,384]{1,0:T(8,128)(2,1)S(1)}, u32[]{:S(2)}, u32[]{:S(2)}) %collective-permute-start.13) | collective-permute-done | bytes 221216 | tf_op jit(solution)/shard_map/ppermute | solution.py:338
  44.3 1.3 %collective-permute-start.14 = (bf16[288,768]{1,0:T(8,128)(2,1)S(1)}, bf16[288,768]{1,0:T(8,128)(2,1)S(1)}, u32[]{:S(2)}, u32[]{:S(2)}) collective-permute-start(bf16[288,768]{1,0:T(8,128)(2,1)S(1)} %get-tuple-element.61), channel_id=1, source_target_pairs={{0,1},{1,0},{2,3},{3,2},{4,5},{5,4},{6,7},{7,6},{8,9},{9,8},{10,11... | collective-permute-start | bytes 1327112 | tf_op jit(solution)/shard_map/ppermute | solution.py:338
  45.9 0.7 collective-permute-start.15
  46.6 5.3 %collective-permute-start.16 = (bf16[288,384]{1,0:T(8,128)(2,1)S(1)}, bf16[288,384]{1,0:T(8,128)(2,1)S(1)}, u32[]{:S(2)}, u32[]{:S(2)}) collective-permute-start(bf16[288,384]{1,0:T(8,128)(2,1)S(1)} %get-tuple-element.64), channel_id=1, source_target_pairs={{1,3},{2,0},{0,1},{3,2},{5,7},{6,4},{4,5},{7,6},{9,11},{10,8},{8,9... | collective-permute-start | bytes 663560 | tf_op jit(solution)/shard_map/ppermute | solution.py:338
  51.9 0.5 collective-permute-start.21
  52.4 7.9 %collective-permute-done.16.rest_1_.far = bf16[288,384]{1,0:T(8,128)(2,1)S(1)} collective-permute-done((bf16[288,384]{1,0:T(8,128)(2,1)S(1)}, bf16[288,384]{1,0:T(8,128)(2,1)S(1)}, u32[]{:S(2)}, u32[]{:S(2)}) %collective-permute-start.16) | collective-permute-done | bytes 221216 | tf_op jit(solution)/shard_map/ppermute | solution.py:338
  60.4 0.3 pair_product.3
  60.7 0.7 collective-permute-start.18
  61.4 5.5 %collective-permute-start.19 = (bf16[288,768]{1,0:T(8,128)(2,1)S(1)}, bf16[288,768]{1,0:T(8,128)(2,1)S(1)}, u32[]{:S(2)}, u32[]{:S(2)}) collective-permute-start(bf16[288,768]{1,0:T(8,128)(2,1)S(1)} %get-tuple-element.68), channel_id=1, source_target_pairs={{1,3},{2,0},{0,1},{3,2},{5,7},{6,4},{4,5},{7,6},{9,11},{10,8},{8,9... | collective-permute-start | bytes 1327112 | tf_op jit(solution)/shard_map/ppermute | solution.py:338
  66.9 0.8 total.2.rest_0_
  67.8 2.8 %text_side.1 = (f32[256,1152]{1,0:T(8,128)}, f32[8,128]{1,0:T(8,128)S(1)}) custom-call(bf16[256,1152]{1,0:T(8,128)(2,1)S(1)} %copy-done.4, f32[8,128]{1,0:T(8,128)S(1)} %get-tuple-element.49.scalars, bf16[256,1152]{1,0:T(8,128)(2,1)S(1)} %get-tuple-element.65.refs_0_, bf16[256,1152]{1,0:T(8,128)(2,1)S(1)} %collective-permute-done.20.refs_1_, ...), custom_call_target="tpu_custom_call" | custom-call | tf_op jit(solution)/shard_map/text_side/pallas_call | solution.py:256
  70.5 13.6 %collective-permute-done.19.far = bf16[288,768]{1,0:T(8,128)(2,1)S(1)} collective-permute-done((bf16[288,768]{1,0:T(8,128)(2,1)S(1)}, bf16[288,768]{1,0:T(8,128)(2,1)S(1)}, u32[]{:S(2)}, u32[]{:S(2)}) %collective-permute-start.19) | collective-permute-done | bytes 442400 | tf_op jit(solution)/shard_map/ppermute | solution.py:338
  84.1 1.0 %total.3 = f32[1,288,1152]{2,1,0:T(8,128)} custom-call(f32[288,768]{1,0:T(8,128)S(1)} %get-tuple-element.66.kept, bf16[288,768]{1,0:T(8,128)(2,1)S(1)} %collective-permute-done.18.near, bf16[288,768]{1,0:T(8,128)(2,1)S(1)} %collective-permute-done.19.far, f32[1,288,1152]{2,1,0:T(8,128)} %total.2.rest_0_, ...), custom_call_target="tpu_custom_call", output_to_operand_aliasing={{}: (3, {})} | custom-call | tf_op jit(solution)/shard_map/total/pallas_call | solution.py:319
  (32 shorter events, 1.0 us)
Async XLA Ops:
  0.6 1.1 %copy-start = (bf16[288,1152]{1,0:T(8,128)(2,1)S(1)}, bf16[288,1152]{1,0:T(8,128)(2,1)}, u32[]{:S(2)}) copy-start(bf16[288,1152]{1,0:T(8,128)(2,1)} %own.3) | copy-start | bytes 1990660
  1.7 25.7 %copy-start.4 = (bf16[256,1152]{1,0:T(8,128)(2,1)S(1)}, bf16[256,1152]{1,0:T(8,128)(2,1)}, u32[]{:S(2)}) copy-start(bf16[256,1152]{1,0:T(8,128)(2,1)} %text) | copy-start | bytes 1769476
  2.1 17.5 %collective-permute-start.4 = (bf16[256,1152]{1,0:T(8,128)(2,1)}, bf16[256,1152]{1,0:T(8,128)(2,1)S(1)}, u32[]{:S(2)}, u32[]{:S(2)}) collective-permute-start(bf16[256,1152]{1,0:T(8,128)(2,1)} %text), channel_id=1, source_target_pairs={{0,8},{4,12},{8,16},{12,20},{16,24},{20,28},{24,0},{28,4},{1,9},{5... | collective-permute-start | bytes 1769480 | tf_op jit(solution)/shard_map/ppermute | solution.py:344
  5.1 12.1 %collective-permute-start.3 = (bf16[80,1152]{1,0:T(8,128)(2,1)S(1)}, bf16[80,1152]{1,0:T(8,128)(2,1)S(1)}, u32[]{:S(2)}, u32[]{:S(2)}) collective-permute-start(bf16[80,1152]{1,0:T(8,128)(2,1)S(1)} %get-tuple-element.41), channel_id=1, source_target_pairs={{0,2},{1,3},{2,0},{3,1},{4,6},{5,7},{6,4},{7,5},{8,10},{9,11},{10,... | collective-permute-start | bytes 552968 | tf_op jit(solution)/shard_map/ppermute | solution.py:338
  7.7 20.4 %collective-permute-start.1 = (bf16[144,1152]{1,0:T(8,128)(2,1)S(1)}, bf16[144,1152]{1,0:T(8,128)(2,1)S(1)}, u32[]{:S(2)}, u32[]{:S(2)}) collective-permute-start(bf16[144,1152]{1,0:T(8,128)(2,1)S(1)} %get-tuple-element.39), channel_id=1, source_target_pairs={{0,3},{1,0},{2,1},{3,2},{4,7},{5,4},{6,5},{7,6},{8,11},{9,8},{10,9... | collective-permute-start | bytes 995336 | tf_op jit(solution)/shard_map/ppermute | solution.py:338
  9.0 19.1 %collective-permute-start = (bf16[144,1152]{1,0:T(8,128)(2,1)S(1)}, bf16[144,1152]{1,0:T(8,128)(2,1)S(1)}, u32[]{:S(2)}, u32[]{:S(2)}) collective-permute-start(bf16[144,1152]{1,0:T(8,128)(2,1)S(1)} %get-tuple-element.39), channel_id=1, source_target_pairs={{0,1},{1,2},{2,3},{3,0},{4,5},{5,6},{6,7},{7,4},{8,9},{9,10},{10,1... | collective-permute-start | bytes 995336 | tf_op jit(solution)/shard_map/ppermute | solution.py:338
  9.7 10.5 %collective-permute-start.2 = (bf16[256,1152]{1,0:T(8,128)(2,1)}, bf16[256,1152]{1,0:T(8,128)(2,1)S(1)}, u32[]{:S(2)}, u32[]{:S(2)}) collective-permute-start(bf16[256,1152]{1,0:T(8,128)(2,1)} %text), channel_id=1, source_target_pairs={{0,4},{4,0},{8,12},{12,8},{16,20},{20,16},{24,28},{28,24},{1,5},{5... | collective-permute-start | bytes 1769480 | tf_op jit(solution)/shard_map/ppermute | solution.py:341
  9.7 1.1 %copy-start.2 = (bf16[256,1152]{1,0:T(8,128)(2,1)S(1)}, bf16[256,1152]{1,0:T(8,128)(2,1)}, u32[]{:S(2)}) copy-start(bf16[256,1152]{1,0:T(8,128)(2,1)} %x.3) | copy-start | bytes 1769476
  19.6 12.8 %copy-start.1 = (bf16[288,1152]{1,0:T(8,128)(2,1)S(1)}, bf16[288,1152]{1,0:T(8,128)(2,1)}, u32[]{:S(2)}) copy-start(bf16[288,1152]{1,0:T(8,128)(2,1)} %own.3) | copy-start | bytes 1990660
  19.6 12.8 %copy-start.3 = (bf16[256,1152]{1,0:T(8,128)(2,1)S(1)}, bf16[256,1152]{1,0:T(8,128)(2,1)}, u32[]{:S(2)}) copy-start(bf16[256,1152]{1,0:T(8,128)(2,1)} %x.3) | copy-start | bytes 1769476
  19.7 5.0 %collective-permute-start.6 = (bf16[128,1152]{1,0:T(8,128)(2,1)S(1)}, bf16[128,1152]{1,0:T(8,128)(2,1)S(1)}, u32[]{:S(2)}, u32[]{:S(2)}) collective-permute-start(bf16[128,1152]{1,0:T(8,128)(2,1)S(1)} %get-tuple-element.72), channel_id=1, source_target_pairs={{0,4},{4,0},{8,12},{12,8},{16,20},{20,16},{24,28},{28,24},{1,5},{5... | collective-permute-start | bytes 884744 | tf_op jit(solution)/shard_map/ppermute | solution.py:341
  19.7 7.7 %collective-permute-start.5 = (bf16[128,1152]{1,0:T(8,128)(2,1)S(1)}, bf16[128,1152]{1,0:T(8,128)(2,1)S(1)}, u32[]{:S(2)}, u32[]{:S(2)}) collective-permute-start(bf16[128,1152]{1,0:T(8,128)(2,1)S(1)} %get-tuple-element.73), channel_id=1, source_target_pairs={{0,4},{4,0},{8,12},{12,8},{16,20},{20,16},{24,28},{28,24},{1,5},{5... | collective-permute-start | bytes 884744 | tf_op jit(solution)/shard_map/ppermute | solution.py:341
  20.2 16.7 %collective-permute-start.12 = (bf16[864,256]{1,0:T(8,128)(2,1)S(1)}, bf16[864,256]{1,0:T(8,128)(2,1)S(1)}, u32[]{:S(2)}, u32[]{:S(2)}) collective-permute-start(bf16[864,256]{1,0:T(8,128)(2,1)S(1)} %get-tuple-element.55), channel_id=1, source_target_pairs={{0,1},{1,0},{2,3},{3,2},{4,5},{5,4},{6,7},{7,6},{8,9},{9,8},{10,11... | collective-permute-start | bytes 1327112 | tf_op jit(solution)/shard_map/ppermute | solution.py:338
  24.6 6.3 %collective-permute-start.7 = (bf16[80,1152]{1,0:T(8,128)(2,1)S(1)}, bf16[80,1152]{1,0:T(8,128)(2,1)S(1)}, u32[]{:S(2)}, u32[]{:S(2)}) collective-permute-start(bf16[80,1152]{1,0:T(8,128)(2,1)S(1)} %collective-permute-done.3.rest_2_), channel_id=1, source_target_pairs={{0,8},{4,12},{8,0},{12,4},{16,24},{20,28},{24,16},{28,20},{1,9},{5... | collective-permute-start | bytes 552968 | tf_op jit(solution)/shard_map/ppermute | solution.py:356
  28.1 4.3 %collective-permute-start.8 = (bf16[144,1152]{1,0:T(8,128)(2,1)S(1)}, bf16[144,1152]{1,0:T(8,128)(2,1)S(1)}, u32[]{:S(2)}, u32[]{:S(2)}) collective-permute-start(bf16[144,1152]{1,0:T(8,128)(2,1)S(1)} %collective-permute-done.rest_0_), channel_id=1, source_target_pairs={{0,4},{4,0},{8,12},{12,8},{16,20},{20,16},{24,28},{28,24},{1,5},{5... | collective-permute-start | bytes 995336 | tf_op jit(solution)/shard_map/ppermute | solution.py:341
  28.2 4.2 %collective-permute-start.9 = (bf16[144,1152]{1,0:T(8,128)(2,1)S(1)}, bf16[144,1152]{1,0:T(8,128)(2,1)S(1)}, u32[]{:S(2)}, u32[]{:S(2)}) collective-permute-start(bf16[144,1152]{1,0:T(8,128)(2,1)S(1)} %collective-permute-done.1.rest_1_), channel_id=1, source_target_pairs={{0,4},{4,0},{8,12},{12,8},{16,20},{20,16},{24,28},{28,24},{1,5},{5... | collective-permute-start | bytes 995336 | tf_op jit(solution)/shard_map/ppermute | solution.py:341
  28.7 2.3 %collective-permute-start.10 = (bf16[80,1152]{1,0:T(8,128)(2,1)S(1)}, bf16[80,1152]{1,0:T(8,128)(2,1)S(1)}, u32[]{:S(2)}, u32[]{:S(2)}) collective-permute-start(bf16[80,1152]{1,0:T(8,128)(2,1)S(1)} %collective-permute-done.3.rest_2_), channel_id=1, source_target_pairs={{0,4},{4,0},{8,12},{12,8},{16,20},{20,16},{24,28},{28,24},{1,5},{5... | collective-permute-start | bytes 552968 | tf_op jit(solution)/shard_map/ppermute | solution.py:341
  31.0 1.4 %collective-permute-start.11 = (bf16[80,1152]{1,0:T(8,128)(2,1)S(1)}, bf16[80,1152]{1,0:T(8,128)(2,1)S(1)}, u32[]{:S(2)}, u32[]{:S(2)}) collective-permute-start(bf16[80,1152]{1,0:T(8,128)(2,1)S(1)} %collective-permute-done.7.rest_3_), channel_id=1, source_target_pairs={{0,4},{4,0},{8,12},{12,8},{16,20},{20,16},{24,28},{28,24},{1,5},{5... | collective-permute-start | bytes 552968 | tf_op jit(solution)/shard_map/ppermute | solution.py:341
  35.3 16.6 %collective-permute-start.17 = (bf16[256,1152]{1,0:T(8,128)(2,1)S(1)}, bf16[256,1152]{1,0:T(8,128)(2,1)S(1)}, u32[]{:S(2)}, u32[]{:S(2)}) collective-permute-start(bf16[256,1152]{1,0:T(8,128)(2,1)S(1)} %get-tuple-element.65.refs_0_), channel_id=1, source_target_pairs={{0,24},{4,28},{8,0},{12,4},{16,8},{20,12},{24,16},{28,20},{1,25},{... | collective-permute-start | bytes 1769480 | tf_op jit(solution)/shard_map/ppermute | solution.py:344
  36.9 7.4 %collective-permute-start.13 = (bf16[288,384]{1,0:T(8,128)(2,1)S(1)}, bf16[288,384]{1,0:T(8,128)(2,1)S(1)}, u32[]{:S(2)}, u32[]{:S(2)}) collective-permute-start(bf16[288,384]{1,0:T(8,128)(2,1)S(1)} %get-tuple-element.60), channel_id=1, source_target_pairs={{0,1},{1,0},{2,3},{3,2},{4,5},{5,4},{6,7},{7,6},{8,9},{9,8},{10,11... | collective-permute-start | bytes 663560 | tf_op jit(solution)/shard_map/ppermute | solution.py:338
  44.3 16.0 %collective-permute-start.14 = (bf16[288,768]{1,0:T(8,128)(2,1)S(1)}, bf16[288,768]{1,0:T(8,128)(2,1)S(1)}, u32[]{:S(2)}, u32[]{:S(2)}) collective-permute-start(bf16[288,768]{1,0:T(8,128)(2,1)S(1)} %get-tuple-element.61), channel_id=1, source_target_pairs={{0,1},{1,0},{2,3},{3,2},{4,5},{5,4},{6,7},{7,6},{8,9},{9,8},{10,11... | collective-permute-start | bytes 1327112 | tf_op jit(solution)/shard_map/ppermute | solution.py:338
  45.9 6.5 %collective-permute-start.15 = (bf16[288,384]{1,0:T(8,128)(2,1)S(1)}, bf16[288,384]{1,0:T(8,128)(2,1)S(1)}, u32[]{:S(2)}, u32[]{:S(2)}) collective-permute-start(bf16[288,384]{1,0:T(8,128)(2,1)S(1)} %get-tuple-element.63), channel_id=1, source_target_pairs={{1,2},{2,1},{0,0},{3,3},{5,6},{6,5},{4,4},{7,7},{9,10},{10,9},{8,8... | collective-permute-start | bytes 663560 | tf_op jit(solution)/shard_map/ppermute | solution.py:338
  46.6 13.7 %collective-permute-start.16 = (bf16[288,384]{1,0:T(8,128)(2,1)S(1)}, bf16[288,384]{1,0:T(8,128)(2,1)S(1)}, u32[]{:S(2)}, u32[]{:S(2)}) collective-permute-start(bf16[288,384]{1,0:T(8,128)(2,1)S(1)} %get-tuple-element.64), channel_id=1, source_target_pairs={{1,3},{2,0},{0,1},{3,2},{5,7},{6,4},{4,5},{7,6},{9,11},{10,8},{8,9... | collective-permute-start | bytes 663560 | tf_op jit(solution)/shard_map/ppermute | solution.py:338
  51.9 15.8 %collective-permute-start.20 = (bf16[256,1152]{1,0:T(8,128)(2,1)S(1)}, bf16[256,1152]{1,0:T(8,128)(2,1)S(1)}, u32[]{:S(2)}, u32[]{:S(2)}) collective-permute-start(bf16[256,1152]{1,0:T(8,128)(2,1)S(1)} %get-tuple-element.65.refs_0_), channel_id=1, source_target_pairs={{0,4},{4,0},{8,12},{12,8},{16,20},{20,16},{24,28},{28,24},{1,5},{5... | collective-permute-start | bytes 1769480 | tf_op jit(solution)/shard_map/ppermute | solution.py:341
  51.9 15.8 %collective-permute-start.21 = (bf16[256,1152]{1,0:T(8,128)(2,1)S(1)}, bf16[256,1152]{1,0:T(8,128)(2,1)S(1)}, u32[]{:S(2)}, u32[]{:S(2)}) collective-permute-start(bf16[256,1152]{1,0:T(8,128)(2,1)S(1)} %collective-permute-done.17.rest_2_.refs_3_), channel_id=1, source_target_pairs={{0,4},{4,0},{8,12},{12,8},{16,20},{20,16},{24,28},{28,24},{1,5},{5... | collective-permute-start | bytes 1769480 | tf_op jit(solution)/shard_map/ppermute | solution.py:341
  60.7 9.8 %collective-permute-start.18 = (bf16[288,768]{1,0:T(8,128)(2,1)S(1)}, bf16[288,768]{1,0:T(8,128)(2,1)S(1)}, u32[]{:S(2)}, u32[]{:S(2)}) collective-permute-start(bf16[288,768]{1,0:T(8,128)(2,1)S(1)} %get-tuple-element.67), channel_id=1, source_target_pairs={{1,2},{2,1},{0,0},{3,3},{5,6},{6,5},{4,4},{7,7},{9,10},{10,9},{8,8... | collective-permute-start | bytes 1327112 | tf_op jit(solution)/shard_map/ppermute | solution.py:338
  61.4 22.8 %collective-permute-start.19 = (bf16[288,768]{1,0:T(8,128)(2,1)S(1)}, bf16[288,768]{1,0:T(8,128)(2,1)S(1)}, u32[]{:S(2)}, u32[]{:S(2)}) collective-permute-start(bf16[288,768]{1,0:T(8,128)(2,1)S(1)} %get-tuple-element.68), channel_id=1, source_target_pairs={{1,3},{2,0},{0,1},{3,2},{5,7},{6,4},{4,5},{7,6},{9,11},{10,8},{8,9... | collective-permute-start | bytes 1327112 | tf_op jit(solution)/shard_map/ppermute | solution.py:338

commit v9 on v8

--- a/solution.py
+++ b/solution.py
@@ -10,7 +10,7 @@
 STEPS = 3
 EPS = 1e-06
 SHARES = (1, 2)
-UNIT_PARTS = 1
+CROSS_PARTS = (1,3)
 TEXT_PARTS = 2
 VMEM_BYTES = 24 * 1024 * 1024
 BF16, F32 = jnp.bfloat16, jnp.float32
@@ -146,8 +146,7 @@
 
 def picture_kernel(x, x_t, units, scalars, own, *rest):
     pieces, outs = rest[:8], rest[8 : 8 + len(SHARES)]
-    unit_parts = rest[8 + len(SHARES) : -4]
-    grad, unit, w, proj = rest[-4:]
+    unit, grad, w, proj = rest[-4:]
     part, core, column = place()
     depth = own.shape[0]
     half = depth // 2
@@ -172,9 +171,6 @@
     values = proj[...]
     inverse = 1.0 / jnp.sqrt(jnp.sum(values * values, axis=-1, keepdims=True) + EPS)
     unit[...] = (values * inverse).astype(BF16)
-    size = rows // UNIT_PARTS
-    for k, out in enumerate(unit_parts):
-        out[...] = unit[k * size : (k + 1) * size, :]
     scale = scalars[0:1, 0:1]
     coefficient, along = weights(unit[...], units[...], scale, scalars[1:2, 0:1])
     slope = jnp.dot(coefficient, units[...], preferred_element_type=F32)
@@ -206,15 +202,13 @@
     out = jax.ShapeDtypeStruct((rows, width), BF16)
     sizes = [width * share // sum(SHARES) for share in SHARES]
     outs = tuple(jax.ShapeDtypeStruct((depth, size), BF16) for size in sizes)
-    part = jax.ShapeDtypeStruct((rows // UNIT_PARTS, width), BF16)
-    outs = outs + (part,) * UNIT_PARTS + (out,)
+    outs = outs + (out, out)
     return pl.pallas_call(
         picture_kernel,
         out_shape=outs,
         in_specs=spaces(13),
         out_specs=spaces(len(outs)),
         scratch_shapes=[
-            pltpu.VMEM((rows, width), BF16),
             pltpu.VMEM((width, width), BF16),
             pltpu.VMEM((rows, width), F32),
         ],
@@ -224,23 +218,11 @@
     )(x, x_t, units, scalars, own, *pieces)
 
 
-def text_kernel(text, scalars, *refs):
-    blocks, (out, done, units) = refs[:-3], refs[-3:]
+def text_kernel(text, scalars, u0, u1, u2, out, done, units):
     rows = text.shape[0]
-    _, core, _ = place()
     done[...] = jnp.zeros_like(done)
-    size = blocks[0].shape[0]
-    for k in range(UNIT_PARTS):
-        u0, twin0, twin2, u2 = blocks[k::UNIT_PARTS]
-        for step, block in ((0, u0), (2, u2)):
-            start = step * rows + k * size
-            units[start : start + size, :] = block[...]
-        for lane, block in ((0, twin0), (1, twin2)):
-
-            @pl.when(core == lane)
-            def _():
-                units[rows + k * size : rows + (k + 1) * size, :] = block[...]
-
+    for k, block in enumerate((u0, u1, u2)):
+        units[k * rows : (k + 1) * rows, :] = block[...]
     values = text[...].astype(F32)
     inverse = 1.0 / jnp.sqrt(jnp.sum(values * values, axis=-1, keepdims=True) + EPS)
     scale = scalars[0:1, 0:1]
@@ -251,22 +233,23 @@
     out[...] = slope * (scale * inverse) - values * (along * inverse * inverse)
 
 
-def text_side(text, scalars, *units):
+def text_side(text, scalars, u0, u1, u2):
     rows, width = text.shape
     return pl.pallas_call(
         text_kernel,
         out_shape=(jax.ShapeDtypeStruct((rows, width), F32), jax.ShapeDtypeStruct((8, 128), F32)),
-        in_specs=spaces(2 + 4 * UNIT_PARTS),
+        in_specs=spaces(5),
         out_specs=tuple(spaces(2)),
         scratch_shapes=[pltpu.VMEM((STEPS * rows, width), BF16)],
         compiler_params=params(),
         cost_estimate=cost(),
         name="text_side",
-    )(text, scalars, *units)
-
-
-def pair_kernel(begin, x_t, far_t, grad, arrived, *rest):
-    kept, near, far = rest[-3:]
+    )(text, scalars, u0, u1, u2)
+
+
+def pair_kernel(begin, parts, x_t, far_t, grad, arrived, *rest):
+    outs = rest[-1 - 2 * parts :]
+    kept, nears, fars = outs[0], outs[1 : 1 + parts], outs[1 + parts :]
     rows = grad.shape[0]
     depth, size = arrived.shape
     part = lax.axis_index("fsdp")
@@ -280,53 +263,60 @@
     def _():
         other = arrived[:rows, :]
         first = jnp.where(part == 1, 1, 0)
-        for block, out in ((3 - part, near), (lax.rem(part + 2, 4), far), (part, kept)):
+        for block, out in ((3 - part, nears), (lax.rem(part + 2, 4), fars), (part, [kept])):
             both = product(block) + jnp.dot(
                 rows_of(far_t, block - first, depth), other, preferred_element_type=F32
             )
-            out[...] = both.astype(out.dtype)
+            size = depth // len(out)
+            for k, piece in enumerate(out):
+                piece[...] = both[k * size : (k + 1) * size].astype(piece.dtype)
 
     @pl.when(jnp.logical_not(inner))
     def _():
         kept[...] = product(part) + arrived[...].astype(F32)
-        near[...] = jnp.zeros_like(near)
-        far[...] = jnp.zeros_like(far)
-
-
-def pair_product(begin, x_t, far_t, grad, arrived, after):
-    outs = tuple(jax.ShapeDtypeStruct(arrived.shape, t) for t in (F32, BF16, BF16))
-    return pl.pallas_call(
-        functools.partial(pair_kernel, begin),
+        for piece in nears + fars:
+            piece[...] = jnp.zeros_like(piece)
+
+
+def pair_product(begin, parts, x_t, far_t, grad, arrived, after):
+    depth, size = arrived.shape
+    piece = jax.ShapeDtypeStruct((depth // parts, size), BF16)
+    outs = (jax.ShapeDtypeStruct((depth, size), F32),) + (piece,) * (2 * parts)
+    return pl.pallas_call(
+        functools.partial(pair_kernel, begin, parts),
         out_shape=outs,
         in_specs=spaces(4 + len(after)),
-        out_specs=spaces(3),
+        out_specs=spaces(len(outs)),
         compiler_params=params(),
         cost_estimate=cost(),
         name="pair_product",
     )(x_t, far_t, grad, arrived, *after)
 
 
-def total_kernel(begin, kept, near, far, *rest):
-    out, summed, sem = rest[-3:]
-    summed[...] = kept[...] + near[...].astype(F32) + far[...].astype(F32)
+def total_kernel(begin, parts, kept, *rest):
+    nears, fars, (out, summed, sem) = rest[:parts], rest[parts : 2 * parts], rest[-3:]
+    size = kept.shape[0] // parts
+    for k, (near, far) in enumerate(zip(nears, fars)):
+        at = slice(k * size, (k + 1) * size)
+        summed[at, :] = kept[at, :] + near[...].astype(F32) + far[...].astype(F32)
     copy = pltpu.make_async_copy(summed, out.at[0, :, begin : begin + kept.shape[1]], sem)
     copy.start()
     copy.wait()
 
 
-def total(begin, width, kept, near, far, held):
-    depth = kept.shape[0]
-    return pl.pallas_call(
-        functools.partial(total_kernel, begin),
+def total(begin, width, kept, nears, fars, held):
+    depth, parts = kept.shape[0], len(nears)
+    return pl.pallas_call(
+        functools.partial(total_kernel, begin, parts),
         out_shape=jax.ShapeDtypeStruct((1, depth, width), F32),
-        in_specs=spaces(3) + [IN_HBM] * len(held[:1]) + spaces(len(held[1:])),
+        in_specs=spaces(1 + 2 * parts) + [IN_HBM] * len(held[:1]) + spaces(len(held[1:])),
         out_specs=IN_HBM,
         scratch_shapes=[pltpu.VMEM(kept.shape, F32), pltpu.SemaphoreType.DMA],
-        input_output_aliases={3: 0} if held else {},
+        input_output_aliases={1 + 2 * parts: 0} if held else {},
         compiler_params=params(),
         cost_estimate=cost(),
         name="total",
-    )(kept, near, far, *held)
+    )(kept, *nears, *fars, *held)
 
 
 def line_body(n_dp, n_fsdp, x, text, w, sharp, bias):
@@ -362,7 +352,7 @@
     pieces = [plus, minus, two, two_crossed]
     pieces = pieces + [across(piece) for piece in pieces]
     results = picture_side(x, x_t, units, scalars, w, pieces)
-    outward, unit, grad = list(results[: len(SHARES)]), results[len(SHARES) : -1], results[-1]
+    *outward, unit, grad = results
     grad, far_t = lax.optimization_barrier((grad, far_t))
     outward[0], far_t = lax.optimization_barrier((outward[0], far_t))
 
@@ -371,17 +361,16 @@
         if arrived:
             block, arrived[-1] = lax.optimization_barrier((block, arrived[-1]))
         arrived.append(along(block, swap))
-    unit2 = [shifted(u, -2) for u in unit]
+    unit1, unit2 = shifted(unit, -1), shifted(unit, -2)
     begin, terms, after = 0, [], []
-    for block in arrived:
-        kept, near, far = pair_product(begin, x_t, far_t, grad, block, after)
-        near = along(near, [(1, 2), (2, 1), (0, 0), (3, 3)])
-        far = along(far, [(1, 3), (2, 0), (0, 1), (3, 2)])
-        after = [near, far, *unit2]
-        terms.append((begin, width, kept, near, far))
+    for parts, block in zip(CROSS_PARTS, arrived):
+        kept, *sent = pair_product(begin, parts, x_t, far_t, grad, block, after)
+        nears = [along(n, [(1, 2), (2, 1), (0, 0), (3, 3)]) for n in sent[:parts]]
+        fars = [along(n, [(1, 3), (2, 0), (0, 1), (3, 2)]) for n in sent[parts:]]
+        after = []
+        terms.append((begin, width, kept, nears, fars))
         begin += block.shape[1]
-    twin0, twin2 = [across(u) for u in unit], [across(u) for u in unit2]
-    text_grad, done = text_side(text, scalars, *unit, *twin0, *twin2, *unit2)
+    text_grad, done = text_side(text, scalars, unit, unit1, unit2)
     head = total(*terms[0], [])
     for term in terms[1:]:
         head = total(*term, [head, done])

time: 85.4 us -> 82.4 us (0.965)
  waiting for transfers between devices: 39.8 us -> 33.7 us
  starting transfers between devices: 31.7 us -> 34.6 us
    ppermute x10 -> x14, waiting for transfers between devices: 33.8 us -> 27.7 us  [along(): return lax.ppermute(value, 'fsdp', pairs)]
    ppermute x10 -> x14, starting transfers between devices: 24 us -> 27.2 us  [along(): return lax.ppermute(value, 'fsdp', pairs)]
    ppermute x9 -> x7, starting transfers between devices: 1.73 us -> 1.22 us  [across(): return lax.ppermute(value, 'dp', [(d, d ^ 1) for d in range(n_dp)])]
    ppermute x2 -> x3, starting transfers between devices: 4.47 us -> 4.74 us  [shifted(): lax.ppermute(value, 'dp', [(d, (d + by) % n_dp) for d in range(n_dp)])]
    ppermute x2 -> x3, waiting for transfers between devices: 2.39 us -> 2.39 us  [shifted(): lax.ppermute(value, 'dp', [(d, (d + by) % n_dp) for d in range(n_dp)])]
  transfers between devices with their start and end apart: 22 -> 25, of which waited for: 8 -> 10; matrix products, arithmetic and copies ran while one was open for 0% -> 0% of each run, Pallas kernels for 9% -> 10%
where the time goes in v9:
time: 82.4 us; the launch traced here: 82.1 us
  starting transfers between devices  34.6 us (42%)
  waiting for transfers between devices  33.7 us (41%)
  Pallas kernels  9.37 us (11%)
  local copies, waits for them, and re-layouts  2.21 us (3%)
  between operations  2.14 us (3%)
    ppermute x14, waiting for transfers between devices, along(): return lax.ppermute(value, 'fsdp', pairs)  27.7 us
    ppermute x14, starting transfers between devices, along(): return lax.ppermute(value, 'fsdp', pairs)  27.2 us
    ppermute x3, starting transfers between devices, shifted(): lax.ppermute(value, 'dp', [(d, (d + by) % n_dp) for d in range(n_dp)])  4.74 us
    pallas_call x1, Pallas kernels, picture_side(): pl.pallas_call(picture_kernel, out_shape=outs, in_specs=spaces(13), out_s...  2.85 us
    pallas_call x1, Pallas kernels, text_side(): pl.pallas_call(text_kernel, out_shape=(jax.ShapeDtypeStruct((rows, width)...  2.76 us
    ppermute x3, waiting for transfers between devices, shifted(): lax.ppermute(value, 'dp', [(d, (d + by) % n_dp) for d in range(n_dp)])  2.39 us
    ppermute x1, waiting for transfers between devices, line_body(): two_crossed = lax.ppermute(two, 'dp', [(d, d ^ 2) for d in range(n_dp)])  2.17 us
    unnamed x10, local copies, waits for them, and re-layouts  2.17 us
  transfers between devices with their start and end apart: 25, of which 10 were waited for; matrix products, arithmetic and copies ran while one was open for 0% of the time, Pallas kernels for 10%

profile of v9, /device:TPU:0, one launch (start us, length us, event | category | flops | bytes accessed | tf_op | source)
XLA Modules:
  0.0 82.1 jit_solution(1184497399305229190)
XLA Ops:
  0.6 1.1 %copy-done = bf16[288,1152]{1,0:T(8,128)(2,1)S(1)} copy-done((bf16[288,1152]{1,0:T(8,128)(2,1)S(1)}, bf16[288,1152]{1,0:T(8,128)(2,1)}, u32[]{:S(2)}) %copy-start) | copy-done | bytes 663576
  2.1 3.0 %collective-permute-start.4 = (bf16[256,1152]{1,0:T(8,128)(2,1)}, bf16[256,1152]{1,0:T(8,128)(2,1)S(1)}, u32[]{:S(2)}, u32[]{:S(2)}) collective-permute-start(bf16[256,1152]{1,0:T(8,128)(2,1)} %text), channel_id=1, source_target_pairs={{0,8},{4,12},{8,16},{12,20},{16,24},{20,28},{24,0},{28,4},{1,9},{5... | collective-permute-start | bytes 1769480 | tf_op jit(solution)/shard_map/ppermute | solution.py:334
  5.1 2.6 %collective-permute-start.3 = (bf16[80,1152]{1,0:T(8,128)(2,1)S(1)}, bf16[80,1152]{1,0:T(8,128)(2,1)S(1)}, u32[]{:S(2)}, u32[]{:S(2)}) collective-permute-start(bf16[80,1152]{1,0:T(8,128)(2,1)S(1)} %get-tuple-element.45), channel_id=1, source_target_pairs={{0,2},{1,3},{2,0},{3,1},{4,6},{5,7},{6,4},{7,5},{8,10},{9,11},{10,... | collective-permute-start | bytes 552968 | tf_op jit(solution)/shard_map/ppermute | solution.py:328
  7.7 1.3 %collective-permute-start.1 = (bf16[144,1152]{1,0:T(8,128)(2,1)S(1)}, bf16[144,1152]{1,0:T(8,128)(2,1)S(1)}, u32[]{:S(2)}, u32[]{:S(2)}) collective-permute-start(bf16[144,1152]{1,0:T(8,128)(2,1)S(1)} %get-tuple-element.43), channel_id=1, source_target_pairs={{0,3},{1,0},{2,1},{3,2},{4,7},{5,4},{6,5},{7,6},{8,11},{9,8},{10,9... | collective-permute-start | bytes 995336 | tf_op jit(solution)/shard_map/ppermute | solution.py:328
  9.0 0.7 collective-permute-start
  9.7 1.1 %copy-done.2 = bf16[256,1152]{1,0:T(8,128)(2,1)S(1)} copy-done((bf16[256,1152]{1,0:T(8,128)(2,1)S(1)}, bf16[256,1152]{1,0:T(8,128)(2,1)}, u32[]{:S(2)}) %copy-start.2) | copy-done | bytes 589848
  11.0 6.2 %collective-permute-done.3.rest_2_ = bf16[80,1152]{1,0:T(8,128)(2,1)S(1)} collective-permute-done((bf16[80,1152]{1,0:T(8,128)(2,1)S(1)}, bf16[80,1152]{1,0:T(8,128)(2,1)S(1)}, u32[]{:S(2)}, u32[]{:S(2)}) %collective-permute-start.3) | collective-permute-done | bytes 184352 | tf_op jit(solution)/shard_map/ppermute | solution.py:328
  17.2 2.4 %collective-permute-done.4.t2 = bf16[256,1152]{1,0:T(8,128)(2,1)S(1)} collective-permute-done((bf16[256,1152]{1,0:T(8,128)(2,1)}, bf16[256,1152]{1,0:T(8,128)(2,1)S(1)}, u32[]{:S(2)}, u32[]{:S(2)}) %collective-permute-start.4) | collective-permute-done | bytes 589856 | tf_op jit(solution)/shard_map/ppermute | solution.py:334
  20.2 4.4 %collective-permute-start.12 = (bf16[864,256]{1,0:T(8,128)(2,1)S(1)}, bf16[864,256]{1,0:T(8,128)(2,1)S(1)}, u32[]{:S(2)}, u32[]{:S(2)}) collective-permute-start(bf16[864,256]{1,0:T(8,128)(2,1)S(1)} %get-tuple-element.59), channel_id=1, source_target_pairs={{0,1},{1,0},{2,3},{3,2},{4,5},{5,4},{6,7},{7,6},{8,9},{9,8},{10,11... | collective-permute-start | bytes 1327112 | tf_op jit(solution)/shard_map/ppermute | solution.py:328
  24.6 1.5 %collective-permute-start.7 = (bf16[80,1152]{1,0:T(8,128)(2,1)S(1)}, bf16[80,1152]{1,0:T(8,128)(2,1)S(1)}, u32[]{:S(2)}, u32[]{:S(2)}) collective-permute-start(bf16[80,1152]{1,0:T(8,128)(2,1)S(1)} %collective-permute-done.3.rest_2_), channel_id=1, source_target_pairs={{0,8},{4,12},{8,0},{12,4},{16,24},{20,28},{24,16},{28,20},{1,9},{5... | collective-permute-start | bytes 552968 | tf_op jit(solution)/shard_map/ppermute | solution.py:346
  27.4 0.7 prepare.1
  28.8 2.2 %collective-permute-done.7.rest_3_ = bf16[80,1152]{1,0:T(8,128)(2,1)S(1)} collective-permute-done((bf16[80,1152]{1,0:T(8,128)(2,1)S(1)}, bf16[80,1152]{1,0:T(8,128)(2,1)S(1)}, u32[]{:S(2)}, u32[]{:S(2)}) %collective-permute-start.7) | collective-permute-done | bytes 184352 | tf_op jit(solution)/shard_map/ppermute | solution.py:346
  31.0 1.4 %collective-permute-done.11.rest_7_ = bf16[80,1152]{1,0:T(8,128)(2,1)S(1)} collective-permute-done((bf16[80,1152]{1,0:T(8,128)(2,1)S(1)}, bf16[80,1152]{1,0:T(8,128)(2,1)S(1)}, u32[]{:S(2)}, u32[]{:S(2)}) %collective-permute-start.11) | collective-permute-done | bytes 184352 | tf_op jit(solution)/shard_map/ppermute | solution.py:331
  32.4 2.9 %picture_side.1 = (bf16[288,384]{1,0:T(8,128)(2,1)S(1)}, bf16[288,768]{1,0:T(8,128)(2,1)S(1)}, bf16[256,1152]{1,0:T(8,128)(2,1)S(1)}, bf16[256,1152]{1,0:T(8,128)(2,1)S(1)}) custom-call(bf16[256,1152]{1,0:T(8,128)(2,1)S(1)} %copy-done.3, bf16[1152,256]{1,0:T(8,128)(2,1)S(1)} %get-tuple-element.51.x_t, bf16[768,1152]{1,0:T(8,128)(2,1)S(1)} %get-tuple-element.52.units, ...), custom_call_target="tpu_custom_call" | custom-call | tf_op jit(solution)/shard_map/picture_side/pallas_call | solution.py:206
  35.3 1.7 %collective-permute-done.12.far_t = bf16[864,256]{1,0:T(8,128)(2,1)S(1)} collective-permute-done((bf16[864,256]{1,0:T(8,128)(2,1)S(1)}, bf16[864,256]{1,0:T(8,128)(2,1)S(1)}, u32[]{:S(2)}, u32[]{:S(2)}) %collective-permute-start.12) | collective-permute-done | bytes 442400 | tf_op jit(solution)/shard_map/ppermute | solution.py:328
  36.9 0.6 collective-permute-start.13
  37.6 1.4 %collective-permute-start.24 = (bf16[256,1152]{1,0:T(8,128)(2,1)S(1)}, bf16[256,1152]{1,0:T(8,128)(2,1)S(1)}, u32[]{:S(2)}, u32[]{:S(2)}) collective-permute-start(bf16[256,1152]{1,0:T(8,128)(2,1)S(1)} %get-tuple-element.77.u0), channel_id=1, source_target_pairs={{0,24},{4,28},{8,0},{12,4},{16,8},{20,12},{24,16},{28,20},{1,25},{... | collective-permute-start | bytes 1769480 | tf_op jit(solution)/shard_map/ppermute | solution.py:334
  39.3 5.0 %collective-permute-done.13.arrived = bf16[288,384]{1,0:T(8,128)(2,1)S(1)} collective-permute-done((bf16[288,384]{1,0:T(8,128)(2,1)S(1)}, bf16[288,384]{1,0:T(8,128)(2,1)S(1)}, u32[]{:S(2)}, u32[]{:S(2)}) %collective-permute-start.13) | collective-permute-done | bytes 221216 | tf_op jit(solution)/shard_map/ppermute | solution.py:328
  44.9 0.7 collective-permute-start.21
  45.6 5.2 %collective-permute-start.22 = (bf16[288,384]{1,0:T(8,128)(2,1)S(1)}, bf16[288,384]{1,0:T(8,128)(2,1)S(1)}, u32[]{:S(2)}, u32[]{:S(2)}) collective-permute-start(bf16[288,384]{1,0:T(8,128)(2,1)S(1)} %get-tuple-element.76), channel_id=1, source_target_pairs={{1,3},{2,0},{0,1},{3,2},{5,7},{6,4},{4,5},{7,6},{9,11},{10,8},{8,9... | collective-permute-start | bytes 663560 | tf_op jit(solution)/shard_map/ppermute | solution.py:328
  50.8 9.6 %collective-permute-done.14.arrived = bf16[288,768]{1,0:T(8,128)(2,1)S(1)} collective-permute-done((bf16[288,768]{1,0:T(8,128)(2,1)S(1)}, bf16[288,768]{1,0:T(8,128)(2,1)S(1)}, u32[]{:S(2)}, u32[]{:S(2)}) %collective-permute-start.14) | collective-permute-done | bytes 442400 | tf_op jit(solution)/shard_map/ppermute | solution.py:328
  60.7 0.7 collective-permute-start.15
  61.4 0.7 collective-permute-start.16
  62.1 0.7 collective-permute-start.17
  62.7 7.7 %collective-permute-start.18 = (bf16[96,768]{1,0:T(8,128)(2,1)S(1)}, bf16[96,768]{1,0:T(8,128)(2,1)S(1)}, u32[]{:S(2)}, u32[]{:S(2)}) collective-permute-start(bf16[96,768]{1,0:T(8,128)(2,1)S(1)} %get-tuple-element.70), channel_id=1, source_target_pairs={{1,3},{2,0},{0,1},{3,2},{5,7},{6,4},{4,5},{7,6},{9,11},{10,8},{8,9... | collective-permute-start | bytes 442376 | tf_op jit(solution)/shard_map/ppermute | solution.py:328
  70.5 1.6 %collective-permute-start.20 = (bf16[96,768]{1,0:T(8,128)(2,1)S(1)}, bf16[96,768]{1,0:T(8,128)(2,1)S(1)}, u32[]{:S(2)}, u32[]{:S(2)}) collective-permute-start(bf16[96,768]{1,0:T(8,128)(2,1)S(1)} %get-tuple-element.72), channel_id=1, source_target_pairs={{1,3},{2,0},{0,1},{3,2},{5,7},{6,4},{4,5},{7,6},{9,11},{10,8},{8,9... | collective-permute-start | bytes 442376 | tf_op jit(solution)/shard_map/ppermute | solution.py:328
  72.2 0.8 %total.2.rest_6_ = f32[1,288,1152]{2,1,0:T(8,128)} custom-call(f32[288,384]{1,0:T(8,128)S(1)} %get-tuple-element.74.kept, bf16[288,384]{1,0:T(8,128)(2,1)S(1)} %collective-permute-done.21.rest_0_, bf16[288,384]{1,0:T(8,128)(2,1)S(1)} %collective-permute-done.22.rest_1_), custom_call_target="tpu_custom_call" | custom-call | tf_op jit(solution)/shard_map/total/pallas_call | solution.py:309
  73.0 2.8 %text_side.1 = (f32[256,1152]{1,0:T(8,128)}, f32[8,128]{1,0:T(8,128)S(1)}) custom-call(bf16[256,1152]{1,0:T(8,128)(2,1)S(1)} %copy-done.4, f32[8,128]{1,0:T(8,128)S(1)} %get-tuple-element.53.scalars, bf16[256,1152]{1,0:T(8,128)(2,1)S(1)} %get-tuple-element.77.u0, bf16[256,1152]{1,0:T(8,128)(2,1)S(1)} %collective-permute-done.23.u1, ...), custom_call_target="tpu_custom_call" | custom-call | tf_op jit(solution)/shard_map/text_side/pallas_call | solution.py:238
  75.8 2.1 %collective-permute-done.18.rest_3_ = bf16[96,768]{1,0:T(8,128)(2,1)S(1)} collective-permute-done((bf16[96,768]{1,0:T(8,128)(2,1)S(1)}, bf16[96,768]{1,0:T(8,128)(2,1)S(1)}, u32[]{:S(2)}, u32[]{:S(2)}) %collective-permute-start.18) | collective-permute-done | bytes 147488 | tf_op jit(solution)/shard_map/ppermute | solution.py:328
  77.9 1.6 %collective-permute-done.19.rest_4_ = bf16[96,768]{1,0:T(8,128)(2,1)S(1)} collective-permute-done((bf16[96,768]{1,0:T(8,128)(2,1)S(1)}, bf16[96,768]{1,0:T(8,128)(2,1)S(1)}, u32[]{:S(2)}, u32[]{:S(2)}) %collective-permute-start.19) | collective-permute-done | bytes 147488 | tf_op jit(solution)/shard_map/ppermute | solution.py:328
  79.5 1.6 %collective-permute-done.20.rest_5_ = bf16[96,768]{1,0:T(8,128)(2,1)S(1)} collective-permute-done((bf16[96,768]{1,0:T(8,128)(2,1)S(1)}, bf16[96,768]{1,0:T(8,128)(2,1)S(1)}, u32[]{:S(2)}, u32[]{:S(2)}) %collective-permute-start.20) | collective-permute-done | bytes 147488 | tf_op jit(solution)/shard_map/ppermute | solution.py:328
  81.0 1.0 %total.3 = f32[1,288,1152]{2,1,0:T(8,128)} custom-call(f32[288,768]{1,0:T(8,128)S(1)} %get-tuple-element.66.kept, bf16[96,768]{1,0:T(8,128)(2,1)S(1)} %collective-permute-done.15.rest_0_, bf16[96,768]{1,0:T(8,128)(2,1)S(1)} %collective-permute-done.16.rest_1_, bf16[96,768]{1,0:T(8,128)(2,1)S(1)} %collective-permute-done.17.rest_2_, ...), custom_call_target="tpu_custom_call", output_to_operand_aliasing={{}: (7, {})} | custom-call | tf_op jit(solution)/shard_map/total/pallas_call | solution.py:309
  (38 shorter events, 3.2 us)
Async XLA Ops:
  0.6 1.1 %copy-start = (bf16[288,1152]{1,0:T(8,128)(2,1)S(1)}, bf16[288,1152]{1,0:T(8,128)(2,1)}, u32[]{:S(2)}) copy-start(bf16[288,1152]{1,0:T(8,128)(2,1)} %own.3) | copy-start | bytes 1990660
  1.7 25.7 %copy-start.4 = (bf16[256,1152]{1,0:T(8,128)(2,1)S(1)}, bf16[256,1152]{1,0:T(8,128)(2,1)}, u32[]{:S(2)}) copy-start(bf16[256,1152]{1,0:T(8,128)(2,1)} %text) | copy-start | bytes 1769476
  2.1 17.5 %collective-permute-start.4 = (bf16[256,1152]{1,0:T(8,128)(2,1)}, bf16[256,1152]{1,0:T(8,128)(2,1)S(1)}, u32[]{:S(2)}, u32[]{:S(2)}) collective-permute-start(bf16[256,1152]{1,0:T(8,128)(2,1)} %text), channel_id=1, source_target_pairs={{0,8},{4,12},{8,16},{12,20},{16,24},{20,28},{24,0},{28,4},{1,9},{5... | collective-permute-start | bytes 1769480 | tf_op jit(solution)/shard_map/ppermute | solution.py:334
  5.1 12.1 %collective-permute-start.3 = (bf16[80,1152]{1,0:T(8,128)(2,1)S(1)}, bf16[80,1152]{1,0:T(8,128)(2,1)S(1)}, u32[]{:S(2)}, u32[]{:S(2)}) collective-permute-start(bf16[80,1152]{1,0:T(8,128)(2,1)S(1)} %get-tuple-element.45), channel_id=1, source_target_pairs={{0,2},{1,3},{2,0},{3,1},{4,6},{5,7},{6,4},{7,5},{8,10},{9,11},{10,... | collective-permute-start | bytes 552968 | tf_op jit(solution)/shard_map/ppermute | solution.py:328
  7.7 20.4 %collective-permute-start.1 = (bf16[144,1152]{1,0:T(8,128)(2,1)S(1)}, bf16[144,1152]{1,0:T(8,128)(2,1)S(1)}, u32[]{:S(2)}, u32[]{:S(2)}) collective-permute-start(bf16[144,1152]{1,0:T(8,128)(2,1)S(1)} %get-tuple-element.43), channel_id=1, source_target_pairs={{0,3},{1,0},{2,1},{3,2},{4,7},{5,4},{6,5},{7,6},{8,11},{9,8},{10,9... | collective-permute-start | bytes 995336 | tf_op jit(solution)/shard_map/ppermute | solution.py:328
  9.0 19.1 %collective-permute-start = (bf16[144,1152]{1,0:T(8,128)(2,1)S(1)}, bf16[144,1152]{1,0:T(8,128)(2,1)S(1)}, u32[]{:S(2)}, u32[]{:S(2)}) collective-permute-start(bf16[144,1152]{1,0:T(8,128)(2,1)S(1)} %get-tuple-element.43), channel_id=1, source_target_pairs={{0,1},{1,2},{2,3},{3,0},{4,5},{5,6},{6,7},{7,4},{8,9},{9,10},{10,1... | collective-permute-start | bytes 995336 | tf_op jit(solution)/shard_map/ppermute | solution.py:328
  9.7 10.5 %collective-permute-start.2 = (bf16[256,1152]{1,0:T(8,128)(2,1)}, bf16[256,1152]{1,0:T(8,128)(2,1)S(1)}, u32[]{:S(2)}, u32[]{:S(2)}) collective-permute-start(bf16[256,1152]{1,0:T(8,128)(2,1)} %text), channel_id=1, source_target_pairs={{0,4},{4,0},{8,12},{12,8},{16,20},{20,16},{24,28},{28,24},{1,5},{5... | collective-permute-start | bytes 1769480 | tf_op jit(solution)/shard_map/ppermute | solution.py:331
  9.7 1.1 %copy-start.2 = (bf16[256,1152]{1,0:T(8,128)(2,1)S(1)}, bf16[256,1152]{1,0:T(8,128)(2,1)}, u32[]{:S(2)}) copy-start(bf16[256,1152]{1,0:T(8,128)(2,1)} %x.3) | copy-start | bytes 1769476
  19.6 12.8 %copy-start.1 = (bf16[288,1152]{1,0:T(8,128)(2,1)S(1)}, bf16[288,1152]{1,0:T(8,128)(2,1)}, u32[]{:S(2)}) copy-start(bf16[288,1152]{1,0:T(8,128)(2,1)} %own.3) | copy-start | bytes 1990660
  19.6 12.8 %copy-start.3 = (bf16[256,1152]{1,0:T(8,128)(2,1)S(1)}, bf16[256,1152]{1,0:T(8,128)(2,1)}, u32[]{:S(2)}) copy-start(bf16[256,1152]{1,0:T(8,128)(2,1)} %x.3) | copy-start | bytes 1769476
  19.7 5.0 %collective-permute-start.6 = (bf16[128,1152]{1,0:T(8,128)(2,1)S(1)}, bf16[128,1152]{1,0:T(8,128)(2,1)S(1)}, u32[]{:S(2)}, u32[]{:S(2)}) collective-permute-start(bf16[128,1152]{1,0:T(8,128)(2,1)S(1)} %get-tuple-element.80), channel_id=1, source_target_pairs={{0,4},{4,0},{8,12},{12,8},{16,20},{20,16},{24,28},{28,24},{1,5},{5... | collective-permute-start | bytes 884744 | tf_op jit(solution)/shard_map/ppermute | solution.py:331
  19.7 7.7 %collective-permute-start.5 = (bf16[128,1152]{1,0:T(8,128)(2,1)S(1)}, bf16[128,1152]{1,0:T(8,128)(2,1)S(1)}, u32[]{:S(2)}, u32[]{:S(2)}) collective-permute-start(bf16[128,1152]{1,0:T(8,128)(2,1)S(1)} %get-tuple-element.81), channel_id=1, source_target_pairs={{0,4},{4,0},{8,12},{12,8},{16,20},{20,16},{24,28},{28,24},{1,5},{5... | collective-permute-start | bytes 884744 | tf_op jit(solution)/shard_map/ppermute | solution.py:331
  20.2 16.7 %collective-permute-start.12 = (bf16[864,256]{1,0:T(8,128)(2,1)S(1)}, bf16[864,256]{1,0:T(8,128)(2,1)S(1)}, u32[]{:S(2)}, u32[]{:S(2)}) collective-permute-start(bf16[864,256]{1,0:T(8,128)(2,1)S(1)} %get-tuple-element.59), channel_id=1, source_target_pairs={{0,1},{1,0},{2,3},{3,2},{4,5},{5,4},{6,7},{7,6},{8,9},{9,8},{10,11... | collective-permute-start | bytes 1327112 | tf_op jit(solution)/shard_map/ppermute | solution.py:328
  24.6 6.3 %collective-permute-start.7 = (bf16[80,1152]{1,0:T(8,128)(2,1)S(1)}, bf16[80,1152]{1,0:T(8,128)(2,1)S(1)}, u32[]{:S(2)}, u32[]{:S(2)}) collective-permute-start(bf16[80,1152]{1,0:T(8,128)(2,1)S(1)} %collective-permute-done.3.rest_2_), channel_id=1, source_target_pairs={{0,8},{4,12},{8,0},{12,4},{16,24},{20,28},{24,16},{28,20},{1,9},{5... | collective-permute-start | bytes 552968 | tf_op jit(solution)/shard_map/ppermute | solution.py:346
  28.1 4.3 %collective-permute-start.8 = (bf16[144,1152]{1,0:T(8,128)(2,1)S(1)}, bf16[144,1152]{1,0:T(8,128)(2,1)S(1)}, u32[]{:S(2)}, u32[]{:S(2)}) collective-permute-start(bf16[144,1152]{1,0:T(8,128)(2,1)S(1)} %collective-permute-done.rest_0_), channel_id=1, source_target_pairs={{0,4},{4,0},{8,12},{12,8},{16,20},{20,16},{24,28},{28,24},{1,5},{5... | collective-permute-start | bytes 995336 | tf_op jit(solution)/shard_map/ppermute | solution.py:331
  28.2 4.2 %collective-permute-start.9 = (bf16[144,1152]{1,0:T(8,128)(2,1)S(1)}, bf16[144,1152]{1,0:T(8,128)(2,1)S(1)}, u32[]{:S(2)}, u32[]{:S(2)}) collective-permute-start(bf16[144,1152]{1,0:T(8,128)(2,1)S(1)} %collective-permute-done.1.rest_1_), channel_id=1, source_target_pairs={{0,4},{4,0},{8,12},{12,8},{16,20},{20,16},{24,28},{28,24},{1,5},{5... | collective-permute-start | bytes 995336 | tf_op jit(solution)/shard_map/ppermute | solution.py:331
  28.7 2.3 %collective-permute-start.10 = (bf16[80,1152]{1,0:T(8,128)(2,1)S(1)}, bf16[80,1152]{1,0:T(8,128)(2,1)S(1)}, u32[]{:S(2)}, u32[]{:S(2)}) collective-permute-start(bf16[80,1152]{1,0:T(8,128)(2,1)S(1)} %collective-permute-done.3.rest_2_), channel_id=1, source_target_pairs={{0,4},{4,0},{8,12},{12,8},{16,20},{20,16},{24,28},{28,24},{1,5},{5... | collective-permute-start | bytes 552968 | tf_op jit(solution)/shard_map/ppermute | solution.py:331
  31.0 1.4 %collective-permute-start.11 = (bf16[80,1152]{1,0:T(8,128)(2,1)S(1)}, bf16[80,1152]{1,0:T(8,128)(2,1)S(1)}, u32[]{:S(2)}, u32[]{:S(2)}) collective-permute-start(bf16[80,1152]{1,0:T(8,128)(2,1)S(1)} %collective-permute-done.7.rest_3_), channel_id=1, source_target_pairs={{0,4},{4,0},{8,12},{12,8},{16,20},{20,16},{24,28},{28,24},{1,5},{5... | collective-permute-start | bytes 552968 | tf_op jit(solution)/shard_map/ppermute | solution.py:331
  36.9 7.4 %collective-permute-start.13 = (bf16[288,384]{1,0:T(8,128)(2,1)S(1)}, bf16[288,384]{1,0:T(8,128)(2,1)S(1)}, u32[]{:S(2)}, u32[]{:S(2)}) collective-permute-start(bf16[288,384]{1,0:T(8,128)(2,1)S(1)} %get-tuple-element.64), channel_id=1, source_target_pairs={{0,1},{1,0},{2,3},{3,2},{4,5},{5,4},{6,7},{7,6},{8,9},{9,8},{10,11... | collective-permute-start | bytes 663560 | tf_op jit(solution)/shard_map/ppermute | solution.py:328
  37.6 25.2 %collective-permute-start.24 = (bf16[256,1152]{1,0:T(8,128)(2,1)S(1)}, bf16[256,1152]{1,0:T(8,128)(2,1)S(1)}, u32[]{:S(2)}, u32[]{:S(2)}) collective-permute-start(bf16[256,1152]{1,0:T(8,128)(2,1)S(1)} %get-tuple-element.77.u0), channel_id=1, source_target_pairs={{0,24},{4,28},{8,0},{12,4},{16,8},{20,12},{24,16},{28,20},{1,25},{... | collective-permute-start | bytes 1769480 | tf_op jit(solution)/shard_map/ppermute | solution.py:334
  39.0 31.5 %collective-permute-start.23 = (bf16[256,1152]{1,0:T(8,128)(2,1)S(1)}, bf16[256,1152]{1,0:T(8,128)(2,1)S(1)}, u32[]{:S(2)}, u32[]{:S(2)}) collective-permute-start(bf16[256,1152]{1,0:T(8,128)(2,1)S(1)} %get-tuple-element.77.u0), channel_id=1, source_target_pairs={{0,28},{4,0},{8,4},{12,8},{16,12},{20,16},{24,20},{28,24},{1,29},{... | collective-permute-start | bytes 1769480 | tf_op jit(solution)/shard_map/ppermute | solution.py:334
  44.3 16.0 %collective-permute-start.14 = (bf16[288,768]{1,0:T(8,128)(2,1)S(1)}, bf16[288,768]{1,0:T(8,128)(2,1)S(1)}, u32[]{:S(2)}, u32[]{:S(2)}) collective-permute-start(bf16[288,768]{1,0:T(8,128)(2,1)S(1)} %get-tuple-element.65), channel_id=1, source_target_pairs={{0,1},{1,0},{2,3},{3,2},{4,5},{5,4},{6,7},{7,6},{8,9},{9,8},{10,11... | collective-permute-start | bytes 1327112 | tf_op jit(solution)/shard_map/ppermute | solution.py:328
  44.9 16.5 %collective-permute-start.21 = (bf16[288,384]{1,0:T(8,128)(2,1)S(1)}, bf16[288,384]{1,0:T(8,128)(2,1)S(1)}, u32[]{:S(2)}, u32[]{:S(2)}) collective-permute-start(bf16[288,384]{1,0:T(8,128)(2,1)S(1)} %get-tuple-element.75), channel_id=1, source_target_pairs={{1,2},{2,1},{0,0},{3,3},{5,6},{6,5},{4,4},{7,7},{9,10},{10,9},{8,8... | collective-permute-start | bytes 663560 | tf_op jit(solution)/shard_map/ppermute | solution.py:328
  45.6 16.5 %collective-permute-start.22 = (bf16[288,384]{1,0:T(8,128)(2,1)S(1)}, bf16[288,384]{1,0:T(8,128)(2,1)S(1)}, u32[]{:S(2)}, u32[]{:S(2)}) collective-permute-start(bf16[288,384]{1,0:T(8,128)(2,1)S(1)} %get-tuple-element.76), channel_id=1, source_target_pairs={{1,3},{2,0},{0,1},{3,2},{5,7},{6,4},{4,5},{7,6},{9,11},{10,8},{8,9... | collective-permute-start | bytes 663560 | tf_op jit(solution)/shard_map/ppermute | solution.py:328
  60.7 9.9 %collective-permute-start.15 = (bf16[96,768]{1,0:T(8,128)(2,1)S(1)}, bf16[96,768]{1,0:T(8,128)(2,1)S(1)}, u32[]{:S(2)}, u32[]{:S(2)}) collective-permute-start(bf16[96,768]{1,0:T(8,128)(2,1)S(1)} %get-tuple-element.67), channel_id=1, source_target_pairs={{1,2},{2,1},{0,0},{3,3},{5,6},{6,5},{4,4},{7,7},{9,10},{10,9},{8,8... | collective-permute-start | bytes 442376 | tf_op jit(solution)/shard_map/ppermute | solution.py:328
  61.4 14.4 %collective-permute-start.16 = (bf16[96,768]{1,0:T(8,128)(2,1)S(1)}, bf16[96,768]{1,0:T(8,128)(2,1)S(1)}, u32[]{:S(2)}, u32[]{:S(2)}) collective-permute-start(bf16[96,768]{1,0:T(8,128)(2,1)S(1)} %get-tuple-element.68), channel_id=1, source_target_pairs={{1,2},{2,1},{0,0},{3,3},{5,6},{6,5},{4,4},{7,7},{9,10},{10,9},{8,8... | collective-permute-start | bytes 442376 | tf_op jit(solution)/shard_map/ppermute | solution.py:328
  62.1 13.7 %collective-permute-start.17 = (bf16[96,768]{1,0:T(8,128)(2,1)S(1)}, bf16[96,768]{1,0:T(8,128)(2,1)S(1)}, u32[]{:S(2)}, u32[]{:S(2)}) collective-permute-start(bf16[96,768]{1,0:T(8,128)(2,1)S(1)} %get-tuple-element.69), channel_id=1, source_target_pairs={{1,2},{2,1},{0,0},{3,3},{5,6},{6,5},{4,4},{7,7},{9,10},{10,9},{8,8... | collective-permute-start | bytes 442376 | tf_op jit(solution)/shard_map/ppermute | solution.py:328
  62.7 15.1 %collective-permute-start.18 = (bf16[96,768]{1,0:T(8,128)(2,1)S(1)}, bf16[96,768]{1,0:T(8,128)(2,1)S(1)}, u32[]{:S(2)}, u32[]{:S(2)}) collective-permute-start(bf16[96,768]{1,0:T(8,128)(2,1)S(1)} %get-tuple-element.70), channel_id=1, source_target_pairs={{1,3},{2,0},{0,1},{3,2},{5,7},{6,4},{4,5},{7,6},{9,11},{10,8},{8,9... | collective-permute-start | bytes 442376 | tf_op jit(solution)/shard_map/ppermute | solution.py:328
  70.5 9.0 %collective-permute-start.19 = (bf16[96,768]{1,0:T(8,128)(2,1)S(1)}, bf16[96,768]{1,0:T(8,128)(2,1)S(1)}, u32[]{:S(2)}, u32[]{:S(2)}) collective-permute-start(bf16[96,768]{1,0:T(8,128)(2,1)S(1)} %get-tuple-element.71), channel_id=1, source_target_pairs={{1,3},{2,0},{0,1},{3,2},{5,7},{6,4},{4,5},{7,6},{9,11},{10,8},{8,9... | collective-permute-start | bytes 442376 | tf_op jit(solution)/shard_map/ppermute | solution.py:328
  70.5 10.5 %collective-permute-start.20 = (bf16[96,768]{1,0:T(8,128)(2,1)S(1)}, bf16[96,768]{1,0:T(8,128)(2,1)S(1)}, u32[]{:S(2)}, u32[]{:S(2)}) collective-permute-start(bf16[96,768]{1,0:T(8,128)(2,1)S(1)} %get-tuple-element.72), channel_id=1, source_target_pairs={{1,3},{2,0},{0,1},{3,2},{5,7},{6,4},{4,5},{7,6},{9,11},{10,8},{8,9... | collective-permute-start | bytes 442376 | tf_op jit(solution)/shard_map/ppermute | solution.py:328

commit v10 on v9

--- a/solution.py
+++ b/solution.py
@@ -366,7 +366,8 @@
     for parts, block in zip(CROSS_PARTS, arrived):
         kept, *sent = pair_product(begin, parts, x_t, far_t, grad, block, after)
         nears = [along(n, [(1, 2), (2, 1), (0, 0), (3, 3)]) for n in sent[:parts]]
-        fars = [along(n, [(1, 3), (2, 0), (0, 1), (3, 2)]) for n in sent[parts:]]
+        ends = [(0, 1), (3, 2)] if begin > 0 else []
+        fars = [along(n, [(1, 3), (2, 0)] + ends) for n in sent[parts:]]
         after = []
         terms.append((begin, width, kept, nears, fars))
         begin += block.shape[1]

time: 82.4 us -> 82.4 us (level)
  starting transfers between devices: 34.6 us -> 30.7 us
  waiting for transfers between devices: 33.7 us -> 37.6 us
    ppermute x14, starting transfers between devices: 27.2 us -> 23.3 us  [along(): return lax.ppermute(value, 'fsdp', pairs)]
    ppermute x14, waiting for transfers between devices: 27.7 us -> 31.6 us  [along(): return lax.ppermute(value, 'fsdp', pairs)]
where the time goes in v10:
time: 82.4 us; the launch traced here: 82.1 us
  waiting for transfers between devices  37.6 us (46%)
  starting transfers between devices  30.7 us (37%)
  Pallas kernels  9.37 us (11%)
  local copies, waits for them, and re-layouts  2.21 us (3%)
  between operations  2.15 us (3%)
    ppermute x14, waiting for transfers between devices, along(): return lax.ppermute(value, 'fsdp', pairs)  31.6 us
    ppermute x14, starting transfers between devices, along(): return lax.ppermute(value, 'fsdp', pairs)  23.3 us
    ppermute x3, starting transfers between devices, shifted(): lax.ppermute(value, 'dp', [(d, (d + by) % n_dp) for d in range(n_dp)])  4.74 us
    pallas_call x1, Pallas kernels, picture_side(): pl.pallas_call(picture_kernel, out_shape=outs, in_specs=spaces(13), out_s...  2.85 us
    pallas_call x1, Pallas kernels, text_side(): pl.pallas_call(text_kernel, out_shape=(jax.ShapeDtypeStruct((rows, width)...  2.76 us
    ppermute x3, waiting for transfers between devices, shifted(): lax.ppermute(value, 'dp', [(d, (d + by) % n_dp) for d in range(n_dp)])  2.39 us
    ppermute x1, waiting for transfers between devices, line_body(): two_crossed = lax.ppermute(two, 'dp', [(d, d ^ 2) for d in range(n_dp)])  2.17 us
    unnamed x10, local copies, waits for them, and re-layouts  2.17 us
  transfers between devices with their start and end apart: 25, of which 10 were waited for; matrix products, arithmetic and copies ran while one was open for 0% of the time, Pallas kernels for 10%

profile of v10, /device:TPU:0, one launch (start us, length us, event | category | flops | bytes accessed | tf_op | source)
XLA Modules:
  0.0 82.1 jit_solution(5939070783792406505)
XLA Ops:
  0.6 1.1 %copy-done = bf16[288,1152]{1,0:T(8,128)(2,1)S(1)} copy-done((bf16[288,1152]{1,0:T(8,128)(2,1)S(1)}, bf16[288,1152]{1,0:T(8,128)(2,1)}, u32[]{:S(2)}) %copy-start) | copy-done | bytes 663576
  2.1 3.0 %collective-permute-start.4 = (bf16[256,1152]{1,0:T(8,128)(2,1)}, bf16[256,1152]{1,0:T(8,128)(2,1)S(1)}, u32[]{:S(2)}, u32[]{:S(2)}) collective-permute-start(bf16[256,1152]{1,0:T(8,128)(2,1)} %text), channel_id=1, source_target_pairs={{0,8},{4,12},{8,16},{12,20},{16,24},{20,28},{24,0},{28,4},{1,9},{5... | collective-permute-start | bytes 1769480 | tf_op jit(solution)/shard_map/ppermute | solution.py:334
  5.1 2.6 %collective-permute-start.3 = (bf16[80,1152]{1,0:T(8,128)(2,1)S(1)}, bf16[80,1152]{1,0:T(8,128)(2,1)S(1)}, u32[]{:S(2)}, u32[]{:S(2)}) collective-permute-start(bf16[80,1152]{1,0:T(8,128)(2,1)S(1)} %get-tuple-element.45), channel_id=1, source_target_pairs={{0,2},{1,3},{2,0},{3,1},{4,6},{5,7},{6,4},{7,5},{8,10},{9,11},{10,... | collective-permute-start | bytes 552968 | tf_op jit(solution)/shard_map/ppermute | solution.py:328
  7.7 1.3 %collective-permute-start.1 = (bf16[144,1152]{1,0:T(8,128)(2,1)S(1)}, bf16[144,1152]{1,0:T(8,128)(2,1)S(1)}, u32[]{:S(2)}, u32[]{:S(2)}) collective-permute-start(bf16[144,1152]{1,0:T(8,128)(2,1)S(1)} %get-tuple-element.43), channel_id=1, source_target_pairs={{0,3},{1,0},{2,1},{3,2},{4,7},{5,4},{6,5},{7,6},{8,11},{9,8},{10,9... | collective-permute-start | bytes 995336 | tf_op jit(solution)/shard_map/ppermute | solution.py:328
  9.0 0.7 collective-permute-start
  9.7 1.1 %copy-done.2 = bf16[256,1152]{1,0:T(8,128)(2,1)S(1)} copy-done((bf16[256,1152]{1,0:T(8,128)(2,1)S(1)}, bf16[256,1152]{1,0:T(8,128)(2,1)}, u32[]{:S(2)}) %copy-start.2) | copy-done | bytes 589848
  11.0 6.2 %collective-permute-done.3.rest_2_ = bf16[80,1152]{1,0:T(8,128)(2,1)S(1)} collective-permute-done((bf16[80,1152]{1,0:T(8,128)(2,1)S(1)}, bf16[80,1152]{1,0:T(8,128)(2,1)S(1)}, u32[]{:S(2)}, u32[]{:S(2)}) %collective-permute-start.3) | collective-permute-done | bytes 184352 | tf_op jit(solution)/shard_map/ppermute | solution.py:328
  17.2 2.4 %collective-permute-done.4.t2 = bf16[256,1152]{1,0:T(8,128)(2,1)S(1)} collective-permute-done((bf16[256,1152]{1,0:T(8,128)(2,1)}, bf16[256,1152]{1,0:T(8,128)(2,1)S(1)}, u32[]{:S(2)}, u32[]{:S(2)}) %collective-permute-start.4) | collective-permute-done | bytes 589856 | tf_op jit(solution)/shard_map/ppermute | solution.py:334
  20.2 4.4 %collective-permute-start.12 = (bf16[864,256]{1,0:T(8,128)(2,1)S(1)}, bf16[864,256]{1,0:T(8,128)(2,1)S(1)}, u32[]{:S(2)}, u32[]{:S(2)}) collective-permute-start(bf16[864,256]{1,0:T(8,128)(2,1)S(1)} %get-tuple-element.59), channel_id=1, source_target_pairs={{0,1},{1,0},{2,3},{3,2},{4,5},{5,4},{6,7},{7,6},{8,9},{9,8},{10,11... | collective-permute-start | bytes 1327112 | tf_op jit(solution)/shard_map/ppermute | solution.py:328
  24.6 1.5 %collective-permute-start.7 = (bf16[80,1152]{1,0:T(8,128)(2,1)S(1)}, bf16[80,1152]{1,0:T(8,128)(2,1)S(1)}, u32[]{:S(2)}, u32[]{:S(2)}) collective-permute-start(bf16[80,1152]{1,0:T(8,128)(2,1)S(1)} %collective-permute-done.3.rest_2_), channel_id=1, source_target_pairs={{0,8},{4,12},{8,0},{12,4},{16,24},{20,28},{24,16},{28,20},{1,9},{5... | collective-permute-start | bytes 552968 | tf_op jit(solution)/shard_map/ppermute | solution.py:346
  27.4 0.7 prepare.1
  28.8 2.2 %collective-permute-done.7.rest_3_ = bf16[80,1152]{1,0:T(8,128)(2,1)S(1)} collective-permute-done((bf16[80,1152]{1,0:T(8,128)(2,1)S(1)}, bf16[80,1152]{1,0:T(8,128)(2,1)S(1)}, u32[]{:S(2)}, u32[]{:S(2)}) %collective-permute-start.7) | collective-permute-done | bytes 184352 | tf_op jit(solution)/shard_map/ppermute | solution.py:346
  31.0 1.4 %collective-permute-done.11.rest_7_ = bf16[80,1152]{1,0:T(8,128)(2,1)S(1)} collective-permute-done((bf16[80,1152]{1,0:T(8,128)(2,1)S(1)}, bf16[80,1152]{1,0:T(8,128)(2,1)S(1)}, u32[]{:S(2)}, u32[]{:S(2)}) %collective-permute-start.11) | collective-permute-done | bytes 184352 | tf_op jit(solution)/shard_map/ppermute | solution.py:331
  32.4 2.9 %picture_side.1 = (bf16[288,384]{1,0:T(8,128)(2,1)S(1)}, bf16[288,768]{1,0:T(8,128)(2,1)S(1)}, bf16[256,1152]{1,0:T(8,128)(2,1)S(1)}, bf16[256,1152]{1,0:T(8,128)(2,1)S(1)}) custom-call(bf16[256,1152]{1,0:T(8,128)(2,1)S(1)} %copy-done.3, bf16[1152,256]{1,0:T(8,128)(2,1)S(1)} %get-tuple-element.51.x_t, bf16[768,1152]{1,0:T(8,128)(2,1)S(1)} %get-tuple-element.52.units, ...), custom_call_target="tpu_custom_call" | custom-call | tf_op jit(solution)/shard_map/picture_side/pallas_call | solution.py:206
  35.3 1.7 %collective-permute-done.12.far_t = bf16[864,256]{1,0:T(8,128)(2,1)S(1)} collective-permute-done((bf16[864,256]{1,0:T(8,128)(2,1)S(1)}, bf16[864,256]{1,0:T(8,128)(2,1)S(1)}, u32[]{:S(2)}, u32[]{:S(2)}) %collective-permute-start.12) | collective-permute-done | bytes 442400 | tf_op jit(solution)/shard_map/ppermute | solution.py:328
  36.9 0.6 collective-permute-start.13
  37.6 1.4 %collective-permute-start.24 = (bf16[256,1152]{1,0:T(8,128)(2,1)S(1)}, bf16[256,1152]{1,0:T(8,128)(2,1)S(1)}, u32[]{:S(2)}, u32[]{:S(2)}) collective-permute-start(bf16[256,1152]{1,0:T(8,128)(2,1)S(1)} %get-tuple-element.77.u0), channel_id=1, source_target_pairs={{0,24},{4,28},{8,0},{12,4},{16,8},{20,12},{24,16},{28,20},{1,25},{... | collective-permute-start | bytes 1769480 | tf_op jit(solution)/shard_map/ppermute | solution.py:334
  39.3 5.0 %collective-permute-done.13.arrived = bf16[288,384]{1,0:T(8,128)(2,1)S(1)} collective-permute-done((bf16[288,384]{1,0:T(8,128)(2,1)S(1)}, bf16[288,384]{1,0:T(8,128)(2,1)S(1)}, u32[]{:S(2)}, u32[]{:S(2)}) %collective-permute-start.13) | collective-permute-done | bytes 221216 | tf_op jit(solution)/shard_map/ppermute | solution.py:328
  44.9 0.7 collective-permute-start.21
  45.6 1.3 %collective-permute-start.22 = (bf16[288,384]{1,0:T(8,128)(2,1)S(1)}, bf16[288,384]{1,0:T(8,128)(2,1)S(1)}, u32[]{:S(2)}, u32[]{:S(2)}) collective-permute-start(bf16[288,384]{1,0:T(8,128)(2,1)S(1)} %get-tuple-element.76), channel_id=1, source_target_pairs={{1,3},{2,0},{5,7},{6,4},{9,11},{10,8},{13,15},{14,12},{17,19},{18,... | collective-permute-start | bytes 663560 | tf_op jit(solution)/shard_map/ppermute | solution.py:328
  46.9 13.5 %collective-permute-done.14.arrived = bf16[288,768]{1,0:T(8,128)(2,1)S(1)} collective-permute-done((bf16[288,768]{1,0:T(8,128)(2,1)S(1)}, bf16[288,768]{1,0:T(8,128)(2,1)S(1)}, u32[]{:S(2)}, u32[]{:S(2)}) %collective-permute-start.14) | collective-permute-done | bytes 442400 | tf_op jit(solution)/shard_map/ppermute | solution.py:328
  60.7 0.7 collective-permute-start.15
  61.4 0.7 collective-permute-start.16
  62.1 0.7 collective-permute-start.17
  62.7 7.7 %collective-permute-start.18 = (bf16[96,768]{1,0:T(8,128)(2,1)S(1)}, bf16[96,768]{1,0:T(8,128)(2,1)S(1)}, u32[]{:S(2)}, u32[]{:S(2)}) collective-permute-start(bf16[96,768]{1,0:T(8,128)(2,1)S(1)} %get-tuple-element.70), channel_id=1, source_target_pairs={{1,3},{2,0},{0,1},{3,2},{5,7},{6,4},{4,5},{7,6},{9,11},{10,8},{8,9... | collective-permute-start | bytes 442376 | tf_op jit(solution)/shard_map/ppermute | solution.py:328
  70.5 1.6 %collective-permute-start.20 = (bf16[96,768]{1,0:T(8,128)(2,1)S(1)}, bf16[96,768]{1,0:T(8,128)(2,1)S(1)}, u32[]{:S(2)}, u32[]{:S(2)}) collective-permute-start(bf16[96,768]{1,0:T(8,128)(2,1)S(1)} %get-tuple-element.72), channel_id=1, source_target_pairs={{1,3},{2,0},{0,1},{3,2},{5,7},{6,4},{4,5},{7,6},{9,11},{10,8},{8,9... | collective-permute-start | bytes 442376 | tf_op jit(solution)/shard_map/ppermute | solution.py:328
  72.2 0.8 %total.2.rest_6_ = f32[1,288,1152]{2,1,0:T(8,128)} custom-call(f32[288,384]{1,0:T(8,128)S(1)} %get-tuple-element.74.kept, bf16[288,384]{1,0:T(8,128)(2,1)S(1)} %collective-permute-done.21.rest_0_, bf16[288,384]{1,0:T(8,128)(2,1)S(1)} %collective-permute-done.22.rest_1_), custom_call_target="tpu_custom_call" | custom-call | tf_op jit(solution)/shard_map/total/pallas_call | solution.py:309
  73.0 2.8 %text_side.1 = (f32[256,1152]{1,0:T(8,128)}, f32[8,128]{1,0:T(8,128)S(1)}) custom-call(bf16[256,1152]{1,0:T(8,128)(2,1)S(1)} %copy-done.4, f32[8,128]{1,0:T(8,128)S(1)} %get-tuple-element.53.scalars, bf16[256,1152]{1,0:T(8,128)(2,1)S(1)} %get-tuple-element.77.u0, bf16[256,1152]{1,0:T(8,128)(2,1)S(1)} %collective-permute-done.23.u1, ...), custom_call_target="tpu_custom_call" | custom-call | tf_op jit(solution)/shard_map/text_side/pallas_call | solution.py:238
  75.8 2.1 %collective-permute-done.18.rest_3_ = bf16[96,768]{1,0:T(8,128)(2,1)S(1)} collective-permute-done((bf16[96,768]{1,0:T(8,128)(2,1)S(1)}, bf16[96,768]{1,0:T(8,128)(2,1)S(1)}, u32[]{:S(2)}, u32[]{:S(2)}) %collective-permute-start.18) | collective-permute-done | bytes 147488 | tf_op jit(solution)/shard_map/ppermute | solution.py:328
  77.9 1.6 %collective-permute-done.19.rest_4_ = bf16[96,768]{1,0:T(8,128)(2,1)S(1)} collective-permute-done((bf16[96,768]{1,0:T(8,128)(2,1)S(1)}, bf16[96,768]{1,0:T(8,128)(2,1)S(1)}, u32[]{:S(2)}, u32[]{:S(2)}) %collective-permute-start.19) | collective-permute-done | bytes 147488 | tf_op jit(solution)/shard_map/ppermute | solution.py:328
  79.5 1.6 %collective-permute-done.20.rest_5_ = bf16[96,768]{1,0:T(8,128)(2,1)S(1)} collective-permute-done((bf16[96,768]{1,0:T(8,128)(2,1)S(1)}, bf16[96,768]{1,0:T(8,128)(2,1)S(1)}, u32[]{:S(2)}, u32[]{:S(2)}) %collective-permute-start.20) | collective-permute-done | bytes 147488 | tf_op jit(solution)/shard_map/ppermute | solution.py:328
  81.0 1.0 %total.3 = f32[1,288,1152]{2,1,0:T(8,128)} custom-call(f32[288,768]{1,0:T(8,128)S(1)} %get-tuple-element.66.kept, bf16[96,768]{1,0:T(8,128)(2,1)S(1)} %collective-permute-done.15.rest_0_, bf16[96,768]{1,0:T(8,128)(2,1)S(1)} %collective-permute-done.16.rest_1_, bf16[96,768]{1,0:T(8,128)(2,1)S(1)} %collective-permute-done.17.rest_2_, ...), custom_call_target="tpu_custom_call", output_to_operand_aliasing={{}: (7, {})} | custom-call | tf_op jit(solution)/shard_map/total/pallas_call | solution.py:309
  (38 shorter events, 3.2 us)
Async XLA Ops:
  0.6 1.1 %copy-start = (bf16[288,1152]{1,0:T(8,128)(2,1)S(1)}, bf16[288,1152]{1,0:T(8,128)(2,1)}, u32[]{:S(2)}) copy-start(bf16[288,1152]{1,0:T(8,128)(2,1)} %own.3) | copy-start | bytes 1990660
  1.7 25.7 %copy-start.4 = (bf16[256,1152]{1,0:T(8,128)(2,1)S(1)}, bf16[256,1152]{1,0:T(8,128)(2,1)}, u32[]{:S(2)}) copy-start(bf16[256,1152]{1,0:T(8,128)(2,1)} %text) | copy-start | bytes 1769476
  2.1 17.5 %collective-permute-start.4 = (bf16[256,1152]{1,0:T(8,128)(2,1)}, bf16[256,1152]{1,0:T(8,128)(2,1)S(1)}, u32[]{:S(2)}, u32[]{:S(2)}) collective-permute-start(bf16[256,1152]{1,0:T(8,128)(2,1)} %text), channel_id=1, source_target_pairs={{0,8},{4,12},{8,16},{12,20},{16,24},{20,28},{24,0},{28,4},{1,9},{5... | collective-permute-start | bytes 1769480 | tf_op jit(solution)/shard_map/ppermute | solution.py:334
  5.1 12.1 %collective-permute-start.3 = (bf16[80,1152]{1,0:T(8,128)(2,1)S(1)}, bf16[80,1152]{1,0:T(8,128)(2,1)S(1)}, u32[]{:S(2)}, u32[]{:S(2)}) collective-permute-start(bf16[80,1152]{1,0:T(8,128)(2,1)S(1)} %get-tuple-element.45), channel_id=1, source_target_pairs={{0,2},{1,3},{2,0},{3,1},{4,6},{5,7},{6,4},{7,5},{8,10},{9,11},{10,... | collective-permute-start | bytes 552968 | tf_op jit(solution)/shard_map/ppermute | solution.py:328
  7.7 20.4 %collective-permute-start.1 = (bf16[144,1152]{1,0:T(8,128)(2,1)S(1)}, bf16[144,1152]{1,0:T(8,128)(2,1)S(1)}, u32[]{:S(2)}, u32[]{:S(2)}) collective-permute-start(bf16[144,1152]{1,0:T(8,128)(2,1)S(1)} %get-tuple-element.43), channel_id=1, source_target_pairs={{0,3},{1,0},{2,1},{3,2},{4,7},{5,4},{6,5},{7,6},{8,11},{9,8},{10,9... | collective-permute-start | bytes 995336 | tf_op jit(solution)/shard_map/ppermute | solution.py:328
  9.0 19.1 %collective-permute-start = (bf16[144,1152]{1,0:T(8,128)(2,1)S(1)}, bf16[144,1152]{1,0:T(8,128)(2,1)S(1)}, u32[]{:S(2)}, u32[]{:S(2)}) collective-permute-start(bf16[144,1152]{1,0:T(8,128)(2,1)S(1)} %get-tuple-element.43), channel_id=1, source_target_pairs={{0,1},{1,2},{2,3},{3,0},{4,5},{5,6},{6,7},{7,4},{8,9},{9,10},{10,1... | collective-permute-start | bytes 995336 | tf_op jit(solution)/shard_map/ppermute | solution.py:328
  9.7 10.5 %collective-permute-start.2 = (bf16[256,1152]{1,0:T(8,128)(2,1)}, bf16[256,1152]{1,0:T(8,128)(2,1)S(1)}, u32[]{:S(2)}, u32[]{:S(2)}) collective-permute-start(bf16[256,1152]{1,0:T(8,128)(2,1)} %text), channel_id=1, source_target_pairs={{0,4},{4,0},{8,12},{12,8},{16,20},{20,16},{24,28},{28,24},{1,5},{5... | collective-permute-start | bytes 1769480 | tf_op jit(solution)/shard_map/ppermute | solution.py:331
  9.7 1.1 %copy-start.2 = (bf16[256,1152]{1,0:T(8,128)(2,1)S(1)}, bf16[256,1152]{1,0:T(8,128)(2,1)}, u32[]{:S(2)}) copy-start(bf16[256,1152]{1,0:T(8,128)(2,1)} %x.3) | copy-start | bytes 1769476
  19.6 12.8 %copy-start.1 = (bf16[288,1152]{1,0:T(8,128)(2,1)S(1)}, bf16[288,1152]{1,0:T(8,128)(2,1)}, u32[]{:S(2)}) copy-start(bf16[288,1152]{1,0:T(8,128)(2,1)} %own.3) | copy-start | bytes 1990660
  19.6 12.8 %copy-start.3 = (bf16[256,1152]{1,0:T(8,128)(2,1)S(1)}, bf16[256,1152]{1,0:T(8,128)(2,1)}, u32[]{:S(2)}) copy-start(bf16[256,1152]{1,0:T(8,128)(2,1)} %x.3) | copy-start | bytes 1769476
  19.7 5.0 %collective-permute-start.6 = (bf16[128,1152]{1,0:T(8,128)(2,1)S(1)}, bf16[128,1152]{1,0:T(8,128)(2,1)S(1)}, u32[]{:S(2)}, u32[]{:S(2)}) collective-permute-start(bf16[128,1152]{1,0:T(8,128)(2,1)S(1)} %get-tuple-element.80), channel_id=1, source_target_pairs={{0,4},{4,0},{8,12},{12,8},{16,20},{20,16},{24,28},{28,24},{1,5},{5... | collective-permute-start | bytes 884744 | tf_op jit(solution)/shard_map/ppermute | solution.py:331
  19.7 7.7 %collective-permute-start.5 = (bf16[128,1152]{1,0:T(8,128)(2,1)S(1)}, bf16[128,1152]{1,0:T(8,128)(2,1)S(1)}, u32[]{:S(2)}, u32[]{:S(2)}) collective-permute-start(bf16[128,1152]{1,0:T(8,128)(2,1)S(1)} %get-tuple-element.81), channel_id=1, source_target_pairs={{0,4},{4,0},{8,12},{12,8},{16,20},{20,16},{24,28},{28,24},{1,5},{5... | collective-permute-start | bytes 884744 | tf_op jit(solution)/shard_map/ppermute | solution.py:331
  20.2 16.7 %collective-permute-start.12 = (bf16[864,256]{1,0:T(8,128)(2,1)S(1)}, bf16[864,256]{1,0:T(8,128)(2,1)S(1)}, u32[]{:S(2)}, u32[]{:S(2)}) collective-permute-start(bf16[864,256]{1,0:T(8,128)(2,1)S(1)} %get-tuple-element.59), channel_id=1, source_target_pairs={{0,1},{1,0},{2,3},{3,2},{4,5},{5,4},{6,7},{7,6},{8,9},{9,8},{10,11... | collective-permute-start | bytes 1327112 | tf_op jit(solution)/shard_map/ppermute | solution.py:328
  24.6 6.3 %collective-permute-start.7 = (bf16[80,1152]{1,0:T(8,128)(2,1)S(1)}, bf16[80,1152]{1,0:T(8,128)(2,1)S(1)}, u32[]{:S(2)}, u32[]{:S(2)}) collective-permute-start(bf16[80,1152]{1,0:T(8,128)(2,1)S(1)} %collective-permute-done.3.rest_2_), channel_id=1, source_target_pairs={{0,8},{4,12},{8,0},{12,4},{16,24},{20,28},{24,16},{28,20},{1,9},{5... | collective-permute-start | bytes 552968 | tf_op jit(solution)/shard_map/ppermute | solution.py:346
  28.1 4.3 %collective-permute-start.8 = (bf16[144,1152]{1,0:T(8,128)(2,1)S(1)}, bf16[144,1152]{1,0:T(8,128)(2,1)S(1)}, u32[]{:S(2)}, u32[]{:S(2)}) collective-permute-start(bf16[144,1152]{1,0:T(8,128)(2,1)S(1)} %collective-permute-done.rest_0_), channel_id=1, source_target_pairs={{0,4},{4,0},{8,12},{12,8},{16,20},{20,16},{24,28},{28,24},{1,5},{5... | collective-permute-start | bytes 995336 | tf_op jit(solution)/shard_map/ppermute | solution.py:331
  28.2 4.2 %collective-permute-start.9 = (bf16[144,1152]{1,0:T(8,128)(2,1)S(1)}, bf16[144,1152]{1,0:T(8,128)(2,1)S(1)}, u32[]{:S(2)}, u32[]{:S(2)}) collective-permute-start(bf16[144,1152]{1,0:T(8,128)(2,1)S(1)} %collective-permute-done.1.rest_1_), channel_id=1, source_target_pairs={{0,4},{4,0},{8,12},{12,8},{16,20},{20,16},{24,28},{28,24},{1,5},{5... | collective-permute-start | bytes 995336 | tf_op jit(solution)/shard_map/ppermute | solution.py:331
  28.7 2.3 %collective-permute-start.10 = (bf16[80,1152]{1,0:T(8,128)(2,1)S(1)}, bf16[80,1152]{1,0:T(8,128)(2,1)S(1)}, u32[]{:S(2)}, u32[]{:S(2)}) collective-permute-start(bf16[80,1152]{1,0:T(8,128)(2,1)S(1)} %collective-permute-done.3.rest_2_), channel_id=1, source_target_pairs={{0,4},{4,0},{8,12},{12,8},{16,20},{20,16},{24,28},{28,24},{1,5},{5... | collective-permute-start | bytes 552968 | tf_op jit(solution)/shard_map/ppermute | solution.py:331
  31.0 1.4 %collective-permute-start.11 = (bf16[80,1152]{1,0:T(8,128)(2,1)S(1)}, bf16[80,1152]{1,0:T(8,128)(2,1)S(1)}, u32[]{:S(2)}, u32[]{:S(2)}) collective-permute-start(bf16[80,1152]{1,0:T(8,128)(2,1)S(1)} %collective-permute-done.7.rest_3_), channel_id=1, source_target_pairs={{0,4},{4,0},{8,12},{12,8},{16,20},{20,16},{24,28},{28,24},{1,5},{5... | collective-permute-start | bytes 552968 | tf_op jit(solution)/shard_map/ppermute | solution.py:331
  36.9 7.4 %collective-permute-start.13 = (bf16[288,384]{1,0:T(8,128)(2,1)S(1)}, bf16[288,384]{1,0:T(8,128)(2,1)S(1)}, u32[]{:S(2)}, u32[]{:S(2)}) collective-permute-start(bf16[288,384]{1,0:T(8,128)(2,1)S(1)} %get-tuple-element.64), channel_id=1, source_target_pairs={{0,1},{1,0},{2,3},{3,2},{4,5},{5,4},{6,7},{7,6},{8,9},{9,8},{10,11... | collective-permute-start | bytes 663560 | tf_op jit(solution)/shard_map/ppermute | solution.py:328
  37.6 25.2 %collective-permute-start.24 = (bf16[256,1152]{1,0:T(8,128)(2,1)S(1)}, bf16[256,1152]{1,0:T(8,128)(2,1)S(1)}, u32[]{:S(2)}, u32[]{:S(2)}) collective-permute-start(bf16[256,1152]{1,0:T(8,128)(2,1)S(1)} %get-tuple-element.77.u0), channel_id=1, source_target_pairs={{0,24},{4,28},{8,0},{12,4},{16,8},{20,12},{24,16},{28,20},{1,25},{... | collective-permute-start | bytes 1769480 | tf_op jit(solution)/shard_map/ppermute | solution.py:334
  39.0 31.5 %collective-permute-start.23 = (bf16[256,1152]{1,0:T(8,128)(2,1)S(1)}, bf16[256,1152]{1,0:T(8,128)(2,1)S(1)}, u32[]{:S(2)}, u32[]{:S(2)}) collective-permute-start(bf16[256,1152]{1,0:T(8,128)(2,1)S(1)} %get-tuple-element.77.u0), channel_id=1, source_target_pairs={{0,28},{4,0},{8,4},{12,8},{16,12},{20,16},{24,20},{28,24},{1,29},{... | collective-permute-start | bytes 1769480 | tf_op jit(solution)/shard_map/ppermute | solution.py:334
  44.3 16.0 %collective-permute-start.14 = (bf16[288,768]{1,0:T(8,128)(2,1)S(1)}, bf16[288,768]{1,0:T(8,128)(2,1)S(1)}, u32[]{:S(2)}, u32[]{:S(2)}) collective-permute-start(bf16[288,768]{1,0:T(8,128)(2,1)S(1)} %get-tuple-element.65), channel_id=1, source_target_pairs={{0,1},{1,0},{2,3},{3,2},{4,5},{5,4},{6,7},{7,6},{8,9},{9,8},{10,11... | collective-permute-start | bytes 1327112 | tf_op jit(solution)/shard_map/ppermute | solution.py:328
  44.9 16.5 %collective-permute-start.21 = (bf16[288,384]{1,0:T(8,128)(2,1)S(1)}, bf16[288,384]{1,0:T(8,128)(2,1)S(1)}, u32[]{:S(2)}, u32[]{:S(2)}) collective-permute-start(bf16[288,384]{1,0:T(8,128)(2,1)S(1)} %get-tuple-element.75), channel_id=1, source_target_pairs={{1,2},{2,1},{0,0},{3,3},{5,6},{6,5},{4,4},{7,7},{9,10},{10,9},{8,8... | collective-permute-start | bytes 663560 | tf_op jit(solution)/shard_map/ppermute | solution.py:328
  45.6 16.5 %collective-permute-start.22 = (bf16[288,384]{1,0:T(8,128)(2,1)S(1)}, bf16[288,384]{1,0:T(8,128)(2,1)S(1)}, u32[]{:S(2)}, u32[]{:S(2)}) collective-permute-start(bf16[288,384]{1,0:T(8,128)(2,1)S(1)} %get-tuple-element.76), channel_id=1, source_target_pairs={{1,3},{2,0},{5,7},{6,4},{9,11},{10,8},{13,15},{14,12},{17,19},{18,... | collective-permute-start | bytes 663560 | tf_op jit(solution)/shard_map/ppermute | solution.py:328
  60.7 9.9 %collective-permute-start.15 = (bf16[96,768]{1,0:T(8,128)(2,1)S(1)}, bf16[96,768]{1,0:T(8,128)(2,1)S(1)}, u32[]{:S(2)}, u32[]{:S(2)}) collective-permute-start(bf16[96,768]{1,0:T(8,128)(2,1)S(1)} %get-tuple-element.67), channel_id=1, source_target_pairs={{1,2},{2,1},{0,0},{3,3},{5,6},{6,5},{4,4},{7,7},{9,10},{10,9},{8,8... | collective-permute-start | bytes 442376 | tf_op jit(solution)/shard_map/ppermute | solution.py:328
  61.4 14.4 %collective-permute-start.16 = (bf16[96,768]{1,0:T(8,128)(2,1)S(1)}, bf16[96,768]{1,0:T(8,128)(2,1)S(1)}, u32[]{:S(2)}, u32[]{:S(2)}) collective-permute-start(bf16[96,768]{1,0:T(8,128)(2,1)S(1)} %get-tuple-element.68), channel_id=1, source_target_pairs={{1,2},{2,1},{0,0},{3,3},{5,6},{6,5},{4,4},{7,7},{9,10},{10,9},{8,8... | collective-permute-start | bytes 442376 | tf_op jit(solution)/shard_map/ppermute | solution.py:328
  62.1 13.7 %collective-permute-start.17 = (bf16[96,768]{1,0:T(8,128)(2,1)S(1)}, bf16[96,768]{1,0:T(8,128)(2,1)S(1)}, u32[]{:S(2)}, u32[]{:S(2)}) collective-permute-start(bf16[96,768]{1,0:T(8,128)(2,1)S(1)} %get-tuple-element.69), channel_id=1, source_target_pairs={{1,2},{2,1},{0,0},{3,3},{5,6},{6,5},{4,4},{7,7},{9,10},{10,9},{8,8... | collective-permute-start | bytes 442376 | tf_op jit(solution)/shard_map/ppermute | solution.py:328
  62.7 15.1 %collective-permute-start.18 = (bf16[96,768]{1,0:T(8,128)(2,1)S(1)}, bf16[96,768]{1,0:T(8,128)(2,1)S(1)}, u32[]{:S(2)}, u32[]{:S(2)}) collective-permute-start(bf16[96,768]{1,0:T(8,128)(2,1)S(1)} %get-tuple-element.70), channel_id=1, source_target_pairs={{1,3},{2,0},{0,1},{3,2},{5,7},{6,4},{4,5},{7,6},{9,11},{10,8},{8,9... | collective-permute-start | bytes 442376 | tf_op jit(solution)/shard_map/ppermute | solution.py:328
  70.5 9.0 %collective-permute-start.19 = (bf16[96,768]{1,0:T(8,128)(2,1)S(1)}, bf16[96,768]{1,0:T(8,128)(2,1)S(1)}, u32[]{:S(2)}, u32[]{:S(2)}) collective-permute-start(bf16[96,768]{1,0:T(8,128)(2,1)S(1)} %get-tuple-element.71), channel_id=1, source_target_pairs={{1,3},{2,0},{0,1},{3,2},{5,7},{6,4},{4,5},{7,6},{9,11},{10,8},{8,9... | collective-permute-start | bytes 442376 | tf_op jit(solution)/shard_map/ppermute | solution.py:328
  70.5 10.5 %collective-permute-start.20 = (bf16[96,768]{1,0:T(8,128)(2,1)S(1)}, bf16[96,768]{1,0:T(8,128)(2,1)S(1)}, u32[]{:S(2)}, u32[]{:S(2)}) collective-permute-start(bf16[96,768]{1,0:T(8,128)(2,1)S(1)} %get-tuple-element.72), channel_id=1, source_target_pairs={{1,3},{2,0},{0,1},{3,2},{5,7},{6,4},{4,5},{7,6},{9,11},{10,8},{8,9... | collective-permute-start | bytes 442376 | tf_op jit(solution)/shard_map/ppermute | solution.py:328

commit v11 on v10

--- a/solution.py
+++ b/solution.py
@@ -9,8 +9,8 @@
 
 STEPS = 3
 EPS = 1e-06
-SHARES = (1, 2)
-CROSS_PARTS = (1,3)
+SHARES = (3, 3, 3)
+CROSS_PARTS = (1, 2, 3)
 TEXT_PARTS = 2
 VMEM_BYTES = 24 * 1024 * 1024
 BF16, F32 = jnp.bfloat16, jnp.float32
@@ -366,7 +366,7 @@
     for parts, block in zip(CROSS_PARTS, arrived):
         kept, *sent = pair_product(begin, parts, x_t, far_t, grad, block, after)
         nears = [along(n, [(1, 2), (2, 1), (0, 0), (3, 3)]) for n in sent[:parts]]
-        ends = [(0, 1), (3, 2)] if begin > 0 else []
+        ends = [(0, 1), (3, 2)] if block is arrived[-1] else []
         fars = [along(n, [(1, 3), (2, 0)] + ends) for n in sent[parts:]]
         after = []
         terms.append((begin, width, kept, nears, fars))
@@ -374,7 +374,7 @@
     text_grad, done = text_side(text, scalars, unit, unit1, unit2)
     head = total(*terms[0], [])
     for term in terms[1:]:
-        head = total(*term, [head, done])
+        head = total(*term, [head, done] if term is terms[-1] else [head])
     return head, text_grad
 
 

time: 82.4 us -> 86.2 us (1.046)
  starting transfers between devices: 30.7 us -> 34.9 us
  waiting for transfers between devices: 37.6 us -> 36.2 us
    ppermute x14 -> x19, starting transfers between devices: 23.3 us -> 27.5 us  [along(): return lax.ppermute(value, 'fsdp', pairs)]
    ppermute x14 -> x19, waiting for transfers between devices: 31.6 us -> 30.2 us  [along(): return lax.ppermute(value, 'fsdp', pairs)]
    pallas_call x2 -> x3, Pallas kernels: 1.89 us -> 2.53 us  [total(): pl.pallas_call(functools.partial(total_kernel, begin, parts), out_shape=j...]
  transfers between devices with their start and end apart: 25 -> 30, of which waited for: 10 -> 10; matrix products, arithmetic and copies ran while one was open for 0% -> 0% of each run, Pallas kernels for 10% -> 11%
where the time goes in v11:
time: 86.2 us; the launch traced here: 85.8 us
  waiting for transfers between devices  36.2 us (42%)
  starting transfers between devices  34.9 us (40%)
  Pallas kernels  10.2 us (12%)
  between operations  2.23 us (3%)
  local copies, waits for them, and re-layouts  2.21 us (3%)
    ppermute x19, waiting for transfers between devices, along(): return lax.ppermute(value, 'fsdp', pairs)  30.2 us
    ppermute x19, starting transfers between devices, along(): return lax.ppermute(value, 'fsdp', pairs)  27.5 us
    ppermute x3, starting transfers between devices, shifted(): lax.ppermute(value, 'dp', [(d, (d + by) % n_dp) for d in range(n_dp)])  4.74 us
    pallas_call x1, Pallas kernels, picture_side(): pl.pallas_call(picture_kernel, out_shape=outs, in_specs=spaces(13), out_s...  2.85 us
    pallas_call x1, Pallas kernels, text_side(): pl.pallas_call(text_kernel, out_shape=(jax.ShapeDtypeStruct((rows, width)...  2.77 us
    pallas_call x3, Pallas kernels, total(): pl.pallas_call(functools.partial(total_kernel, begin, parts), out_shape=j...  2.53 us
    ppermute x3, waiting for transfers between devices, shifted(): lax.ppermute(value, 'dp', [(d, (d + by) % n_dp) for d in range(n_dp)])  2.39 us
    ppermute x1, waiting for transfers between devices, line_body(): two_crossed = lax.ppermute(two, 'dp', [(d, d ^ 2) for d in range(n_dp)])  2.17 us
  transfers between devices with their start and end apart: 30, of which 10 were waited for; matrix products, arithmetic and copies ran while one was open for 0% of the time, Pallas kernels for 11%

profile of v11, /device:TPU:0, one launch (start us, length us, event | category | flops | bytes accessed | tf_op | source)
XLA Modules:
  0.0 85.8 jit_solution(11529039823285972705)
XLA Ops:
  0.6 1.1 %copy-done = bf16[288,1152]{1,0:T(8,128)(2,1)S(1)} copy-done((bf16[288,1152]{1,0:T(8,128)(2,1)S(1)}, bf16[288,1152]{1,0:T(8,128)(2,1)}, u32[]{:S(2)}) %copy-start) | copy-done | bytes 663576
  2.1 3.0 %collective-permute-start.4 = (bf16[256,1152]{1,0:T(8,128)(2,1)}, bf16[256,1152]{1,0:T(8,128)(2,1)S(1)}, u32[]{:S(2)}, u32[]{:S(2)}) collective-permute-start(bf16[256,1152]{1,0:T(8,128)(2,1)} %text), channel_id=1, source_target_pairs={{0,8},{4,12},{8,16},{12,20},{16,24},{20,28},{24,0},{28,4},{1,9},{5... | collective-permute-start | bytes 1769480 | tf_op jit(solution)/shard_map/ppermute | solution.py:334
  5.1 2.6 %collective-permute-start.3 = (bf16[80,1152]{1,0:T(8,128)(2,1)S(1)}, bf16[80,1152]{1,0:T(8,128)(2,1)S(1)}, u32[]{:S(2)}, u32[]{:S(2)}) collective-permute-start(bf16[80,1152]{1,0:T(8,128)(2,1)S(1)} %get-tuple-element.53), channel_id=1, source_target_pairs={{0,2},{1,3},{2,0},{3,1},{4,6},{5,7},{6,4},{7,5},{8,10},{9,11},{10,... | collective-permute-start | bytes 552968 | tf_op jit(solution)/shard_map/ppermute | solution.py:328
  7.7 1.3 %collective-permute-start.1 = (bf16[144,1152]{1,0:T(8,128)(2,1)S(1)}, bf16[144,1152]{1,0:T(8,128)(2,1)S(1)}, u32[]{:S(2)}, u32[]{:S(2)}) collective-permute-start(bf16[144,1152]{1,0:T(8,128)(2,1)S(1)} %get-tuple-element.51), channel_id=1, source_target_pairs={{0,3},{1,0},{2,1},{3,2},{4,7},{5,4},{6,5},{7,6},{8,11},{9,8},{10,9... | collective-permute-start | bytes 995336 | tf_op jit(solution)/shard_map/ppermute | solution.py:328
  9.0 0.7 collective-permute-start
  9.7 1.1 %copy-done.2 = bf16[256,1152]{1,0:T(8,128)(2,1)S(1)} copy-done((bf16[256,1152]{1,0:T(8,128)(2,1)S(1)}, bf16[256,1152]{1,0:T(8,128)(2,1)}, u32[]{:S(2)}) %copy-start.2) | copy-done | bytes 589848
  11.0 6.2 %collective-permute-done.3.rest_2_ = bf16[80,1152]{1,0:T(8,128)(2,1)S(1)} collective-permute-done((bf16[80,1152]{1,0:T(8,128)(2,1)S(1)}, bf16[80,1152]{1,0:T(8,128)(2,1)S(1)}, u32[]{:S(2)}, u32[]{:S(2)}) %collective-permute-start.3) | collective-permute-done | bytes 184352 | tf_op jit(solution)/shard_map/ppermute | solution.py:328
  17.2 2.4 %collective-permute-done.4.t2 = bf16[256,1152]{1,0:T(8,128)(2,1)S(1)} collective-permute-done((bf16[256,1152]{1,0:T(8,128)(2,1)}, bf16[256,1152]{1,0:T(8,128)(2,1)S(1)}, u32[]{:S(2)}, u32[]{:S(2)}) %collective-permute-start.4) | collective-permute-done | bytes 589856 | tf_op jit(solution)/shard_map/ppermute | solution.py:334
  20.2 4.4 %collective-permute-start.12 = (bf16[864,256]{1,0:T(8,128)(2,1)S(1)}, bf16[864,256]{1,0:T(8,128)(2,1)S(1)}, u32[]{:S(2)}, u32[]{:S(2)}) collective-permute-start(bf16[864,256]{1,0:T(8,128)(2,1)S(1)} %get-tuple-element.67), channel_id=1, source_target_pairs={{0,1},{1,0},{2,3},{3,2},{4,5},{5,4},{6,7},{7,6},{8,9},{9,8},{10,11... | collective-permute-start | bytes 1327112 | tf_op jit(solution)/shard_map/ppermute | solution.py:328
  24.6 1.5 %collective-permute-start.7 = (bf16[80,1152]{1,0:T(8,128)(2,1)S(1)}, bf16[80,1152]{1,0:T(8,128)(2,1)S(1)}, u32[]{:S(2)}, u32[]{:S(2)}) collective-permute-start(bf16[80,1152]{1,0:T(8,128)(2,1)S(1)} %collective-permute-done.3.rest_2_), channel_id=1, source_target_pairs={{0,8},{4,12},{8,0},{12,4},{16,24},{20,28},{24,16},{28,20},{1,9},{5... | collective-permute-start | bytes 552968 | tf_op jit(solution)/shard_map/ppermute | solution.py:346
  27.4 0.7 prepare.1
  28.8 2.2 %collective-permute-done.7.rest_3_ = bf16[80,1152]{1,0:T(8,128)(2,1)S(1)} collective-permute-done((bf16[80,1152]{1,0:T(8,128)(2,1)S(1)}, bf16[80,1152]{1,0:T(8,128)(2,1)S(1)}, u32[]{:S(2)}, u32[]{:S(2)}) %collective-permute-start.7) | collective-permute-done | bytes 184352 | tf_op jit(solution)/shard_map/ppermute | solution.py:346
  31.0 1.4 %collective-permute-done.11.rest_7_ = bf16[80,1152]{1,0:T(8,128)(2,1)S(1)} collective-permute-done((bf16[80,1152]{1,0:T(8,128)(2,1)S(1)}, bf16[80,1152]{1,0:T(8,128)(2,1)S(1)}, u32[]{:S(2)}, u32[]{:S(2)}) %collective-permute-start.11) | collective-permute-done | bytes 184352 | tf_op jit(solution)/shard_map/ppermute | solution.py:331
  32.4 2.9 %picture_side.1 = (bf16[288,384]{1,0:T(8,128)(2,1)S(1)}, bf16[288,384]{1,0:T(8,128)(2,1)S(1)}, bf16[288,384]{1,0:T(8,128)(2,1)S(1)}, bf16[256,1152]{1,0:T(8,128)(2,1)S(1)}, bf16[256,1152]{1,0:T(8,128)(2,1)S(1)}) custom-call(bf16[256,1152]{1,0:T(8,128)(2,1)S(1)} %copy-done.3, bf16[1152,256]{1,0:T(8,128)(2,1)S(1)} %get-tuple-element.59.x_t, ...), custom_call_target="tpu_custom_call" | custom-call | tf_op jit(solution)/shard_map/picture_side/pallas_call | solution.py:206
  35.3 1.7 %collective-permute-done.12.far_t = bf16[864,256]{1,0:T(8,128)(2,1)S(1)} collective-permute-done((bf16[864,256]{1,0:T(8,128)(2,1)S(1)}, bf16[864,256]{1,0:T(8,128)(2,1)S(1)}, u32[]{:S(2)}, u32[]{:S(2)}) %collective-permute-start.12) | collective-permute-done | bytes 442400 | tf_op jit(solution)/shard_map/ppermute | solution.py:328
  37.6 1.4 %collective-permute-start.29 = (bf16[256,1152]{1,0:T(8,128)(2,1)S(1)}, bf16[256,1152]{1,0:T(8,128)(2,1)S(1)}, u32[]{:S(2)}, u32[]{:S(2)}) collective-permute-start(bf16[256,1152]{1,0:T(8,128)(2,1)S(1)} %get-tuple-element.93.u0), channel_id=1, source_target_pairs={{0,24},{4,28},{8,0},{12,4},{16,8},{20,12},{24,16},{28,20},{1,25},{... | collective-permute-start | bytes 1769480 | tf_op jit(solution)/shard_map/ppermute | solution.py:334
  39.3 5.0 %collective-permute-done.13.arrived = bf16[288,384]{1,0:T(8,128)(2,1)S(1)} collective-permute-done((bf16[288,384]{1,0:T(8,128)(2,1)S(1)}, bf16[288,384]{1,0:T(8,128)(2,1)S(1)}, u32[]{:S(2)}, u32[]{:S(2)}) %collective-permute-start.13) | collective-permute-done | bytes 221216 | tf_op jit(solution)/shard_map/ppermute | solution.py:328
  44.9 0.7 collective-permute-start.26
  45.6 1.3 %collective-permute-start.27 = (bf16[288,384]{1,0:T(8,128)(2,1)S(1)}, bf16[288,384]{1,0:T(8,128)(2,1)S(1)}, u32[]{:S(2)}, u32[]{:S(2)}) collective-permute-start(bf16[288,384]{1,0:T(8,128)(2,1)S(1)} %get-tuple-element.92), channel_id=1, source_target_pairs={{1,3},{2,0},{5,7},{6,4},{9,11},{10,8},{13,15},{14,12},{17,19},{18,... | collective-permute-start | bytes 663560 | tf_op jit(solution)/shard_map/ppermute | solution.py:328
  46.9 4.0 %collective-permute-done.14.arrived = bf16[288,384]{1,0:T(8,128)(2,1)S(1)} collective-permute-done((bf16[288,384]{1,0:T(8,128)(2,1)S(1)}, bf16[288,384]{1,0:T(8,128)(2,1)S(1)}, u32[]{:S(2)}, u32[]{:S(2)}) %collective-permute-start.14) | collective-permute-done | bytes 221216 | tf_op jit(solution)/shard_map/ppermute | solution.py:328
  50.9 1.2 %collective-permute-start.15 = (bf16[288,384]{1,0:T(8,128)(2,1)S(1)}, bf16[288,384]{1,0:T(8,128)(2,1)S(1)}, u32[]{:S(2)}, u32[]{:S(2)}) collective-permute-start(bf16[288,384]{1,0:T(8,128)(2,1)S(1)} %get-tuple-element.75), channel_id=1, source_target_pairs={{0,1},{1,0},{2,3},{3,2},{4,5},{5,4},{6,7},{7,6},{8,9},{9,8},{10,11... | collective-permute-start | bytes 663560 | tf_op jit(solution)/shard_map/ppermute | solution.py:328
  53.1 7.6 %collective-permute-done.27.rest_1_ = bf16[288,384]{1,0:T(8,128)(2,1)S(1)} collective-permute-done((bf16[288,384]{1,0:T(8,128)(2,1)S(1)}, bf16[288,384]{1,0:T(8,128)(2,1)S(1)}, u32[]{:S(2)}, u32[]{:S(2)}) %collective-permute-start.27) | collective-permute-done | bytes 221216 | tf_op jit(solution)/shard_map/ppermute | solution.py:328
  61.3 1.3 %collective-permute-start.24 = (bf16[144,384]{1,0:T(8,128)(2,1)S(1)}, bf16[144,384]{1,0:T(8,128)(2,1)S(1)}, u32[]{:S(2)}, u32[]{:S(2)}) collective-permute-start(bf16[144,384]{1,0:T(8,128)(2,1)S(1)} %get-tuple-element.87), channel_id=1, source_target_pairs={{1,3},{2,0},{5,7},{6,4},{9,11},{10,8},{13,15},{14,12},{17,19},{18,... | collective-permute-start | bytes 331784 | tf_op jit(solution)/shard_map/ppermute | solution.py:328
  62.6 1.3 %collective-permute-start.25 = (bf16[144,384]{1,0:T(8,128)(2,1)S(1)}, bf16[144,384]{1,0:T(8,128)(2,1)S(1)}, u32[]{:S(2)}, u32[]{:S(2)}) collective-permute-start(bf16[144,384]{1,0:T(8,128)(2,1)S(1)} %get-tuple-element.88), channel_id=1, source_target_pairs={{1,3},{2,0},{5,7},{6,4},{9,11},{10,8},{13,15},{14,12},{17,19},{18,... | collective-permute-start | bytes 331784 | tf_op jit(solution)/shard_map/ppermute | solution.py:328
  64.9 4.5 %collective-permute-done.24.rest_2_ = bf16[144,384]{1,0:T(8,128)(2,1)S(1)} collective-permute-done((bf16[144,384]{1,0:T(8,128)(2,1)S(1)}, bf16[144,384]{1,0:T(8,128)(2,1)S(1)}, u32[]{:S(2)}, u32[]{:S(2)}) %collective-permute-start.24) | collective-permute-done | bytes 110624 | tf_op jit(solution)/shard_map/ppermute | solution.py:328
  70.1 1.2 %collective-permute-done.25.rest_3_ = bf16[144,384]{1,0:T(8,128)(2,1)S(1)} collective-permute-done((bf16[144,384]{1,0:T(8,128)(2,1)S(1)}, bf16[144,384]{1,0:T(8,128)(2,1)S(1)}, u32[]{:S(2)}, u32[]{:S(2)}) %collective-permute-start.25) | collective-permute-done | bytes 110624 | tf_op jit(solution)/shard_map/ppermute | solution.py:328
  72.0 5.0 %collective-permute-start.19 = (bf16[96,384]{1,0:T(8,128)(2,1)S(1)}, bf16[96,384]{1,0:T(8,128)(2,1)S(1)}, u32[]{:S(2)}, u32[]{:S(2)}) collective-permute-start(bf16[96,384]{1,0:T(8,128)(2,1)S(1)} %get-tuple-element.80), channel_id=1, source_target_pairs={{1,3},{2,0},{0,1},{3,2},{5,7},{6,4},{4,5},{7,6},{9,11},{10,8},{8,9... | collective-permute-start | bytes 221192 | tf_op jit(solution)/shard_map/ppermute | solution.py:328
  77.1 3.4 %collective-permute-start.21 = (bf16[96,384]{1,0:T(8,128)(2,1)S(1)}, bf16[96,384]{1,0:T(8,128)(2,1)S(1)}, u32[]{:S(2)}, u32[]{:S(2)}) collective-permute-start(bf16[96,384]{1,0:T(8,128)(2,1)S(1)} %get-tuple-element.82), channel_id=1, source_target_pairs={{1,3},{2,0},{0,1},{3,2},{5,7},{6,4},{4,5},{7,6},{9,11},{10,8},{8,9... | collective-permute-start | bytes 221192 | tf_op jit(solution)/shard_map/ppermute | solution.py:328
  80.5 0.8 total.3.rest_4_
  81.3 0.9 total.4.rest_6_
  82.2 2.8 %text_side.1 = (f32[256,1152]{1,0:T(8,128)}, f32[8,128]{1,0:T(8,128)S(1)}) custom-call(bf16[256,1152]{1,0:T(8,128)(2,1)S(1)} %copy-done.4, f32[8,128]{1,0:T(8,128)S(1)} %get-tuple-element.61.scalars, bf16[256,1152]{1,0:T(8,128)(2,1)S(1)} %get-tuple-element.93.u0, bf16[256,1152]{1,0:T(8,128)(2,1)S(1)} %collective-permute-done.28.u1, ...), custom_call_target="tpu_custom_call" | custom-call | tf_op jit(solution)/shard_map/text_side/pallas_call | solution.py:238
  85.0 0.8 total.5
  (50 shorter events, 7.3 us)
Async XLA Ops:
  1.7 25.7 %copy-start.4 = (bf16[256,1152]{1,0:T(8,128)(2,1)S(1)}, bf16[256,1152]{1,0:T(8,128)(2,1)}, u32[]{:S(2)}) copy-start(bf16[256,1152]{1,0:T(8,128)(2,1)} %text) | copy-start | bytes 1769476
  2.1 17.5 %collective-permute-start.4 = (bf16[256,1152]{1,0:T(8,128)(2,1)}, bf16[256,1152]{1,0:T(8,128)(2,1)S(1)}, u32[]{:S(2)}, u32[]{:S(2)}) collective-permute-start(bf16[256,1152]{1,0:T(8,128)(2,1)} %text), channel_id=1, source_target_pairs={{0,8},{4,12},{8,16},{12,20},{16,24},{20,28},{24,0},{28,4},{1,9},{5... | collective-permute-start | bytes 1769480 | tf_op jit(solution)/shard_map/ppermute | solution.py:334
  5.1 12.1 %collective-permute-start.3 = (bf16[80,1152]{1,0:T(8,128)(2,1)S(1)}, bf16[80,1152]{1,0:T(8,128)(2,1)S(1)}, u32[]{:S(2)}, u32[]{:S(2)}) collective-permute-start(bf16[80,1152]{1,0:T(8,128)(2,1)S(1)} %get-tuple-element.53), channel_id=1, source_target_pairs={{0,2},{1,3},{2,0},{3,1},{4,6},{5,7},{6,4},{7,5},{8,10},{9,11},{10,... | collective-permute-start | bytes 552968 | tf_op jit(solution)/shard_map/ppermute | solution.py:328
  7.7 20.4 %collective-permute-start.1 = (bf16[144,1152]{1,0:T(8,128)(2,1)S(1)}, bf16[144,1152]{1,0:T(8,128)(2,1)S(1)}, u32[]{:S(2)}, u32[]{:S(2)}) collective-permute-start(bf16[144,1152]{1,0:T(8,128)(2,1)S(1)} %get-tuple-element.51), channel_id=1, source_target_pairs={{0,3},{1,0},{2,1},{3,2},{4,7},{5,4},{6,5},{7,6},{8,11},{9,8},{10,9... | collective-permute-start | bytes 995336 | tf_op jit(solution)/shard_map/ppermute | solution.py:328
  9.0 19.1 %collective-permute-start = (bf16[144,1152]{1,0:T(8,128)(2,1)S(1)}, bf16[144,1152]{1,0:T(8,128)(2,1)S(1)}, u32[]{:S(2)}, u32[]{:S(2)}) collective-permute-start(bf16[144,1152]{1,0:T(8,128)(2,1)S(1)} %get-tuple-element.51), channel_id=1, source_target_pairs={{0,1},{1,2},{2,3},{3,0},{4,5},{5,6},{6,7},{7,4},{8,9},{9,10},{10,1... | collective-permute-start | bytes 995336 | tf_op jit(solution)/shard_map/ppermute | solution.py:328
  9.7 10.5 %collective-permute-start.2 = (bf16[256,1152]{1,0:T(8,128)(2,1)}, bf16[256,1152]{1,0:T(8,128)(2,1)S(1)}, u32[]{:S(2)}, u32[]{:S(2)}) collective-permute-start(bf16[256,1152]{1,0:T(8,128)(2,1)} %text), channel_id=1, source_target_pairs={{0,4},{4,0},{8,12},{12,8},{16,20},{20,16},{24,28},{28,24},{1,5},{5... | collective-permute-start | bytes 1769480 | tf_op jit(solution)/shard_map/ppermute | solution.py:331
  19.6 12.8 %copy-start.1 = (bf16[288,1152]{1,0:T(8,128)(2,1)S(1)}, bf16[288,1152]{1,0:T(8,128)(2,1)}, u32[]{:S(2)}) copy-start(bf16[288,1152]{1,0:T(8,128)(2,1)} %own.3) | copy-start | bytes 1990660
  19.7 5.0 %collective-permute-start.6 = (bf16[128,1152]{1,0:T(8,128)(2,1)S(1)}, bf16[128,1152]{1,0:T(8,128)(2,1)S(1)}, u32[]{:S(2)}, u32[]{:S(2)}) collective-permute-start(bf16[128,1152]{1,0:T(8,128)(2,1)S(1)} %get-tuple-element.96), channel_id=1, source_target_pairs={{0,4},{4,0},{8,12},{12,8},{16,20},{20,16},{24,28},{28,24},{1,5},{5... | collective-permute-start | bytes 884744 | tf_op jit(solution)/shard_map/ppermute | solution.py:331
  19.7 7.7 %collective-permute-start.5 = (bf16[128,1152]{1,0:T(8,128)(2,1)S(1)}, bf16[128,1152]{1,0:T(8,128)(2,1)S(1)}, u32[]{:S(2)}, u32[]{:S(2)}) collective-permute-start(bf16[128,1152]{1,0:T(8,128)(2,1)S(1)} %get-tuple-element.97), channel_id=1, source_target_pairs={{0,4},{4,0},{8,12},{12,8},{16,20},{20,16},{24,28},{28,24},{1,5},{5... | collective-permute-start | bytes 884744 | tf_op jit(solution)/shard_map/ppermute | solution.py:331
  20.2 16.7 %collective-permute-start.12 = (bf16[864,256]{1,0:T(8,128)(2,1)S(1)}, bf16[864,256]{1,0:T(8,128)(2,1)S(1)}, u32[]{:S(2)}, u32[]{:S(2)}) collective-permute-start(bf16[864,256]{1,0:T(8,128)(2,1)S(1)} %get-tuple-element.67), channel_id=1, source_target_pairs={{0,1},{1,0},{2,3},{3,2},{4,5},{5,4},{6,7},{7,6},{8,9},{9,8},{10,11... | collective-permute-start | bytes 1327112 | tf_op jit(solution)/shard_map/ppermute | solution.py:328
  24.6 6.3 %collective-permute-start.7 = (bf16[80,1152]{1,0:T(8,128)(2,1)S(1)}, bf16[80,1152]{1,0:T(8,128)(2,1)S(1)}, u32[]{:S(2)}, u32[]{:S(2)}) collective-permute-start(bf16[80,1152]{1,0:T(8,128)(2,1)S(1)} %collective-permute-done.3.rest_2_), channel_id=1, source_target_pairs={{0,8},{4,12},{8,0},{12,4},{16,24},{20,28},{24,16},{28,20},{1,9},{5... | collective-permute-start | bytes 552968 | tf_op jit(solution)/shard_map/ppermute | solution.py:346
  28.1 4.3 %collective-permute-start.8 = (bf16[144,1152]{1,0:T(8,128)(2,1)S(1)}, bf16[144,1152]{1,0:T(8,128)(2,1)S(1)}, u32[]{:S(2)}, u32[]{:S(2)}) collective-permute-start(bf16[144,1152]{1,0:T(8,128)(2,1)S(1)} %collective-permute-done.rest_0_), channel_id=1, source_target_pairs={{0,4},{4,0},{8,12},{12,8},{16,20},{20,16},{24,28},{28,24},{1,5},{5... | collective-permute-start | bytes 995336 | tf_op jit(solution)/shard_map/ppermute | solution.py:331
  28.2 4.2 %collective-permute-start.9 = (bf16[144,1152]{1,0:T(8,128)(2,1)S(1)}, bf16[144,1152]{1,0:T(8,128)(2,1)S(1)}, u32[]{:S(2)}, u32[]{:S(2)}) collective-permute-start(bf16[144,1152]{1,0:T(8,128)(2,1)S(1)} %collective-permute-done.1.rest_1_), channel_id=1, source_target_pairs={{0,4},{4,0},{8,12},{12,8},{16,20},{20,16},{24,28},{28,24},{1,5},{5... | collective-permute-start | bytes 995336 | tf_op jit(solution)/shard_map/ppermute | solution.py:331
  28.7 2.3 %collective-permute-start.10 = (bf16[80,1152]{1,0:T(8,128)(2,1)S(1)}, bf16[80,1152]{1,0:T(8,128)(2,1)S(1)}, u32[]{:S(2)}, u32[]{:S(2)}) collective-permute-start(bf16[80,1152]{1,0:T(8,128)(2,1)S(1)} %collective-permute-done.3.rest_2_), channel_id=1, source_target_pairs={{0,4},{4,0},{8,12},{12,8},{16,20},{20,16},{24,28},{28,24},{1,5},{5... | collective-permute-start | bytes 552968 | tf_op jit(solution)/shard_map/ppermute | solution.py:331
  31.0 1.4 %collective-permute-start.11 = (bf16[80,1152]{1,0:T(8,128)(2,1)S(1)}, bf16[80,1152]{1,0:T(8,128)(2,1)S(1)}, u32[]{:S(2)}, u32[]{:S(2)}) collective-permute-start(bf16[80,1152]{1,0:T(8,128)(2,1)S(1)} %collective-permute-done.7.rest_3_), channel_id=1, source_target_pairs={{0,4},{4,0},{8,12},{12,8},{16,20},{20,16},{24,28},{28,24},{1,5},{5... | collective-permute-start | bytes 552968 | tf_op jit(solution)/shard_map/ppermute | solution.py:331
  36.9 7.4 %collective-permute-start.13 = (bf16[288,384]{1,0:T(8,128)(2,1)S(1)}, bf16[288,384]{1,0:T(8,128)(2,1)S(1)}, u32[]{:S(2)}, u32[]{:S(2)}) collective-permute-start(bf16[288,384]{1,0:T(8,128)(2,1)S(1)} %get-tuple-element.73), channel_id=1, source_target_pairs={{0,1},{1,0},{2,3},{3,2},{4,5},{5,4},{6,7},{7,6},{8,9},{9,8},{10,11... | collective-permute-start | bytes 663560 | tf_op jit(solution)/shard_map/ppermute | solution.py:328
  37.6 34.4 %collective-permute-start.29 = (bf16[256,1152]{1,0:T(8,128)(2,1)S(1)}, bf16[256,1152]{1,0:T(8,128)(2,1)S(1)}, u32[]{:S(2)}, u32[]{:S(2)}) collective-permute-start(bf16[256,1152]{1,0:T(8,128)(2,1)S(1)} %get-tuple-element.93.u0), channel_id=1, source_target_pairs={{0,24},{4,28},{8,0},{12,4},{16,8},{20,12},{24,16},{28,20},{1,25},{... | collective-permute-start | bytes 1769480 | tf_op jit(solution)/shard_map/ppermute | solution.py:334
  39.0 38.0 %collective-permute-start.28 = (bf16[256,1152]{1,0:T(8,128)(2,1)S(1)}, bf16[256,1152]{1,0:T(8,128)(2,1)S(1)}, u32[]{:S(2)}, u32[]{:S(2)}) collective-permute-start(bf16[256,1152]{1,0:T(8,128)(2,1)S(1)} %get-tuple-element.93.u0), channel_id=1, source_target_pairs={{0,28},{4,0},{8,4},{12,8},{16,12},{20,16},{24,20},{28,24},{1,29},{... | collective-permute-start | bytes 1769480 | tf_op jit(solution)/shard_map/ppermute | solution.py:334
  44.3 6.5 %collective-permute-start.14 = (bf16[288,384]{1,0:T(8,128)(2,1)S(1)}, bf16[288,384]{1,0:T(8,128)(2,1)S(1)}, u32[]{:S(2)}, u32[]{:S(2)}) collective-permute-start(bf16[288,384]{1,0:T(8,128)(2,1)S(1)} %get-tuple-element.74), channel_id=1, source_target_pairs={{0,1},{1,0},{2,3},{3,2},{4,5},{5,4},{6,7},{7,6},{8,9},{9,8},{10,11... | collective-permute-start | bytes 663560 | tf_op jit(solution)/shard_map/ppermute | solution.py:328
  44.9 7.5 %collective-permute-start.26 = (bf16[288,384]{1,0:T(8,128)(2,1)S(1)}, bf16[288,384]{1,0:T(8,128)(2,1)S(1)}, u32[]{:S(2)}, u32[]{:S(2)}) collective-permute-start(bf16[288,384]{1,0:T(8,128)(2,1)S(1)} %get-tuple-element.91), channel_id=1, source_target_pairs={{1,2},{2,1},{0,0},{3,3},{5,6},{6,5},{4,4},{7,7},{9,10},{10,9},{8,8... | collective-permute-start | bytes 663560 | tf_op jit(solution)/shard_map/ppermute | solution.py:328
  45.6 15.1 %collective-permute-start.27 = (bf16[288,384]{1,0:T(8,128)(2,1)S(1)}, bf16[288,384]{1,0:T(8,128)(2,1)S(1)}, u32[]{:S(2)}, u32[]{:S(2)}) collective-permute-start(bf16[288,384]{1,0:T(8,128)(2,1)S(1)} %get-tuple-element.92), channel_id=1, source_target_pairs={{1,3},{2,0},{5,7},{6,4},{9,11},{10,8},{13,15},{14,12},{17,19},{18,... | collective-permute-start | bytes 663560 | tf_op jit(solution)/shard_map/ppermute | solution.py:328
  50.9 11.8 %collective-permute-start.15 = (bf16[288,384]{1,0:T(8,128)(2,1)S(1)}, bf16[288,384]{1,0:T(8,128)(2,1)S(1)}, u32[]{:S(2)}, u32[]{:S(2)}) collective-permute-start(bf16[288,384]{1,0:T(8,128)(2,1)S(1)} %get-tuple-element.75), channel_id=1, source_target_pairs={{0,1},{1,0},{2,3},{3,2},{4,5},{5,4},{6,7},{7,6},{8,9},{9,8},{10,11... | collective-permute-start | bytes 663560 | tf_op jit(solution)/shard_map/ppermute | solution.py:328
  52.4 8.9 %collective-permute-start.22 = (bf16[144,384]{1,0:T(8,128)(2,1)S(1)}, bf16[144,384]{1,0:T(8,128)(2,1)S(1)}, u32[]{:S(2)}, u32[]{:S(2)}) collective-permute-start(bf16[144,384]{1,0:T(8,128)(2,1)S(1)} %get-tuple-element.85), channel_id=1, source_target_pairs={{1,2},{2,1},{0,0},{3,3},{5,6},{6,5},{4,4},{7,7},{9,10},{10,9},{8,8... | collective-permute-start | bytes 331784 | tf_op jit(solution)/shard_map/ppermute | solution.py:328
  60.7 3.6 %collective-permute-start.23 = (bf16[144,384]{1,0:T(8,128)(2,1)S(1)}, bf16[144,384]{1,0:T(8,128)(2,1)S(1)}, u32[]{:S(2)}, u32[]{:S(2)}) collective-permute-start(bf16[144,384]{1,0:T(8,128)(2,1)S(1)} %get-tuple-element.86), channel_id=1, source_target_pairs={{1,2},{2,1},{0,0},{3,3},{5,6},{6,5},{4,4},{7,7},{9,10},{10,9},{8,8... | collective-permute-start | bytes 331784 | tf_op jit(solution)/shard_map/ppermute | solution.py:328
  61.3 8.1 %collective-permute-start.24 = (bf16[144,384]{1,0:T(8,128)(2,1)S(1)}, bf16[144,384]{1,0:T(8,128)(2,1)S(1)}, u32[]{:S(2)}, u32[]{:S(2)}) collective-permute-start(bf16[144,384]{1,0:T(8,128)(2,1)S(1)} %get-tuple-element.87), channel_id=1, source_target_pairs={{1,3},{2,0},{5,7},{6,4},{9,11},{10,8},{13,15},{14,12},{17,19},{18,... | collective-permute-start | bytes 331784 | tf_op jit(solution)/shard_map/ppermute | solution.py:328
  62.6 8.6 %collective-permute-start.25 = (bf16[144,384]{1,0:T(8,128)(2,1)S(1)}, bf16[144,384]{1,0:T(8,128)(2,1)S(1)}, u32[]{:S(2)}, u32[]{:S(2)}) collective-permute-start(bf16[144,384]{1,0:T(8,128)(2,1)S(1)} %get-tuple-element.88), channel_id=1, source_target_pairs={{1,3},{2,0},{5,7},{6,4},{9,11},{10,8},{13,15},{14,12},{17,19},{18,... | collective-permute-start | bytes 331784 | tf_op jit(solution)/shard_map/ppermute | solution.py:328
  64.2 12.8 %collective-permute-start.16 = (bf16[96,384]{1,0:T(8,128)(2,1)S(1)}, bf16[96,384]{1,0:T(8,128)(2,1)S(1)}, u32[]{:S(2)}, u32[]{:S(2)}) collective-permute-start(bf16[96,384]{1,0:T(8,128)(2,1)S(1)} %get-tuple-element.77), channel_id=1, source_target_pairs={{1,2},{2,1},{0,0},{3,3},{5,6},{6,5},{4,4},{7,7},{9,10},{10,9},{8,8... | collective-permute-start | bytes 221192 | tf_op jit(solution)/shard_map/ppermute | solution.py:328
  69.4 15.5 %collective-permute-start.17 = (bf16[96,384]{1,0:T(8,128)(2,1)S(1)}, bf16[96,384]{1,0:T(8,128)(2,1)S(1)}, u32[]{:S(2)}, u32[]{:S(2)}) collective-permute-start(bf16[96,384]{1,0:T(8,128)(2,1)S(1)} %get-tuple-element.78), channel_id=1, source_target_pairs={{1,2},{2,1},{0,0},{3,3},{5,6},{6,5},{4,4},{7,7},{9,10},{10,9},{8,8... | collective-permute-start | bytes 221192 | tf_op jit(solution)/shard_map/ppermute | solution.py:328
  71.3 13.7 %collective-permute-start.18 = (bf16[96,384]{1,0:T(8,128)(2,1)S(1)}, bf16[96,384]{1,0:T(8,128)(2,1)S(1)}, u32[]{:S(2)}, u32[]{:S(2)}) collective-permute-start(bf16[96,384]{1,0:T(8,128)(2,1)S(1)} %get-tuple-element.79), channel_id=1, source_target_pairs={{1,2},{2,1},{0,0},{3,3},{5,6},{6,5},{4,4},{7,7},{9,10},{10,9},{8,8... | collective-permute-start | bytes 221192 | tf_op jit(solution)/shard_map/ppermute | solution.py:328
  72.0 13.0 %collective-permute-start.19 = (bf16[96,384]{1,0:T(8,128)(2,1)S(1)}, bf16[96,384]{1,0:T(8,128)(2,1)S(1)}, u32[]{:S(2)}, u32[]{:S(2)}) collective-permute-start(bf16[96,384]{1,0:T(8,128)(2,1)S(1)} %get-tuple-element.80), channel_id=1, source_target_pairs={{1,3},{2,0},{0,1},{3,2},{5,7},{6,4},{4,5},{7,6},{9,11},{10,8},{8,9... | collective-permute-start | bytes 221192 | tf_op jit(solution)/shard_map/ppermute | solution.py:328
  77.0 8.0 %collective-permute-start.20 = (bf16[96,384]{1,0:T(8,128)(2,1)S(1)}, bf16[96,384]{1,0:T(8,128)(2,1)S(1)}, u32[]{:S(2)}, u32[]{:S(2)}) collective-permute-start(bf16[96,384]{1,0:T(8,128)(2,1)S(1)} %get-tuple-element.81), channel_id=1, source_target_pairs={{1,3},{2,0},{0,1},{3,2},{5,7},{6,4},{4,5},{7,6},{9,11},{10,8},{8,9... | collective-permute-start | bytes 221192 | tf_op jit(solution)/shard_map/ppermute | solution.py:328
  77.1 7.9 %collective-permute-start.21 = (bf16[96,384]{1,0:T(8,128)(2,1)S(1)}, bf16[96,384]{1,0:T(8,128)(2,1)S(1)}, u32[]{:S(2)}, u32[]{:S(2)}) collective-permute-start(bf16[96,384]{1,0:T(8,128)(2,1)S(1)} %get-tuple-element.82), channel_id=1, source_target_pairs={{1,3},{2,0},{0,1},{3,2},{5,7},{6,4},{4,5},{7,6},{9,11},{10,8},{8,9... | collective-permute-start | bytes 221192 | tf_op jit(solution)/shard_map/ppermute | solution.py:328
  (3 other events, 14.9 us)

commit v12 on v9

--- a/solution.py
+++ b/solution.py
@@ -10,7 +10,7 @@
 STEPS = 3
 EPS = 1e-06
 SHARES = (1, 2)
-CROSS_PARTS = (1,3)
+CROSS_PARTS = (1, 3)
 TEXT_PARTS = 2
 VMEM_BYTES = 24 * 1024 * 1024
 BF16, F32 = jnp.bfloat16, jnp.float32
@@ -249,7 +249,7 @@
 
 def pair_kernel(begin, parts, x_t, far_t, grad, arrived, *rest):
     outs = rest[-1 - 2 * parts :]
-    kept, nears, fars = outs[0], outs[1 : 1 + parts], outs[1 + parts :]
+    kept, fars, nears = outs[0], outs[1 : 1 + parts], outs[1 + parts :]
     rows = grad.shape[0]
     depth, size = arrived.shape
     part = lax.axis_index("fsdp")
@@ -365,10 +365,10 @@
     begin, terms, after = 0, [], []
     for parts, block in zip(CROSS_PARTS, arrived):
         kept, *sent = pair_product(begin, parts, x_t, far_t, grad, block, after)
-        nears = [along(n, [(1, 2), (2, 1), (0, 0), (3, 3)]) for n in sent[:parts]]
-        fars = [along(n, [(1, 3), (2, 0), (0, 1), (3, 2)]) for n in sent[parts:]]
+        fars = [along(n, [(1, 3), (2, 0), (0, 1), (3, 2)]) for n in sent[:parts]]
+        nears = [along(n, [(1, 2), (2, 1), (0, 0), (3, 3)]) for n in sent[parts:]]
         after = []
-        terms.append((begin, width, kept, nears, fars))
+        terms.append((begin, width, kept, fars, nears))
         begin += block.shape[1]
     text_grad, done = text_side(text, scalars, unit, unit1, unit2)
     head = total(*terms[0], [])

time: 82.4 us -> 80.6 us (0.978)
  the two profiles are of different devices: /device:TPU:0 before, /device:TPU:18 now
where the time goes in v12:
time: 80.6 us; the launch traced here: 80.3 us
  waiting for transfers between devices  33 us (41%)
  starting transfers between devices  32.3 us (40%)
  Pallas kernels  10.6 us (13%)
  local copies, waits for them, and re-layouts  2.21 us (3%)
  between operations  2.14 us (3%)
    ppermute x14, starting transfers between devices, along(): return lax.ppermute(value, 'fsdp', pairs)  28.1 us
    ppermute x14, waiting for transfers between devices, along(): return lax.ppermute(value, 'fsdp', pairs)  25.9 us
    ppermute x3, waiting for transfers between devices, shifted(): lax.ppermute(value, 'dp', [(d, (d + by) % n_dp) for d in range(n_dp)])  4.73 us
    pallas_call x1, Pallas kernels, picture_side(): pl.pallas_call(picture_kernel, out_shape=outs, in_specs=spaces(13), out_s...  3.16 us
    pallas_call x1, Pallas kernels, text_side(): pl.pallas_call(text_kernel, out_shape=(jax.ShapeDtypeStruct((rows, width)...  2.76 us
    ppermute x3, starting transfers between devices, shifted(): lax.ppermute(value, 'dp', [(d, (d + by) % n_dp) for d in range(n_dp)])  2.6 us
    unnamed x10, local copies, waits for them, and re-layouts  2.16 us
    pallas_call x2, Pallas kernels, total(): pl.pallas_call(functools.partial(total_kernel, begin, parts), out_shape=j...  1.89 us
  transfers between devices with their start and end apart: 25, of which 11 were waited for; matrix products, arithmetic and copies ran while one was open for 0% of the time, Pallas kernels for 11%

profile of v12, /device:TPU:18, one launch (start us, length us, event | category | flops | bytes accessed | tf_op | source)
XLA Modules:
  0.0 80.3 jit_solution(8144571346511465912)
XLA Ops:
  0.6 1.1 %copy-done = bf16[288,1152]{1,0:T(8,128)(2,1)S(1)} copy-done((bf16[288,1152]{1,0:T(8,128)(2,1)S(1)}, bf16[288,1152]{1,0:T(8,128)(2,1)}, u32[]{:S(2)}) %copy-start) | copy-done | bytes 663576
  2.1 1.5 %collective-permute-start.4 = (bf16[256,1152]{1,0:T(8,128)(2,1)}, bf16[256,1152]{1,0:T(8,128)(2,1)S(1)}, u32[]{:S(2)}, u32[]{:S(2)}) collective-permute-start(bf16[256,1152]{1,0:T(8,128)(2,1)} %text), channel_id=1, source_target_pairs={{0,8},{4,12},{8,16},{12,20},{16,24},{20,28},{24,0},{28,4},{1,9},{5... | collective-permute-start | bytes 1769480 | tf_op jit(solution)/shard_map/ppermute | solution.py:334
  4.0 2.7 %collective-permute-start.1 = (bf16[144,1152]{1,0:T(8,128)(2,1)S(1)}, bf16[144,1152]{1,0:T(8,128)(2,1)S(1)}, u32[]{:S(2)}, u32[]{:S(2)}) collective-permute-start(bf16[144,1152]{1,0:T(8,128)(2,1)S(1)} %get-tuple-element.43), channel_id=1, source_target_pairs={{0,3},{1,0},{2,1},{3,2},{4,7},{5,4},{6,5},{7,6},{8,11},{9,8},{10,9... | collective-permute-start | bytes 995336 | tf_op jit(solution)/shard_map/ppermute | solution.py:328
  6.7 1.1 %copy-done.2 = bf16[256,1152]{1,0:T(8,128)(2,1)S(1)} copy-done((bf16[256,1152]{1,0:T(8,128)(2,1)S(1)}, bf16[256,1152]{1,0:T(8,128)(2,1)}, u32[]{:S(2)}) %copy-start.2) | copy-done | bytes 589848
  8.0 4.7 %collective-permute-done.3.rest_2_ = bf16[80,1152]{1,0:T(8,128)(2,1)S(1)} collective-permute-done((bf16[80,1152]{1,0:T(8,128)(2,1)S(1)}, bf16[80,1152]{1,0:T(8,128)(2,1)S(1)}, u32[]{:S(2)}, u32[]{:S(2)}) %collective-permute-start.3) | collective-permute-done | bytes 184352 | tf_op jit(solution)/shard_map/ppermute | solution.py:328
  12.7 4.7 %collective-permute-done.4.t2 = bf16[256,1152]{1,0:T(8,128)(2,1)S(1)} collective-permute-done((bf16[256,1152]{1,0:T(8,128)(2,1)}, bf16[256,1152]{1,0:T(8,128)(2,1)S(1)}, u32[]{:S(2)}, u32[]{:S(2)}) %collective-permute-start.4) | collective-permute-done | bytes 589856 | tf_op jit(solution)/shard_map/ppermute | solution.py:334
  18.1 5.9 %collective-permute-start.12 = (bf16[864,256]{1,0:T(8,128)(2,1)S(1)}, bf16[864,256]{1,0:T(8,128)(2,1)S(1)}, u32[]{:S(2)}, u32[]{:S(2)}) collective-permute-start(bf16[864,256]{1,0:T(8,128)(2,1)S(1)} %get-tuple-element.59), channel_id=1, source_target_pairs={{0,1},{1,0},{2,3},{3,2},{4,5},{5,4},{6,7},{7,6},{8,9},{9,8},{10,11... | collective-permute-start | bytes 1327112 | tf_op jit(solution)/shard_map/ppermute | solution.py:328
  24.0 0.5 collective-permute-start.7
  25.8 0.7 prepare.1
  26.5 2.3 %collective-permute-done.rest_0_ = bf16[144,1152]{1,0:T(8,128)(2,1)S(1)} collective-permute-done((bf16[144,1152]{1,0:T(8,128)(2,1)S(1)}, bf16[144,1152]{1,0:T(8,128)(2,1)S(1)}, u32[]{:S(2)}, u32[]{:S(2)}) %collective-permute-start) | collective-permute-done | bytes 331808 | tf_op jit(solution)/shard_map/ppermute | solution.py:328
  29.4 0.9 %collective-permute-done.7.rest_3_ = bf16[80,1152]{1,0:T(8,128)(2,1)S(1)} collective-permute-done((bf16[80,1152]{1,0:T(8,128)(2,1)S(1)}, bf16[80,1152]{1,0:T(8,128)(2,1)S(1)}, u32[]{:S(2)}, u32[]{:S(2)}) %collective-permute-start.7) | collective-permute-done | bytes 184352 | tf_op jit(solution)/shard_map/ppermute | solution.py:346
  30.3 0.9 %collective-permute-done.10.rest_6_ = bf16[80,1152]{1,0:T(8,128)(2,1)S(1)} collective-permute-done((bf16[80,1152]{1,0:T(8,128)(2,1)S(1)}, bf16[80,1152]{1,0:T(8,128)(2,1)S(1)}, u32[]{:S(2)}, u32[]{:S(2)}) %collective-permute-start.10) | collective-permute-done | bytes 184352 | tf_op jit(solution)/shard_map/ppermute | solution.py:331
  31.7 3.2 %picture_side.1 = (bf16[288,384]{1,0:T(8,128)(2,1)S(1)}, bf16[288,768]{1,0:T(8,128)(2,1)S(1)}, bf16[256,1152]{1,0:T(8,128)(2,1)S(1)}, bf16[256,1152]{1,0:T(8,128)(2,1)S(1)}) custom-call(bf16[256,1152]{1,0:T(8,128)(2,1)S(1)} %copy-done.3, bf16[1152,256]{1,0:T(8,128)(2,1)S(1)} %get-tuple-element.51.x_t, bf16[768,1152]{1,0:T(8,128)(2,1)S(1)} %get-tuple-element.52.units, ...), custom_call_target="tpu_custom_call" | custom-call | tf_op jit(solution)/shard_map/picture_side/pallas_call | solution.py:206
  34.9 1.2 %collective-permute-start.13 = (bf16[288,384]{1,0:T(8,128)(2,1)S(1)}, bf16[288,384]{1,0:T(8,128)(2,1)S(1)}, u32[]{:S(2)}, u32[]{:S(2)}) collective-permute-start(bf16[288,384]{1,0:T(8,128)(2,1)S(1)} %get-tuple-element.64), channel_id=1, source_target_pairs={{0,1},{1,0},{2,3},{3,2},{4,5},{5,4},{6,7},{7,6},{8,9},{9,8},{10,11... | collective-permute-start | bytes 663560 | tf_op jit(solution)/shard_map/ppermute | solution.py:328
  36.2 0.5 collective-permute-start.24
  37.2 5.2 %collective-permute-done.13.arrived = bf16[288,384]{1,0:T(8,128)(2,1)S(1)} collective-permute-done((bf16[288,384]{1,0:T(8,128)(2,1)S(1)}, bf16[288,384]{1,0:T(8,128)(2,1)S(1)}, u32[]{:S(2)}, u32[]{:S(2)}) %collective-permute-start.13) | collective-permute-done | bytes 221216 | tf_op jit(solution)/shard_map/ppermute | solution.py:328
  42.5 1.1 %collective-permute-start.14 = (bf16[288,768]{1,0:T(8,128)(2,1)S(1)}, bf16[288,768]{1,0:T(8,128)(2,1)S(1)}, u32[]{:S(2)}, u32[]{:S(2)}) collective-permute-start(bf16[288,768]{1,0:T(8,128)(2,1)S(1)} %get-tuple-element.65), channel_id=1, source_target_pairs={{0,1},{1,0},{2,3},{3,2},{4,5},{5,4},{6,7},{7,6},{8,9},{9,8},{10,11... | collective-permute-start | bytes 1327112 | tf_op jit(solution)/shard_map/ppermute | solution.py:328
  43.6 0.6 pair_product.3
  44.3 3.9 %collective-permute-start.22 = (bf16[288,384]{1,0:T(8,128)(2,1)S(1)}, bf16[288,384]{1,0:T(8,128)(2,1)S(1)}, u32[]{:S(2)}, u32[]{:S(2)}) collective-permute-start(bf16[288,384]{1,0:T(8,128)(2,1)S(1)} %get-tuple-element.76), channel_id=1, source_target_pairs={{1,2},{2,1},{0,0},{3,3},{5,6},{6,5},{4,4},{7,7},{9,10},{10,9},{8,8... | collective-permute-start | bytes 663560 | tf_op jit(solution)/shard_map/ppermute | solution.py:328
  48.2 8.9 %collective-permute-done.14.arrived = bf16[288,768]{1,0:T(8,128)(2,1)S(1)} collective-permute-done((bf16[288,768]{1,0:T(8,128)(2,1)S(1)}, bf16[288,768]{1,0:T(8,128)(2,1)S(1)}, u32[]{:S(2)}, u32[]{:S(2)}) %collective-permute-start.14) | collective-permute-done | bytes 442400 | tf_op jit(solution)/shard_map/ppermute | solution.py:328
  57.1 0.9 %pair_product.2 = (f32[288,768]{1,0:T(8,128)S(1)}, bf16[96,768]{1,0:T(8,128)(2,1)S(1)}, bf16[96,768]{1,0:T(8,128)(2,1)S(1)}, bf16[96,768]{1,0:T(8,128)(2,1)S(1)}...) custom-call(bf16[1152,256]{1,0:T(8,128)(2,1)S(1)} %get-tuple-element.51.x_t, ...), custom_call_target="tpu_custom_call" | custom-call | tf_op jit(solution)/shard_map/pair_product/pallas_call | solution.py:285
  58.0 1.6 %collective-permute-start.15 = (bf16[96,768]{1,0:T(8,128)(2,1)S(1)}, bf16[96,768]{1,0:T(8,128)(2,1)S(1)}, u32[]{:S(2)}, u32[]{:S(2)}) collective-permute-start(bf16[96,768]{1,0:T(8,128)(2,1)S(1)} %get-tuple-element.67), channel_id=1, source_target_pairs={{1,3},{2,0},{0,1},{3,2},{5,7},{6,4},{4,5},{7,6},{9,11},{10,8},{8,9... | collective-permute-start | bytes 442376 | tf_op jit(solution)/shard_map/ppermute | solution.py:328
  59.8 3.1 %collective-permute-start.17 = (bf16[96,768]{1,0:T(8,128)(2,1)S(1)}, bf16[96,768]{1,0:T(8,128)(2,1)S(1)}, u32[]{:S(2)}, u32[]{:S(2)}) collective-permute-start(bf16[96,768]{1,0:T(8,128)(2,1)S(1)} %get-tuple-element.69), channel_id=1, source_target_pairs={{1,3},{2,0},{0,1},{3,2},{5,7},{6,4},{4,5},{7,6},{9,11},{10,8},{8,9... | collective-permute-start | bytes 442376 | tf_op jit(solution)/shard_map/ppermute | solution.py:328
  62.9 2.1 %collective-permute-start.18 = (bf16[96,768]{1,0:T(8,128)(2,1)S(1)}, bf16[96,768]{1,0:T(8,128)(2,1)S(1)}, u32[]{:S(2)}, u32[]{:S(2)}) collective-permute-start(bf16[96,768]{1,0:T(8,128)(2,1)S(1)} %get-tuple-element.70), channel_id=1, source_target_pairs={{1,2},{2,1},{0,0},{3,3},{5,6},{6,5},{4,4},{7,7},{9,10},{10,9},{8,8... | collective-permute-start | bytes 442376 | tf_op jit(solution)/shard_map/ppermute | solution.py:328
  65.0 3.7 %collective-permute-start.19 = (bf16[96,768]{1,0:T(8,128)(2,1)S(1)}, bf16[96,768]{1,0:T(8,128)(2,1)S(1)}, u32[]{:S(2)}, u32[]{:S(2)}) collective-permute-start(bf16[96,768]{1,0:T(8,128)(2,1)S(1)} %get-tuple-element.71), channel_id=1, source_target_pairs={{1,2},{2,1},{0,0},{3,3},{5,6},{6,5},{4,4},{7,7},{9,10},{10,9},{8,8... | collective-permute-start | bytes 442376 | tf_op jit(solution)/shard_map/ppermute | solution.py:328
  68.8 2.1 %collective-permute-start.20 = (bf16[96,768]{1,0:T(8,128)(2,1)S(1)}, bf16[96,768]{1,0:T(8,128)(2,1)S(1)}, u32[]{:S(2)}, u32[]{:S(2)}) collective-permute-start(bf16[96,768]{1,0:T(8,128)(2,1)S(1)} %get-tuple-element.72), channel_id=1, source_target_pairs={{1,2},{2,1},{0,0},{3,3},{5,6},{6,5},{4,4},{7,7},{9,10},{10,9},{8,8... | collective-permute-start | bytes 442376 | tf_op jit(solution)/shard_map/ppermute | solution.py:328
  70.9 0.8 %total.2.rest_6_ = f32[1,288,1152]{2,1,0:T(8,128)} custom-call(f32[288,384]{1,0:T(8,128)S(1)} %get-tuple-element.74.kept, bf16[288,384]{1,0:T(8,128)(2,1)S(1)} %collective-permute-done.21.rest_0_, bf16[288,384]{1,0:T(8,128)(2,1)S(1)} %collective-permute-done.22.rest_1_), custom_call_target="tpu_custom_call" | custom-call | tf_op jit(solution)/shard_map/total/pallas_call | solution.py:309
  71.8 2.8 %text_side.1 = (f32[256,1152]{1,0:T(8,128)}, f32[8,128]{1,0:T(8,128)S(1)}) custom-call(bf16[256,1152]{1,0:T(8,128)(2,1)S(1)} %copy-done.4, f32[8,128]{1,0:T(8,128)S(1)} %get-tuple-element.53.scalars, bf16[256,1152]{1,0:T(8,128)(2,1)S(1)} %get-tuple-element.77.u0, bf16[256,1152]{1,0:T(8,128)(2,1)S(1)} %collective-permute-done.23.u1, ...), custom_call_target="tpu_custom_call" | custom-call | tf_op jit(solution)/shard_map/text_side/pallas_call | solution.py:238
  74.5 1.1 %collective-permute-done.18.rest_3_ = bf16[96,768]{1,0:T(8,128)(2,1)S(1)} collective-permute-done((bf16[96,768]{1,0:T(8,128)(2,1)S(1)}, bf16[96,768]{1,0:T(8,128)(2,1)S(1)}, u32[]{:S(2)}, u32[]{:S(2)}) %collective-permute-start.18) | collective-permute-done | bytes 147488 | tf_op jit(solution)/shard_map/ppermute | solution.py:328
  75.7 2.0 %collective-permute-done.19.rest_4_ = bf16[96,768]{1,0:T(8,128)(2,1)S(1)} collective-permute-done((bf16[96,768]{1,0:T(8,128)(2,1)S(1)}, bf16[96,768]{1,0:T(8,128)(2,1)S(1)}, u32[]{:S(2)}, u32[]{:S(2)}) %collective-permute-start.19) | collective-permute-done | bytes 147488 | tf_op jit(solution)/shard_map/ppermute | solution.py:328
  77.7 1.6 %collective-permute-done.20.rest_5_ = bf16[96,768]{1,0:T(8,128)(2,1)S(1)} collective-permute-done((bf16[96,768]{1,0:T(8,128)(2,1)S(1)}, bf16[96,768]{1,0:T(8,128)(2,1)S(1)}, u32[]{:S(2)}, u32[]{:S(2)}) %collective-permute-start.20) | collective-permute-done | bytes 147488 | tf_op jit(solution)/shard_map/ppermute | solution.py:328
  79.2 1.0 %total.3 = f32[1,288,1152]{2,1,0:T(8,128)} custom-call(f32[288,768]{1,0:T(8,128)S(1)} %get-tuple-element.66.kept, bf16[96,768]{1,0:T(8,128)(2,1)S(1)} %collective-permute-done.15.rest_0_, bf16[96,768]{1,0:T(8,128)(2,1)S(1)} %collective-permute-done.16.rest_1_, bf16[96,768]{1,0:T(8,128)(2,1)S(1)} %collective-permute-done.17.rest_2_, ...), custom_call_target="tpu_custom_call", output_to_operand_aliasing={{}: (7, {})} | custom-call | tf_op jit(solution)/shard_map/total/pallas_call | solution.py:309
  (38 shorter events, 3.3 us)
Async XLA Ops:
  0.6 1.1 %copy-start = (bf16[288,1152]{1,0:T(8,128)(2,1)S(1)}, bf16[288,1152]{1,0:T(8,128)(2,1)}, u32[]{:S(2)}) copy-start(bf16[288,1152]{1,0:T(8,128)(2,1)} %own.3) | copy-start | bytes 1990660
  1.7 24.1 %copy-start.4 = (bf16[256,1152]{1,0:T(8,128)(2,1)S(1)}, bf16[256,1152]{1,0:T(8,128)(2,1)}, u32[]{:S(2)}) copy-start(bf16[256,1152]{1,0:T(8,128)(2,1)} %text) | copy-start | bytes 1769476
  2.1 15.3 %collective-permute-start.4 = (bf16[256,1152]{1,0:T(8,128)(2,1)}, bf16[256,1152]{1,0:T(8,128)(2,1)S(1)}, u32[]{:S(2)}, u32[]{:S(2)}) collective-permute-start(bf16[256,1152]{1,0:T(8,128)(2,1)} %text), channel_id=1, source_target_pairs={{0,8},{4,12},{8,16},{12,20},{16,24},{20,28},{24,0},{28,4},{1,9},{5... | collective-permute-start | bytes 1769480 | tf_op jit(solution)/shard_map/ppermute | solution.py:334
  3.6 9.1 %collective-permute-start.3 = (bf16[80,1152]{1,0:T(8,128)(2,1)S(1)}, bf16[80,1152]{1,0:T(8,128)(2,1)S(1)}, u32[]{:S(2)}, u32[]{:S(2)}) collective-permute-start(bf16[80,1152]{1,0:T(8,128)(2,1)S(1)} %get-tuple-element.45), channel_id=1, source_target_pairs={{0,2},{1,3},{2,0},{3,1},{4,6},{5,7},{6,4},{7,5},{8,10},{9,11},{10,... | collective-permute-start | bytes 552968 | tf_op jit(solution)/shard_map/ppermute | solution.py:328
  4.0 22.5 %collective-permute-start.1 = (bf16[144,1152]{1,0:T(8,128)(2,1)S(1)}, bf16[144,1152]{1,0:T(8,128)(2,1)S(1)}, u32[]{:S(2)}, u32[]{:S(2)}) collective-permute-start(bf16[144,1152]{1,0:T(8,128)(2,1)S(1)} %get-tuple-element.43), channel_id=1, source_target_pairs={{0,3},{1,0},{2,1},{3,2},{4,7},{5,4},{6,5},{7,6},{8,11},{9,8},{10,9... | collective-permute-start | bytes 995336 | tf_op jit(solution)/shard_map/ppermute | solution.py:328
  6.7 22.2 %collective-permute-start = (bf16[144,1152]{1,0:T(8,128)(2,1)S(1)}, bf16[144,1152]{1,0:T(8,128)(2,1)S(1)}, u32[]{:S(2)}, u32[]{:S(2)}) collective-permute-start(bf16[144,1152]{1,0:T(8,128)(2,1)S(1)} %get-tuple-element.43), channel_id=1, source_target_pairs={{0,1},{1,2},{2,3},{3,0},{4,5},{5,6},{6,7},{7,4},{8,9},{9,10},{10,1... | collective-permute-start | bytes 995336 | tf_op jit(solution)/shard_map/ppermute | solution.py:328
  6.7 11.4 %collective-permute-start.2 = (bf16[256,1152]{1,0:T(8,128)(2,1)}, bf16[256,1152]{1,0:T(8,128)(2,1)S(1)}, u32[]{:S(2)}, u32[]{:S(2)}) collective-permute-start(bf16[256,1152]{1,0:T(8,128)(2,1)} %text), channel_id=1, source_target_pairs={{0,4},{4,0},{8,12},{12,8},{16,20},{20,16},{24,28},{28,24},{1,5},{5... | collective-permute-start | bytes 1769480 | tf_op jit(solution)/shard_map/ppermute | solution.py:331
  6.7 1.1 %copy-start.2 = (bf16[256,1152]{1,0:T(8,128)(2,1)S(1)}, bf16[256,1152]{1,0:T(8,128)(2,1)}, u32[]{:S(2)}) copy-start(bf16[256,1152]{1,0:T(8,128)(2,1)} %x.3) | copy-start | bytes 1769476
  17.5 14.3 %copy-start.1 = (bf16[288,1152]{1,0:T(8,128)(2,1)S(1)}, bf16[288,1152]{1,0:T(8,128)(2,1)}, u32[]{:S(2)}) copy-start(bf16[288,1152]{1,0:T(8,128)(2,1)} %own.3) | copy-start | bytes 1990660
  17.5 14.3 %copy-start.3 = (bf16[256,1152]{1,0:T(8,128)(2,1)S(1)}, bf16[256,1152]{1,0:T(8,128)(2,1)}, u32[]{:S(2)}) copy-start(bf16[256,1152]{1,0:T(8,128)(2,1)} %x.3) | copy-start | bytes 1769476
  17.5 6.5 %collective-permute-start.6 = (bf16[128,1152]{1,0:T(8,128)(2,1)S(1)}, bf16[128,1152]{1,0:T(8,128)(2,1)S(1)}, u32[]{:S(2)}, u32[]{:S(2)}) collective-permute-start(bf16[128,1152]{1,0:T(8,128)(2,1)S(1)} %get-tuple-element.80), channel_id=1, source_target_pairs={{0,4},{4,0},{8,12},{12,8},{16,20},{20,16},{24,28},{28,24},{1,5},{5... | collective-permute-start | bytes 884744 | tf_op jit(solution)/shard_map/ppermute | solution.py:331
  17.6 8.2 %collective-permute-start.5 = (bf16[128,1152]{1,0:T(8,128)(2,1)S(1)}, bf16[128,1152]{1,0:T(8,128)(2,1)S(1)}, u32[]{:S(2)}, u32[]{:S(2)}) collective-permute-start(bf16[128,1152]{1,0:T(8,128)(2,1)S(1)} %get-tuple-element.81), channel_id=1, source_target_pairs={{0,4},{4,0},{8,12},{12,8},{16,20},{20,16},{24,28},{28,24},{1,5},{5... | collective-permute-start | bytes 884744 | tf_op jit(solution)/shard_map/ppermute | solution.py:331
  18.1 16.8 %collective-permute-start.12 = (bf16[864,256]{1,0:T(8,128)(2,1)S(1)}, bf16[864,256]{1,0:T(8,128)(2,1)S(1)}, u32[]{:S(2)}, u32[]{:S(2)}) collective-permute-start(bf16[864,256]{1,0:T(8,128)(2,1)S(1)} %get-tuple-element.59), channel_id=1, source_target_pairs={{0,1},{1,0},{2,3},{3,2},{4,5},{5,4},{6,7},{7,6},{8,9},{9,8},{10,11... | collective-permute-start | bytes 1327112 | tf_op jit(solution)/shard_map/ppermute | solution.py:328
  24.0 6.3 %collective-permute-start.7 = (bf16[80,1152]{1,0:T(8,128)(2,1)S(1)}, bf16[80,1152]{1,0:T(8,128)(2,1)S(1)}, u32[]{:S(2)}, u32[]{:S(2)}) collective-permute-start(bf16[80,1152]{1,0:T(8,128)(2,1)S(1)} %collective-permute-done.3.rest_2_), channel_id=1, source_target_pairs={{0,8},{4,12},{8,0},{12,4},{16,24},{20,28},{24,16},{28,20},{1,9},{5... | collective-permute-start | bytes 552968 | tf_op jit(solution)/shard_map/ppermute | solution.py:346
  28.8 2.9 %collective-permute-start.8 = (bf16[144,1152]{1,0:T(8,128)(2,1)S(1)}, bf16[144,1152]{1,0:T(8,128)(2,1)S(1)}, u32[]{:S(2)}, u32[]{:S(2)}) collective-permute-start(bf16[144,1152]{1,0:T(8,128)(2,1)S(1)} %collective-permute-done.rest_0_), channel_id=1, source_target_pairs={{0,4},{4,0},{8,12},{12,8},{16,20},{20,16},{24,28},{28,24},{1,5},{5... | collective-permute-start | bytes 995336 | tf_op jit(solution)/shard_map/ppermute | solution.py:331
  28.9 2.9 %collective-permute-start.9 = (bf16[144,1152]{1,0:T(8,128)(2,1)S(1)}, bf16[144,1152]{1,0:T(8,128)(2,1)S(1)}, u32[]{:S(2)}, u32[]{:S(2)}) collective-permute-start(bf16[144,1152]{1,0:T(8,128)(2,1)S(1)} %collective-permute-done.1.rest_1_), channel_id=1, source_target_pairs={{0,4},{4,0},{8,12},{12,8},{16,20},{20,16},{24,28},{28,24},{1,5},{5... | collective-permute-start | bytes 995336 | tf_op jit(solution)/shard_map/ppermute | solution.py:331
  29.4 1.9 %collective-permute-start.10 = (bf16[80,1152]{1,0:T(8,128)(2,1)S(1)}, bf16[80,1152]{1,0:T(8,128)(2,1)S(1)}, u32[]{:S(2)}, u32[]{:S(2)}) collective-permute-start(bf16[80,1152]{1,0:T(8,128)(2,1)S(1)} %collective-permute-done.3.rest_2_), channel_id=1, source_target_pairs={{0,4},{4,0},{8,12},{12,8},{16,20},{20,16},{24,28},{28,24},{1,5},{5... | collective-permute-start | bytes 552968 | tf_op jit(solution)/shard_map/ppermute | solution.py:331
  30.3 1.4 %collective-permute-start.11 = (bf16[80,1152]{1,0:T(8,128)(2,1)S(1)}, bf16[80,1152]{1,0:T(8,128)(2,1)S(1)}, u32[]{:S(2)}, u32[]{:S(2)}) collective-permute-start(bf16[80,1152]{1,0:T(8,128)(2,1)S(1)} %collective-permute-done.7.rest_3_), channel_id=1, source_target_pairs={{0,4},{4,0},{8,12},{12,8},{16,20},{20,16},{24,28},{28,24},{1,5},{5... | collective-permute-start | bytes 552968 | tf_op jit(solution)/shard_map/ppermute | solution.py:331
  34.9 7.5 %collective-permute-start.13 = (bf16[288,384]{1,0:T(8,128)(2,1)S(1)}, bf16[288,384]{1,0:T(8,128)(2,1)S(1)}, u32[]{:S(2)}, u32[]{:S(2)}) collective-permute-start(bf16[288,384]{1,0:T(8,128)(2,1)S(1)} %get-tuple-element.64), channel_id=1, source_target_pairs={{0,1},{1,0},{2,3},{3,2},{4,5},{5,4},{6,7},{7,6},{8,9},{9,8},{10,11... | collective-permute-start | bytes 663560 | tf_op jit(solution)/shard_map/ppermute | solution.py:328
  36.2 26.7 %collective-permute-start.24 = (bf16[256,1152]{1,0:T(8,128)(2,1)S(1)}, bf16[256,1152]{1,0:T(8,128)(2,1)S(1)}, u32[]{:S(2)}, u32[]{:S(2)}) collective-permute-start(bf16[256,1152]{1,0:T(8,128)(2,1)S(1)} %get-tuple-element.77.u0), channel_id=1, source_target_pairs={{0,24},{4,28},{8,0},{12,4},{16,8},{20,12},{24,16},{28,20},{1,25},{... | collective-permute-start | bytes 1769480 | tf_op jit(solution)/shard_map/ppermute | solution.py:334
  36.7 28.3 %collective-permute-start.23 = (bf16[256,1152]{1,0:T(8,128)(2,1)S(1)}, bf16[256,1152]{1,0:T(8,128)(2,1)S(1)}, u32[]{:S(2)}, u32[]{:S(2)}) collective-permute-start(bf16[256,1152]{1,0:T(8,128)(2,1)S(1)} %get-tuple-element.77.u0), channel_id=1, source_target_pairs={{0,28},{4,0},{8,4},{12,8},{16,12},{20,16},{24,20},{28,24},{1,29},{... | collective-permute-start | bytes 1769480 | tf_op jit(solution)/shard_map/ppermute | solution.py:334
  42.5 14.6 %collective-permute-start.14 = (bf16[288,768]{1,0:T(8,128)(2,1)S(1)}, bf16[288,768]{1,0:T(8,128)(2,1)S(1)}, u32[]{:S(2)}, u32[]{:S(2)}) collective-permute-start(bf16[288,768]{1,0:T(8,128)(2,1)S(1)} %get-tuple-element.65), channel_id=1, source_target_pairs={{0,1},{1,0},{2,3},{3,2},{4,5},{5,4},{6,7},{7,6},{8,9},{9,8},{10,11... | collective-permute-start | bytes 1327112 | tf_op jit(solution)/shard_map/ppermute | solution.py:328
  44.2 15.4 %collective-permute-start.21 = (bf16[288,384]{1,0:T(8,128)(2,1)S(1)}, bf16[288,384]{1,0:T(8,128)(2,1)S(1)}, u32[]{:S(2)}, u32[]{:S(2)}) collective-permute-start(bf16[288,384]{1,0:T(8,128)(2,1)S(1)} %get-tuple-element.75), channel_id=1, source_target_pairs={{1,3},{2,0},{0,1},{3,2},{5,7},{6,4},{4,5},{7,6},{9,11},{10,8},{8,9... | collective-permute-start | bytes 663560 | tf_op jit(solution)/shard_map/ppermute | solution.py:328
  44.3 15.5 %collective-permute-start.22 = (bf16[288,384]{1,0:T(8,128)(2,1)S(1)}, bf16[288,384]{1,0:T(8,128)(2,1)S(1)}, u32[]{:S(2)}, u32[]{:S(2)}) collective-permute-start(bf16[288,384]{1,0:T(8,128)(2,1)S(1)} %get-tuple-element.76), channel_id=1, source_target_pairs={{1,2},{2,1},{0,0},{3,3},{5,6},{6,5},{4,4},{7,7},{9,10},{10,9},{8,8... | collective-permute-start | bytes 663560 | tf_op jit(solution)/shard_map/ppermute | solution.py:328
  58.0 10.8 %collective-permute-start.15 = (bf16[96,768]{1,0:T(8,128)(2,1)S(1)}, bf16[96,768]{1,0:T(8,128)(2,1)S(1)}, u32[]{:S(2)}, u32[]{:S(2)}) collective-permute-start(bf16[96,768]{1,0:T(8,128)(2,1)S(1)} %get-tuple-element.67), channel_id=1, source_target_pairs={{1,3},{2,0},{0,1},{3,2},{5,7},{6,4},{4,5},{7,6},{9,11},{10,8},{8,9... | collective-permute-start | bytes 442376 | tf_op jit(solution)/shard_map/ppermute | solution.py:328
  59.6 14.9 %collective-permute-start.16 = (bf16[96,768]{1,0:T(8,128)(2,1)S(1)}, bf16[96,768]{1,0:T(8,128)(2,1)S(1)}, u32[]{:S(2)}, u32[]{:S(2)}) collective-permute-start(bf16[96,768]{1,0:T(8,128)(2,1)S(1)} %get-tuple-element.68), channel_id=1, source_target_pairs={{1,3},{2,0},{0,1},{3,2},{5,7},{6,4},{4,5},{7,6},{9,11},{10,8},{8,9... | collective-permute-start | bytes 442376 | tf_op jit(solution)/shard_map/ppermute | solution.py:328
  59.8 14.8 %collective-permute-start.17 = (bf16[96,768]{1,0:T(8,128)(2,1)S(1)}, bf16[96,768]{1,0:T(8,128)(2,1)S(1)}, u32[]{:S(2)}, u32[]{:S(2)}) collective-permute-start(bf16[96,768]{1,0:T(8,128)(2,1)S(1)} %get-tuple-element.69), channel_id=1, source_target_pairs={{1,3},{2,0},{0,1},{3,2},{5,7},{6,4},{4,5},{7,6},{9,11},{10,8},{8,9... | collective-permute-start | bytes 442376 | tf_op jit(solution)/shard_map/ppermute | solution.py:328
  62.9 12.8 %collective-permute-start.18 = (bf16[96,768]{1,0:T(8,128)(2,1)S(1)}, bf16[96,768]{1,0:T(8,128)(2,1)S(1)}, u32[]{:S(2)}, u32[]{:S(2)}) collective-permute-start(bf16[96,768]{1,0:T(8,128)(2,1)S(1)} %get-tuple-element.70), channel_id=1, source_target_pairs={{1,2},{2,1},{0,0},{3,3},{5,6},{6,5},{4,4},{7,7},{9,10},{10,9},{8,8... | collective-permute-start | bytes 442376 | tf_op jit(solution)/shard_map/ppermute | solution.py:328
  65.0 12.6 %collective-permute-start.19 = (bf16[96,768]{1,0:T(8,128)(2,1)S(1)}, bf16[96,768]{1,0:T(8,128)(2,1)S(1)}, u32[]{:S(2)}, u32[]{:S(2)}) collective-permute-start(bf16[96,768]{1,0:T(8,128)(2,1)S(1)} %get-tuple-element.71), channel_id=1, source_target_pairs={{1,2},{2,1},{0,0},{3,3},{5,6},{6,5},{4,4},{7,7},{9,10},{10,9},{8,8... | collective-permute-start | bytes 442376 | tf_op jit(solution)/shard_map/ppermute | solution.py:328
  68.8 10.5 %collective-permute-start.20 = (bf16[96,768]{1,0:T(8,128)(2,1)S(1)}, bf16[96,768]{1,0:T(8,128)(2,1)S(1)}, u32[]{:S(2)}, u32[]{:S(2)}) collective-permute-start(bf16[96,768]{1,0:T(8,128)(2,1)S(1)} %get-tuple-element.72), channel_id=1, source_target_pairs={{1,2},{2,1},{0,0},{3,3},{5,6},{6,5},{4,4},{7,7},{9,10},{10,9},{8,8... | collective-permute-start | bytes 442376 | tf_op jit(solution)/shard_map/ppermute | solution.py:328

commit v13 on v12

--- a/solution.py
+++ b/solution.py
@@ -9,8 +9,8 @@
 
 STEPS = 3
 EPS = 1e-06
-SHARES = (1, 2)
-CROSS_PARTS = (1, 3)
+SHARES = (4, 5)
+CROSS_PARTS = (1, 2)
 TEXT_PARTS = 2
 VMEM_BYTES = 24 * 1024 * 1024
 BF16, F32 = jnp.bfloat16, jnp.float32

time: 80.6 us -> 78.9 us (0.979)
  starting transfers between devices: 32.3 us -> 27 us
  waiting for transfers between devices: 33 us -> 36.7 us
    ppermute x14 -> x12, starting transfers between devices: 28.1 us -> 22.8 us  [along(): return lax.ppermute(value, 'fsdp', pairs)]
    ppermute x14 -> x12, waiting for transfers between devices: 25.9 us -> 29.6 us  [along(): return lax.ppermute(value, 'fsdp', pairs)]
  transfers between devices with their start and end apart: 25 -> 23, of which waited for: 11 -> 10; matrix products, arithmetic and copies ran while one was open for 0% -> 0% of each run, Pallas kernels for 11% -> 12%
where the time goes in v13:
time: 78.9 us; the launch traced here: 78.6 us
  waiting for transfers between devices  36.7 us (47%)
  starting transfers between devices  27 us (34%)
  Pallas kernels  10.6 us (13%)
  local copies, waits for them, and re-layouts  2.21 us (3%)
  between operations  2.14 us (3%)
    ppermute x12, waiting for transfers between devices, along(): return lax.ppermute(value, 'fsdp', pairs)  29.6 us
    ppermute x12, starting transfers between devices, along(): return lax.ppermute(value, 'fsdp', pairs)  22.8 us
    ppermute x3, waiting for transfers between devices, shifted(): lax.ppermute(value, 'dp', [(d, (d + by) % n_dp) for d in range(n_dp)])  4.73 us
    pallas_call x1, Pallas kernels, picture_side(): pl.pallas_call(picture_kernel, out_shape=outs, in_specs=spaces(13), out_s...  3.17 us
    pallas_call x1, Pallas kernels, text_side(): pl.pallas_call(text_kernel, out_shape=(jax.ShapeDtypeStruct((rows, width)...  2.76 us
    ppermute x3, starting transfers between devices, shifted(): lax.ppermute(value, 'dp', [(d, (d + by) % n_dp) for d in range(n_dp)])  2.61 us
    unnamed x10, local copies, waits for them, and re-layouts  2.16 us
    pallas_call x2, Pallas kernels, total(): pl.pallas_call(functools.partial(total_kernel, begin, parts), out_shape=j...  1.9 us
  transfers between devices with their start and end apart: 23, of which 10 were waited for; matrix products, arithmetic and copies ran while one was open for 0% of the time, Pallas kernels for 12%

profile of v13, /device:TPU:18, one launch (start us, length us, event | category | flops | bytes accessed | tf_op | source)
XLA Modules:
  0.0 78.6 jit_solution(694196694197855542)
XLA Ops:
  0.6 1.1 %copy-done = bf16[288,1152]{1,0:T(8,128)(2,1)S(1)} copy-done((bf16[288,1152]{1,0:T(8,128)(2,1)S(1)}, bf16[288,1152]{1,0:T(8,128)(2,1)}, u32[]{:S(2)}) %copy-start) | copy-done | bytes 663576
  2.1 1.5 %collective-permute-start.4 = (bf16[256,1152]{1,0:T(8,128)(2,1)}, bf16[256,1152]{1,0:T(8,128)(2,1)S(1)}, u32[]{:S(2)}, u32[]{:S(2)}) collective-permute-start(bf16[256,1152]{1,0:T(8,128)(2,1)} %text), channel_id=1, source_target_pairs={{0,8},{4,12},{8,16},{12,20},{16,24},{20,28},{24,0},{28,4},{1,9},{5... | collective-permute-start | bytes 1769480 | tf_op jit(solution)/shard_map/ppermute | solution.py:334
  4.0 2.7 %collective-permute-start.1 = (bf16[144,1152]{1,0:T(8,128)(2,1)S(1)}, bf16[144,1152]{1,0:T(8,128)(2,1)S(1)}, u32[]{:S(2)}, u32[]{:S(2)}) collective-permute-start(bf16[144,1152]{1,0:T(8,128)(2,1)S(1)} %get-tuple-element.41), channel_id=1, source_target_pairs={{0,3},{1,0},{2,1},{3,2},{4,7},{5,4},{6,5},{7,6},{8,11},{9,8},{10,9... | collective-permute-start | bytes 995336 | tf_op jit(solution)/shard_map/ppermute | solution.py:328
  6.7 1.1 %copy-done.2 = bf16[256,1152]{1,0:T(8,128)(2,1)S(1)} copy-done((bf16[256,1152]{1,0:T(8,128)(2,1)S(1)}, bf16[256,1152]{1,0:T(8,128)(2,1)}, u32[]{:S(2)}) %copy-start.2) | copy-done | bytes 589848
  8.0 4.7 %collective-permute-done.3.rest_2_ = bf16[80,1152]{1,0:T(8,128)(2,1)S(1)} collective-permute-done((bf16[80,1152]{1,0:T(8,128)(2,1)S(1)}, bf16[80,1152]{1,0:T(8,128)(2,1)S(1)}, u32[]{:S(2)}, u32[]{:S(2)}) %collective-permute-start.3) | collective-permute-done | bytes 184352 | tf_op jit(solution)/shard_map/ppermute | solution.py:328
  12.7 4.7 %collective-permute-done.4.t2 = bf16[256,1152]{1,0:T(8,128)(2,1)S(1)} collective-permute-done((bf16[256,1152]{1,0:T(8,128)(2,1)}, bf16[256,1152]{1,0:T(8,128)(2,1)S(1)}, u32[]{:S(2)}, u32[]{:S(2)}) %collective-permute-start.4) | collective-permute-done | bytes 589856 | tf_op jit(solution)/shard_map/ppermute | solution.py:334
  17.6 0.5 collective-permute-start.5
  18.1 5.9 %collective-permute-start.12 = (bf16[864,256]{1,0:T(8,128)(2,1)S(1)}, bf16[864,256]{1,0:T(8,128)(2,1)S(1)}, u32[]{:S(2)}, u32[]{:S(2)}) collective-permute-start(bf16[864,256]{1,0:T(8,128)(2,1)S(1)} %get-tuple-element.57), channel_id=1, source_target_pairs={{0,1},{1,0},{2,3},{3,2},{4,5},{5,4},{6,7},{7,6},{8,9},{9,8},{10,11... | collective-permute-start | bytes 1327112 | tf_op jit(solution)/shard_map/ppermute | solution.py:328
  24.0 0.5 collective-permute-start.7
  25.8 0.7 prepare.1
  26.5 2.3 %collective-permute-done.rest_0_ = bf16[144,1152]{1,0:T(8,128)(2,1)S(1)} collective-permute-done((bf16[144,1152]{1,0:T(8,128)(2,1)S(1)}, bf16[144,1152]{1,0:T(8,128)(2,1)S(1)}, u32[]{:S(2)}, u32[]{:S(2)}) %collective-permute-start) | collective-permute-done | bytes 331808 | tf_op jit(solution)/shard_map/ppermute | solution.py:328
  29.4 0.9 %collective-permute-done.7.rest_3_ = bf16[80,1152]{1,0:T(8,128)(2,1)S(1)} collective-permute-done((bf16[80,1152]{1,0:T(8,128)(2,1)S(1)}, bf16[80,1152]{1,0:T(8,128)(2,1)S(1)}, u32[]{:S(2)}, u32[]{:S(2)}) %collective-permute-start.7) | collective-permute-done | bytes 184352 | tf_op jit(solution)/shard_map/ppermute | solution.py:346
  30.3 0.9 %collective-permute-done.10.rest_6_ = bf16[80,1152]{1,0:T(8,128)(2,1)S(1)} collective-permute-done((bf16[80,1152]{1,0:T(8,128)(2,1)S(1)}, bf16[80,1152]{1,0:T(8,128)(2,1)S(1)}, u32[]{:S(2)}, u32[]{:S(2)}) %collective-permute-start.10) | collective-permute-done | bytes 184352 | tf_op jit(solution)/shard_map/ppermute | solution.py:331
  31.2 0.5 collective-permute-done.11.rest_7_
  31.7 3.2 %picture_side.1 = (bf16[288,512]{1,0:T(8,128)(2,1)S(1)}, bf16[288,640]{1,0:T(8,128)(2,1)S(1)}, bf16[256,1152]{1,0:T(8,128)(2,1)S(1)}, bf16[256,1152]{1,0:T(8,128)(2,1)S(1)}) custom-call(bf16[256,1152]{1,0:T(8,128)(2,1)S(1)} %copy-done.3, bf16[1152,256]{1,0:T(8,128)(2,1)S(1)} %get-tuple-element.49.x_t, bf16[768,1152]{1,0:T(8,128)(2,1)S(1)} %get-tuple-element.50.units, ...), custom_call_target="tpu_custom_call" | custom-call | tf_op jit(solution)/shard_map/picture_side/pallas_call | solution.py:206
  34.9 1.2 %collective-permute-start.13 = (bf16[288,512]{1,0:T(8,128)(2,1)S(1)}, bf16[288,512]{1,0:T(8,128)(2,1)S(1)}, u32[]{:S(2)}, u32[]{:S(2)}) collective-permute-start(bf16[288,512]{1,0:T(8,128)(2,1)S(1)} %get-tuple-element.62), channel_id=1, source_target_pairs={{0,1},{1,0},{2,3},{3,2},{4,5},{5,4},{6,7},{7,6},{8,9},{9,8},{10,11... | collective-permute-start | bytes 884744 | tf_op jit(solution)/shard_map/ppermute | solution.py:328
  36.2 0.5 collective-permute-start.22
  36.7 0.5 collective-permute-start.21
  37.2 6.8 %collective-permute-done.13.arrived = bf16[288,512]{1,0:T(8,128)(2,1)S(1)} collective-permute-done((bf16[288,512]{1,0:T(8,128)(2,1)S(1)}, bf16[288,512]{1,0:T(8,128)(2,1)S(1)}, u32[]{:S(2)}, u32[]{:S(2)}) %collective-permute-start.13) | collective-permute-done | bytes 294944 | tf_op jit(solution)/shard_map/ppermute | solution.py:328
  44.1 1.1 %collective-permute-start.14 = (bf16[288,640]{1,0:T(8,128)(2,1)S(1)}, bf16[288,640]{1,0:T(8,128)(2,1)S(1)}, u32[]{:S(2)}, u32[]{:S(2)}) collective-permute-start(bf16[288,640]{1,0:T(8,128)(2,1)S(1)} %get-tuple-element.63), channel_id=1, source_target_pairs={{0,1},{1,0},{2,3},{3,2},{4,5},{5,4},{6,7},{7,6},{8,9},{9,8},{10,11... | collective-permute-start | bytes 1105928 | tf_op jit(solution)/shard_map/ppermute | solution.py:328
  45.1 0.6 pair_product.3
  45.9 3.9 %collective-permute-start.20 = (bf16[288,512]{1,0:T(8,128)(2,1)S(1)}, bf16[288,512]{1,0:T(8,128)(2,1)S(1)}, u32[]{:S(2)}, u32[]{:S(2)}) collective-permute-start(bf16[288,512]{1,0:T(8,128)(2,1)S(1)} %get-tuple-element.72), channel_id=1, source_target_pairs={{1,2},{2,1},{0,0},{3,3},{5,6},{6,5},{4,4},{7,7},{9,10},{10,9},{8,8... | collective-permute-start | bytes 884744 | tf_op jit(solution)/shard_map/ppermute | solution.py:328
  49.8 8.9 %collective-permute-done.14.arrived = bf16[288,640]{1,0:T(8,128)(2,1)S(1)} collective-permute-done((bf16[288,640]{1,0:T(8,128)(2,1)S(1)}, bf16[288,640]{1,0:T(8,128)(2,1)S(1)}, u32[]{:S(2)}, u32[]{:S(2)}) %collective-permute-start.14) | collective-permute-done | bytes 368672 | tf_op jit(solution)/shard_map/ppermute | solution.py:328
  58.7 0.9 %pair_product.2 = (f32[288,640]{1,0:T(8,128)S(1)}, bf16[144,640]{1,0:T(8,128)(2,1)S(1)}, bf16[144,640]{1,0:T(8,128)(2,1)S(1)}, bf16[144,640]{1,0:T(8,128)(2,1)S(1)}, bf16[144,640]{1,0:T(8,128)(2,1)S(1)}) custom-call(bf16[1152,256]{1,0:T(8,128)(2,1)S(1)} %get-tuple-element.49.x_t, bf16[864,256]{1,0:T(8,128)(2,1)S(1)} %collective-permute-done.12.far_t, ...), custom_call_target="tpu_custom_call" | custom-call | tf_op jit(solution)/shard_map/pair_product/pallas_call | solution.py:285
  59.6 1.6 %collective-permute-start.15 = (bf16[144,640]{1,0:T(8,128)(2,1)S(1)}, bf16[144,640]{1,0:T(8,128)(2,1)S(1)}, u32[]{:S(2)}, u32[]{:S(2)}) collective-permute-start(bf16[144,640]{1,0:T(8,128)(2,1)S(1)} %get-tuple-element.65), channel_id=1, source_target_pairs={{1,3},{2,0},{0,1},{3,2},{5,7},{6,4},{4,5},{7,6},{9,11},{10,8},{8,9... | collective-permute-start | bytes 552968 | tf_op jit(solution)/shard_map/ppermute | solution.py:328
  61.3 3.7 %collective-permute-start.17 = (bf16[144,640]{1,0:T(8,128)(2,1)S(1)}, bf16[144,640]{1,0:T(8,128)(2,1)S(1)}, u32[]{:S(2)}, u32[]{:S(2)}) collective-permute-start(bf16[144,640]{1,0:T(8,128)(2,1)S(1)} %get-tuple-element.67), channel_id=1, source_target_pairs={{1,2},{2,1},{0,0},{3,3},{5,6},{6,5},{4,4},{7,7},{9,10},{10,9},{8,8... | collective-permute-start | bytes 552968 | tf_op jit(solution)/shard_map/ppermute | solution.py:328
  65.1 2.1 %collective-permute-start.18 = (bf16[144,640]{1,0:T(8,128)(2,1)S(1)}, bf16[144,640]{1,0:T(8,128)(2,1)S(1)}, u32[]{:S(2)}, u32[]{:S(2)}) collective-permute-start(bf16[144,640]{1,0:T(8,128)(2,1)S(1)} %get-tuple-element.68), channel_id=1, source_target_pairs={{1,2},{2,1},{0,0},{3,3},{5,6},{6,5},{4,4},{7,7},{9,10},{10,9},{8,8... | collective-permute-start | bytes 552968 | tf_op jit(solution)/shard_map/ppermute | solution.py:328
  67.2 2.8 %text_side.1 = (f32[256,1152]{1,0:T(8,128)}, f32[8,128]{1,0:T(8,128)S(1)}) custom-call(bf16[256,1152]{1,0:T(8,128)(2,1)S(1)} %copy-done.4, f32[8,128]{1,0:T(8,128)S(1)} %get-tuple-element.51.scalars, bf16[256,1152]{1,0:T(8,128)(2,1)S(1)} %get-tuple-element.73.u0, bf16[256,1152]{1,0:T(8,128)(2,1)S(1)} %collective-permute-done.21.u1, ...), custom_call_target="tpu_custom_call" | custom-call | tf_op jit(solution)/shard_map/text_side/pallas_call | solution.py:238
  70.0 0.9 %total.2.rest_4_ = f32[1,288,1152]{2,1,0:T(8,128)} custom-call(f32[288,512]{1,0:T(8,128)S(1)} %get-tuple-element.70.kept, bf16[288,512]{1,0:T(8,128)(2,1)S(1)} %collective-permute-done.19.rest_0_, bf16[288,512]{1,0:T(8,128)(2,1)S(1)} %collective-permute-done.20.rest_1_), custom_call_target="tpu_custom_call" | custom-call | tf_op jit(solution)/shard_map/total/pallas_call | solution.py:309
  70.9 4.8 %collective-permute-done.17.rest_2_ = bf16[144,640]{1,0:T(8,128)(2,1)S(1)} collective-permute-done((bf16[144,640]{1,0:T(8,128)(2,1)S(1)}, bf16[144,640]{1,0:T(8,128)(2,1)S(1)}, u32[]{:S(2)}, u32[]{:S(2)}) %collective-permute-start.17) | collective-permute-done | bytes 184352 | tf_op jit(solution)/shard_map/ppermute | solution.py:328
  75.7 2.0 %collective-permute-done.18.rest_3_ = bf16[144,640]{1,0:T(8,128)(2,1)S(1)} collective-permute-done((bf16[144,640]{1,0:T(8,128)(2,1)S(1)}, bf16[144,640]{1,0:T(8,128)(2,1)S(1)}, u32[]{:S(2)}, u32[]{:S(2)}) %collective-permute-start.18) | collective-permute-done | bytes 184352 | tf_op jit(solution)/shard_map/ppermute | solution.py:328
  77.7 1.0 %total.3 = f32[1,288,1152]{2,1,0:T(8,128)} custom-call(f32[288,640]{1,0:T(8,128)S(1)} %get-tuple-element.64.kept, bf16[144,640]{1,0:T(8,128)(2,1)S(1)} %collective-permute-done.15.rest_0_, bf16[144,640]{1,0:T(8,128)(2,1)S(1)} %collective-permute-done.16.rest_1_, ...), custom_call_target="tpu_custom_call", output_to_operand_aliasing={{}: (5, {})} | custom-call | tf_op jit(solution)/shard_map/total/pallas_call | solution.py:309
  (34 shorter events, 1.8 us)
Async XLA Ops:
  0.6 1.1 %copy-start = (bf16[288,1152]{1,0:T(8,128)(2,1)S(1)}, bf16[288,1152]{1,0:T(8,128)(2,1)}, u32[]{:S(2)}) copy-start(bf16[288,1152]{1,0:T(8,128)(2,1)} %own.3) | copy-start | bytes 1990660
  1.7 24.1 %copy-start.4 = (bf16[256,1152]{1,0:T(8,128)(2,1)S(1)}, bf16[256,1152]{1,0:T(8,128)(2,1)}, u32[]{:S(2)}) copy-start(bf16[256,1152]{1,0:T(8,128)(2,1)} %text) | copy-start | bytes 1769476
  2.1 15.3 %collective-permute-start.4 = (bf16[256,1152]{1,0:T(8,128)(2,1)}, bf16[256,1152]{1,0:T(8,128)(2,1)S(1)}, u32[]{:S(2)}, u32[]{:S(2)}) collective-permute-start(bf16[256,1152]{1,0:T(8,128)(2,1)} %text), channel_id=1, source_target_pairs={{0,8},{4,12},{8,16},{12,20},{16,24},{20,28},{24,0},{28,4},{1,9},{5... | collective-permute-start | bytes 1769480 | tf_op jit(solution)/shard_map/ppermute | solution.py:334
  3.6 9.1 %collective-permute-start.3 = (bf16[80,1152]{1,0:T(8,128)(2,1)S(1)}, bf16[80,1152]{1,0:T(8,128)(2,1)S(1)}, u32[]{:S(2)}, u32[]{:S(2)}) collective-permute-start(bf16[80,1152]{1,0:T(8,128)(2,1)S(1)} %get-tuple-element.43), channel_id=1, source_target_pairs={{0,2},{1,3},{2,0},{3,1},{4,6},{5,7},{6,4},{7,5},{8,10},{9,11},{10,... | collective-permute-start | bytes 552968 | tf_op jit(solution)/shard_map/ppermute | solution.py:328
  4.0 22.5 %collective-permute-start.1 = (bf16[144,1152]{1,0:T(8,128)(2,1)S(1)}, bf16[144,1152]{1,0:T(8,128)(2,1)S(1)}, u32[]{:S(2)}, u32[]{:S(2)}) collective-permute-start(bf16[144,1152]{1,0:T(8,128)(2,1)S(1)} %get-tuple-element.41), channel_id=1, source_target_pairs={{0,3},{1,0},{2,1},{3,2},{4,7},{5,4},{6,5},{7,6},{8,11},{9,8},{10,9... | collective-permute-start | bytes 995336 | tf_op jit(solution)/shard_map/ppermute | solution.py:328
  6.7 22.2 %collective-permute-start = (bf16[144,1152]{1,0:T(8,128)(2,1)S(1)}, bf16[144,1152]{1,0:T(8,128)(2,1)S(1)}, u32[]{:S(2)}, u32[]{:S(2)}) collective-permute-start(bf16[144,1152]{1,0:T(8,128)(2,1)S(1)} %get-tuple-element.41), channel_id=1, source_target_pairs={{0,1},{1,2},{2,3},{3,0},{4,5},{5,6},{6,7},{7,4},{8,9},{9,10},{10,1... | collective-permute-start | bytes 995336 | tf_op jit(solution)/shard_map/ppermute | solution.py:328
  6.7 11.4 %collective-permute-start.2 = (bf16[256,1152]{1,0:T(8,128)(2,1)}, bf16[256,1152]{1,0:T(8,128)(2,1)S(1)}, u32[]{:S(2)}, u32[]{:S(2)}) collective-permute-start(bf16[256,1152]{1,0:T(8,128)(2,1)} %text), channel_id=1, source_target_pairs={{0,4},{4,0},{8,12},{12,8},{16,20},{20,16},{24,28},{28,24},{1,5},{5... | collective-permute-start | bytes 1769480 | tf_op jit(solution)/shard_map/ppermute | solution.py:331
  6.7 1.1 %copy-start.2 = (bf16[256,1152]{1,0:T(8,128)(2,1)S(1)}, bf16[256,1152]{1,0:T(8,128)(2,1)}, u32[]{:S(2)}) copy-start(bf16[256,1152]{1,0:T(8,128)(2,1)} %x.3) | copy-start | bytes 1769476
  17.5 14.3 %copy-start.1 = (bf16[288,1152]{1,0:T(8,128)(2,1)S(1)}, bf16[288,1152]{1,0:T(8,128)(2,1)}, u32[]{:S(2)}) copy-start(bf16[288,1152]{1,0:T(8,128)(2,1)} %own.3) | copy-start | bytes 1990660
  17.5 14.3 %copy-start.3 = (bf16[256,1152]{1,0:T(8,128)(2,1)S(1)}, bf16[256,1152]{1,0:T(8,128)(2,1)}, u32[]{:S(2)}) copy-start(bf16[256,1152]{1,0:T(8,128)(2,1)} %x.3) | copy-start | bytes 1769476
  17.5 6.5 %collective-permute-start.6 = (bf16[128,1152]{1,0:T(8,128)(2,1)S(1)}, bf16[128,1152]{1,0:T(8,128)(2,1)S(1)}, u32[]{:S(2)}, u32[]{:S(2)}) collective-permute-start(bf16[128,1152]{1,0:T(8,128)(2,1)S(1)} %get-tuple-element.76), channel_id=1, source_target_pairs={{0,4},{4,0},{8,12},{12,8},{16,20},{20,16},{24,28},{28,24},{1,5},{5... | collective-permute-start | bytes 884744 | tf_op jit(solution)/shard_map/ppermute | solution.py:331
  17.6 8.2 %collective-permute-start.5 = (bf16[128,1152]{1,0:T(8,128)(2,1)S(1)}, bf16[128,1152]{1,0:T(8,128)(2,1)S(1)}, u32[]{:S(2)}, u32[]{:S(2)}) collective-permute-start(bf16[128,1152]{1,0:T(8,128)(2,1)S(1)} %get-tuple-element.77), channel_id=1, source_target_pairs={{0,4},{4,0},{8,12},{12,8},{16,20},{20,16},{24,28},{28,24},{1,5},{5... | collective-permute-start | bytes 884744 | tf_op jit(solution)/shard_map/ppermute | solution.py:331
  18.1 16.8 %collective-permute-start.12 = (bf16[864,256]{1,0:T(8,128)(2,1)S(1)}, bf16[864,256]{1,0:T(8,128)(2,1)S(1)}, u32[]{:S(2)}, u32[]{:S(2)}) collective-permute-start(bf16[864,256]{1,0:T(8,128)(2,1)S(1)} %get-tuple-element.57), channel_id=1, source_target_pairs={{0,1},{1,0},{2,3},{3,2},{4,5},{5,4},{6,7},{7,6},{8,9},{9,8},{10,11... | collective-permute-start | bytes 1327112 | tf_op jit(solution)/shard_map/ppermute | solution.py:328
  24.0 6.3 %collective-permute-start.7 = (bf16[80,1152]{1,0:T(8,128)(2,1)S(1)}, bf16[80,1152]{1,0:T(8,128)(2,1)S(1)}, u32[]{:S(2)}, u32[]{:S(2)}) collective-permute-start(bf16[80,1152]{1,0:T(8,128)(2,1)S(1)} %collective-permute-done.3.rest_2_), channel_id=1, source_target_pairs={{0,8},{4,12},{8,0},{12,4},{16,24},{20,28},{24,16},{28,20},{1,9},{5... | collective-permute-start | bytes 552968 | tf_op jit(solution)/shard_map/ppermute | solution.py:346
  28.8 2.9 %collective-permute-start.8 = (bf16[144,1152]{1,0:T(8,128)(2,1)S(1)}, bf16[144,1152]{1,0:T(8,128)(2,1)S(1)}, u32[]{:S(2)}, u32[]{:S(2)}) collective-permute-start(bf16[144,1152]{1,0:T(8,128)(2,1)S(1)} %collective-permute-done.rest_0_), channel_id=1, source_target_pairs={{0,4},{4,0},{8,12},{12,8},{16,20},{20,16},{24,28},{28,24},{1,5},{5... | collective-permute-start | bytes 995336 | tf_op jit(solution)/shard_map/ppermute | solution.py:331
  28.9 2.9 %collective-permute-start.9 = (bf16[144,1152]{1,0:T(8,128)(2,1)S(1)}, bf16[144,1152]{1,0:T(8,128)(2,1)S(1)}, u32[]{:S(2)}, u32[]{:S(2)}) collective-permute-start(bf16[144,1152]{1,0:T(8,128)(2,1)S(1)} %collective-permute-done.1.rest_1_), channel_id=1, source_target_pairs={{0,4},{4,0},{8,12},{12,8},{16,20},{20,16},{24,28},{28,24},{1,5},{5... | collective-permute-start | bytes 995336 | tf_op jit(solution)/shard_map/ppermute | solution.py:331
  29.4 1.9 %collective-permute-start.10 = (bf16[80,1152]{1,0:T(8,128)(2,1)S(1)}, bf16[80,1152]{1,0:T(8,128)(2,1)S(1)}, u32[]{:S(2)}, u32[]{:S(2)}) collective-permute-start(bf16[80,1152]{1,0:T(8,128)(2,1)S(1)} %collective-permute-done.3.rest_2_), channel_id=1, source_target_pairs={{0,4},{4,0},{8,12},{12,8},{16,20},{20,16},{24,28},{28,24},{1,5},{5... | collective-permute-start | bytes 552968 | tf_op jit(solution)/shard_map/ppermute | solution.py:331
  30.3 1.4 %collective-permute-start.11 = (bf16[80,1152]{1,0:T(8,128)(2,1)S(1)}, bf16[80,1152]{1,0:T(8,128)(2,1)S(1)}, u32[]{:S(2)}, u32[]{:S(2)}) collective-permute-start(bf16[80,1152]{1,0:T(8,128)(2,1)S(1)} %collective-permute-done.7.rest_3_), channel_id=1, source_target_pairs={{0,4},{4,0},{8,12},{12,8},{16,20},{20,16},{24,28},{28,24},{1,5},{5... | collective-permute-start | bytes 552968 | tf_op jit(solution)/shard_map/ppermute | solution.py:331
  34.9 9.1 %collective-permute-start.13 = (bf16[288,512]{1,0:T(8,128)(2,1)S(1)}, bf16[288,512]{1,0:T(8,128)(2,1)S(1)}, u32[]{:S(2)}, u32[]{:S(2)}) collective-permute-start(bf16[288,512]{1,0:T(8,128)(2,1)S(1)} %get-tuple-element.62), channel_id=1, source_target_pairs={{0,1},{1,0},{2,3},{3,2},{4,5},{5,4},{6,7},{7,6},{8,9},{9,8},{10,11... | collective-permute-start | bytes 884744 | tf_op jit(solution)/shard_map/ppermute | solution.py:328
  36.2 25.0 %collective-permute-start.22 = (bf16[256,1152]{1,0:T(8,128)(2,1)S(1)}, bf16[256,1152]{1,0:T(8,128)(2,1)S(1)}, u32[]{:S(2)}, u32[]{:S(2)}) collective-permute-start(bf16[256,1152]{1,0:T(8,128)(2,1)S(1)} %get-tuple-element.73.u0), channel_id=1, source_target_pairs={{0,24},{4,28},{8,0},{12,4},{16,8},{20,12},{24,16},{28,20},{1,25},{... | collective-permute-start | bytes 1769480 | tf_op jit(solution)/shard_map/ppermute | solution.py:334
  36.7 24.6 %collective-permute-start.21 = (bf16[256,1152]{1,0:T(8,128)(2,1)S(1)}, bf16[256,1152]{1,0:T(8,128)(2,1)S(1)}, u32[]{:S(2)}, u32[]{:S(2)}) collective-permute-start(bf16[256,1152]{1,0:T(8,128)(2,1)S(1)} %get-tuple-element.73.u0), channel_id=1, source_target_pairs={{0,28},{4,0},{8,4},{12,8},{16,12},{20,16},{24,20},{28,24},{1,29},{... | collective-permute-start | bytes 1769480 | tf_op jit(solution)/shard_map/ppermute | solution.py:334
  44.1 14.6 %collective-permute-start.14 = (bf16[288,640]{1,0:T(8,128)(2,1)S(1)}, bf16[288,640]{1,0:T(8,128)(2,1)S(1)}, u32[]{:S(2)}, u32[]{:S(2)}) collective-permute-start(bf16[288,640]{1,0:T(8,128)(2,1)S(1)} %get-tuple-element.63), channel_id=1, source_target_pairs={{0,1},{1,0},{2,3},{3,2},{4,5},{5,4},{6,7},{7,6},{8,9},{9,8},{10,11... | collective-permute-start | bytes 1105928 | tf_op jit(solution)/shard_map/ppermute | solution.py:328
  45.8 19.3 %collective-permute-start.19 = (bf16[288,512]{1,0:T(8,128)(2,1)S(1)}, bf16[288,512]{1,0:T(8,128)(2,1)S(1)}, u32[]{:S(2)}, u32[]{:S(2)}) collective-permute-start(bf16[288,512]{1,0:T(8,128)(2,1)S(1)} %get-tuple-element.71), channel_id=1, source_target_pairs={{1,3},{2,0},{0,1},{3,2},{5,7},{6,4},{4,5},{7,6},{9,11},{10,8},{8,9... | collective-permute-start | bytes 884744 | tf_op jit(solution)/shard_map/ppermute | solution.py:328
  45.9 24.1 %collective-permute-start.20 = (bf16[288,512]{1,0:T(8,128)(2,1)S(1)}, bf16[288,512]{1,0:T(8,128)(2,1)S(1)}, u32[]{:S(2)}, u32[]{:S(2)}) collective-permute-start(bf16[288,512]{1,0:T(8,128)(2,1)S(1)} %get-tuple-element.72), channel_id=1, source_target_pairs={{1,2},{2,1},{0,0},{3,3},{5,6},{6,5},{4,4},{7,7},{9,10},{10,9},{8,8... | collective-permute-start | bytes 884744 | tf_op jit(solution)/shard_map/ppermute | solution.py:328
  59.6 11.3 %collective-permute-start.15 = (bf16[144,640]{1,0:T(8,128)(2,1)S(1)}, bf16[144,640]{1,0:T(8,128)(2,1)S(1)}, u32[]{:S(2)}, u32[]{:S(2)}) collective-permute-start(bf16[144,640]{1,0:T(8,128)(2,1)S(1)} %get-tuple-element.65), channel_id=1, source_target_pairs={{1,3},{2,0},{0,1},{3,2},{5,7},{6,4},{4,5},{7,6},{9,11},{10,8},{8,9... | collective-permute-start | bytes 552968 | tf_op jit(solution)/shard_map/ppermute | solution.py:328
  61.2 9.7 %collective-permute-start.16 = (bf16[144,640]{1,0:T(8,128)(2,1)S(1)}, bf16[144,640]{1,0:T(8,128)(2,1)S(1)}, u32[]{:S(2)}, u32[]{:S(2)}) collective-permute-start(bf16[144,640]{1,0:T(8,128)(2,1)S(1)} %get-tuple-element.66), channel_id=1, source_target_pairs={{1,3},{2,0},{0,1},{3,2},{5,7},{6,4},{4,5},{7,6},{9,11},{10,8},{8,9... | collective-permute-start | bytes 552968 | tf_op jit(solution)/shard_map/ppermute | solution.py:328
  61.3 14.4 %collective-permute-start.17 = (bf16[144,640]{1,0:T(8,128)(2,1)S(1)}, bf16[144,640]{1,0:T(8,128)(2,1)S(1)}, u32[]{:S(2)}, u32[]{:S(2)}) collective-permute-start(bf16[144,640]{1,0:T(8,128)(2,1)S(1)} %get-tuple-element.67), channel_id=1, source_target_pairs={{1,2},{2,1},{0,0},{3,3},{5,6},{6,5},{4,4},{7,7},{9,10},{10,9},{8,8... | collective-permute-start | bytes 552968 | tf_op jit(solution)/shard_map/ppermute | solution.py:328
  65.1 12.6 %collective-permute-start.18 = (bf16[144,640]{1,0:T(8,128)(2,1)S(1)}, bf16[144,640]{1,0:T(8,128)(2,1)S(1)}, u32[]{:S(2)}, u32[]{:S(2)}) collective-permute-start(bf16[144,640]{1,0:T(8,128)(2,1)S(1)} %get-tuple-element.68), channel_id=1, source_target_pairs={{1,2},{2,1},{0,0},{3,3},{5,6},{6,5},{4,4},{7,7},{9,10},{10,9},{8,8... | collective-permute-start | bytes 552968 | tf_op jit(solution)/shard_map/ppermute | solution.py:328

commit v14 on v13

--- a/solution.py
+++ b/solution.py
@@ -9,7 +9,7 @@
 
 STEPS = 3
 EPS = 1e-06
-SHARES = (4, 5)
+SHARES = (5, 4)
 CROSS_PARTS = (1, 2)
 TEXT_PARTS = 2
 VMEM_BYTES = 24 * 1024 * 1024

time: 78.9 us -> 80.2 us (1.016)
  waiting for transfers between devices: 36.7 us -> 39.2 us
  starting transfers between devices: 27 us -> 25.7 us
    ppermute x12, waiting for transfers between devices: 29.6 us -> 32.1 us  [along(): return lax.ppermute(value, 'fsdp', pairs)]
    ppermute x12, starting transfers between devices: 22.8 us -> 21.5 us  [along(): return lax.ppermute(value, 'fsdp', pairs)]
where the time goes in v14:
time: 80.2 us; the launch traced here: 79.9 us
  waiting for transfers between devices  39.2 us (49%)
  starting transfers between devices  25.7 us (32%)
  Pallas kernels  10.6 us (13%)
  local copies, waits for them, and re-layouts  2.21 us (3%)
  between operations  2.13 us (3%)
    ppermute x12, waiting for transfers between devices, along(): return lax.ppermute(value, 'fsdp', pairs)  32.1 us
    ppermute x12, starting transfers between devices, along(): return lax.ppermute(value, 'fsdp', pairs)  21.5 us
    ppermute x3, waiting for transfers between devices, shifted(): lax.ppermute(value, 'dp', [(d, (d + by) % n_dp) for d in range(n_dp)])  4.73 us
    pallas_call x1, Pallas kernels, picture_side(): pl.pallas_call(picture_kernel, out_shape=outs, in_specs=spaces(13), out_s...  3.16 us
    pallas_call x1, Pallas kernels, text_side(): pl.pallas_call(text_kernel, out_shape=(jax.ShapeDtypeStruct((rows, width)...  2.76 us
    ppermute x3, starting transfers between devices, shifted(): lax.ppermute(value, 'dp', [(d, (d + by) % n_dp) for d in range(n_dp)])  2.6 us
    unnamed x10, local copies, waits for them, and re-layouts  2.16 us
    pallas_call x2, Pallas kernels, total(): pl.pallas_call(functools.partial(total_kernel, begin, parts), out_shape=j...  1.92 us
  transfers between devices with their start and end apart: 23, of which 10 were waited for; matrix products, arithmetic and copies ran while one was open for 0% of the time, Pallas kernels for 12%

profile of v14, /device:TPU:18, one launch (start us, length us, event | category | flops | bytes accessed | tf_op | source)
XLA Modules:
  0.0 79.9 jit_solution(14045989920246354120)
XLA Ops:
  0.6 1.1 %copy-done = bf16[288,1152]{1,0:T(8,128)(2,1)S(1)} copy-done((bf16[288,1152]{1,0:T(8,128)(2,1)S(1)}, bf16[288,1152]{1,0:T(8,128)(2,1)}, u32[]{:S(2)}) %copy-start) | copy-done | bytes 663576
  2.1 1.5 %collective-permute-start.4 = (bf16[256,1152]{1,0:T(8,128)(2,1)}, bf16[256,1152]{1,0:T(8,128)(2,1)S(1)}, u32[]{:S(2)}, u32[]{:S(2)}) collective-permute-start(bf16[256,1152]{1,0:T(8,128)(2,1)} %text), channel_id=1, source_target_pairs={{0,8},{4,12},{8,16},{12,20},{16,24},{20,28},{24,0},{28,4},{1,9},{5... | collective-permute-start | bytes 1769480 | tf_op jit(solution)/shard_map/ppermute | solution.py:334
  4.0 2.7 %collective-permute-start.1 = (bf16[144,1152]{1,0:T(8,128)(2,1)S(1)}, bf16[144,1152]{1,0:T(8,128)(2,1)S(1)}, u32[]{:S(2)}, u32[]{:S(2)}) collective-permute-start(bf16[144,1152]{1,0:T(8,128)(2,1)S(1)} %get-tuple-element.41), channel_id=1, source_target_pairs={{0,3},{1,0},{2,1},{3,2},{4,7},{5,4},{6,5},{7,6},{8,11},{9,8},{10,9... | collective-permute-start | bytes 995336 | tf_op jit(solution)/shard_map/ppermute | solution.py:328
  6.7 1.1 %copy-done.2 = bf16[256,1152]{1,0:T(8,128)(2,1)S(1)} copy-done((bf16[256,1152]{1,0:T(8,128)(2,1)S(1)}, bf16[256,1152]{1,0:T(8,128)(2,1)}, u32[]{:S(2)}) %copy-start.2) | copy-done | bytes 589848
  8.0 4.7 %collective-permute-done.3.rest_2_ = bf16[80,1152]{1,0:T(8,128)(2,1)S(1)} collective-permute-done((bf16[80,1152]{1,0:T(8,128)(2,1)S(1)}, bf16[80,1152]{1,0:T(8,128)(2,1)S(1)}, u32[]{:S(2)}, u32[]{:S(2)}) %collective-permute-start.3) | collective-permute-done | bytes 184352 | tf_op jit(solution)/shard_map/ppermute | solution.py:328
  12.7 4.7 %collective-permute-done.4.t2 = bf16[256,1152]{1,0:T(8,128)(2,1)S(1)} collective-permute-done((bf16[256,1152]{1,0:T(8,128)(2,1)}, bf16[256,1152]{1,0:T(8,128)(2,1)S(1)}, u32[]{:S(2)}, u32[]{:S(2)}) %collective-permute-start.4) | collective-permute-done | bytes 589856 | tf_op jit(solution)/shard_map/ppermute | solution.py:334
  17.6 0.5 collective-permute-start.5
  18.1 5.9 %collective-permute-start.12 = (bf16[864,256]{1,0:T(8,128)(2,1)S(1)}, bf16[864,256]{1,0:T(8,128)(2,1)S(1)}, u32[]{:S(2)}, u32[]{:S(2)}) collective-permute-start(bf16[864,256]{1,0:T(8,128)(2,1)S(1)} %get-tuple-element.57), channel_id=1, source_target_pairs={{0,1},{1,0},{2,3},{3,2},{4,5},{5,4},{6,7},{7,6},{8,9},{9,8},{10,11... | collective-permute-start | bytes 1327112 | tf_op jit(solution)/shard_map/ppermute | solution.py:328
  24.0 0.5 collective-permute-start.7
  25.8 0.7 prepare.1
  26.5 2.3 %collective-permute-done.rest_0_ = bf16[144,1152]{1,0:T(8,128)(2,1)S(1)} collective-permute-done((bf16[144,1152]{1,0:T(8,128)(2,1)S(1)}, bf16[144,1152]{1,0:T(8,128)(2,1)S(1)}, u32[]{:S(2)}, u32[]{:S(2)}) %collective-permute-start) | collective-permute-done | bytes 331808 | tf_op jit(solution)/shard_map/ppermute | solution.py:328
  29.4 0.9 %collective-permute-done.7.rest_3_ = bf16[80,1152]{1,0:T(8,128)(2,1)S(1)} collective-permute-done((bf16[80,1152]{1,0:T(8,128)(2,1)S(1)}, bf16[80,1152]{1,0:T(8,128)(2,1)S(1)}, u32[]{:S(2)}, u32[]{:S(2)}) %collective-permute-start.7) | collective-permute-done | bytes 184352 | tf_op jit(solution)/shard_map/ppermute | solution.py:346
  30.3 0.9 %collective-permute-done.10.rest_6_ = bf16[80,1152]{1,0:T(8,128)(2,1)S(1)} collective-permute-done((bf16[80,1152]{1,0:T(8,128)(2,1)S(1)}, bf16[80,1152]{1,0:T(8,128)(2,1)S(1)}, u32[]{:S(2)}, u32[]{:S(2)}) %collective-permute-start.10) | collective-permute-done | bytes 184352 | tf_op jit(solution)/shard_map/ppermute | solution.py:331
  31.2 0.5 collective-permute-done.11.rest_7_
  31.7 3.2 %picture_side.1 = (bf16[288,640]{1,0:T(8,128)(2,1)S(1)}, bf16[288,512]{1,0:T(8,128)(2,1)S(1)}, bf16[256,1152]{1,0:T(8,128)(2,1)S(1)}, bf16[256,1152]{1,0:T(8,128)(2,1)S(1)}) custom-call(bf16[256,1152]{1,0:T(8,128)(2,1)S(1)} %copy-done.3, bf16[1152,256]{1,0:T(8,128)(2,1)S(1)} %get-tuple-element.49.x_t, bf16[768,1152]{1,0:T(8,128)(2,1)S(1)} %get-tuple-element.50.units, ...), custom_call_target="tpu_custom_call" | custom-call | tf_op jit(solution)/shard_map/picture_side/pallas_call | solution.py:206
  34.9 1.2 %collective-permute-start.13 = (bf16[288,640]{1,0:T(8,128)(2,1)S(1)}, bf16[288,640]{1,0:T(8,128)(2,1)S(1)}, u32[]{:S(2)}, u32[]{:S(2)}) collective-permute-start(bf16[288,640]{1,0:T(8,128)(2,1)S(1)} %get-tuple-element.62), channel_id=1, source_target_pairs={{0,1},{1,0},{2,3},{3,2},{4,5},{5,4},{6,7},{7,6},{8,9},{9,8},{10,11... | collective-permute-start | bytes 1105928 | tf_op jit(solution)/shard_map/ppermute | solution.py:328
  36.2 0.5 collective-permute-start.22
  36.7 0.5 collective-permute-start.21
  37.2 8.4 %collective-permute-done.13.arrived = bf16[288,640]{1,0:T(8,128)(2,1)S(1)} collective-permute-done((bf16[288,640]{1,0:T(8,128)(2,1)S(1)}, bf16[288,640]{1,0:T(8,128)(2,1)S(1)}, u32[]{:S(2)}, u32[]{:S(2)}) %collective-permute-start.13) | collective-permute-done | bytes 368672 | tf_op jit(solution)/shard_map/ppermute | solution.py:328
  45.6 0.9 %pair_product.3 = (f32[288,640]{1,0:T(8,128)S(1)}, bf16[288,640]{1,0:T(8,128)(2,1)S(1)}, bf16[288,640]{1,0:T(8,128)(2,1)S(1)}) custom-call(bf16[1152,256]{1,0:T(8,128)(2,1)S(1)} %get-tuple-element.49.x_t, bf16[864,256]{1,0:T(8,128)(2,1)S(1)} %collective-permute-done.12.far_t, bf16[256,1152]{1,0:T(8,128)(2,1)S(1)} %get-tuple-element.60.grad, ...), custom_call_target="tpu_custom_call" | custom-call | tf_op jit(solution)/shard_map/pair_product/pallas_call | solution.py:285
  46.7 1.9 %collective-permute-start.14 = (bf16[288,512]{1,0:T(8,128)(2,1)S(1)}, bf16[288,512]{1,0:T(8,128)(2,1)S(1)}, u32[]{:S(2)}, u32[]{:S(2)}) collective-permute-start(bf16[288,512]{1,0:T(8,128)(2,1)S(1)} %get-tuple-element.63), channel_id=1, source_target_pairs={{0,1},{1,0},{2,3},{3,2},{4,5},{5,4},{6,7},{7,6},{8,9},{9,8},{10,11... | collective-permute-start | bytes 884744 | tf_op jit(solution)/shard_map/ppermute | solution.py:328
  48.6 1.9 %collective-permute-start.20 = (bf16[288,640]{1,0:T(8,128)(2,1)S(1)}, bf16[288,640]{1,0:T(8,128)(2,1)S(1)}, u32[]{:S(2)}, u32[]{:S(2)}) collective-permute-start(bf16[288,640]{1,0:T(8,128)(2,1)S(1)} %get-tuple-element.72), channel_id=1, source_target_pairs={{1,2},{2,1},{0,0},{3,3},{5,6},{6,5},{4,4},{7,7},{9,10},{10,9},{8,8... | collective-permute-start | bytes 1105928 | tf_op jit(solution)/shard_map/ppermute | solution.py:328
  50.5 12.2 %collective-permute-done.14.arrived = bf16[288,512]{1,0:T(8,128)(2,1)S(1)} collective-permute-done((bf16[288,512]{1,0:T(8,128)(2,1)S(1)}, bf16[288,512]{1,0:T(8,128)(2,1)S(1)}, u32[]{:S(2)}, u32[]{:S(2)}) %collective-permute-start.14) | collective-permute-done | bytes 294944 | tf_op jit(solution)/shard_map/ppermute | solution.py:328
  62.7 0.6 pair_product.2
  63.4 0.9 %collective-permute-start.15 = (bf16[144,512]{1,0:T(8,128)(2,1)S(1)}, bf16[144,512]{1,0:T(8,128)(2,1)S(1)}, u32[]{:S(2)}, u32[]{:S(2)}) collective-permute-start(bf16[144,512]{1,0:T(8,128)(2,1)S(1)} %get-tuple-element.65), channel_id=1, source_target_pairs={{1,3},{2,0},{0,1},{3,2},{5,7},{6,4},{4,5},{7,6},{9,11},{10,8},{8,9... | collective-permute-start | bytes 442376 | tf_op jit(solution)/shard_map/ppermute | solution.py:328
  64.3 4.5 %collective-permute-start.17 = (bf16[144,512]{1,0:T(8,128)(2,1)S(1)}, bf16[144,512]{1,0:T(8,128)(2,1)S(1)}, u32[]{:S(2)}, u32[]{:S(2)}) collective-permute-start(bf16[144,512]{1,0:T(8,128)(2,1)S(1)} %get-tuple-element.67), channel_id=1, source_target_pairs={{1,2},{2,1},{0,0},{3,3},{5,6},{6,5},{4,4},{7,7},{9,10},{10,9},{8,8... | collective-permute-start | bytes 442376 | tf_op jit(solution)/shard_map/ppermute | solution.py:328
  68.8 1.9 %collective-permute-start.18 = (bf16[144,512]{1,0:T(8,128)(2,1)S(1)}, bf16[144,512]{1,0:T(8,128)(2,1)S(1)}, u32[]{:S(2)}, u32[]{:S(2)}) collective-permute-start(bf16[144,512]{1,0:T(8,128)(2,1)S(1)} %get-tuple-element.68), channel_id=1, source_target_pairs={{1,2},{2,1},{0,0},{3,3},{5,6},{6,5},{4,4},{7,7},{9,10},{10,9},{8,8... | collective-permute-start | bytes 442376 | tf_op jit(solution)/shard_map/ppermute | solution.py:328
  70.7 2.8 %text_side.1 = (f32[256,1152]{1,0:T(8,128)}, f32[8,128]{1,0:T(8,128)S(1)}) custom-call(bf16[256,1152]{1,0:T(8,128)(2,1)S(1)} %copy-done.4, f32[8,128]{1,0:T(8,128)S(1)} %get-tuple-element.51.scalars, bf16[256,1152]{1,0:T(8,128)(2,1)S(1)} %get-tuple-element.73.u0, bf16[256,1152]{1,0:T(8,128)(2,1)S(1)} %collective-permute-done.21.u1, ...), custom_call_target="tpu_custom_call" | custom-call | tf_op jit(solution)/shard_map/text_side/pallas_call | solution.py:238
  73.5 1.0 %total.2.rest_4_ = f32[1,288,1152]{2,1,0:T(8,128)} custom-call(f32[288,640]{1,0:T(8,128)S(1)} %get-tuple-element.70.kept, bf16[288,640]{1,0:T(8,128)(2,1)S(1)} %collective-permute-done.19.rest_0_, bf16[288,640]{1,0:T(8,128)(2,1)S(1)} %collective-permute-done.20.rest_1_), custom_call_target="tpu_custom_call" | custom-call | tf_op jit(solution)/shard_map/total/pallas_call | solution.py:309
  74.5 2.3 %collective-permute-done.17.rest_2_ = bf16[144,512]{1,0:T(8,128)(2,1)S(1)} collective-permute-done((bf16[144,512]{1,0:T(8,128)(2,1)S(1)}, bf16[144,512]{1,0:T(8,128)(2,1)S(1)}, u32[]{:S(2)}, u32[]{:S(2)}) %collective-permute-start.17) | collective-permute-done | bytes 147488 | tf_op jit(solution)/shard_map/ppermute | solution.py:328
  76.8 2.2 %collective-permute-done.18.rest_3_ = bf16[144,512]{1,0:T(8,128)(2,1)S(1)} collective-permute-done((bf16[144,512]{1,0:T(8,128)(2,1)S(1)}, bf16[144,512]{1,0:T(8,128)(2,1)S(1)}, u32[]{:S(2)}, u32[]{:S(2)}) %collective-permute-start.18) | collective-permute-done | bytes 147488 | tf_op jit(solution)/shard_map/ppermute | solution.py:328
  79.0 0.9 %total.3 = f32[1,288,1152]{2,1,0:T(8,128)} custom-call(f32[288,512]{1,0:T(8,128)S(1)} %get-tuple-element.64.kept, bf16[144,512]{1,0:T(8,128)(2,1)S(1)} %collective-permute-done.15.rest_0_, bf16[144,512]{1,0:T(8,128)(2,1)S(1)} %collective-permute-done.16.rest_1_, ...), custom_call_target="tpu_custom_call", output_to_operand_aliasing={{}: (5, {})} | custom-call | tf_op jit(solution)/shard_map/total/pallas_call | solution.py:309
  (34 shorter events, 1.9 us)
Async XLA Ops:
  0.6 1.1 %copy-start = (bf16[288,1152]{1,0:T(8,128)(2,1)S(1)}, bf16[288,1152]{1,0:T(8,128)(2,1)}, u32[]{:S(2)}) copy-start(bf16[288,1152]{1,0:T(8,128)(2,1)} %own.3) | copy-start | bytes 1990660
  1.7 24.1 %copy-start.4 = (bf16[256,1152]{1,0:T(8,128)(2,1)S(1)}, bf16[256,1152]{1,0:T(8,128)(2,1)}, u32[]{:S(2)}) copy-start(bf16[256,1152]{1,0:T(8,128)(2,1)} %text) | copy-start | bytes 1769476
  2.1 15.3 %collective-permute-start.4 = (bf16[256,1152]{1,0:T(8,128)(2,1)}, bf16[256,1152]{1,0:T(8,128)(2,1)S(1)}, u32[]{:S(2)}, u32[]{:S(2)}) collective-permute-start(bf16[256,1152]{1,0:T(8,128)(2,1)} %text), channel_id=1, source_target_pairs={{0,8},{4,12},{8,16},{12,20},{16,24},{20,28},{24,0},{28,4},{1,9},{5... | collective-permute-start | bytes 1769480 | tf_op jit(solution)/shard_map/ppermute | solution.py:334
  3.6 9.1 %collective-permute-start.3 = (bf16[80,1152]{1,0:T(8,128)(2,1)S(1)}, bf16[80,1152]{1,0:T(8,128)(2,1)S(1)}, u32[]{:S(2)}, u32[]{:S(2)}) collective-permute-start(bf16[80,1152]{1,0:T(8,128)(2,1)S(1)} %get-tuple-element.43), channel_id=1, source_target_pairs={{0,2},{1,3},{2,0},{3,1},{4,6},{5,7},{6,4},{7,5},{8,10},{9,11},{10,... | collective-permute-start | bytes 552968 | tf_op jit(solution)/shard_map/ppermute | solution.py:328
  4.0 22.5 %collective-permute-start.1 = (bf16[144,1152]{1,0:T(8,128)(2,1)S(1)}, bf16[144,1152]{1,0:T(8,128)(2,1)S(1)}, u32[]{:S(2)}, u32[]{:S(2)}) collective-permute-start(bf16[144,1152]{1,0:T(8,128)(2,1)S(1)} %get-tuple-element.41), channel_id=1, source_target_pairs={{0,3},{1,0},{2,1},{3,2},{4,7},{5,4},{6,5},{7,6},{8,11},{9,8},{10,9... | collective-permute-start | bytes 995336 | tf_op jit(solution)/shard_map/ppermute | solution.py:328
  6.7 22.2 %collective-permute-start = (bf16[144,1152]{1,0:T(8,128)(2,1)S(1)}, bf16[144,1152]{1,0:T(8,128)(2,1)S(1)}, u32[]{:S(2)}, u32[]{:S(2)}) collective-permute-start(bf16[144,1152]{1,0:T(8,128)(2,1)S(1)} %get-tuple-element.41), channel_id=1, source_target_pairs={{0,1},{1,2},{2,3},{3,0},{4,5},{5,6},{6,7},{7,4},{8,9},{9,10},{10,1... | collective-permute-start | bytes 995336 | tf_op jit(solution)/shard_map/ppermute | solution.py:328
  6.7 11.4 %collective-permute-start.2 = (bf16[256,1152]{1,0:T(8,128)(2,1)}, bf16[256,1152]{1,0:T(8,128)(2,1)S(1)}, u32[]{:S(2)}, u32[]{:S(2)}) collective-permute-start(bf16[256,1152]{1,0:T(8,128)(2,1)} %text), channel_id=1, source_target_pairs={{0,4},{4,0},{8,12},{12,8},{16,20},{20,16},{24,28},{28,24},{1,5},{5... | collective-permute-start | bytes 1769480 | tf_op jit(solution)/shard_map/ppermute | solution.py:331
  6.7 1.1 %copy-start.2 = (bf16[256,1152]{1,0:T(8,128)(2,1)S(1)}, bf16[256,1152]{1,0:T(8,128)(2,1)}, u32[]{:S(2)}) copy-start(bf16[256,1152]{1,0:T(8,128)(2,1)} %x.3) | copy-start | bytes 1769476
  17.5 14.3 %copy-start.1 = (bf16[288,1152]{1,0:T(8,128)(2,1)S(1)}, bf16[288,1152]{1,0:T(8,128)(2,1)}, u32[]{:S(2)}) copy-start(bf16[288,1152]{1,0:T(8,128)(2,1)} %own.3) | copy-start | bytes 1990660
  17.5 14.3 %copy-start.3 = (bf16[256,1152]{1,0:T(8,128)(2,1)S(1)}, bf16[256,1152]{1,0:T(8,128)(2,1)}, u32[]{:S(2)}) copy-start(bf16[256,1152]{1,0:T(8,128)(2,1)} %x.3) | copy-start | bytes 1769476
  17.5 6.5 %collective-permute-start.6 = (bf16[128,1152]{1,0:T(8,128)(2,1)S(1)}, bf16[128,1152]{1,0:T(8,128)(2,1)S(1)}, u32[]{:S(2)}, u32[]{:S(2)}) collective-permute-start(bf16[128,1152]{1,0:T(8,128)(2,1)S(1)} %get-tuple-element.76), channel_id=1, source_target_pairs={{0,4},{4,0},{8,12},{12,8},{16,20},{20,16},{24,28},{28,24},{1,5},{5... | collective-permute-start | bytes 884744 | tf_op jit(solution)/shard_map/ppermute | solution.py:331
  17.6 8.2 %collective-permute-start.5 = (bf16[128,1152]{1,0:T(8,128)(2,1)S(1)}, bf16[128,1152]{1,0:T(8,128)(2,1)S(1)}, u32[]{:S(2)}, u32[]{:S(2)}) collective-permute-start(bf16[128,1152]{1,0:T(8,128)(2,1)S(1)} %get-tuple-element.77), channel_id=1, source_target_pairs={{0,4},{4,0},{8,12},{12,8},{16,20},{20,16},{24,28},{28,24},{1,5},{5... | collective-permute-start | bytes 884744 | tf_op jit(solution)/shard_map/ppermute | solution.py:331
  18.1 16.8 %collective-permute-start.12 = (bf16[864,256]{1,0:T(8,128)(2,1)S(1)}, bf16[864,256]{1,0:T(8,128)(2,1)S(1)}, u32[]{:S(2)}, u32[]{:S(2)}) collective-permute-start(bf16[864,256]{1,0:T(8,128)(2,1)S(1)} %get-tuple-element.57), channel_id=1, source_target_pairs={{0,1},{1,0},{2,3},{3,2},{4,5},{5,4},{6,7},{7,6},{8,9},{9,8},{10,11... | collective-permute-start | bytes 1327112 | tf_op jit(solution)/shard_map/ppermute | solution.py:328
  24.0 6.3 %collective-permute-start.7 = (bf16[80,1152]{1,0:T(8,128)(2,1)S(1)}, bf16[80,1152]{1,0:T(8,128)(2,1)S(1)}, u32[]{:S(2)}, u32[]{:S(2)}) collective-permute-start(bf16[80,1152]{1,0:T(8,128)(2,1)S(1)} %collective-permute-done.3.rest_2_), channel_id=1, source_target_pairs={{0,8},{4,12},{8,0},{12,4},{16,24},{20,28},{24,16},{28,20},{1,9},{5... | collective-permute-start | bytes 552968 | tf_op jit(solution)/shard_map/ppermute | solution.py:346
  28.8 2.9 %collective-permute-start.8 = (bf16[144,1152]{1,0:T(8,128)(2,1)S(1)}, bf16[144,1152]{1,0:T(8,128)(2,1)S(1)}, u32[]{:S(2)}, u32[]{:S(2)}) collective-permute-start(bf16[144,1152]{1,0:T(8,128)(2,1)S(1)} %collective-permute-done.rest_0_), channel_id=1, source_target_pairs={{0,4},{4,0},{8,12},{12,8},{16,20},{20,16},{24,28},{28,24},{1,5},{5... | collective-permute-start | bytes 995336 | tf_op jit(solution)/shard_map/ppermute | solution.py:331
  28.9 2.9 %collective-permute-start.9 = (bf16[144,1152]{1,0:T(8,128)(2,1)S(1)}, bf16[144,1152]{1,0:T(8,128)(2,1)S(1)}, u32[]{:S(2)}, u32[]{:S(2)}) collective-permute-start(bf16[144,1152]{1,0:T(8,128)(2,1)S(1)} %collective-permute-done.1.rest_1_), channel_id=1, source_target_pairs={{0,4},{4,0},{8,12},{12,8},{16,20},{20,16},{24,28},{28,24},{1,5},{5... | collective-permute-start | bytes 995336 | tf_op jit(solution)/shard_map/ppermute | solution.py:331
  29.4 1.9 %collective-permute-start.10 = (bf16[80,1152]{1,0:T(8,128)(2,1)S(1)}, bf16[80,1152]{1,0:T(8,128)(2,1)S(1)}, u32[]{:S(2)}, u32[]{:S(2)}) collective-permute-start(bf16[80,1152]{1,0:T(8,128)(2,1)S(1)} %collective-permute-done.3.rest_2_), channel_id=1, source_target_pairs={{0,4},{4,0},{8,12},{12,8},{16,20},{20,16},{24,28},{28,24},{1,5},{5... | collective-permute-start | bytes 552968 | tf_op jit(solution)/shard_map/ppermute | solution.py:331
  30.3 1.4 %collective-permute-start.11 = (bf16[80,1152]{1,0:T(8,128)(2,1)S(1)}, bf16[80,1152]{1,0:T(8,128)(2,1)S(1)}, u32[]{:S(2)}, u32[]{:S(2)}) collective-permute-start(bf16[80,1152]{1,0:T(8,128)(2,1)S(1)} %collective-permute-done.7.rest_3_), channel_id=1, source_target_pairs={{0,4},{4,0},{8,12},{12,8},{16,20},{20,16},{24,28},{28,24},{1,5},{5... | collective-permute-start | bytes 552968 | tf_op jit(solution)/shard_map/ppermute | solution.py:331
  34.9 10.7 %collective-permute-start.13 = (bf16[288,640]{1,0:T(8,128)(2,1)S(1)}, bf16[288,640]{1,0:T(8,128)(2,1)S(1)}, u32[]{:S(2)}, u32[]{:S(2)}) collective-permute-start(bf16[288,640]{1,0:T(8,128)(2,1)S(1)} %get-tuple-element.62), channel_id=1, source_target_pairs={{0,1},{1,0},{2,3},{3,2},{4,5},{5,4},{6,7},{7,6},{8,9},{9,8},{10,11... | collective-permute-start | bytes 1105928 | tf_op jit(solution)/shard_map/ppermute | solution.py:328
  36.2 28.0 %collective-permute-start.22 = (bf16[256,1152]{1,0:T(8,128)(2,1)S(1)}, bf16[256,1152]{1,0:T(8,128)(2,1)S(1)}, u32[]{:S(2)}, u32[]{:S(2)}) collective-permute-start(bf16[256,1152]{1,0:T(8,128)(2,1)S(1)} %get-tuple-element.73.u0), channel_id=1, source_target_pairs={{0,24},{4,28},{8,0},{12,4},{16,8},{20,12},{24,16},{28,20},{1,25},{... | collective-permute-start | bytes 1769480 | tf_op jit(solution)/shard_map/ppermute | solution.py:334
  36.7 27.6 %collective-permute-start.21 = (bf16[256,1152]{1,0:T(8,128)(2,1)S(1)}, bf16[256,1152]{1,0:T(8,128)(2,1)S(1)}, u32[]{:S(2)}, u32[]{:S(2)}) collective-permute-start(bf16[256,1152]{1,0:T(8,128)(2,1)S(1)} %get-tuple-element.73.u0), channel_id=1, source_target_pairs={{0,28},{4,0},{8,4},{12,8},{16,12},{20,16},{24,20},{28,24},{1,29},{... | collective-permute-start | bytes 1769480 | tf_op jit(solution)/shard_map/ppermute | solution.py:334
  46.5 22.3 %collective-permute-start.19 = (bf16[288,640]{1,0:T(8,128)(2,1)S(1)}, bf16[288,640]{1,0:T(8,128)(2,1)S(1)}, u32[]{:S(2)}, u32[]{:S(2)}) collective-permute-start(bf16[288,640]{1,0:T(8,128)(2,1)S(1)} %get-tuple-element.71), channel_id=1, source_target_pairs={{1,3},{2,0},{0,1},{3,2},{5,7},{6,4},{4,5},{7,6},{9,11},{10,8},{8,9... | collective-permute-start | bytes 1105928 | tf_op jit(solution)/shard_map/ppermute | solution.py:328
  46.7 16.0 %collective-permute-start.14 = (bf16[288,512]{1,0:T(8,128)(2,1)S(1)}, bf16[288,512]{1,0:T(8,128)(2,1)S(1)}, u32[]{:S(2)}, u32[]{:S(2)}) collective-permute-start(bf16[288,512]{1,0:T(8,128)(2,1)S(1)} %get-tuple-element.63), channel_id=1, source_target_pairs={{0,1},{1,0},{2,3},{3,2},{4,5},{5,4},{6,7},{7,6},{8,9},{9,8},{10,11... | collective-permute-start | bytes 884744 | tf_op jit(solution)/shard_map/ppermute | solution.py:328
  48.6 24.9 %collective-permute-start.20 = (bf16[288,640]{1,0:T(8,128)(2,1)S(1)}, bf16[288,640]{1,0:T(8,128)(2,1)S(1)}, u32[]{:S(2)}, u32[]{:S(2)}) collective-permute-start(bf16[288,640]{1,0:T(8,128)(2,1)S(1)} %get-tuple-element.72), channel_id=1, source_target_pairs={{1,2},{2,1},{0,0},{3,3},{5,6},{6,5},{4,4},{7,7},{9,10},{10,9},{8,8... | collective-permute-start | bytes 1105928 | tf_op jit(solution)/shard_map/ppermute | solution.py:328
  63.4 11.2 %collective-permute-start.15 = (bf16[144,512]{1,0:T(8,128)(2,1)S(1)}, bf16[144,512]{1,0:T(8,128)(2,1)S(1)}, u32[]{:S(2)}, u32[]{:S(2)}) collective-permute-start(bf16[144,512]{1,0:T(8,128)(2,1)S(1)} %get-tuple-element.65), channel_id=1, source_target_pairs={{1,3},{2,0},{0,1},{3,2},{5,7},{6,4},{4,5},{7,6},{9,11},{10,8},{8,9... | collective-permute-start | bytes 442376 | tf_op jit(solution)/shard_map/ppermute | solution.py:328
  64.2 10.3 %collective-permute-start.16 = (bf16[144,512]{1,0:T(8,128)(2,1)S(1)}, bf16[144,512]{1,0:T(8,128)(2,1)S(1)}, u32[]{:S(2)}, u32[]{:S(2)}) collective-permute-start(bf16[144,512]{1,0:T(8,128)(2,1)S(1)} %get-tuple-element.66), channel_id=1, source_target_pairs={{1,3},{2,0},{0,1},{3,2},{5,7},{6,4},{4,5},{7,6},{9,11},{10,8},{8,9... | collective-permute-start | bytes 442376 | tf_op jit(solution)/shard_map/ppermute | solution.py:328
  64.3 12.5 %collective-permute-start.17 = (bf16[144,512]{1,0:T(8,128)(2,1)S(1)}, bf16[144,512]{1,0:T(8,128)(2,1)S(1)}, u32[]{:S(2)}, u32[]{:S(2)}) collective-permute-start(bf16[144,512]{1,0:T(8,128)(2,1)S(1)} %get-tuple-element.67), channel_id=1, source_target_pairs={{1,2},{2,1},{0,0},{3,3},{5,6},{6,5},{4,4},{7,7},{9,10},{10,9},{8,8... | collective-permute-start | bytes 442376 | tf_op jit(solution)/shard_map/ppermute | solution.py:328
  68.8 10.2 %collective-permute-start.18 = (bf16[144,512]{1,0:T(8,128)(2,1)S(1)}, bf16[144,512]{1,0:T(8,128)(2,1)S(1)}, u32[]{:S(2)}, u32[]{:S(2)}) collective-permute-start(bf16[144,512]{1,0:T(8,128)(2,1)S(1)} %get-tuple-element.68), channel_id=1, source_target_pairs={{1,2},{2,1},{0,0},{3,3},{5,6},{6,5},{4,4},{7,7},{9,10},{10,9},{8,8... | collective-permute-start | bytes 442376 | tf_op jit(solution)/shard_map/ppermute | solution.py:328

commit v15 on v13

--- a/solution.py
+++ b/solution.py
@@ -296,12 +296,15 @@
 def total_kernel(begin, parts, kept, *rest):
     nears, fars, (out, summed, sem) = rest[:parts], rest[parts : 2 * parts], rest[-3:]
     size = kept.shape[0] // parts
+    copies = []
     for k, (near, far) in enumerate(zip(nears, fars)):
         at = slice(k * size, (k + 1) * size)
         summed[at, :] = kept[at, :] + near[...].astype(F32) + far[...].astype(F32)
-    copy = pltpu.make_async_copy(summed, out.at[0, :, begin : begin + kept.shape[1]], sem)
-    copy.start()
-    copy.wait()
+        target = out.at[0, at, begin : begin + kept.shape[1]]
+        copies.append(pltpu.make_async_copy(summed.at[at, :], target, sem.at[k]))
+        copies[-1].start()
+    for copy in copies:
+        copy.wait()
 
 
 def total(begin, width, kept, nears, fars, held):
@@ -311,7 +314,7 @@
         out_shape=jax.ShapeDtypeStruct((1, depth, width), F32),
         in_specs=spaces(1 + 2 * parts) + [IN_HBM] * len(held[:1]) + spaces(len(held[1:])),
         out_specs=IN_HBM,
-        scratch_shapes=[pltpu.VMEM(kept.shape, F32), pltpu.SemaphoreType.DMA],
+        scratch_shapes=[pltpu.VMEM(kept.shape, F32), pltpu.SemaphoreType.DMA((parts,))],
         input_output_aliases={1 + 2 * parts: 0} if held else {},
         compiler_params=params(),
         cost_estimate=cost(),

time: 78.9 us -> 78.9 us (level)
  no operation moved by 1% of the time
where the time goes in v15:
time: 78.9 us; the launch traced here: 78.6 us
  waiting for transfers between devices  36.7 us (47%)
  starting transfers between devices  27 us (34%)
  Pallas kernels  10.6 us (13%)
  local copies, waits for them, and re-layouts  2.21 us (3%)
  between operations  2.14 us (3%)
    ppermute x12, waiting for transfers between devices, along(): return lax.ppermute(value, 'fsdp', pairs)  29.6 us
    ppermute x12, starting transfers between devices, along(): return lax.ppermute(value, 'fsdp', pairs)  22.8 us
    ppermute x3, waiting for transfers between devices, shifted(): lax.ppermute(value, 'dp', [(d, (d + by) % n_dp) for d in range(n_dp)])  4.73 us
    pallas_call x1, Pallas kernels, picture_side(): pl.pallas_call(picture_kernel, out_shape=outs, in_specs=spaces(13), out_s...  3.17 us
    pallas_call x1, Pallas kernels, text_side(): pl.pallas_call(text_kernel, out_shape=(jax.ShapeDtypeStruct((rows, width)...  2.76 us
    ppermute x3, starting transfers between devices, shifted(): lax.ppermute(value, 'dp', [(d, (d + by) % n_dp) for d in range(n_dp)])  2.61 us
    unnamed x10, local copies, waits for them, and re-layouts  2.16 us
    pallas_call x2, Pallas kernels, total(): pl.pallas_call(functools.partial(total_kernel, begin, parts), out_shape=j...  1.84 us
  transfers between devices with their start and end apart: 23, of which 10 were waited for; matrix products, arithmetic and copies ran while one was open for 0% of the time, Pallas kernels for 12%

profile of v15, /device:TPU:18, one launch (start us, length us, event | category | flops | bytes accessed | tf_op | source)
XLA Modules:
  0.0 78.6 jit_solution(379554423555310895)
XLA Ops:
  0.6 1.1 %copy-done = bf16[288,1152]{1,0:T(8,128)(2,1)S(1)} copy-done((bf16[288,1152]{1,0:T(8,128)(2,1)S(1)}, bf16[288,1152]{1,0:T(8,128)(2,1)}, u32[]{:S(2)}) %copy-start) | copy-done | bytes 663576
  2.1 1.5 %collective-permute-start.4 = (bf16[256,1152]{1,0:T(8,128)(2,1)}, bf16[256,1152]{1,0:T(8,128)(2,1)S(1)}, u32[]{:S(2)}, u32[]{:S(2)}) collective-permute-start(bf16[256,1152]{1,0:T(8,128)(2,1)} %text), channel_id=1, source_target_pairs={{0,8},{4,12},{8,16},{12,20},{16,24},{20,28},{24,0},{28,4},{1,9},{5... | collective-permute-start | bytes 1769480 | tf_op jit(solution)/shard_map/ppermute | solution.py:337
  4.0 2.7 %collective-permute-start.1 = (bf16[144,1152]{1,0:T(8,128)(2,1)S(1)}, bf16[144,1152]{1,0:T(8,128)(2,1)S(1)}, u32[]{:S(2)}, u32[]{:S(2)}) collective-permute-start(bf16[144,1152]{1,0:T(8,128)(2,1)S(1)} %get-tuple-element.41), channel_id=1, source_target_pairs={{0,3},{1,0},{2,1},{3,2},{4,7},{5,4},{6,5},{7,6},{8,11},{9,8},{10,9... | collective-permute-start | bytes 995336 | tf_op jit(solution)/shard_map/ppermute | solution.py:331
  6.7 1.1 %copy-done.2 = bf16[256,1152]{1,0:T(8,128)(2,1)S(1)} copy-done((bf16[256,1152]{1,0:T(8,128)(2,1)S(1)}, bf16[256,1152]{1,0:T(8,128)(2,1)}, u32[]{:S(2)}) %copy-start.2) | copy-done | bytes 589848
  8.0 4.7 %collective-permute-done.3.rest_2_ = bf16[80,1152]{1,0:T(8,128)(2,1)S(1)} collective-permute-done((bf16[80,1152]{1,0:T(8,128)(2,1)S(1)}, bf16[80,1152]{1,0:T(8,128)(2,1)S(1)}, u32[]{:S(2)}, u32[]{:S(2)}) %collective-permute-start.3) | collective-permute-done | bytes 184352 | tf_op jit(solution)/shard_map/ppermute | solution.py:331
  12.7 4.7 %collective-permute-done.4.t2 = bf16[256,1152]{1,0:T(8,128)(2,1)S(1)} collective-permute-done((bf16[256,1152]{1,0:T(8,128)(2,1)}, bf16[256,1152]{1,0:T(8,128)(2,1)S(1)}, u32[]{:S(2)}, u32[]{:S(2)}) %collective-permute-start.4) | collective-permute-done | bytes 589856 | tf_op jit(solution)/shard_map/ppermute | solution.py:337
  17.6 0.5 collective-permute-start.5
  18.1 5.9 %collective-permute-start.12 = (bf16[864,256]{1,0:T(8,128)(2,1)S(1)}, bf16[864,256]{1,0:T(8,128)(2,1)S(1)}, u32[]{:S(2)}, u32[]{:S(2)}) collective-permute-start(bf16[864,256]{1,0:T(8,128)(2,1)S(1)} %get-tuple-element.57), channel_id=1, source_target_pairs={{0,1},{1,0},{2,3},{3,2},{4,5},{5,4},{6,7},{7,6},{8,9},{9,8},{10,11... | collective-permute-start | bytes 1327112 | tf_op jit(solution)/shard_map/ppermute | solution.py:331
  24.0 0.5 collective-permute-start.7
  25.8 0.7 prepare.1
  26.5 2.3 %collective-permute-done.rest_0_ = bf16[144,1152]{1,0:T(8,128)(2,1)S(1)} collective-permute-done((bf16[144,1152]{1,0:T(8,128)(2,1)S(1)}, bf16[144,1152]{1,0:T(8,128)(2,1)S(1)}, u32[]{:S(2)}, u32[]{:S(2)}) %collective-permute-start) | collective-permute-done | bytes 331808 | tf_op jit(solution)/shard_map/ppermute | solution.py:331
  29.4 0.9 %collective-permute-done.7.rest_3_ = bf16[80,1152]{1,0:T(8,128)(2,1)S(1)} collective-permute-done((bf16[80,1152]{1,0:T(8,128)(2,1)S(1)}, bf16[80,1152]{1,0:T(8,128)(2,1)S(1)}, u32[]{:S(2)}, u32[]{:S(2)}) %collective-permute-start.7) | collective-permute-done | bytes 184352 | tf_op jit(solution)/shard_map/ppermute | solution.py:349
  30.3 0.9 %collective-permute-done.10.rest_6_ = bf16[80,1152]{1,0:T(8,128)(2,1)S(1)} collective-permute-done((bf16[80,1152]{1,0:T(8,128)(2,1)S(1)}, bf16[80,1152]{1,0:T(8,128)(2,1)S(1)}, u32[]{:S(2)}, u32[]{:S(2)}) %collective-permute-start.10) | collective-permute-done | bytes 184352 | tf_op jit(solution)/shard_map/ppermute | solution.py:334
  31.2 0.5 collective-permute-done.11.rest_7_
  31.7 3.2 %picture_side.1 = (bf16[288,512]{1,0:T(8,128)(2,1)S(1)}, bf16[288,640]{1,0:T(8,128)(2,1)S(1)}, bf16[256,1152]{1,0:T(8,128)(2,1)S(1)}, bf16[256,1152]{1,0:T(8,128)(2,1)S(1)}) custom-call(bf16[256,1152]{1,0:T(8,128)(2,1)S(1)} %copy-done.3, bf16[1152,256]{1,0:T(8,128)(2,1)S(1)} %get-tuple-element.49.x_t, bf16[768,1152]{1,0:T(8,128)(2,1)S(1)} %get-tuple-element.50.units, ...), custom_call_target="tpu_custom_call" | custom-call | tf_op jit(solution)/shard_map/picture_side/pallas_call | solution.py:206
  34.9 1.2 %collective-permute-start.13 = (bf16[288,512]{1,0:T(8,128)(2,1)S(1)}, bf16[288,512]{1,0:T(8,128)(2,1)S(1)}, u32[]{:S(2)}, u32[]{:S(2)}) collective-permute-start(bf16[288,512]{1,0:T(8,128)(2,1)S(1)} %get-tuple-element.62), channel_id=1, source_target_pairs={{0,1},{1,0},{2,3},{3,2},{4,5},{5,4},{6,7},{7,6},{8,9},{9,8},{10,11... | collective-permute-start | bytes 884744 | tf_op jit(solution)/shard_map/ppermute | solution.py:331
  36.2 0.5 collective-permute-start.22
  36.7 0.5 collective-permute-start.21
  37.2 6.8 %collective-permute-done.13.arrived = bf16[288,512]{1,0:T(8,128)(2,1)S(1)} collective-permute-done((bf16[288,512]{1,0:T(8,128)(2,1)S(1)}, bf16[288,512]{1,0:T(8,128)(2,1)S(1)}, u32[]{:S(2)}, u32[]{:S(2)}) %collective-permute-start.13) | collective-permute-done | bytes 294944 | tf_op jit(solution)/shard_map/ppermute | solution.py:331
  44.1 1.1 %collective-permute-start.14 = (bf16[288,640]{1,0:T(8,128)(2,1)S(1)}, bf16[288,640]{1,0:T(8,128)(2,1)S(1)}, u32[]{:S(2)}, u32[]{:S(2)}) collective-permute-start(bf16[288,640]{1,0:T(8,128)(2,1)S(1)} %get-tuple-element.63), channel_id=1, source_target_pairs={{0,1},{1,0},{2,3},{3,2},{4,5},{5,4},{6,7},{7,6},{8,9},{9,8},{10,11... | collective-permute-start | bytes 1105928 | tf_op jit(solution)/shard_map/ppermute | solution.py:331
  45.1 0.6 pair_product.3
  45.9 3.9 %collective-permute-start.20 = (bf16[288,512]{1,0:T(8,128)(2,1)S(1)}, bf16[288,512]{1,0:T(8,128)(2,1)S(1)}, u32[]{:S(2)}, u32[]{:S(2)}) collective-permute-start(bf16[288,512]{1,0:T(8,128)(2,1)S(1)} %get-tuple-element.72), channel_id=1, source_target_pairs={{1,2},{2,1},{0,0},{3,3},{5,6},{6,5},{4,4},{7,7},{9,10},{10,9},{8,8... | collective-permute-start | bytes 884744 | tf_op jit(solution)/shard_map/ppermute | solution.py:331
  49.8 8.9 %collective-permute-done.14.arrived = bf16[288,640]{1,0:T(8,128)(2,1)S(1)} collective-permute-done((bf16[288,640]{1,0:T(8,128)(2,1)S(1)}, bf16[288,640]{1,0:T(8,128)(2,1)S(1)}, u32[]{:S(2)}, u32[]{:S(2)}) %collective-permute-start.14) | collective-permute-done | bytes 368672 | tf_op jit(solution)/shard_map/ppermute | solution.py:331
  58.7 0.9 %pair_product.2 = (f32[288,640]{1,0:T(8,128)S(1)}, bf16[144,640]{1,0:T(8,128)(2,1)S(1)}, bf16[144,640]{1,0:T(8,128)(2,1)S(1)}, bf16[144,640]{1,0:T(8,128)(2,1)S(1)}, bf16[144,640]{1,0:T(8,128)(2,1)S(1)}) custom-call(bf16[1152,256]{1,0:T(8,128)(2,1)S(1)} %get-tuple-element.49.x_t, bf16[864,256]{1,0:T(8,128)(2,1)S(1)} %collective-permute-done.12.far_t, ...), custom_call_target="tpu_custom_call" | custom-call | tf_op jit(solution)/shard_map/pair_product/pallas_call | solution.py:285
  59.6 1.6 %collective-permute-start.15 = (bf16[144,640]{1,0:T(8,128)(2,1)S(1)}, bf16[144,640]{1,0:T(8,128)(2,1)S(1)}, u32[]{:S(2)}, u32[]{:S(2)}) collective-permute-start(bf16[144,640]{1,0:T(8,128)(2,1)S(1)} %get-tuple-element.65), channel_id=1, source_target_pairs={{1,3},{2,0},{0,1},{3,2},{5,7},{6,4},{4,5},{7,6},{9,11},{10,8},{8,9... | collective-permute-start | bytes 552968 | tf_op jit(solution)/shard_map/ppermute | solution.py:331
  61.3 3.7 %collective-permute-start.17 = (bf16[144,640]{1,0:T(8,128)(2,1)S(1)}, bf16[144,640]{1,0:T(8,128)(2,1)S(1)}, u32[]{:S(2)}, u32[]{:S(2)}) collective-permute-start(bf16[144,640]{1,0:T(8,128)(2,1)S(1)} %get-tuple-element.67), channel_id=1, source_target_pairs={{1,2},{2,1},{0,0},{3,3},{5,6},{6,5},{4,4},{7,7},{9,10},{10,9},{8,8... | collective-permute-start | bytes 552968 | tf_op jit(solution)/shard_map/ppermute | solution.py:331
  65.1 2.1 %collective-permute-start.18 = (bf16[144,640]{1,0:T(8,128)(2,1)S(1)}, bf16[144,640]{1,0:T(8,128)(2,1)S(1)}, u32[]{:S(2)}, u32[]{:S(2)}) collective-permute-start(bf16[144,640]{1,0:T(8,128)(2,1)S(1)} %get-tuple-element.68), channel_id=1, source_target_pairs={{1,2},{2,1},{0,0},{3,3},{5,6},{6,5},{4,4},{7,7},{9,10},{10,9},{8,8... | collective-permute-start | bytes 552968 | tf_op jit(solution)/shard_map/ppermute | solution.py:331
  67.2 2.8 %text_side.1 = (f32[256,1152]{1,0:T(8,128)}, f32[8,128]{1,0:T(8,128)S(1)}) custom-call(bf16[256,1152]{1,0:T(8,128)(2,1)S(1)} %copy-done.4, f32[8,128]{1,0:T(8,128)S(1)} %get-tuple-element.51.scalars, bf16[256,1152]{1,0:T(8,128)(2,1)S(1)} %get-tuple-element.73.u0, bf16[256,1152]{1,0:T(8,128)(2,1)S(1)} %collective-permute-done.21.u1, ...), custom_call_target="tpu_custom_call" | custom-call | tf_op jit(solution)/shard_map/text_side/pallas_call | solution.py:238
  70.0 0.9 %total.2.rest_4_ = f32[1,288,1152]{2,1,0:T(8,128)} custom-call(f32[288,512]{1,0:T(8,128)S(1)} %get-tuple-element.70.kept, bf16[288,512]{1,0:T(8,128)(2,1)S(1)} %collective-permute-done.19.rest_0_, bf16[288,512]{1,0:T(8,128)(2,1)S(1)} %collective-permute-done.20.rest_1_), custom_call_target="tpu_custom_call" | custom-call | tf_op jit(solution)/shard_map/total/pallas_call | solution.py:312
  70.9 4.8 %collective-permute-done.17.rest_2_ = bf16[144,640]{1,0:T(8,128)(2,1)S(1)} collective-permute-done((bf16[144,640]{1,0:T(8,128)(2,1)S(1)}, bf16[144,640]{1,0:T(8,128)(2,1)S(1)}, u32[]{:S(2)}, u32[]{:S(2)}) %collective-permute-start.17) | collective-permute-done | bytes 184352 | tf_op jit(solution)/shard_map/ppermute | solution.py:331
  75.7 2.0 %collective-permute-done.18.rest_3_ = bf16[144,640]{1,0:T(8,128)(2,1)S(1)} collective-permute-done((bf16[144,640]{1,0:T(8,128)(2,1)S(1)}, bf16[144,640]{1,0:T(8,128)(2,1)S(1)}, u32[]{:S(2)}, u32[]{:S(2)}) %collective-permute-start.18) | collective-permute-done | bytes 184352 | tf_op jit(solution)/shard_map/ppermute | solution.py:331
  77.7 0.9 %total.3 = f32[1,288,1152]{2,1,0:T(8,128)} custom-call(f32[288,640]{1,0:T(8,128)S(1)} %get-tuple-element.64.kept, bf16[144,640]{1,0:T(8,128)(2,1)S(1)} %collective-permute-done.15.rest_0_, bf16[144,640]{1,0:T(8,128)(2,1)S(1)} %collective-permute-done.16.rest_1_, ...), custom_call_target="tpu_custom_call", output_to_operand_aliasing={{}: (5, {})} | custom-call | tf_op jit(solution)/shard_map/total/pallas_call | solution.py:312
  (34 shorter events, 1.8 us)
Async XLA Ops:
  0.6 1.1 %copy-start = (bf16[288,1152]{1,0:T(8,128)(2,1)S(1)}, bf16[288,1152]{1,0:T(8,128)(2,1)}, u32[]{:S(2)}) copy-start(bf16[288,1152]{1,0:T(8,128)(2,1)} %own.3) | copy-start | bytes 1990660
  1.7 24.1 %copy-start.4 = (bf16[256,1152]{1,0:T(8,128)(2,1)S(1)}, bf16[256,1152]{1,0:T(8,128)(2,1)}, u32[]{:S(2)}) copy-start(bf16[256,1152]{1,0:T(8,128)(2,1)} %text) | copy-start | bytes 1769476
  2.1 15.3 %collective-permute-start.4 = (bf16[256,1152]{1,0:T(8,128)(2,1)}, bf16[256,1152]{1,0:T(8,128)(2,1)S(1)}, u32[]{:S(2)}, u32[]{:S(2)}) collective-permute-start(bf16[256,1152]{1,0:T(8,128)(2,1)} %text), channel_id=1, source_target_pairs={{0,8},{4,12},{8,16},{12,20},{16,24},{20,28},{24,0},{28,4},{1,9},{5... | collective-permute-start | bytes 1769480 | tf_op jit(solution)/shard_map/ppermute | solution.py:337
  3.6 9.1 %collective-permute-start.3 = (bf16[80,1152]{1,0:T(8,128)(2,1)S(1)}, bf16[80,1152]{1,0:T(8,128)(2,1)S(1)}, u32[]{:S(2)}, u32[]{:S(2)}) collective-permute-start(bf16[80,1152]{1,0:T(8,128)(2,1)S(1)} %get-tuple-element.43), channel_id=1, source_target_pairs={{0,2},{1,3},{2,0},{3,1},{4,6},{5,7},{6,4},{7,5},{8,10},{9,11},{10,... | collective-permute-start | bytes 552968 | tf_op jit(solution)/shard_map/ppermute | solution.py:331
  4.0 22.5 %collective-permute-start.1 = (bf16[144,1152]{1,0:T(8,128)(2,1)S(1)}, bf16[144,1152]{1,0:T(8,128)(2,1)S(1)}, u32[]{:S(2)}, u32[]{:S(2)}) collective-permute-start(bf16[144,1152]{1,0:T(8,128)(2,1)S(1)} %get-tuple-element.41), channel_id=1, source_target_pairs={{0,3},{1,0},{2,1},{3,2},{4,7},{5,4},{6,5},{7,6},{8,11},{9,8},{10,9... | collective-permute-start | bytes 995336 | tf_op jit(solution)/shard_map/ppermute | solution.py:331
  6.7 22.2 %collective-permute-start = (bf16[144,1152]{1,0:T(8,128)(2,1)S(1)}, bf16[144,1152]{1,0:T(8,128)(2,1)S(1)}, u32[]{:S(2)}, u32[]{:S(2)}) collective-permute-start(bf16[144,1152]{1,0:T(8,128)(2,1)S(1)} %get-tuple-element.41), channel_id=1, source_target_pairs={{0,1},{1,2},{2,3},{3,0},{4,5},{5,6},{6,7},{7,4},{8,9},{9,10},{10,1... | collective-permute-start | bytes 995336 | tf_op jit(solution)/shard_map/ppermute | solution.py:331
  6.7 11.4 %collective-permute-start.2 = (bf16[256,1152]{1,0:T(8,128)(2,1)}, bf16[256,1152]{1,0:T(8,128)(2,1)S(1)}, u32[]{:S(2)}, u32[]{:S(2)}) collective-permute-start(bf16[256,1152]{1,0:T(8,128)(2,1)} %text), channel_id=1, source_target_pairs={{0,4},{4,0},{8,12},{12,8},{16,20},{20,16},{24,28},{28,24},{1,5},{5... | collective-permute-start | bytes 1769480 | tf_op jit(solution)/shard_map/ppermute | solution.py:334
  6.7 1.1 %copy-start.2 = (bf16[256,1152]{1,0:T(8,128)(2,1)S(1)}, bf16[256,1152]{1,0:T(8,128)(2,1)}, u32[]{:S(2)}) copy-start(bf16[256,1152]{1,0:T(8,128)(2,1)} %x.3) | copy-start | bytes 1769476
  17.5 14.3 %copy-start.1 = (bf16[288,1152]{1,0:T(8,128)(2,1)S(1)}, bf16[288,1152]{1,0:T(8,128)(2,1)}, u32[]{:S(2)}) copy-start(bf16[288,1152]{1,0:T(8,128)(2,1)} %own.3) | copy-start | bytes 1990660
  17.5 14.3 %copy-start.3 = (bf16[256,1152]{1,0:T(8,128)(2,1)S(1)}, bf16[256,1152]{1,0:T(8,128)(2,1)}, u32[]{:S(2)}) copy-start(bf16[256,1152]{1,0:T(8,128)(2,1)} %x.3) | copy-start | bytes 1769476
  17.5 6.5 %collective-permute-start.6 = (bf16[128,1152]{1,0:T(8,128)(2,1)S(1)}, bf16[128,1152]{1,0:T(8,128)(2,1)S(1)}, u32[]{:S(2)}, u32[]{:S(2)}) collective-permute-start(bf16[128,1152]{1,0:T(8,128)(2,1)S(1)} %get-tuple-element.76), channel_id=1, source_target_pairs={{0,4},{4,0},{8,12},{12,8},{16,20},{20,16},{24,28},{28,24},{1,5},{5... | collective-permute-start | bytes 884744 | tf_op jit(solution)/shard_map/ppermute | solution.py:334
  17.6 8.2 %collective-permute-start.5 = (bf16[128,1152]{1,0:T(8,128)(2,1)S(1)}, bf16[128,1152]{1,0:T(8,128)(2,1)S(1)}, u32[]{:S(2)}, u32[]{:S(2)}) collective-permute-start(bf16[128,1152]{1,0:T(8,128)(2,1)S(1)} %get-tuple-element.77), channel_id=1, source_target_pairs={{0,4},{4,0},{8,12},{12,8},{16,20},{20,16},{24,28},{28,24},{1,5},{5... | collective-permute-start | bytes 884744 | tf_op jit(solution)/shard_map/ppermute | solution.py:334
  18.1 16.8 %collective-permute-start.12 = (bf16[864,256]{1,0:T(8,128)(2,1)S(1)}, bf16[864,256]{1,0:T(8,128)(2,1)S(1)}, u32[]{:S(2)}, u32[]{:S(2)}) collective-permute-start(bf16[864,256]{1,0:T(8,128)(2,1)S(1)} %get-tuple-element.57), channel_id=1, source_target_pairs={{0,1},{1,0},{2,3},{3,2},{4,5},{5,4},{6,7},{7,6},{8,9},{9,8},{10,11... | collective-permute-start | bytes 1327112 | tf_op jit(solution)/shard_map/ppermute | solution.py:331
  24.0 6.3 %collective-permute-start.7 = (bf16[80,1152]{1,0:T(8,128)(2,1)S(1)}, bf16[80,1152]{1,0:T(8,128)(2,1)S(1)}, u32[]{:S(2)}, u32[]{:S(2)}) collective-permute-start(bf16[80,1152]{1,0:T(8,128)(2,1)S(1)} %collective-permute-done.3.rest_2_), channel_id=1, source_target_pairs={{0,8},{4,12},{8,0},{12,4},{16,24},{20,28},{24,16},{28,20},{1,9},{5... | collective-permute-start | bytes 552968 | tf_op jit(solution)/shard_map/ppermute | solution.py:349
  28.8 2.9 %collective-permute-start.8 = (bf16[144,1152]{1,0:T(8,128)(2,1)S(1)}, bf16[144,1152]{1,0:T(8,128)(2,1)S(1)}, u32[]{:S(2)}, u32[]{:S(2)}) collective-permute-start(bf16[144,1152]{1,0:T(8,128)(2,1)S(1)} %collective-permute-done.rest_0_), channel_id=1, source_target_pairs={{0,4},{4,0},{8,12},{12,8},{16,20},{20,16},{24,28},{28,24},{1,5},{5... | collective-permute-start | bytes 995336 | tf_op jit(solution)/shard_map/ppermute | solution.py:334
  28.9 2.9 %collective-permute-start.9 = (bf16[144,1152]{1,0:T(8,128)(2,1)S(1)}, bf16[144,1152]{1,0:T(8,128)(2,1)S(1)}, u32[]{:S(2)}, u32[]{:S(2)}) collective-permute-start(bf16[144,1152]{1,0:T(8,128)(2,1)S(1)} %collective-permute-done.1.rest_1_), channel_id=1, source_target_pairs={{0,4},{4,0},{8,12},{12,8},{16,20},{20,16},{24,28},{28,24},{1,5},{5... | collective-permute-start | bytes 995336 | tf_op jit(solution)/shard_map/ppermute | solution.py:334
  29.4 1.9 %collective-permute-start.10 = (bf16[80,1152]{1,0:T(8,128)(2,1)S(1)}, bf16[80,1152]{1,0:T(8,128)(2,1)S(1)}, u32[]{:S(2)}, u32[]{:S(2)}) collective-permute-start(bf16[80,1152]{1,0:T(8,128)(2,1)S(1)} %collective-permute-done.3.rest_2_), channel_id=1, source_target_pairs={{0,4},{4,0},{8,12},{12,8},{16,20},{20,16},{24,28},{28,24},{1,5},{5... | collective-permute-start | bytes 552968 | tf_op jit(solution)/shard_map/ppermute | solution.py:334
  30.3 1.4 %collective-permute-start.11 = (bf16[80,1152]{1,0:T(8,128)(2,1)S(1)}, bf16[80,1152]{1,0:T(8,128)(2,1)S(1)}, u32[]{:S(2)}, u32[]{:S(2)}) collective-permute-start(bf16[80,1152]{1,0:T(8,128)(2,1)S(1)} %collective-permute-done.7.rest_3_), channel_id=1, source_target_pairs={{0,4},{4,0},{8,12},{12,8},{16,20},{20,16},{24,28},{28,24},{1,5},{5... | collective-permute-start | bytes 552968 | tf_op jit(solution)/shard_map/ppermute | solution.py:334
  34.9 9.1 %collective-permute-start.13 = (bf16[288,512]{1,0:T(8,128)(2,1)S(1)}, bf16[288,512]{1,0:T(8,128)(2,1)S(1)}, u32[]{:S(2)}, u32[]{:S(2)}) collective-permute-start(bf16[288,512]{1,0:T(8,128)(2,1)S(1)} %get-tuple-element.62), channel_id=1, source_target_pairs={{0,1},{1,0},{2,3},{3,2},{4,5},{5,4},{6,7},{7,6},{8,9},{9,8},{10,11... | collective-permute-start | bytes 884744 | tf_op jit(solution)/shard_map/ppermute | solution.py:331
  36.2 25.0 %collective-permute-start.22 = (bf16[256,1152]{1,0:T(8,128)(2,1)S(1)}, bf16[256,1152]{1,0:T(8,128)(2,1)S(1)}, u32[]{:S(2)}, u32[]{:S(2)}) collective-permute-start(bf16[256,1152]{1,0:T(8,128)(2,1)S(1)} %get-tuple-element.73.u0), channel_id=1, source_target_pairs={{0,24},{4,28},{8,0},{12,4},{16,8},{20,12},{24,16},{28,20},{1,25},{... | collective-permute-start | bytes 1769480 | tf_op jit(solution)/shard_map/ppermute | solution.py:337
  36.7 24.6 %collective-permute-start.21 = (bf16[256,1152]{1,0:T(8,128)(2,1)S(1)}, bf16[256,1152]{1,0:T(8,128)(2,1)S(1)}, u32[]{:S(2)}, u32[]{:S(2)}) collective-permute-start(bf16[256,1152]{1,0:T(8,128)(2,1)S(1)} %get-tuple-element.73.u0), channel_id=1, source_target_pairs={{0,28},{4,0},{8,4},{12,8},{16,12},{20,16},{24,20},{28,24},{1,29},{... | collective-permute-start | bytes 1769480 | tf_op jit(solution)/shard_map/ppermute | solution.py:337
  44.1 14.6 %collective-permute-start.14 = (bf16[288,640]{1,0:T(8,128)(2,1)S(1)}, bf16[288,640]{1,0:T(8,128)(2,1)S(1)}, u32[]{:S(2)}, u32[]{:S(2)}) collective-permute-start(bf16[288,640]{1,0:T(8,128)(2,1)S(1)} %get-tuple-element.63), channel_id=1, source_target_pairs={{0,1},{1,0},{2,3},{3,2},{4,5},{5,4},{6,7},{7,6},{8,9},{9,8},{10,11... | collective-permute-start | bytes 1105928 | tf_op jit(solution)/shard_map/ppermute | solution.py:331
  45.8 19.3 %collective-permute-start.19 = (bf16[288,512]{1,0:T(8,128)(2,1)S(1)}, bf16[288,512]{1,0:T(8,128)(2,1)S(1)}, u32[]{:S(2)}, u32[]{:S(2)}) collective-permute-start(bf16[288,512]{1,0:T(8,128)(2,1)S(1)} %get-tuple-element.71), channel_id=1, source_target_pairs={{1,3},{2,0},{0,1},{3,2},{5,7},{6,4},{4,5},{7,6},{9,11},{10,8},{8,9... | collective-permute-start | bytes 884744 | tf_op jit(solution)/shard_map/ppermute | solution.py:331
  45.9 24.1 %collective-permute-start.20 = (bf16[288,512]{1,0:T(8,128)(2,1)S(1)}, bf16[288,512]{1,0:T(8,128)(2,1)S(1)}, u32[]{:S(2)}, u32[]{:S(2)}) collective-permute-start(bf16[288,512]{1,0:T(8,128)(2,1)S(1)} %get-tuple-element.72), channel_id=1, source_target_pairs={{1,2},{2,1},{0,0},{3,3},{5,6},{6,5},{4,4},{7,7},{9,10},{10,9},{8,8... | collective-permute-start | bytes 884744 | tf_op jit(solution)/shard_map/ppermute | solution.py:331
  59.6 11.3 %collective-permute-start.15 = (bf16[144,640]{1,0:T(8,128)(2,1)S(1)}, bf16[144,640]{1,0:T(8,128)(2,1)S(1)}, u32[]{:S(2)}, u32[]{:S(2)}) collective-permute-start(bf16[144,640]{1,0:T(8,128)(2,1)S(1)} %get-tuple-element.65), channel_id=1, source_target_pairs={{1,3},{2,0},{0,1},{3,2},{5,7},{6,4},{4,5},{7,6},{9,11},{10,8},{8,9... | collective-permute-start | bytes 552968 | tf_op jit(solution)/shard_map/ppermute | solution.py:331
  61.2 9.7 %collective-permute-start.16 = (bf16[144,640]{1,0:T(8,128)(2,1)S(1)}, bf16[144,640]{1,0:T(8,128)(2,1)S(1)}, u32[]{:S(2)}, u32[]{:S(2)}) collective-permute-start(bf16[144,640]{1,0:T(8,128)(2,1)S(1)} %get-tuple-element.66), channel_id=1, source_target_pairs={{1,3},{2,0},{0,1},{3,2},{5,7},{6,4},{4,5},{7,6},{9,11},{10,8},{8,9... | collective-permute-start | bytes 552968 | tf_op jit(solution)/shard_map/ppermute | solution.py:331
  61.3 14.4 %collective-permute-start.17 = (bf16[144,640]{1,0:T(8,128)(2,1)S(1)}, bf16[144,640]{1,0:T(8,128)(2,1)S(1)}, u32[]{:S(2)}, u32[]{:S(2)}) collective-permute-start(bf16[144,640]{1,0:T(8,128)(2,1)S(1)} %get-tuple-element.67), channel_id=1, source_target_pairs={{1,2},{2,1},{0,0},{3,3},{5,6},{6,5},{4,4},{7,7},{9,10},{10,9},{8,8... | collective-permute-start | bytes 552968 | tf_op jit(solution)/shard_map/ppermute | solution.py:331
  65.1 12.6 %collective-permute-start.18 = (bf16[144,640]{1,0:T(8,128)(2,1)S(1)}, bf16[144,640]{1,0:T(8,128)(2,1)S(1)}, u32[]{:S(2)}, u32[]{:S(2)}) collective-permute-start(bf16[144,640]{1,0:T(8,128)(2,1)S(1)} %get-tuple-element.68), channel_id=1, source_target_pairs={{1,2},{2,1},{0,0},{3,3},{5,6},{6,5},{4,4},{7,7},{9,10},{10,9},{8,8... | collective-permute-start | bytes 552968 | tf_op jit(solution)/shard_map/ppermute | solution.py:331
